TPU v7x, 32 devices: a whole 2x2x4 slice. The times are simulated.
32 devices in a mesh: seq: 4 (over y, x), fsdp: 8 (over z, core).
Axes of the slice: x: 2, y: 2, z: 4, core: 2. Of those that a mesh axis runs over, the one named last changes fastest.
Arguments:
- tokens: bfloat16 [2, 3072, 1600], P(None, ('seq', 'fsdp')), may hold values from -6 to 6
- cotangent: bfloat16 [2, 3072, 1600], P(None, ('seq', 'fsdp')), may hold values from -6 to 6
- route: int32 [2, 3072], P(None, 'seq'), may hold values from 0 to 767, as said below
- lengths: int32 [2, 8, 3], P(None, 'fsdp'), may hold values from 1 to 336, as said below
- gain_in: float32 [1600], replicated, may hold values from 0.5 to 1.5
- w_qkv: bfloat16 [1600, 2240], P('fsdp'), may hold values from -0.15625 to 0.15625
- w_mix_in: bfloat16 [1600, 6400], P('fsdp'), may hold values from -0.15625 to 0.15625
- w_x: bfloat16 [3200, 132], P('fsdp'), may hold values from -0.109375 to 0.109375
- w_dt: bfloat16 [3200, 100], P('fsdp'), may hold values from -0.625 to 0.625
- w_small: bfloat16 [3200, 23], P('fsdp'), may hold values from -10 to 3, as said below
- gain_att: float32 [1600], replicated, may hold values from 0.5 to 1.5
- gain_ssm: float32 [3200], replicated, may hold values from 0.5 to 1.5
- w_out_att: bfloat16 [1600, 1600], P('fsdp'), may hold values from -0.15625 to 0.15625
- w_out_ssm: bfloat16 [3200, 1600], P('fsdp'), may hold values from -0.109375 to 0.109375
- gain_ffn: float32 [1600], replicated, may hold values from 0.5 to 1.5
- w_gate: bfloat16 [1600, 5504], P('fsdp'), may hold values from -0.15625 to 0.15625
- w_up: bfloat16 [1600, 5504], P('fsdp'), may hold values from -0.15625 to 0.15625
- w_down: bfloat16 [5504, 1600], P('fsdp'), may hold values from -0.078125 to 0.078125
Outputs:
- output: bfloat16 [2, 3072, 1600], P(None, ('seq', 'fsdp'))
- grad_tokens: bfloat16 [2, 3072, 1600], P(None, ('seq', 'fsdp'))
- grad_gain_in: float32 [1600], replicated
- grad_w_qkv: float32 [1600, 2240], P('fsdp', 'seq')
- grad_w_mix_in: float32 [1600, 6400], P('fsdp', 'seq')
- grad_w_x: float32 [3200, 132], P('fsdp', 'seq')
- grad_w_dt: float32 [3200, 100], P('fsdp', 'seq')
- grad_w_small: float32 [3200, 23], P('fsdp')
- grad_dt_bias: float32 [3200], P('fsdp')
- grad_gain_att: float32 [1600], replicated
- grad_gain_ssm: float32 [3200], replicated
- grad_w_out_att: float32 [1600, 1600], P('fsdp', 'seq')
- grad_w_out_ssm: float32 [3200, 1600], P('fsdp', 'seq')
- grad_gain_ffn: float32 [1600], replicated
- grad_w_gate: float32 [1600, 5504], P('fsdp', 'seq')
- grad_w_up: float32 [1600, 5504], P('fsdp', 'seq')
- grad_w_down: float32 [5504, 1600], P('fsdp', 'seq')
- rms: float32 [6], replicated
Inputs may be any that keep to these rules, and one draw needn't show every extreme that they name: For each micro-batch and seq index, route maps the 768 rows of that slice one to one onto 0 to 767; of each run of 96 given rows, exactly 12 have route // 96 equal to each fsdp index. The 3 lengths of a pack sum to 384; one of them is 336. `w_small`: columns hold conv_w, conv_b, dt_bias, skip_d and log_a in this order.
All inputs are finite; a program needn't handle non-finite values.
Results may differ from a plain program's by a relative error of at most 0.02.
Values may be sent and summed in bfloat16 or wider, within the bound.
A program may use at most 448 MiB of HBM per device.

v0:
```python
from functools import partial

import jax
import jax.numpy as jnp
from jax import lax
from jax.sharding import PartitionSpec as P

D = 1600
HEADS = 25
KV_HEADS = 5
HEAD = 64
INNER = 3200
STATE = 16
CONV = 4
DT_RANK = 100
MICRO = 2
SCAN_BLOCK = 16
ATT = 1600
KV_WIDTH = 320


EPS = 1e-05


def passed_along(array, axis, by):
    size = lax.axis_size(axis)
    pairs = [(i, i + by) for i in range(size) if 0 <= i + by < size]
    return lax.ppermute(array, axis, pairs)


def prefix_2(array, axis, combine, identity, reverse):
    size, here = (lax.axis_size(axis), lax.axis_index(axis))
    everything = jax.tree.map(
        lambda part, kind: lax.all_gather(part.astype(kind), axis),
        array,
        (jnp.bfloat16, jnp.bfloat16),
    )
    start = jax.tree.map(
        lambda part, zero: jnp.broadcast_to(jnp.asarray(zero, part.dtype), part.shape),
        array,
        identity,
    )

    def hop(k, before):
        at = size - 1 - k if reverse else k
        reached = at > here if reverse else at < here
        new = combine(
            before, jax.tree.map(lambda part, own: part[at].astype(own.dtype), everything, array)
        )
        return jax.tree.map(lambda a, b: jnp.where(reached, a, b), new, before)

    return lax.fori_loop(0, size, hop, start)


def contract(left_op, right_op, left_dim, right_dim):
    return lax.dot_general(
        left_op,
        right_op,
        (((left_dim,), (right_dim,)), ((), ())),
        preferred_element_type=jnp.float32,
    )


def rms_scale(row_vals, gain_vec):
    return (
        row_vals * lax.rsqrt(jnp.mean(row_vals * row_vals, axis=-1, keepdims=True) + EPS) * gain_vec
    )


def seq_layout(seq_lens, span_len):
    places = jnp.arange(span_len, dtype=jnp.int32)
    seq_ends = jnp.cumsum(seq_lens)
    segment = jnp.sum((places[:, None] >= seq_ends[None, :]).astype(jnp.int32), axis=1)
    starts = seq_ends - seq_lens
    picked = (segment[:, None] == jnp.arange(seq_lens.shape[0], dtype=jnp.int32)[None, :]).astype(
        jnp.int32
    )
    position = places - jnp.sum(picked * starts[None, :], axis=1)
    return (segment, position)


def routing(route_row, tok_rows, fsdp_count, fsdp_rank):
    per_peer = tok_rows // fsdp_count
    target_dev = (route_row // tok_rows).reshape(fsdp_count, tok_rows)
    target_slot = (route_row % tok_rows).reshape(fsdp_count, tok_rows)
    peer_ids = jnp.arange(fsdp_count, dtype=jnp.int32)
    onehot = (target_dev[:, :, None] == peer_ids[None, None, :]).astype(jnp.int32)
    peer_rank = jnp.sum(jnp.cumsum(onehot, axis=1) * onehot, axis=2) - 1
    send_slot = target_dev * per_peer + peer_rank
    send_place = lax.dynamic_index_in_dim(send_slot, fsdp_rank, 0, keepdims=False)
    row_steps = jnp.arange(tok_rows, dtype=jnp.int32)
    send_index = jnp.zeros((tok_rows,), jnp.int32).at[send_place].set(row_steps)
    arrival = peer_ids[:, None] * per_peer + peer_rank
    to_me = target_dev == fsdp_rank
    own_index = (
        jnp.zeros((tok_rows,), jnp.int32)
        .at[jnp.where(to_me, target_slot, tok_rows).reshape(-1)]
        .set(arrival.reshape(-1), mode="drop")
    )
    recv_slot = (
        jnp.zeros((tok_rows,), jnp.int32)
        .at[jnp.where(to_me, arrival, tok_rows).reshape(-1)]
        .set(target_slot.reshape(-1), mode="drop")
    )
    return (send_index, own_index, recv_slot, send_place)


def deal(first_rows, second_rows):
    return (
        lax.all_to_all(first_rows, "fsdp", split_axis=0, concat_axis=0, tiled=True),
        lax.all_to_all(second_rows, "fsdp", split_axis=0, concat_axis=0, tiled=True),
    )


def mixer_weights(w_qkv, w_mix_in, w_x, w_dt, w_small, w_out_att, w_out_ssm):
    return (
        lax.all_gather(w_qkv, "fsdp", axis=0, tiled=True),
        lax.all_gather(w_mix_in, "fsdp", axis=0, tiled=True),
        lax.all_gather(w_x, "fsdp", axis=0, tiled=True),
        lax.all_gather(w_dt, "fsdp", axis=0, tiled=True),
        lax.all_gather(w_small, "fsdp", axis=0, tiled=True),
        lax.all_gather(w_out_att, "fsdp", axis=0, tiled=True),
        lax.all_gather(w_out_ssm, "fsdp", axis=0, tiled=True),
    )


def ffn_weights(w_gate, w_up, w_down):
    return (
        lax.all_gather(w_gate, "fsdp", axis=0, tiled=True),
        lax.all_gather(w_up, "fsdp", axis=0, tiled=True),
        lax.all_gather(w_down, "fsdp", axis=0, tiled=True),
    )


def scatter_rows(term_fn, shard_rows):
    return lax.psum_scatter(
        term_fn(jnp.int32(0), shard_rows * lax.axis_size("fsdp")).astype(jnp.bfloat16),
        "fsdp",
        scatter_dimension=0,
        tiled=True,
    ).astype(jnp.float32)


def slice_rows(whole, row_start, row_count):
    return whole


def row_term(left_op, right_op, factor):

    def term_fn(row_start, row_count):
        return factor * contract(left_op, right_op, 0, 0)

    return term_fn


def conv_act(position, ext_rows, tap_weights, tap_bias):
    row_count = position.shape[0]
    conv_sum = tap_bias[None, :] + jnp.zeros((row_count, ext_rows.shape[1]), jnp.float32)
    for tap_idx in range(CONV):
        shifted = ext_rows[CONV - 1 - tap_idx : CONV - 1 - tap_idx + row_count]
        conv_sum = (
            conv_sum
            + tap_weights[:, tap_idx][None, :]
            * shifted
            * (position >= tap_idx).astype(jnp.float32)[:, None]
        )
    return jax.nn.silu(conv_sum)


def combine(earlier_pair, later_pair):
    return (earlier_pair[0] * later_pair[0], later_pair[0] * earlier_pair[1] + later_pair[1])


def ssm_local(keep_mask, inner_u, step_dt, in_b, out_c, decay_a, start_state):

    def ssm_one_block(carry_state, pieces):

        def one_step(state_now, piece_now):
            u_now, dt_now, b_now, c_now, keep_now = piece_now
            state_now = (
                keep_now * jnp.exp(dt_now[:, None] * decay_a) * state_now
                + (dt_now * u_now)[:, None] * b_now[None, :]
            )
            return (state_now, jnp.sum(state_now * c_now[None, :], axis=1))

        return lax.scan(one_step, carry_state, pieces)

    row_count = inner_u.shape[0]
    shaped = tuple(
        (
            member.reshape((row_count // SCAN_BLOCK, SCAN_BLOCK) + member.shape[1:])
            for member in (inner_u, step_dt, in_b, out_c, keep_mask)
        )
    )
    end_state, core_rows = lax.scan(jax.checkpoint(ssm_one_block), start_state, shaped)
    return (core_rows.reshape(row_count, INNER), end_state)


def decay_sum(mask_rows, spread, left_rows, right_rows, decay_a):
    row_count = mask_rows.shape[0]

    def decay_one_block(totals, pieces):
        mask_b, spread_b, left_b, right_b = pieces
        weight = jnp.exp(spread_b[:, :, None] * decay_a[None, :, :]) * mask_b[:, None, None]
        return (totals + jnp.sum(weight * left_b[:, :, None] * right_b[:, None, :], axis=0), None)

    shaped = tuple(
        (
            member.reshape((row_count // SCAN_BLOCK, SCAN_BLOCK) + member.shape[1:])
            for member in (mask_rows, spread, left_rows, right_rows)
        )
    )
    totals, unused = lax.scan(decay_one_block, jnp.zeros((INNER, STATE), jnp.float32), shaped)
    return totals


def gate_mix(core, inner_u, skip_d, gate_z):
    return (core + skip_d[None, :] * inner_u) * jax.nn.silu(gate_z)


def branch_norms(context, ssm_out, gain_att, gain_ssm):
    return (rms_scale(context, gain_att), rms_scale(ssm_out, gain_ssm))


def soft_step(dt_lin, dt_bias):
    return jax.nn.softplus(dt_lin + dt_bias[None, :])


def decay_of(log_a):
    return -jnp.exp(log_a)


def swiglu(gate_proj, up_proj):
    return jax.nn.silu(gate_proj) * up_proj


def squares(row_vals):
    return jnp.sum(row_vals * row_vals)


def local(
    tokens,
    cotangent,
    route,
    lengths,
    gain_in,
    w_qkv,
    w_mix_in,
    w_x,
    w_dt,
    w_small,
    gain_att,
    gain_ssm,
    w_out_att,
    w_out_ssm,
    gain_ffn,
    w_gate,
    w_up,
    w_down,
):
    seq_count = lax.axis_size("seq")
    fsdp_count = lax.axis_size("fsdp")
    seq_rank = lax.axis_index("seq")
    fsdp_rank = lax.axis_index("fsdp")
    tok_rows = tokens.shape[1]
    pack_len = tok_rows * seq_count
    groups = HEADS // KV_HEADS
    shards = [w_qkv, w_mix_in, w_x, w_dt, w_small, w_out_att, w_out_ssm, w_gate, w_up, w_down]
    scales = [1.0, 1.0, 1.0, 1.0, 1.0, 0.5, 0.5, 1.0, 1.0, 1.0]
    grad_acc = [jnp.zeros(shard.shape, jnp.float32) for shard in shards]
    pending = [[] for shard in shards]
    stat_acc = jnp.zeros((6,), jnp.float32)
    gain_sums = [
        jnp.zeros_like(gain_in),
        jnp.zeros_like(gain_att),
        jnp.zeros_like(gain_ssm),
        jnp.zeros_like(gain_ffn),
    ]

    def add_grad(grad_slot, left_op, right_op):
        pending[grad_slot].append((left_op, right_op))

    def add_small(small_grad):
        pending[4].append(small_grad)

    held_mixer = mixer_weights(w_qkv, w_mix_in, w_x, w_dt, w_small, w_out_att, w_out_ssm)
    held_ffn = ffn_weights(w_gate, w_up, w_down)
    outputs = []
    input_grads = []
    for batch_idx in range(MICRO):
        send_index, own_index, recv_slot, send_place = routing(
            route[batch_idx], tok_rows, fsdp_count, fsdp_rank
        )
        got_x, got_cot = deal(
            jnp.take(tokens[batch_idx], send_index, axis=0),
            jnp.take(cotangent[batch_idx], send_index, axis=0),
        )
        x_own = jnp.take(got_x, own_index, axis=0).astype(jnp.float32)
        cot_own = jnp.take(got_cot, own_index, axis=0).astype(jnp.float32)
        segment, position = seq_layout(lengths[batch_idx, 0], pack_len)
        my_segment = lax.dynamic_slice_in_dim(segment, seq_rank * tok_rows, tok_rows)
        my_position = lax.dynamic_slice_in_dim(position, seq_rank * tok_rows, tok_rows)
        qkv_full, mix_in_full, x_full, dt_full, small_full, att_out_full, ssm_out_full = held_mixer
        normed, norm_back = jax.vjp(rms_scale, x_own, gain_in)
        normed_low = normed.astype(jnp.bfloat16)
        qkv_low = jnp.dot(normed_low, qkv_full, preferred_element_type=jnp.float32).astype(
            jnp.bfloat16
        )
        queries = qkv_low[:, :ATT].reshape(tok_rows, KV_HEADS, groups, HEAD)
        key_value = lax.all_gather(qkv_low[:, ATT:], "seq", axis=0, tiled=True)
        all_keys = key_value[:, :KV_WIDTH].reshape(pack_len, KV_HEADS, HEAD)
        all_values = key_value[:, KV_WIDTH:].reshape(pack_len, KV_HEADS, HEAD)
        visible = (my_segment[:, None] == segment[None, :]) & (
            position[None, :] <= my_position[:, None]
        )
        scores = (
            jnp.einsum("tkgd,ukd->kgtu", queries, all_keys, preferred_element_type=jnp.float32)
            * 0.125
        )
        masked = jnp.where(visible, scores, -1e30)
        row_top = jnp.max(masked, axis=-1, keepdims=True)
        exp_terms = jnp.exp(masked - row_top)
        row_total = jnp.sum(exp_terms, axis=-1, keepdims=True)
        log_total = row_top + jnp.log(row_total)
        softmax_p = exp_terms / row_total
        context = jnp.einsum(
            "kgtu,ukd->tkgd",
            softmax_p.astype(jnp.bfloat16),
            all_values,
            preferred_element_type=jnp.float32,
        ).reshape(tok_rows, ATT)
        mixed_low = jnp.dot(normed_low, mix_in_full, preferred_element_type=jnp.float32).astype(
            jnp.bfloat16
        )
        inner_low = mixed_low[:, :INNER]
        gate_z = mixed_low[:, INNER:].astype(jnp.float32)
        edge_rows = passed_along(inner_low[tok_rows - (CONV - 1) :], "seq", 1)
        extended = jnp.concatenate([edge_rows, inner_low], axis=0).astype(jnp.float32)
        small_par = small_full.astype(jnp.float32)
        conv_w = small_par[:, :CONV]
        conv_b = small_par[:, CONV]
        dt_bias = small_par[:, CONV + 1]
        skip_d = small_par[:, CONV + 2]
        log_a = small_par[:, CONV + 3 :]
        inner_u, conv_back = jax.vjp(partial(conv_act, my_position), extended, conv_w, conv_b)
        u_low = inner_u.astype(jnp.bfloat16)
        projected_low = jnp.dot(u_low, x_full, preferred_element_type=jnp.float32).astype(
            jnp.bfloat16
        )
        dt_low = projected_low[:, :DT_RANK]
        projected = projected_low.astype(jnp.float32)
        in_b = projected[:, DT_RANK : DT_RANK + STATE]
        out_c = projected[:, DT_RANK + STATE :]
        dt_lin = contract(dt_low, dt_full, 1, 1)
        step_dt, dt_back = jax.vjp(soft_step, dt_lin, dt_bias)
        decay_a, decay_back = jax.vjp(decay_of, log_a)
        keep_mask = (my_position > 0).astype(jnp.float32)
        row_steps = jnp.arange(tok_rows, dtype=jnp.int32)
        first_reset = jnp.min(jnp.where(my_position == 0, row_steps, tok_rows))
        last_reset = jnp.max(jnp.where(my_position == 0, row_steps, -1))
        alive_mask = (row_steps < first_reset).astype(jnp.float32)
        tail_mask = (row_steps >= last_reset).astype(jnp.float32)
        running = jnp.cumsum(step_dt, axis=0)
        through = jnp.where(first_reset == tok_rows, jnp.exp(decay_a * running[-1][:, None]), 0.0)
        local_end = decay_sum(
            tail_mask, running[-1][None, :] - running, step_dt * inner_u, in_b, decay_a
        )
        unit_pair = (jnp.ones((INNER, STATE), jnp.float32), jnp.zeros((INNER, STATE), jnp.float32))
        prefix = prefix_2((through, local_end), "seq", combine, unit_pair, False)
        (core, end_state), ssm_back = jax.vjp(
            partial(ssm_local, keep_mask), inner_u, step_dt, in_b, out_c, decay_a, prefix[1]
        )
        ssm_out, gate_back = jax.vjp(gate_mix, core, inner_u, skip_d, gate_z)
        (branch_att, branch_ssm), post_back = jax.vjp(
            branch_norms, context, ssm_out, gain_att, gain_ssm
        )
        att_low = branch_att.astype(jnp.bfloat16)
        ssm_low = branch_ssm.astype(jnp.bfloat16)
        mixer_out = 0.5 * (
            jnp.dot(att_low, att_out_full, preferred_element_type=jnp.float32)
            + jnp.dot(ssm_low, ssm_out_full, preferred_element_type=jnp.float32)
        )
        hidden = x_own + mixer_out
        gate_full, up_full, down_full = held_ffn
        ffn_in, ffn_norm_back = jax.vjp(rms_scale, hidden, gain_ffn)
        ffn_low = ffn_in.astype(jnp.bfloat16)
        gate_proj = jnp.dot(ffn_low, gate_full, preferred_element_type=jnp.float32)
        up_proj = jnp.dot(ffn_low, up_full, preferred_element_type=jnp.float32)
        act_val, act_back = jax.vjp(swiglu, gate_proj, up_proj)
        act_low = act_val.astype(jnp.bfloat16)
        ffn_out = jnp.dot(act_low, down_full, preferred_element_type=jnp.float32)
        result = hidden + ffn_out
        stat_acc = stat_acc + jnp.stack(
            [
                squares(x_own),
                squares(context),
                squares(ssm_out),
                squares(mixer_out),
                squares(ffn_out),
                squares(result),
            ]
        )
        down_low = cot_own.astype(jnp.bfloat16)
        d_act = contract(down_low, down_full, 1, 1)
        add_grad(9, act_low, down_low)
        d_gate, d_up = act_back(d_act)
        dgate_low = d_gate.astype(jnp.bfloat16)
        dup_low = d_up.astype(jnp.bfloat16)
        d_ffn_in = contract(dgate_low, gate_full, 1, 1) + contract(dup_low, up_full, 1, 1)
        add_grad(7, ffn_low, dgate_low)
        add_grad(8, ffn_low, dup_low)
        d_hidden_norm, d_gain_ffn = ffn_norm_back(d_ffn_in)
        d_hidden = cot_own + d_hidden_norm
        dmix_low = d_hidden.astype(jnp.bfloat16)
        d_branch_att = 0.5 * contract(dmix_low, att_out_full, 1, 1)
        d_branch_ssm = 0.5 * contract(dmix_low, ssm_out_full, 1, 1)
        add_grad(5, att_low, dmix_low)
        add_grad(6, ssm_low, dmix_low)
        d_context, d_ssm_out, d_gain_att, d_gain_ssm = post_back((d_branch_att, d_branch_ssm))
        d_core, d_u_gate, d_skip, d_gate_z = gate_back(d_ssm_out)
        reach = decay_sum(alive_mask, running, d_core, out_c, decay_a)
        suffix = prefix_2((through, reach), "seq", combine, unit_pair, True)
        d_u_scan, d_step, d_in_b, d_out_c, d_decay, d_start = ssm_back((d_core, suffix[1]))
        d_dt_lin, d_dt_bias = dt_back(d_step)
        ddt_low = d_dt_lin.astype(jnp.bfloat16)
        d_dt_in = jnp.dot(ddt_low, dt_full, preferred_element_type=jnp.float32)
        add_grad(3, ddt_low, dt_low)
        dproj_low = jnp.concatenate([d_dt_in, d_in_b, d_out_c], axis=1).astype(jnp.bfloat16)
        d_inner_u = d_u_gate + d_u_scan + contract(dproj_low, x_full, 1, 1)
        add_grad(2, u_low, dproj_low)
        (d_log_a,) = decay_back(d_decay)
        d_extended, d_conv_w, d_conv_b = conv_back(d_inner_u)
        returned = passed_along(d_extended[: CONV - 1].astype(jnp.bfloat16), "seq", -1).astype(
            jnp.float32
        )
        d_inner = d_extended[CONV - 1 :].at[tok_rows - (CONV - 1) :].add(returned)
        dmixed_low = jnp.concatenate([d_inner, d_gate_z], axis=1).astype(jnp.bfloat16)
        add_grad(1, normed_low, dmixed_low)
        small_grad = jnp.concatenate(
            [d_conv_w, d_conv_b[:, None], d_dt_bias[:, None], d_skip[:, None], d_log_a], axis=1
        )
        add_small(small_grad)
        dctx_low = d_context.astype(jnp.bfloat16).reshape(tok_rows, KV_HEADS, groups, HEAD)
        probs_again = jnp.exp(
            jnp.where(
                visible,
                jnp.einsum("tkgd,ukd->kgtu", queries, all_keys, preferred_element_type=jnp.float32)
                * 0.125,
                -1e30,
            )
            - log_total
        )
        d_values = jnp.einsum(
            "kgtu,tkgd->ukd",
            probs_again.astype(jnp.bfloat16),
            dctx_low,
            preferred_element_type=jnp.float32,
        )
        d_probs = jnp.einsum(
            "tkgd,ukd->kgtu", dctx_low, all_values, preferred_element_type=jnp.float32
        )
        dscore_low = (
            probs_again * (d_probs - jnp.sum(probs_again * d_probs, axis=-1, keepdims=True))
        ).astype(jnp.bfloat16)
        d_queries = (
            jnp.einsum("kgtu,ukd->tkgd", dscore_low, all_keys, preferred_element_type=jnp.float32)
            * 0.125
        )
        d_keys = (
            jnp.einsum("kgtu,tkgd->ukd", dscore_low, queries, preferred_element_type=jnp.float32)
            * 0.125
        )
        kv_term = jnp.concatenate(
            [d_keys.reshape(pack_len, KV_WIDTH), d_values.reshape(pack_len, KV_WIDTH)], axis=1
        )
        my_kv = lax.psum_scatter(
            slice_rows(kv_term, jnp.int32(0), tok_rows * lax.axis_size("seq")).astype(jnp.bfloat16),
            "seq",
            scatter_dimension=0,
            tiled=True,
        ).astype(jnp.float32)
        dqkv_low = jnp.concatenate([d_queries.reshape(tok_rows, ATT), my_kv], axis=1).astype(
            jnp.bfloat16
        )
        add_grad(0, normed_low, dqkv_low)
        d_normed = contract(dqkv_low, qkv_full, 1, 1) + contract(dmixed_low, mix_in_full, 1, 1)
        d_x_norm, d_gain_in = norm_back(d_normed)
        d_x = d_hidden + d_x_norm
        gain_sums = [
            gain_sums[0] + d_gain_in,
            gain_sums[1] + d_gain_att,
            gain_sums[2] + d_gain_ssm,
            gain_sums[3] + d_gain_ffn,
        ]
        back_out, back_dx = deal(
            jnp.take(result.astype(jnp.bfloat16), recv_slot, axis=0),
            jnp.take(d_x.astype(jnp.bfloat16), recv_slot, axis=0),
        )
        outputs.append(jnp.take(back_out, send_place, axis=0))
        input_grads.append(jnp.take(back_dx, send_place, axis=0))
    for grad_slot in range(len(shards)):
        shard_rows = shards[grad_slot].shape[0]
        if grad_slot == 4:
            small_total = pending[4][0]
            for further in pending[4][1:]:
                small_total = small_total + further
            grad_acc[4] = scatter_rows(partial(slice_rows, small_total), shard_rows)
        else:
            left_all = jnp.concatenate([member[0] for member in pending[grad_slot]], axis=0)
            right_all = jnp.concatenate([member[1] for member in pending[grad_slot]], axis=0)
            grad_acc[grad_slot] = scatter_rows(
                row_term(left_all, right_all, scales[grad_slot]), shard_rows
            )
    summed = (
        lax.psum_scatter(
            grad_acc[0].astype(jnp.bfloat16), "seq", scatter_dimension=1, tiled=True
        ).astype(jnp.float32),
        lax.psum_scatter(
            grad_acc[1].astype(jnp.bfloat16), "seq", scatter_dimension=1, tiled=True
        ).astype(jnp.float32),
        lax.psum_scatter(
            grad_acc[2].astype(jnp.bfloat16), "seq", scatter_dimension=1, tiled=True
        ).astype(jnp.float32),
        lax.psum_scatter(
            grad_acc[3].astype(jnp.bfloat16), "seq", scatter_dimension=1, tiled=True
        ).astype(jnp.float32),
        lax.psum_scatter(
            grad_acc[5].astype(jnp.bfloat16), "seq", scatter_dimension=1, tiled=True
        ).astype(jnp.float32),
        lax.psum_scatter(
            grad_acc[6].astype(jnp.bfloat16), "seq", scatter_dimension=1, tiled=True
        ).astype(jnp.float32),
        lax.psum_scatter(
            grad_acc[7].astype(jnp.bfloat16), "seq", scatter_dimension=1, tiled=True
        ).astype(jnp.float32),
        lax.psum_scatter(
            grad_acc[8].astype(jnp.bfloat16), "seq", scatter_dimension=1, tiled=True
        ).astype(jnp.float32),
        lax.psum_scatter(
            grad_acc[9].astype(jnp.bfloat16), "seq", scatter_dimension=1, tiled=True
        ).astype(jnp.float32),
    )
    small_sum = lax.psum(grad_acc[4], "seq")
    stat_sum, g_in_sum, g_att_sum, g_ssm_sum, g_ffn_sum = lax.psum(
        (stat_acc, gain_sums[0], gain_sums[1], gain_sums[2], gain_sums[3]), ("seq", "fsdp")
    )
    widths = jnp.array([D, ATT, INNER, D, D, D], jnp.float32)
    row_count_all = MICRO * tok_rows * seq_count * fsdp_count
    rms = jnp.sqrt(stat_sum / (widths * row_count_all))
    bias_grad = small_sum[:, CONV + 1]
    return (
        jnp.stack(outputs),
        jnp.stack(input_grads),
        g_in_sum,
        summed[0],
        summed[1],
        summed[2],
        summed[3],
        small_sum,
        bias_grad,
        g_att_sum,
        g_ssm_sum,
        summed[4],
        summed[5],
        g_ffn_sum,
        summed[6],
        summed[7],
        summed[8],
        rms,
    )


def solution(mesh):
    placed = (
        P(None, ("seq", "fsdp"), None),
        P(None, ("seq", "fsdp"), None),
        P(None, "seq"),
        P(None, "fsdp", None),
        P(),
        P("fsdp", None),
        P("fsdp", None),
        P("fsdp", None),
        P("fsdp", None),
        P("fsdp", None),
        P(),
        P(),
        P("fsdp", None),
        P("fsdp", None),
        P(),
        P("fsdp", None),
        P("fsdp", None),
        P("fsdp", None),
    )
    return jax.shard_map(
        local,
        mesh=mesh,
        in_specs=placed,
        out_specs=(
            P(None, ("seq", "fsdp"), None),
            P(None, ("seq", "fsdp"), None),
            P(),
            P("fsdp", "seq"),
            P("fsdp", "seq"),
            P("fsdp", "seq"),
            P("fsdp", "seq"),
            P("fsdp", None),
            P("fsdp"),
            P(),
            P(),
            P("fsdp", "seq"),
            P("fsdp", "seq"),
            P(),
            P("fsdp", "seq"),
            P("fsdp", "seq"),
            P("fsdp", "seq"),
            P(),
        ),
        check_vma=False,
    )
```

profile of v0, /device:TPU:0, one launch (start us, length us, event | category | flops | bytes accessed | tf_op | source)
XLA Modules:
  0.0 4251.0 jit_solution(11913863126938682567)
XLA Ops:
  235.6 79.9 %all-gather.20.cloned.1.call-done = bf16[1600,6400]{1,0:T(8,128)(2,1)} async-done(((bf16[200,6400]{1,0:T(8,128)(2,1)}), bf16[1600,6400]{1,0:T(8,128)(2,1)}) %all-gather.20.cloned.1.call-update) | async-done | bytes 20480016 | tf_op jit(solution)/shard_map/all_gather | solution.py:118
  390.4 190.9 %while.445 = (s32[]{:T(128)}, f32[3200,16]{0,1:T(8,128)S(1)}, f32[6,16,3200]{2,1,0:T(8,128)}, f32[6,3200,16]{1,2,0:T(8,128)}, f32[6,16,3200]{2,1,0:T(8,128)}, /*...) while((s32[]{:T(128)}, f32[3200,16]{0,1:T(8,128)S(1)}, ...), condition=%wide.region_23.26_spmd, body=%wide.region_19.25_spmd.sunk | while | flops 358404 | bytes 2437010 | solution.py:195
  617.2 190.2 %while.447 = (s32[]{:T(128)}, f32[3200,16]{0,1:T(8,128)S(1)}, f32[6,16,3200]{2,1,0:T(8,128)}, f32[6,3200,16]{1,2,0:T(8,128)}, f32[6,16,3200]{2,1,0:T(8,128)S(1)}...) while((s32[]{:T(128)}, f32[3200,16]{0,1:T(8,128)S(1)}, ...), condition=%wide.region_50.53_spmd, body=%wide.region_46.52_spmd.sunk | while | flops 358404 | bytes 2437010 | solution.py:195
  846.9 105.6 %all-gather.28.cloned.1.call-done = bf16[5504,1600]{1,0:T(8,128)(2,1)} async-done(((bf16[688,1600]{1,0:T(8,128)(2,1)}), bf16[5504,1600]{1,0:T(8,128)(2,1)}) %all-gather.28.cloned.1.call-update) | async-done | bytes 17612816 | tf_op jit(solution)/shard_map/all_gather | solution.py:131
  1141.5 782.1 %while.456 = (s32[]{:T(128)}, f32[3200,16]{0,1:T(8,128)}, f32[3200,16]{0,1:T(8,128)S(1)}, f32[6,16,3200]{2,1,0:T(8,128)}, f32[6,16,3200]{2,1,0:T(8,128)}, /*inde...) while((s32[]{:T(128)}, f32[3200,16]{0,1:T(8,128)}, ...), condition=%wide.region_73.76_spmd.clone, body=%wide.region_64.75_spmd.clone.sunk | while | flops 1340778 | bytes 8473007 | solution.py:195
  1146.8 48.6 %while.464 = (s32[]{:T(128)}, f32[3200,16]{0,1:T(8,128)S(1)}, f32[16,3200,1]{1,2,0:T(1,128)S(1)}, f32[16,3200,16]{1,2,0:T(8,128)}, f32[16,3200,16]{1,2,0:T(8,128...) while((s32[]{:T(128)}, f32[3200,16]{0,1:T(8,128)S(1)}, ...), condition=%wide.region_66.68_spmd, body=%wide.region_65.67_spmd.sunk | while | flops 364802 | bytes 1627461 | solution.py:186
  1196.2 73.4 %while.465 = (s32[]{:T(128)}, f32[3200,16]{0,1:T(8,128)S(1)}, f32[3200,16]{0,1:T(8,128)S(1)}, f32[16,3200]{1,0:T(8,128)S(1)}, f32[16,3200]{1,0:T(8,128)S(1)}, /*...) while((s32[]{:T(128)}, f32[3200,16]{0,1:T(8,128)S(1)}, ...), condition=%wide.region_72.74_spmd.clone, body=%wide.region_67.73_spmd.clone.sunk | while | flops 873572 | bytes 2522463 | solution.py:186
  1276.4 48.6 %while.464 = (s32[]{:T(128)}, f32[3200,16]{0,1:T(8,128)S(1)}, f32[16,3200,1]{1,2,0:T(1,128)S(1)}, f32[16,3200,16]{1,2,0:T(8,128)}, f32[16,3200,16]{1,2,0:T(8,128...) while((s32[]{:T(128)}, f32[3200,16]{0,1:T(8,128)S(1)}, ...), condition=%wide.region_66.68_spmd, body=%wide.region_65.67_spmd.sunk | while | flops 364802 | bytes 1627461 | solution.py:186
  1325.7 73.4 %while.465 = (s32[]{:T(128)}, f32[3200,16]{0,1:T(8,128)S(1)}, f32[3200,16]{0,1:T(8,128)S(1)}, f32[16,3200]{1,0:T(8,128)S(1)}, f32[16,3200]{1,0:T(8,128)S(1)}, /*...) while((s32[]{:T(128)}, f32[3200,16]{0,1:T(8,128)S(1)}, ...), condition=%wide.region_72.74_spmd.clone, body=%wide.region_67.73_spmd.clone.sunk | while | flops 873572 | bytes 2522463 | solution.py:186
  1406.8 48.6 %while.464 = (s32[]{:T(128)}, f32[3200,16]{0,1:T(8,128)S(1)}, f32[16,3200,1]{1,2,0:T(1,128)S(1)}, f32[16,3200,16]{1,2,0:T(8,128)}, f32[16,3200,16]{1,2,0:T(8,128...) while((s32[]{:T(128)}, f32[3200,16]{0,1:T(8,128)S(1)}, ...), condition=%wide.region_66.68_spmd, body=%wide.region_65.67_spmd.sunk | while | flops 364802 | bytes 1627461 | solution.py:186
  1456.2 73.4 %while.465 = (s32[]{:T(128)}, f32[3200,16]{0,1:T(8,128)S(1)}, f32[3200,16]{0,1:T(8,128)S(1)}, f32[16,3200]{1,0:T(8,128)S(1)}, f32[16,3200]{1,0:T(8,128)S(1)}, /*...) while((s32[]{:T(128)}, f32[3200,16]{0,1:T(8,128)S(1)}, ...), condition=%wide.region_72.74_spmd.clone, body=%wide.region_67.73_spmd.clone.sunk | while | flops 873572 | bytes 2522463 | solution.py:186
  1537.3 48.6 %while.464 = (s32[]{:T(128)}, f32[3200,16]{0,1:T(8,128)S(1)}, f32[16,3200,1]{1,2,0:T(1,128)S(1)}, f32[16,3200,16]{1,2,0:T(8,128)}, f32[16,3200,16]{1,2,0:T(8,128...) while((s32[]{:T(128)}, f32[3200,16]{0,1:T(8,128)S(1)}, ...), condition=%wide.region_66.68_spmd, body=%wide.region_65.67_spmd.sunk | while | flops 364802 | bytes 1627461 | solution.py:186
  1586.7 73.4 %while.465 = (s32[]{:T(128)}, f32[3200,16]{0,1:T(8,128)S(1)}, f32[3200,16]{0,1:T(8,128)S(1)}, f32[16,3200]{1,0:T(8,128)S(1)}, f32[16,3200]{1,0:T(8,128)S(1)}, /*...) while((s32[]{:T(128)}, f32[3200,16]{0,1:T(8,128)S(1)}, ...), condition=%wide.region_72.74_spmd.clone, body=%wide.region_67.73_spmd.clone.sunk | while | flops 873572 | bytes 2522463 | solution.py:186
  1667.8 48.6 %while.464 = (s32[]{:T(128)}, f32[3200,16]{0,1:T(8,128)S(1)}, f32[16,3200,1]{1,2,0:T(1,128)S(1)}, f32[16,3200,16]{1,2,0:T(8,128)}, f32[16,3200,16]{1,2,0:T(8,128...) while((s32[]{:T(128)}, f32[3200,16]{0,1:T(8,128)S(1)}, ...), condition=%wide.region_66.68_spmd, body=%wide.region_65.67_spmd.sunk | while | flops 364802 | bytes 1627461 | solution.py:186
  1717.2 73.4 %while.465 = (s32[]{:T(128)}, f32[3200,16]{0,1:T(8,128)S(1)}, f32[3200,16]{0,1:T(8,128)S(1)}, f32[16,3200]{1,0:T(8,128)S(1)}, f32[16,3200]{1,0:T(8,128)S(1)}, /*...) while((s32[]{:T(128)}, f32[3200,16]{0,1:T(8,128)S(1)}, ...), condition=%wide.region_72.74_spmd.clone, body=%wide.region_67.73_spmd.clone.sunk | while | flops 873572 | bytes 2522463 | solution.py:186
  1798.3 48.6 %while.464 = (s32[]{:T(128)}, f32[3200,16]{0,1:T(8,128)S(1)}, f32[16,3200,1]{1,2,0:T(1,128)S(1)}, f32[16,3200,16]{1,2,0:T(8,128)}, f32[16,3200,16]{1,2,0:T(8,128...) while((s32[]{:T(128)}, f32[3200,16]{0,1:T(8,128)S(1)}, ...), condition=%wide.region_66.68_spmd, body=%wide.region_65.67_spmd.sunk | while | flops 364802 | bytes 1627461 | solution.py:186
  1847.7 73.4 %while.465 = (s32[]{:T(128)}, f32[3200,16]{0,1:T(8,128)S(1)}, f32[3200,16]{0,1:T(8,128)S(1)}, f32[16,3200]{1,0:T(8,128)S(1)}, f32[16,3200]{1,0:T(8,128)S(1)}, /*...) while((s32[]{:T(128)}, f32[3200,16]{0,1:T(8,128)S(1)}, ...), condition=%wide.region_72.74_spmd.clone, body=%wide.region_67.73_spmd.clone.sunk | while | flops 873572 | bytes 2522463 | solution.py:186
  1975.0 765.4 %while.461 = (s32[]{:T(128)}, f32[3200,16]{0,1:T(8,128)S(1)}, f32[3200,16]{0,1:T(8,128)S(1)}, f32[6,16,3200]{2,1,0:T(8,128)}, f32[6,16,3200]{2,1,0:T(8,128)}, /*...) while((s32[]{:T(128)}, f32[3200,16]{0,1:T(8,128)S(1)}, ...), condition=%wide.region_94.97_spmd.clone, body=%wide.region_85.96_spmd.clone.sunk | while | flops 1340778 | bytes 8473007 | solution.py:195
  1980.1 47.9 %while.466 = (s32[]{:T(128)}, f32[3200,16]{0,1:T(8,128)S(1)}, f32[16,3200,1]{1,2,0:T(1,128)S(1)}, f32[16,3200,16]{1,2,0:T(8,128)}, f32[16,3200,16]{1,2,0:T(8,128...) while((s32[]{:T(128)}, f32[3200,16]{0,1:T(8,128)S(1)}, ...), condition=%wide.region_87.89_spmd, body=%wide.region_86.88_spmd.sunk | while | flops 364802 | bytes 1627461 | solution.py:186
  2028.8 73.0 %while.467 = (s32[]{:T(128)}, f32[3200,16]{0,1:T(8,128)S(1)}, f32[3200,16]{0,1:T(8,128)S(1)}, f32[16,3200]{1,0:T(8,128)S(1)}, f32[16,3200]{1,0:T(8,128)S(1)}, /*...) while((s32[]{:T(128)}, f32[3200,16]{0,1:T(8,128)S(1)}, ...), condition=%wide.region_93.95_spmd.clone, body=%wide.region_88.94_spmd.clone.sunk | while | flops 873572 | bytes 2522463 | solution.py:186
  2156.3 73.0 %while.467 = (s32[]{:T(128)}, f32[3200,16]{0,1:T(8,128)S(1)}, f32[3200,16]{0,1:T(8,128)S(1)}, f32[16,3200]{1,0:T(8,128)S(1)}, f32[16,3200]{1,0:T(8,128)S(1)}, /*...) while((s32[]{:T(128)}, f32[3200,16]{0,1:T(8,128)S(1)}, ...), condition=%wide.region_93.95_spmd.clone, body=%wide.region_88.94_spmd.clone.sunk | while | flops 873572 | bytes 2522463 | solution.py:186
  2235.2 47.9 %while.466 = (s32[]{:T(128)}, f32[3200,16]{0,1:T(8,128)S(1)}, f32[16,3200,1]{1,2,0:T(1,128)S(1)}, f32[16,3200,16]{1,2,0:T(8,128)}, f32[16,3200,16]{1,2,0:T(8,128...) while((s32[]{:T(128)}, f32[3200,16]{0,1:T(8,128)S(1)}, ...), condition=%wide.region_87.89_spmd, body=%wide.region_86.88_spmd.sunk | while | flops 364802 | bytes 1627461 | solution.py:186
  2283.9 73.0 %while.467 = (s32[]{:T(128)}, f32[3200,16]{0,1:T(8,128)S(1)}, f32[3200,16]{0,1:T(8,128)S(1)}, f32[16,3200]{1,0:T(8,128)S(1)}, f32[16,3200]{1,0:T(8,128)S(1)}, /*...) while((s32[]{:T(128)}, f32[3200,16]{0,1:T(8,128)S(1)}, ...), condition=%wide.region_93.95_spmd.clone, body=%wide.region_88.94_spmd.clone.sunk | while | flops 873572 | bytes 2522463 | solution.py:186
  2411.4 73.0 %while.467 = (s32[]{:T(128)}, f32[3200,16]{0,1:T(8,128)S(1)}, f32[3200,16]{0,1:T(8,128)S(1)}, f32[16,3200]{1,0:T(8,128)S(1)}, f32[16,3200]{1,0:T(8,128)S(1)}, /*...) while((s32[]{:T(128)}, f32[3200,16]{0,1:T(8,128)S(1)}, ...), condition=%wide.region_93.95_spmd.clone, body=%wide.region_88.94_spmd.clone.sunk | while | flops 873572 | bytes 2522463 | solution.py:186
  2539.0 73.0 %while.467 = (s32[]{:T(128)}, f32[3200,16]{0,1:T(8,128)S(1)}, f32[3200,16]{0,1:T(8,128)S(1)}, f32[16,3200]{1,0:T(8,128)S(1)}, f32[16,3200]{1,0:T(8,128)S(1)}, /*...) while((s32[]{:T(128)}, f32[3200,16]{0,1:T(8,128)S(1)}, ...), condition=%wide.region_93.95_spmd.clone, body=%wide.region_88.94_spmd.clone.sunk | while | flops 873572 | bytes 2522463 | solution.py:186
  2666.5 73.0 %while.467 = (s32[]{:T(128)}, f32[3200,16]{0,1:T(8,128)S(1)}, f32[3200,16]{0,1:T(8,128)S(1)}, f32[16,3200]{1,0:T(8,128)S(1)}, f32[16,3200]{1,0:T(8,128)S(1)}, /*...) while((s32[]{:T(128)}, f32[3200,16]{0,1:T(8,128)S(1)}, ...), condition=%wide.region_93.95_spmd.clone, body=%wide.region_88.94_spmd.clone.sunk | while | flops 873572 | bytes 2522463 | solution.py:186
  2848.8 70.6 %reduce-scatter.53.cloned.1.call-done = bf16[200,2240]{1,0:T(8,128)(2,1)} async-done(((bf16[1600,2240]{1,0:T(8,128)(2,1)}), bf16[200,2240]{1,0:T(8,128)(2,1)}) %reduce-scatter.53.cloned.1.call-update) | async-done | bytes 896016 | tf_op jit(solution)/shard_map/reduce_scatter | solution.py:136
  2921.8 109.6 %reduce-scatter.57.cloned.1.call-done = bf16[400,1600]{1,0:T(8,128)(2,1)} async-done(((bf16[3200,1600]{1,0:T(8,128)(2,1)}), bf16[400,1600]{1,0:T(8,128)(2,1)}) %reduce-scatter.57.cloned.1.call-update) | async-done | bytes 1280016 | tf_op jit(solution)/shard_map/reduce_scatter | solution.py:136
  3034.9 194.4 %reduce-scatter.87.cloned.1.call-done = bf16[200,5504]{1,0:T(8,128)(2,1)} async-done(((bf16[1600,5504]{1,0:T(8,128)(2,1)}), bf16[200,5504]{1,0:T(8,128)(2,1)}) %reduce-scatter.87.cloned.1.call-update) | async-done | bytes 2201616
  3233.8 216.7 %reduce-scatter.89.cloned.1.call-done = bf16[200,5504]{1,0:T(8,128)(2,1)} async-done(((bf16[1600,5504]{1,0:T(8,128)(2,1)}), bf16[200,5504]{1,0:T(8,128)(2,1)}) %reduce-scatter.89.cloned.1.call-update) | async-done | bytes 2201616
  3459.1 187.6 %reduce-scatter.59.cloned.1.call-done = bf16[688,1600]{1,0:T(8,128)(2,1)} async-done(((bf16[5504,1600]{1,0:T(8,128)(2,1)}), bf16[688,1600]{1,0:T(8,128)(2,1)}) %reduce-scatter.59.cloned.1.call-update) | async-done | bytes 2201616 | tf_op jit(solution)/shard_map/reduce_scatter | solution.py:136
  3688.5 163.0 %reduce-scatter.83.cloned.1.call-done = bf16[200,6400]{1,0:T(8,128)(2,1)} async-done(((bf16[1600,6400]{1,0:T(8,128)(2,1)}), bf16[200,6400]{1,0:T(8,128)(2,1)}) %reduce-scatter.83.cloned.1.call-update) | async-done | bytes 2560016
  (6379 shorter events, 3692.4 us)
Async XLA Ops:
  7.2 175.7 %all-gather.16.cloned.1.call-start = ((), (), s32[]{:S(2)}) async-start(), calls=%async_computation.27 | async-start | bytes 8294400 | tf_op jit(solution)/shard_map/all_gather | solution.py:117
  7.9 307.5 %all-gather.20.cloned.1.call-start = ((), (), s32[]{:S(2)}) async-start(), calls=%async_computation.29 | async-start | bytes 23040000 | tf_op jit(solution)/shard_map/all_gather | solution.py:118
  8.7 804.9 %all-gather.22.cloned.1.call-start = ((), (), s32[]{:S(2)}) async-start(), calls=%async_computation.30 | async-start | bytes 11980800 | tf_op jit(solution)/shard_map/all_gather | solution.py:123
  9.4 811.3 %all-gather.18.cloned.1.call-start = ((), (), s32[]{:S(2)}) async-start(), calls=%async_computation.28 | async-start | bytes 5990400 | tf_op jit(solution)/shard_map/all_gather | solution.py:122
  10.0 815.3 %all-gather.24.cloned.1.call-start = ((), (), s32[]{:S(2)}) async-start(), calls=%async_computation.31 | async-start | bytes 19814400 | tf_op jit(solution)/shard_map/all_gather | solution.py:129
  10.6 825.6 %all-gather.26.cloned.1.call-start = ((), (), s32[]{:S(2)}) async-start(), calls=%async_computation.32 | async-start | bytes 19814400 | tf_op jit(solution)/shard_map/all_gather | solution.py:130
  23.3 62.7 %all-to-all-start.2 = ((bf16[8,12,1600]{2,1,0:T(8,128)(2,1)}), bf16[8,12,1600]{2,1,0:T(8,128)(2,1)S(1)}, u32[]{:S(2)}, u32[]{:S(2)}) async-start(bf16[8,12,1600]{2,1,0:T(8,128)(2,1)} %all_to_all.70), calls=%async_computation.2 | async-start | bytes 851968 | tf_op jit(solution)/shard_map/all_to_all | solution.py:110
  29.6 922.9 %all-gather.28.cloned.1.call-start = ((), (), s32[]{:S(2)}) async-start(), calls=%async_computation.33 | async-start | bytes 20606976 | tf_op jit(solution)/shard_map/all_gather | solution.py:131
  86.0 35.0 all-to-all-start
  121.0 29.7 all-to-all-start.4
  150.7 28.6 all-to-all-start.6
  154.2 2601.2 %reduce-scatter.61.cloned.1.call-start = ((), (), s32[]{:S(2)}) async-start(), calls=%async_computation.38 | async-start | bytes 614400
  1964.7 791.8 %reduce-scatter.63.cloned.1.call-start = ((), (), s32[]{:S(2)}) async-start(), calls=%async_computation.39 | async-start | bytes 614400
  1972.7 867.8 %reduce-scatter.55.cloned.1.call-start = ((), (), s32[]{:S(2)}) async-start(), calls=%async_computation.35 | async-start | bytes 921600 | tf_op jit(solution)/shard_map/reduce_scatter | solution.py:136
  2746.9 99.6 %reduce-scatter.85.cloned.1.call-start = ((), (), s32[]{:S(2)}) async-start(), calls=%async_computation.51 | async-start | bytes 5990400
  2751.1 168.3 %reduce-scatter.53.cloned.1.call-start = ((), (), s32[]{:S(2)}) async-start(), calls=%async_computation.34 | async-start | bytes 8294400 | tf_op jit(solution)/shard_map/reduce_scatter | solution.py:136
  2763.4 268.0 %reduce-scatter.57.cloned.1.call-start = ((), (), s32[]{:S(2)}) async-start(), calls=%async_computation.36 | async-start | bytes 11980800 | tf_op jit(solution)/shard_map/reduce_scatter | solution.py:136
  2771.8 457.5 %reduce-scatter.87.cloned.1.call-start = ((), (), s32[]{:S(2)}) async-start(), calls=%async_computation.52 | async-start | bytes 19814400
  2782.3 668.2 %reduce-scatter.89.cloned.1.call-start = ((), (), s32[]{:S(2)}) async-start(), calls=%async_computation.53 | async-start | bytes 19814400
  2792.8 853.9 %reduce-scatter.59.cloned.1.call-start = ((), (), s32[]{:S(2)}) async-start(), calls=%async_computation.37 | async-start | bytes 20606976 | tf_op jit(solution)/shard_map/reduce_scatter | solution.py:136
  2803.8 1047.6 %reduce-scatter.83.cloned.1.call-start = ((), (), s32[]{:S(2)}) async-start(), calls=%async_computation.50 | async-start | bytes 23040000
  2836.5 1081.8 %reduce-scatter.71.cloned.1.call-start = ((), (), s32[]{:S(2)}) async-start(), calls=%async_computation.43 | async-start | bytes 921600
  2840.4 1145.7 %all-reduce.26.cloned.1.call-start = ((), (), s32[]{:S(2)}) async-start(), calls=%async_computation.49 | async-start | bytes 204800
  2841.2 1151.8 %reduce-scatter.69.cloned.1.call-start = ((), (), s32[]{:S(2)}) async-start(), calls=%async_computation.42 | async-start | bytes 1843200
  2846.4 1176.5 %reduce-scatter.73.cloned.1.call-start = ((), (), s32[]{:S(2)}) async-start(), calls=%async_computation.44 | async-start | bytes 1024000
  2848.8 1178.8 %reduce-scatter.65.cloned.1.call-start = ((), (), s32[]{:S(2)}) async-start(), calls=%async_computation.40 | async-start | bytes 1433600
  2921.7 1140.6 %reduce-scatter.75.cloned.1.call-start = ((), (), s32[]{:S(2)}) async-start(), calls=%async_computation.45 | async-start | bytes 2048000
  3034.9 1071.9 %reduce-scatter.77.cloned.1.call-start = ((), (), s32[]{:S(2)}) async-start(), calls=%async_computation.46 | async-start | bytes 3522560
  3233.8 917.6 %reduce-scatter.79.cloned.1.call-start = ((), (), s32[]{:S(2)}) async-start(), calls=%async_computation.47 | async-start | bytes 3522560
  3454.9 737.9 %reduce-scatter.81.cloned.1.call-start = ((), (), s32[]{:S(2)}) async-start(), calls=%async_computation.48 | async-start | bytes 3072000
  3651.2 589.8 %reduce-scatter.67.cloned.1.call-start = ((), (), s32[]{:S(2)}) async-start(), calls=%async_computation.41 | async-start | bytes 4096000
  3914.7 76.1 %all-to-all-start.1 = ((bf16[8,12,1600]{2,1,0:T(8,128)(2,1)}), bf16[8,12,1600]{2,1,0:T(8,128)(2,1)S(1)}, u32[]{:S(2)}, u32[]{:S(2)}) async-start(bf16[8,12,1600]{2,1,0:T(8,128)(2,1)} %all_to_all.67), calls=%async_computation.1 | async-start | bytes 851968 | tf_op jit(solution)/shard_map/all_to_all | solution.py:110
  (298 other events, 8115.4 us)
Sparse Core Ops, SparseCore 0:
  9.7 105.8 all-gather.15
  117.2 198.2 all-gather.19
  317.1 99.1 all-gather.21
  417.8 55.0 all-gather.17
  474.4 156.7 all-gather.23
  632.6 156.2 all-gather.25
  790.5 161.9 all-gather.27
  1964.9 21.9 reduce-scatter.60
  1989.9 24.6 reduce-scatter.62
  2747.0 28.9 reduce-scatter.54
  2778.4 59.4 reduce-scatter.84
  2840.1 79.2 reduce-scatter.52
  2921.8 109.5 reduce-scatter.56
  3033.7 195.5 reduce-scatter.86
  3231.6 218.8 reduce-scatter.88
  3452.8 193.8 reduce-scatter.58
  3649.1 202.3 reduce-scatter.82
  3854.3 32.0 reduce-scatter.70
  3889.3 39.1 all-reduce.25
  3930.8 35.3 reduce-scatter.68
  3969.9 24.6 reduce-scatter.72
  3998.4 29.1 reduce-scatter.64
  4030.9 31.4 reduce-scatter.74
  4065.5 41.2 reduce-scatter.76
  4110.1 41.1 reduce-scatter.78
  4154.6 38.1 reduce-scatter.80
  4196.0 45.0 reduce-scatter.66
where the time goes:
time: 4300 us; the launch traced here: 4250 us
  waiting for transfers between devices  1410 us (33%)
  other arithmetic  1140 us (27%)
  local copies, waits for them, and re-layouts  1060 us (25%)
  matrix products  314 us (7%)
  blocking collectives  226 us (5%)
  starting transfers between devices  45.2 us (1%)
    unnamed x44, waiting for transfers between devices  785 us
    dynamic_slice x1344, local copies, waits for them, and re-layouts, ssm_one_block(): return lax.scan(one_step, carry_state, pieces)  556 us
    dynamic_update_slice x384, other arithmetic, ssm_one_block(): return lax.scan(one_step, carry_state, pieces)  431 us
    reduce_sum x192, other arithmetic, one_step(): (dt_now * u_now)[:, None] * b_now[None, :]  425 us
    reduce_scatter x4, waiting for transfers between devices, scatter_rows(): lax.psum_scatter(term_fn(jnp.int32(0), shard_rows * lax.axis_size('fsdp')...  368 us
    dynamic_update_slice x1152, local copies, waits for them, and re-layouts, ssm_one_block(): return lax.scan(one_step, carry_state, pieces)  194 us
    dot_general x27, matrix products, contract(): lax.dot_general(left_op, right_op, (((left_dim,), (right_dim,)), ((), ())...  190 us
    reduce_sum x192, other arithmetic, one_step(): return (state_now, jnp.sum(state_now * c_now[None, :], axis=1))  147 us

commit v1 on v0

v1 whole, which is shorter than its diff:
```python
from functools import partial

import jax
import jax.numpy as jnp
from jax import lax
from jax.experimental import pallas as pl
from jax.experimental.pallas import tpu as pltpu
from jax.sharding import PartitionSpec as P

D = 1600
HEADS = 25
KV_HEADS = 5
HEAD = 64
INNER = 3200
STATE = 16
CONV = 4
DT_RANK = 100
MICRO = 2
ATT = 1600
KV_WIDTH = 320
PROJ = DT_RANK + 2 * STATE
PROJ_PAD = 144
LANES = 128
EPS = 1e-05
BF = jnp.bfloat16
F32 = jnp.float32


def dot(left_op, right_op, left_dim, right_dim):
    return lax.dot_general(
        left_op, right_op, (((left_dim,), (right_dim,)), ((), ())), preferred_element_type=F32
    )


def rms_scale(row_vals, gain_vec):
    return (
        row_vals * lax.rsqrt(jnp.mean(row_vals * row_vals, axis=-1, keepdims=True) + EPS) * gain_vec
    )


def seq_layout(seq_lens, span_len):
    places = jnp.arange(span_len, dtype=jnp.int32)
    seq_ends = jnp.cumsum(seq_lens)
    segment = jnp.sum((places[:, None] >= seq_ends[None, :]).astype(jnp.int32), axis=1)
    starts = seq_ends - seq_lens
    picked = (segment[:, None] == jnp.arange(seq_lens.shape[0], dtype=jnp.int32)[None, :]).astype(
        jnp.int32
    )
    position = places - jnp.sum(picked * starts[None, :], axis=1)
    return (segment, position)


def swap(array, k):
    size = lax.axis_size("seq")
    return lax.ppermute(array, "seq", [(i, i ^ k) for i in range(size)])


def pick(blocks, at):
    return lax.dynamic_index_in_dim(blocks, at, 0, keepdims=False)


def seq_deal(blocks):
    size, here = lax.axis_size("seq"), lax.axis_index("seq")
    out = blocks
    for k in range(1, size):
        there = here ^ k
        out = lax.dynamic_update_index_in_dim(out, swap(pick(blocks, there), k), there, 0)
    return out


def seq_gather(block):
    size, here = lax.axis_size("seq"), lax.axis_index("seq")
    out = lax.dynamic_update_index_in_dim(
        jnp.zeros((size,) + block.shape, block.dtype), block, here, 0
    )
    for k in range(1, size):
        out = lax.dynamic_update_index_in_dim(out, swap(block, k), here ^ k, 0)
    return out


def seq_scatter(blocks):
    size, here = lax.axis_size("seq"), lax.axis_index("seq")
    total = pick(blocks, here).astype(F32)
    for k in range(1, size):
        total = total + swap(pick(blocks, here ^ k).astype(BF), k).astype(F32)
    return total


def seq_sum(array):
    return jnp.sum(seq_gather(array).astype(F32), axis=0)


def routing(route_rows, tok_rows):
    fsdp_count, fsdp_rank = lax.axis_size("fsdp"), lax.axis_index("fsdp")
    micro = route_rows.shape[0]
    per_peer = tok_rows // fsdp_count
    target_dev = (route_rows // tok_rows).reshape(micro, fsdp_count, tok_rows)
    target_slot = (route_rows % tok_rows).reshape(micro, fsdp_count, tok_rows)
    steps = jnp.arange(tok_rows, dtype=jnp.int32)
    same = target_dev[:, :, :, None] == target_dev[:, :, None, :]
    earlier = steps[None, :] < steps[:, None]
    rank = jnp.sum((same & earlier).astype(jnp.int32), axis=3)
    my_dev = lax.dynamic_index_in_dim(target_dev, fsdp_rank, 1, keepdims=False)
    my_rank = lax.dynamic_index_in_dim(rank, fsdp_rank, 1, keepdims=False)
    micros = jnp.arange(micro, dtype=jnp.int32)
    send_at = (my_dev * micro + micros[:, None]) * per_peer + my_rank
    ranks = jnp.arange(per_peer, dtype=jnp.int32)
    mine = (target_dev == fsdp_rank)[:, :, None, :] & (rank[:, :, None, :] == ranks[:, None])
    slot = jnp.sum(mine.astype(jnp.int32) * target_slot[:, :, None, :], axis=3)
    land_at = (micros[:, None, None] * tok_rows + slot).transpose(1, 0, 2).reshape(-1)
    rows = jnp.arange(micro * tok_rows, dtype=jnp.int32)
    send_hot = (rows[:, None] == send_at.reshape(-1)[None, :]).astype(BF)
    land_hot = (rows[:, None] == land_at[None, :]).astype(BF)
    return send_hot, land_hot


def exchange(rows):
    return lax.all_to_all(rows, "fsdp", split_axis=0, concat_axis=0, tiled=True)


def bring(rows, send_hot, land_hot):
    sent = dot(send_hot, rows, 1, 0).astype(BF)
    return dot(land_hot, exchange(sent), 1, 0).astype(BF)


def give(rows, send_hot, land_hot):
    sent = dot(land_hot, rows, 0, 0).astype(BF)
    return dot(send_hot, exchange(sent), 0, 0).astype(BF)


def lane_groups(channels, most=4):
    tiles, out, first = channels // LANES, [], 0
    while first < tiles:
        count = min(most, tiles - first)
        out.append((first, count))
        first += count
    return out


def scan_kernel(groups, steps, dtm_ref, dtu_ref, b_ref, c_ref, a_ref, core_ref):
    place = lax.broadcasted_iota(jnp.int32, (8, LANES), 0)
    for first, count in groups:
        spans = [pl.ds((first + i) * LANES, LANES) for i in range(count)]
        rates = [a_ref[:, span] for span in spans]

        def block(k, held):
            held = list(held)
            base = pl.multiple_of(k * 8, 8)
            rows = pl.ds(base, 8)
            dts = [dtm_ref[rows, span] for span in spans]
            dus = [dtu_ref[rows, span] for span in spans]
            ys = [jnp.zeros((8, LANES), F32)] * count
            for j in range(8):
                b_now, c_now = b_ref[base + j], c_ref[base + j]
                for i in range(count):
                    decay = jnp.exp(dts[i][j : j + 1] * rates[i])
                    held[i] = decay * held[i] + dus[i][j : j + 1] * b_now
                    y = jnp.sum(held[i] * c_now, axis=0, keepdims=True)
                    ys[i] = jnp.where(place == j, y, ys[i])
            for i, span in enumerate(spans):
                core_ref[rows, span] = ys[i]
            return tuple(held)

        zero = jnp.zeros((STATE, LANES), F32)
        lax.fori_loop(0, steps // 8, block, (zero,) * count)


def scan_back_kernel(
    groups,
    steps,
    dtm_ref,
    dtu_ref,
    dcore_ref,
    b_ref,
    c_ref,
    a_ref,
    ddtu_ref,
    ddt_ref,
    da_ref,
    db_ref,
    dc_ref,
    hs,
    acc_b,
    acc_c,
):
    place = lax.broadcasted_iota(jnp.int32, (8, LANES), 0)
    zero = jnp.zeros((STATE, LANES), F32)
    for at, (first, count) in enumerate(groups):
        spans = [pl.ds((first + i) * LANES, LANES) for i in range(count)]
        slots = [pl.ds(i * LANES, LANES) for i in range(count)]
        rates = [a_ref[:, span] for span in spans]
        for slot in slots:
            hs[0, :, slot] = zero

        def block(k, held):
            held = list(held)
            base = pl.multiple_of(k * 8, 8)
            rows = pl.ds(base, 8)
            dts = [dtm_ref[rows, span] for span in spans]
            dus = [dtu_ref[rows, span] for span in spans]
            for j in range(8):
                b_now = b_ref[base + j]
                for i in range(count):
                    decay = jnp.exp(dts[i][j : j + 1] * rates[i])
                    held[i] = decay * held[i] + dus[i][j : j + 1] * b_now
                    hs[base + j + 1, :, slots[i]] = held[i]
            return tuple(held)

        lax.fori_loop(0, steps // 8, block, (zero,) * count)

        def back(k, carry):
            carry = list(carry)
            base = pl.multiple_of(steps - 8 - k * 8, 8)
            rows = pl.ds(base, 8)
            dts = [dtm_ref[rows, span] for span in spans]
            dus = [dtu_ref[rows, span] for span in spans]
            dys = [dcore_ref[rows, span] for span in spans]
            out_u = [jnp.zeros((8, LANES), F32)] * count
            out_t = [jnp.zeros((8, LANES), F32)] * count
            for j in reversed(range(8)):
                t = base + j
                b_now, c_now = b_ref[t], c_ref[t]
                sum_b = sum_c = zero
                for i in range(count):
                    later, rate_sum = carry[i]
                    dt, du, dy = dts[i][j : j + 1], dus[i][j : j + 1], dys[i][j : j + 1]
                    g = later + dy * c_now
                    sum_c = sum_c + hs[t + 1, :, slots[i]] * dy
                    sum_b = sum_b + g * du
                    through = g * jnp.exp(dt * rates[i])
                    moved = through * hs[t, :, slots[i]]
                    to_u = jnp.sum(g * b_now, axis=0, keepdims=True)
                    to_t = jnp.sum(moved * rates[i], axis=0, keepdims=True)
                    out_u[i] = jnp.where(place == j, to_u, out_u[i])
                    out_t[i] = jnp.where(place == j, to_t, out_t[i])
                    carry[i] = (through, rate_sum + moved * dt)
                if at == 0:
                    acc_b[t] = sum_b
                    acc_c[t] = sum_c
                else:
                    acc_b[t] = acc_b[t] + sum_b
                    acc_c[t] = acc_c[t] + sum_c
            for i, span in enumerate(spans):
                ddtu_ref[rows, span] = out_u[i]
                ddt_ref[rows, span] = out_t[i]
            return tuple(carry)

        ends = lax.fori_loop(0, steps // 8, back, ((zero, zero),) * count)
        for i, span in enumerate(spans):
            da_ref[:, span] = ends[i][1]
    ones = jnp.ones((8, LANES), F32)
    for acc, out in ((acc_b, db_ref), (acc_c, dc_ref)):
        out[...] = lax.dot_general(
            ones,
            acc[...].reshape(steps * STATE, LANES),
            (((1,), (1,)), ((), ())),
            precision=lax.Precision.HIGHEST,
            preferred_element_type=F32,
        )


VMEM_BYTES = 60 * 2**20


def scan_forward(dtm, dtu, b_wide, c_wide, rates):
    steps, channels = dtm.shape
    return pl.pallas_call(
        partial(scan_kernel, lane_groups(channels), steps),
        out_shape=jax.ShapeDtypeStruct((steps, channels), F32),
        in_specs=[pl.BlockSpec(memory_space=pltpu.VMEM)] * 5,
        out_specs=pl.BlockSpec(memory_space=pltpu.VMEM),
        compiler_params=pltpu.CompilerParams(vmem_limit_bytes=VMEM_BYTES),
        cost_estimate=pl.CostEstimate(
            flops=16 * steps * channels * STATE,
            bytes_accessed=40_000_000,
            transcendentals=steps * channels * STATE,
        ),
        name="scan_forward",
    )(dtm, dtu, b_wide, c_wide, rates)


def scan_backward(dtm, dtu, dcore, b_wide, c_wide, rates):
    steps, channels = dtm.shape
    groups = lane_groups(channels)
    rows = jax.ShapeDtypeStruct((steps, channels), F32)
    flat = jax.ShapeDtypeStruct((8, steps * STATE), F32)
    ddtu, ddt, da, db, dc = pl.pallas_call(
        partial(scan_back_kernel, groups, steps),
        out_shape=[rows, rows, jax.ShapeDtypeStruct((STATE, channels), F32), flat, flat],
        in_specs=[pl.BlockSpec(memory_space=pltpu.VMEM)] * 6,
        out_specs=[pl.BlockSpec(memory_space=pltpu.VMEM)] * 5,
        scratch_shapes=[
            pltpu.VMEM((steps + 1, STATE, groups[0][1] * LANES), F32),
            pltpu.VMEM((steps, STATE, LANES), F32),
            pltpu.VMEM((steps, STATE, LANES), F32),
        ],
        compiler_params=pltpu.CompilerParams(vmem_limit_bytes=VMEM_BYTES),
        cost_estimate=pl.CostEstimate(
            flops=40 * steps * channels * STATE,
            bytes_accessed=100_000_000,
            transcendentals=2 * steps * channels * STATE,
        ),
        name="scan_backward",
    )(dtm, dtu, dcore, b_wide, c_wide, rates)
    return ddtu, ddt, da, db[0].reshape(steps, STATE), dc[0].reshape(steps, STATE)


def conv_act(position, inner, tap_weights, tap_bias):
    row_count = inner.shape[0]
    ext_rows = jnp.pad(inner, ((CONV - 1, 0), (0, 0)))
    conv_sum = tap_bias[None, :] + jnp.zeros(inner.shape, F32)
    for tap_idx in range(CONV):
        shifted = ext_rows[CONV - 1 - tap_idx : CONV - 1 - tap_idx + row_count]
        conv_sum = (
            conv_sum
            + tap_weights[:, tap_idx][None, :]
            * shifted
            * (position >= tap_idx).astype(F32)[:, None]
        )
    return jax.nn.silu(conv_sum)


def gate_mix(core, inner_u, skip_d, gate_z):
    return (core + skip_d[None, :] * inner_u) * jax.nn.silu(gate_z)


def swiglu(gate_proj, up_proj):
    return jax.nn.silu(gate_proj) * up_proj


def squares(row_vals):
    return jnp.sum(row_vals * row_vals)


def local(
    tokens,
    cotangent,
    route,
    lengths,
    gain_in,
    w_qkv,
    w_mix_in,
    w_x,
    w_dt,
    w_small,
    gain_att,
    gain_ssm,
    w_out_att,
    w_out_ssm,
    gain_ffn,
    w_gate,
    w_up,
    w_down,
):
    S, N = lax.axis_size("seq"), lax.axis_size("fsdp")
    s = lax.axis_index("seq")
    micro, tok = tokens.shape[:2]
    pack = tok * S
    rows_d = gain_in.shape[0] // N
    ff = w_gate.shape[1]
    ch_piece, ff_piece = INNER // (N * S), ff // (N * S)
    ch = -(-INNER // (S * LANES)) * LANES
    ffs = -(-ff // (S * LANES)) * LANES
    cols = D // S
    groups = HEADS // KV_HEADS
    first_heads = [(HEADS * i + S - 1) // S for i in range(S + 1)]
    head_counts = [first_heads[i + 1] - first_heads[i] for i in range(S)]
    most = max(head_counts)
    width = most * HEAD
    first_head = jnp.array(first_heads, jnp.int32)[s]
    head_live = jnp.arange(most) < jnp.array(head_counts, jnp.int32)[s]
    live = jnp.repeat(head_live, HEAD).astype(F32)[None, :]
    in_low = (first_head + jnp.arange(most)) // groups <= s

    def gather(shard):
        return lax.all_gather(shard, "fsdp", axis=0, tiled=True)

    def scatter(whole):
        rows, wide = whole.shape[0] // N, whole.shape[1]
        fill = -rows % 8
        whole = whole.astype(BF)
        if fill:
            whole = jnp.pad(whole.reshape(N, rows, wide), ((0, 0), (0, fill), (0, 0)))
            whole = whole.reshape(N * (rows + fill), wide)
        return lax.psum_scatter(whole, "fsdp", scatter_dimension=0, tiled=True)[:rows]

    def part(shard, axis, chunks, wide):
        shape = shard.shape
        piece = shape[axis] // (chunks * S)
        shaped = shard.reshape(shape[:axis] + (chunks, S, piece) + shape[axis + 1 :])
        picked = lax.dynamic_index_in_dim(shaped, s, axis + 1, keepdims=False)
        fill = [(0, 0)] * picked.ndim
        fill[axis + 1] = (0, wide - piece)
        return jnp.pad(picked, fill).reshape(
            shape[:axis] + (chunks * wide,) + shape[axis + 1 :]
        )

    def span(array, axis, start, size):
        return lax.dynamic_slice_in_dim(array, start, size, axis)

    send_hot, land_hot = routing(route, tok)
    x_own = bring(tokens.reshape(micro * tok, D), send_hot, land_hot)
    x_own = x_own.reshape(micro, tok, D)
    q_start = first_head * HEAD
    mix_parts = part(w_mix_in, 1, 2 * N, ch // N)
    small_shard = jnp.concatenate(
        [w_x, w_dt, w_small, jnp.zeros((w_x.shape[0], 1), BF)], axis=1
    )
    w_in = gather(
        jnp.concatenate(
            [
                span(w_qkv, 1, q_start, width),
                span(w_qkv, 1, ATT + s * HEAD, 2 * HEAD),
                span(w_qkv, 1, ATT + KV_WIDTH + s * HEAD, 2 * HEAD),
                mix_parts,
            ],
            axis=1,
        )
    )
    w_small_part = gather(part(small_shard, 0, 1, ch // N))
    w_out_part = gather(part(w_out_ssm, 0, 1, ch // N))
    w_att_cols = gather(span(w_out_att, 1, s * cols, cols))
    w_gu = gather(jnp.concatenate([part(w_gate, 1, N, ffs // N), part(w_up, 1, N, ffs // N)], axis=1))
    w_down_part = gather(part(w_down, 0, 1, ffs // N))
    cot_own = bring(cotangent.reshape(micro * tok, D), send_hot, land_hot)
    cot_own = cot_own.reshape(micro, tok, D)

    w_att_pad = jnp.pad(w_att_cols, ((0, width), (0, 0)))
    w_att_part = (
        seq_deal(jnp.stack([w_att_pad[h * HEAD : h * HEAD + width] for h in first_heads[:S]]))
        .transpose(1, 0, 2)
        .reshape(width, D)
    )

    w_x_part = jnp.pad(w_small_part[:, :PROJ], ((0, 0), (0, PROJ_PAD - PROJ)))
    w_dt_part = w_small_part[:, PROJ : PROJ + DT_RANK]
    small_par = w_small_part[:, PROJ + DT_RANK : PROJ + DT_RANK + CONV + 3 + STATE].astype(F32)
    conv_w = small_par[:, :CONV]
    conv_b = small_par[:, CONV]
    dt_bias = small_par[:, CONV + 1]
    skip_d = small_par[:, CONV + 2]
    decay_a = -jnp.exp(small_par[:, CONV + 3 :])
    rates = decay_a.T
    gain_att_part = span(jnp.pad(gain_att, (0, width)), 0, q_start, width)
    gain_ssm_part = part(gain_ssm, 0, N, ch // N)

    def to_pack(block):
        return seq_gather(block).reshape(pack, block.shape[-1])

    def to_own(partial_rows):
        return seq_scatter(partial_rows.reshape(S, tok, partial_rows.shape[-1]))

    stats = jnp.zeros((6,), F32)
    gains = [jnp.zeros((n,), F32) for n in (D, width, ch, D)]
    kept = []
    results = []
    for m in range(micro):
        segment, position = seq_layout(lengths[m, 0], pack)
        visible = (segment[:, None] == segment[None, :]) & (position[None, :] <= position[:, None])
        x_mine = x_own[m].astype(F32)
        x_pack = to_pack(x_own[m]).astype(F32)
        normed_low = rms_scale(x_pack, gain_in).astype(BF)
        opened = dot(normed_low, w_in, 1, 0).astype(BF)
        q = opened[:, :width].reshape(pack, most, HEAD)
        kv = opened[:, width : width + 4 * HEAD].reshape(pack, 4, HEAD)
        pick_low = in_low[None, :, None]
        keys = jnp.where(pick_low, kv[:, 0:1], kv[:, 1:2])
        values = jnp.where(pick_low, kv[:, 2:3], kv[:, 3:4])
        scores = jnp.einsum("thd,uhd->htu", q, keys, preferred_element_type=F32) * 0.125
        masked = jnp.where(visible, scores, -1e30)
        row_top = jnp.max(masked, axis=-1, keepdims=True)
        exp_terms = jnp.exp(masked - row_top)
        row_total = jnp.sum(exp_terms, axis=-1, keepdims=True)
        probs = exp_terms / row_total
        context = (
            jnp.einsum("htu,uhd->thd", probs.astype(BF), values, preferred_element_type=F32)
        ).reshape(pack, width) * live
        at = width + 4 * HEAD
        inner = opened[:, at : at + ch].astype(F32)
        gate_z = opened[:, at + ch :].astype(F32)
        inner_u, conv_back = jax.vjp(partial(conv_act, position), inner, conv_w, conv_b)
        u_low = inner_u.astype(BF)
        projected = seq_sum(dot(w_x_part, u_low, 0, 1).astype(BF)).astype(BF)
        dt_in = projected[:DT_RANK]
        in_b = projected[DT_RANK : DT_RANK + STATE].astype(F32)
        out_c = projected[DT_RANK + STATE : PROJ].astype(F32)
        dt_lin = dot(dt_in, w_dt_part, 0, 1) + dt_bias[None, :]
        step_dt = jax.nn.softplus(dt_lin)
        dtm = jnp.where((position > 0)[:, None], step_dt, 1e30)
        dtu = step_dt * inner_u
        b_wide = jnp.broadcast_to(in_b.T[:, :, None], (pack, STATE, LANES))
        c_wide = jnp.broadcast_to(out_c.T[:, :, None], (pack, STATE, LANES))
        core = scan_forward(dtm, dtu, b_wide, c_wide, rates)
        ssm_out, gate_back = jax.vjp(gate_mix, core, inner_u, skip_d, gate_z)
        row_sums = jnp.stack(
            [jnp.sum(context * context, axis=1), jnp.sum(ssm_out * ssm_out, axis=1)]
        )
        row_sums = seq_sum(row_sums)
        scale_att = lax.rsqrt(row_sums[0] / ATT + EPS)[:, None]
        scale_ssm = lax.rsqrt(row_sums[1] / INNER + EPS)[:, None]
        att_low = (context * scale_att * gain_att_part).astype(BF)
        ssm_low = (ssm_out * scale_ssm * gain_ssm_part).astype(BF)
        mixer_out = to_own(
            0.5 * (dot(att_low, w_att_part, 1, 0) + dot(ssm_low, w_out_part, 1, 0))
        )
        hidden = x_mine + mixer_out
        ffn_in, ffn_norm_back = jax.vjp(rms_scale, hidden, gain_ffn)
        ffn_low = to_pack(ffn_in.astype(BF))
        gate_proj = dot(ffn_low, w_gu[:, :ffs], 1, 0)
        up_proj = dot(ffn_low, w_gu[:, ffs:], 1, 0)
        act_val, act_back = jax.vjp(swiglu, gate_proj, up_proj)
        act_low = act_val.astype(BF)
        ffn_out = to_own(dot(act_low, w_down_part, 1, 0))
        result = hidden + ffn_out
        results.append(result.astype(BF))
        here = lax.dynamic_slice_in_dim(row_sums, s * tok, tok, 1)
        stats = stats + jnp.stack(
            [
                squares(x_mine),
                jnp.sum(here[0]),
                jnp.sum(here[1]),
                squares(mixer_out),
                squares(ffn_out),
                squares(result),
            ]
        )
        cot_mine = cot_own[m].astype(F32)
        cot_low = to_pack(cot_own[m])
        d_act = dot(cot_low, w_down_part, 1, 1)
        d_gate, d_up = act_back(d_act)
        dgu_low = jnp.concatenate([d_gate, d_up], axis=1).astype(BF)
        d_ffn_in = to_own(dot(dgu_low, w_gu, 1, 1))
        d_hidden_norm, d_gain_ffn = ffn_norm_back(d_ffn_in)
        d_hidden = cot_mine + d_hidden_norm
        dmix_low = to_pack(d_hidden.astype(BF))
        d_att = 0.5 * dot(dmix_low, w_att_part, 1, 1) * live
        d_ssm = lax.optimization_barrier(0.5 * dot(dmix_low, w_out_part, 1, 1))
        d_gain_att = jnp.sum(d_att * context * scale_att, axis=0)
        d_gain_ssm = jnp.sum(d_ssm * ssm_out * scale_ssm, axis=0)
        t_att = d_att * gain_att_part
        t_ssm = d_ssm * gain_ssm_part
        back_sums = seq_sum(
            jnp.stack([jnp.sum(t_att * context, axis=1), jnp.sum(t_ssm * ssm_out, axis=1)])
        )
        d_context = (
            t_att * scale_att - context * scale_att**3 * (back_sums[0] / ATT)[:, None]
        ) * live
        d_ssm_out = t_ssm * scale_ssm - ssm_out * scale_ssm**3 * (back_sums[1] / INNER)[:, None]
        d_core, d_u_gate, d_skip, d_gate_z = gate_back(d_ssm_out)
        ddtu, ddt, d_rates, d_in_b, d_out_c = scan_backward(
            dtm, dtu, d_core, b_wide, c_wide, rates
        )
        d_decay = d_rates.T
        d_step = ddt + ddtu * inner_u
        d_lin = d_step * jax.nn.sigmoid(dt_lin)
        d_dt_bias = jnp.sum(d_lin, axis=0)
        ddt_low = d_lin.astype(BF)
        dproj = jnp.concatenate(
            [
                dot(w_dt_part, ddt_low, 0, 1),
                d_in_b.T,
                d_out_c.T,
                jnp.zeros((PROJ_PAD - PROJ, pack), F32),
            ],
            axis=0,
        )
        dproj_low = seq_sum(dproj.astype(BF)).astype(BF)
        d_inner_u = d_u_gate + ddtu * step_dt + dot(dproj_low, w_x_part, 0, 1)
        d_inner, d_conv_w, d_conv_b = conv_back(d_inner_u)
        small_grad = jnp.concatenate(
            [d_conv_w, d_conv_b[:, None], d_dt_bias[:, None], d_skip[:, None], d_decay * decay_a],
            axis=1,
        )
        dctx_low = d_context.astype(BF).reshape(pack, most, HEAD)
        d_values = jnp.einsum(
            "htu,thd->uhd", probs.astype(BF), dctx_low, preferred_element_type=F32
        )
        d_probs = jnp.einsum("thd,uhd->htu", dctx_low, values, preferred_element_type=F32)
        dscore_low = (
            probs * (d_probs - jnp.sum(probs * d_probs, axis=-1, keepdims=True))
        ).astype(BF)
        d_q = jnp.einsum("htu,uhd->thd", dscore_low, keys, preferred_element_type=F32) * 0.125
        d_keys = jnp.einsum("htu,thd->uhd", dscore_low, q, preferred_element_type=F32) * 0.125
        low_part, high_part = pick_low, ~pick_low

        def kv_sum(d_heads):
            return [
                jnp.sum(jnp.where(low_part, d_heads, 0.0), axis=1),
                jnp.sum(jnp.where(high_part, d_heads, 0.0), axis=1),
            ]

        d_opened = jnp.concatenate(
            [d_q.reshape(pack, width)] + kv_sum(d_keys) + kv_sum(d_values) + [d_inner, d_gate_z],
            axis=1,
        ).astype(BF)
        d_normed = to_own(dot(d_opened, w_in, 1, 1))
        _, norm_back = jax.vjp(rms_scale, x_mine, gain_in)
        d_x_norm, d_gain_in = norm_back(d_normed)
        d_x = d_hidden + d_x_norm
        gains = [
            a + b for a, b in zip(gains, (d_gain_in, d_gain_att, d_gain_ssm, d_gain_ffn))
        ]
        kept.append(
            dict(
                act=act_low,
                cot=cot_low,
                ffn=ffn_low,
                dgu=dgu_low,
                att=att_low,
                ssm=ssm_low,
                dmix=dmix_low,
                u=u_low,
                dproj=dproj_low,
                dt_in=dt_in,
                ddt=ddt_low,
                normed=normed_low,
                opened=d_opened,
                small=small_grad,
                dx=d_x.astype(BF),
            )
        )

    def both(name, axis=0):
        return jnp.concatenate([one[name] for one in kept], axis=axis)

    g_down = scatter(dot(both("act"), both("cot"), 0, 0))
    g_gu = scatter(dot(both("ffn"), both("dgu"), 0, 0))
    g_att_rows = (0.5 * dot(both("att"), both("dmix"), 0, 0)).astype(BF)
    g_att_blocks = seq_deal(g_att_rows.reshape(width, S, cols).transpose(1, 0, 2))
    g_att_whole = jnp.concatenate(
        [g_att_blocks[i, : head_counts[i] * HEAD] for i in range(S)], axis=0
    )
    g_att = scatter(g_att_whole).astype(F32)
    g_ssm = scatter(0.5 * dot(both("ssm"), both("dmix"), 0, 0))
    g_xdt = jnp.concatenate(
        [
            dot(both("u"), both("dproj", 1), 0, 1)[:, :PROJ],
            dot(both("ddt"), both("dt_in", 1), 0, 1),
            kept[0]["small"] + kept[1]["small"],
            jnp.zeros((ch, 1), F32),
        ],
        axis=1,
    )
    g_xdt = scatter(g_xdt)
    g_in = scatter(dot(both("normed"), both("opened"), 0, 0))

    def rows_back(shard):
        blocks = seq_deal(shard.reshape(shard.shape[0], S, cols).transpose(1, 0, 2))
        return blocks.reshape(S * shard.shape[0], cols).astype(F32)

    def cols_back(shard, chunks, piece):
        rows = shard.shape[0]
        blocks = shard.reshape(rows, S, chunks // S, -1)[..., :piece].transpose(1, 0, 2, 3)
        got = seq_deal(blocks)
        return got.transpose(1, 2, 0, 3).reshape(rows, chunks * piece).astype(F32)

    out_down = rows_back(g_down[:ff_piece])
    out_ssm = rows_back(g_ssm[:ch_piece])
    out_gate = cols_back(g_gu[:, :ffs], N, ff_piece)
    out_up = cols_back(g_gu[:, ffs:], N, ff_piece)
    at = width + 4 * HEAD
    out_mix = cols_back(g_in[:, at:], 2 * N, ch_piece)
    kv_at = jnp.zeros((rows_d, 2 * KV_WIDTH), BF)
    kv_at = lax.dynamic_update_slice_in_dim(kv_at, g_in[:, width : width + 2 * HEAD], s * HEAD, 1)
    kv_at = lax.dynamic_update_slice_in_dim(
        kv_at, g_in[:, width + 2 * HEAD : at], KV_WIDTH + s * HEAD, 1
    )
    q_at = jnp.zeros((rows_d, ATT + width), BF)
    q_live = jnp.where(live > 0, g_in[:, :width], 0)
    q_at = lax.dynamic_update_slice_in_dim(q_at, q_live, q_start, 1)
    qkv_at = jnp.concatenate([q_at[:, :ATT], kv_at], axis=1)
    out_qkv = seq_scatter(qkv_at.reshape(rows_d, S, -1).transpose(1, 0, 2))
    small_all = seq_gather(g_xdt[:ch_piece]).reshape(-1, g_xdt.shape[1]).astype(F32)
    out_x = span(small_all[:, :PROJ], 1, s * (PROJ // S), PROJ // S)
    out_dt = span(small_all[:, PROJ : PROJ + DT_RANK], 1, s * (DT_RANK // S), DT_RANK // S)
    out_small = small_all[:, PROJ + DT_RANK : PROJ + DT_RANK + CONV + 3 + STATE]

    att_at = lax.dynamic_update_slice_in_dim(
        jnp.zeros((ATT + width,), F32), gains[1] * live[0], q_start, 0
    )[:ATT]
    ssm_at = lax.dynamic_update_index_in_dim(
        jnp.zeros((N, S, ch_piece), F32), gains[2].reshape(N, -1)[:, :ch_piece], s, 1
    ).reshape(INNER)
    sums = lax.psum(
        jnp.concatenate([gains[0], att_at, ssm_at, gains[3], stats]), ("seq", "fsdp")
    )
    ends = [0, D, D + ATT, D + ATT + INNER, D + ATT + INNER + D, D + ATT + INNER + D + 6]
    g_gain_in, g_gain_att, g_gain_ssm, g_gain_ffn, stat_sum = [
        sums[a:b] for a, b in zip(ends[:-1], ends[1:])
    ]
    widths = jnp.array([D, ATT, INNER, D, D, D], F32)
    rms = jnp.sqrt(stat_sum / (widths * (micro * pack * N)))
    outputs = give(jnp.concatenate(results, axis=0), send_hot, land_hot)
    input_grads = give(both("dx"), send_hot, land_hot)
    return (
        outputs.reshape(tokens.shape),
        input_grads.reshape(tokens.shape),
        g_gain_in,
        out_qkv,
        out_mix,
        out_x,
        out_dt,
        out_small,
        out_small[:, CONV + 1],
        g_gain_att,
        g_gain_ssm,
        g_att,
        out_ssm,
        g_gain_ffn,
        out_gate,
        out_up,
        out_down,
        rms,
    )


def solution(mesh):
    rows = P(None, ("seq", "fsdp"), None)
    shard = P("fsdp", None)
    both = P("fsdp", "seq")
    placed = (rows, rows, P(None, "seq"), P(None, "fsdp", None), P())
    placed += (shard,) * 5 + (P(), P(), shard, shard, P(), shard, shard, shard)
    return jax.shard_map(
        local,
        mesh=mesh,
        in_specs=placed,
        out_specs=(
            rows,
            rows,
            P(),
            both,
            both,
            both,
            both,
            shard,
            P("fsdp"),
            P(),
            P(),
            both,
            both,
            P(),
            both,
            both,
            both,
            P(),
        ),
        check_vma=False,
    )
```

time: 4300 us -> 1110 us (0.26)
  waiting for transfers between devices: 1410 us -> 237 us
  other arithmetic: 1140 us -> 97.2 us
  local copies, waits for them, and re-layouts: 1060 us -> 249 us
  blocking collectives: 226 us -> 57.4 us
  matrix products: 314 us -> 199 us
  starting transfers between devices: 45.2 us -> 145 us
  Pallas kernels: 0 us -> 94.7 us
    unnamed x44 -> x13, waiting for transfers between devices: 785 us -> 0.18 us
    reduce_sum x412 -> x19, other arithmetic: 598 us -> 24.5 us  [the longest x1 6.79 us: local(): jnp.sum(ssm_out * ssm_out, axis=1)]
    dynamic_slice x1346 -> x13, local copies, waits for them, and re-layouts: 556 us -> 16.1 us  [the longest x3 10.1 us: part(): picked = lax.dynamic_index_in_dim(shaped, s, axis + 1, keepdims=False)]
    dynamic_update_slice x384 -> x7, other arithmetic: 431 us -> 3.2 us  [the longest x6 3.08 us: seq_gather(): lax.dynamic_update_index_in_dim(jnp.zeros((size,) + block.shape, block.dt...]
    reduce_scatter x4, waiting for transfers between devices: 368 us -> 76 us  [scatter(): lax.psum_scatter(whole, 'fsdp', scatter_dimension=0, tiled=True)[:rows]]
    all_gather x7 -> x5, waiting for transfers between devices: 186 us -> 0.06 us  [gather(): return lax.all_gather(shard, 'fsdp', axis=0, tiled=True)]
    dynamic_update_slice x1200 -> x84, local copies, waits for them, and re-layouts: 220 us -> 47.9 us  [the longest x51 34.4 us: seq_gather(): out = lax.dynamic_update_index_in_dim(out, swap(block, k), here ^ k, 0)]
    all_gather x11 -> x1, blocking collectives: 144 us -> 17.2 us  [gather(): return lax.all_gather(shard, 'fsdp', axis=0, tiled=True)]
where the time goes in v1:
time: 1110 us; the launch traced here: 1100 us
  local copies, waits for them, and re-layouts  249 us (22%)
  waiting for transfers between devices  237 us (21%)
  matrix products  199 us (18%)
  starting transfers between devices  145 us (13%)
  other arithmetic  97.2 us (9%)
  Pallas kernels  94.7 us (9%)
  blocking collectives  57.4 us (5%)
  between operations  18.8 us (2%)
    dot_general x45, matrix products, dot(): lax.dot_general(left_op, right_op, (((left_dim,), (right_dim,)), ((), ())...  184 us
    ppermute x99, starting transfers between devices, swap(): return lax.ppermute(array, 'seq', [(i, i ^ k) for i in range(size)])  122 us
    ppermute x99, waiting for transfers between devices, swap(): return lax.ppermute(array, 'seq', [(i, i ^ k) for i in range(size)])  116 us
    reduce_scatter x4, waiting for transfers between devices, scatter(): lax.psum_scatter(whole, 'fsdp', scatter_dimension=0, tiled=True)[:rows]  76 us
    pallas_call x2, Pallas kernels, scan_backward(): pl.pallas_call(partial(scan_back_kernel, groups, steps), out_shape=[rows,...  65.8 us
    all_to_all x4, waiting for transfers between devices, exchange(): return lax.all_to_all(rows, 'fsdp', split_axis=0, concat_axis=0, tiled=True)  44.9 us
    psum x1, blocking collectives, local(): lax.psum(jnp.concatenate([gains[0], att_at, ssm_at, gains[3], stats]), ('...  40.3 us
    reshape x7, local copies, waits for them, and re-layouts, part(): shaped = shard.reshape(shape[:axis] + (chunks, S, piece) + shape[axis + 1:])  38.9 us
  transfers between devices with their start and end apart: 114, of which 39 were waited for; matrix products, arithmetic and copies ran while one was open for 43% of the time, Pallas kernels for 6%

profile of v1, /device:TPU:0, one launch (start us, length us, event | category | flops | bytes accessed | tf_op | source)
XLA Modules:
  0.0 1098.7 jit_solution(8518090469809190434)
XLA Ops:
  13.3 14.6 %reshape.956 = bf16[200,16,4,100]{3,2,1,0:T(4,128)(2,1)} reshape(bf16[200,6400]{1,0:T(8,128)(2,1)} %param.27) | data formatting | bytes 5120000 | tf_op jit(solution)/shard_map/reshape | solution.py:390
  40.8 6.3 all-to-all-start
  47.3 10.3 reshape.970
  57.6 11.6 %reshape.972 = bf16[200,8,4,172]{3,2,1,0:T(4,128)(2,1)} reshape(bf16[200,5504]{1,0:T(8,128)(2,1)} %param.37) | data formatting | bytes 4403200 | tf_op jit(solution)/shard_map/reshape | solution.py:390
  69.2 6.4 constant_dynamic-slice_fusion.10
  85.5 17.2 %all-gather = bf16[1,896,256]{2,1,0:T(8,128)(2,1)S(1)} all-gather(bf16[1,112,256]{2,1,0:T(8,128)(2,1)S(1)} %pad.104), channel_id=2, replica_groups=mesh['seq'=4,'fsdp'=8] {'fsdp'}, dimensions={1}, use_global_device_ids=true | all-gather | bytes 516096 | tf_op jit(solution)/shard_map/all_gather | solution.py:376
  110.1 7.1 all-to-all-start.2
  127.6 25.4 %all-to-all-done.2 = bf16[8,24,1600]{2,1,0:T(8,128)(2,1)} async-done(((bf16[8,24,1600]{2,1,0:T(8,128)(2,1)}), bf16[8,24,1600]{2,1,0:T(8,128)(2,1)}, u32[]{:S(2)}, u32[]{:S(2)}) %all-to-all-start.2) | async-done | bytes 614432 | tf_op jit(solution)/shard_map/all_to_all | solution.py:118
  194.7 9.7 collective-permute-done.9
  208.5 17.0 %collective-permute-done.10 = bf16[448,400]{1,0:T(8,128)(2,1)S(1)} collective-permute-done((bf16[448,400]{1,0:T(8,128)(2,1)S(1)}, bf16[448,400]{1,0:T(8,128)(2,1)S(1)}, u32[]{:S(2)}, u32[]{:S(2)}) %collective-permute-start.10) | collective-permute-done | bytes 358432 | tf_op jit(solution)/shard_map/ppermute | solution.py:55
  229.6 6.6 fusion.4
  239.8 7.6 convolution_convert_fusion.4
  306.0 14.3 %scan_forward.3 = f32[384,896]{1,0:T(8,128)} custom-call(f32[384,896]{1,0:T(8,128)} %get-tuple-element.297.dtm_ref, f32[384,896]{1,0:T(8,128)} %get-tuple-element.296.dtu_ref, f32[384,16,128]{2,1,0:T(8,128)} %broadcast_in_dim.654.b_ref, f32[384,16,128]{2,1,0:T(8,128)} %broadcast_in_dim.655.c_ref, f32[16,896]{1,0:T(8,128)} %fusion.259.a_ref), custom_call_target="tpu_custom_call" | custom-call | flops 88080384 | bytes 40000000 | tf_op jit(solution)/shard_map/scan_forward/pallas_call | solution.py:267
  329.3 14.5 %scan_forward.2 = f32[384,896]{1,0:T(8,128)} custom-call(f32[384,896]{1,0:T(8,128)} %get-tuple-element.295.dtm_ref, f32[384,896]{1,0:T(8,128)} %get-tuple-element.294.dtu_ref, f32[384,16,128]{2,1,0:T(8,128)} %broadcast_in_dim.624.b_ref, f32[384,16,128]{2,1,0:T(8,128)} %broadcast_in_dim.625.c_ref, f32[16,896]{1,0:T(8,128)} %fusion.259.a_ref), custom_call_target="tpu_custom_call" | custom-call | flops 88080384 | bytes 40000000 | tf_op jit(solution)/shard_map/scan_forward/pallas_call | solution.py:267
  343.9 6.8 multiply_reduce_fusion.19
  451.9 7.7 fusion.60
  467.0 6.5 multiply_convert_fusion.5
  473.5 8.8 fusion.64
  553.6 6.8 multiply_reduce_fusion.4
  564.0 33.0 %scan_backward.3 = (f32[384,896]{1,0:T(8,128)}, f32[384,896]{1,0:T(8,128)}, f32[16,896]{1,0:T(8,128)}, f32[8,6144]{1,0:T(8,128)}, f32[8,6144]{1,0:T(8,128)}) custom-call(f32[384,896]{1,0:T(8,128)} %get-tuple-element.297.dtm_ref, f32[384,896]{1,0:T(8,128)} %get-tuple-element.296.dtu_ref, f32[384,896]{1,0:T(8,128)} %get-tuple-element.204.dcore_ref, ...), custom_call_target="tpu_custom_call" | custom-call | flops 220200960 | bytes 100000000 | tf_op jit(solution)/shard_map/scan_backward/pallas_call | solution.py:287
  611.3 32.9 %scan_backward.2 = (f32[384,896]{1,0:T(8,128)}, f32[384,896]{1,0:T(8,128)}, f32[16,896]{1,0:T(8,128)}, f32[8,6144]{1,0:T(8,128)}, f32[8,6144]{1,0:T(8,128)}) custom-call(f32[384,896]{1,0:T(8,128)} %get-tuple-element.295.dtm_ref, f32[384,896]{1,0:T(8,128)} %get-tuple-element.294.dtu_ref, f32[384,896]{1,0:T(8,128)} %get-tuple-element.208.dcore_ref, ...), custom_call_target="tpu_custom_call" | custom-call | flops 220200960 | bytes 100000000 | tf_op jit(solution)/shard_map/scan_backward/pallas_call | solution.py:287
  668.5 8.8 multiply_reduce_fusion.8
  681.6 6.7 multiply_reduce_fusion.13
  726.9 8.2 convolution_convert_fusion.2
  769.5 10.8 convolution_convert_fusion.1
  781.8 16.9 %convolution_convert_fusion = bf16[1600,2816]{1,0:T(8,128)(2,1)} fusion(bf16[384,1408]{1,0:T(8,128)(2,1)} %get-tuple-element.246, bf16[384,1408]{1,0:T(8,128)(2,1)} %copy-done.221, bf16[384,1408]{1,0:T(8,128)(2,1)S(1)} %copy-done.220, bf16[384,1408]{1,0:T(8,128)(2,1)S(1)} %copy-done.218, bf16[384,1600]{1,0:T(8,128)(2,1)} %bitcast.102, ...), kind=kOutput, calls=%fused_computation.2 | convolution fusion | flops 6947323904 | bytes 15794176 | tf_op jit(solution)/shard_map/dot_general | solution.py:30
  801.0 6.5 fusion.339
  811.1 6.3 fusion.338
  846.6 40.3 %psum.7 = f32[8006]{0:T(1024)S(1)} all-reduce(f32[8006]{0:T(1024)S(1)} %concatenate.152), channel_id=1, replica_groups=mesh['seq'=4,'fsdp'=8] {'seq','fsdp'}, use_global_device_ids=true, to_apply=%region_68.69 | all-reduce | flops 8006 | bytes 64048 | tf_op jit(solution)/shard_map/psum | solution.py:684
  912.2 19.5 %all-to-all-done.1 = bf16[8,24,1600]{2,1,0:T(8,128)(2,1)S(1)} async-done(((bf16[8,24,1600]{2,1,0:T(8,128)(2,1)}), bf16[8,24,1600]{2,1,0:T(8,128)(2,1)S(1)}, u32[]{:S(2)}, u32[]{:S(2)}) %all-to-all-start.1) | async-done | bytes 614432 | tf_op jit(solution)/shard_map/all_to_all | solution.py:118
  953.8 9.9 reduce-scatter.11.cloned.1.call-done
  996.8 66.1 %reduce-scatter.15.cloned.1.call-done = bf16[200,2816]{1,0:T(8,128)(2,1)} async-done(((bf16[1600,2816]{1,0:T(8,128)(2,1)}), bf16[200,2816]{1,0:T(8,128)(2,1)}) %reduce-scatter.15.cloned.1.call-update) | async-done | bytes 1126416 | tf_op jit(solution)/shard_map/reduce_scatter | solution.py:385
  (1172 shorter events, 609.2 us)
Async XLA Ops:
  7.2 183.0 %all-gather.11.cloned.1.call-start = ((), (), s32[]{:S(2)}) async-start(), calls=%async_computation.11 | async-start | bytes 1843200 | tf_op jit(solution)/shard_map/all_gather | solution.py:376
  9.1 220.4 %all-gather.17.cloned.1.call-start = ((), (), s32[]{:S(2)}) async-start(), calls=%async_computation.18 | async-start | bytes 5271552 | tf_op jit(solution)/shard_map/all_gather | solution.py:376
  12.0 227.8 %all-gather.9.cloned.1.call-start = ((), (), s32[]{:S(2)}) async-start(), calls=%async_computation.10 | async-start | bytes 9216000 | tf_op jit(solution)/shard_map/all_gather | solution.py:376
  37.3 328.9 %all-gather.15.cloned.1.call-start = ((), (), s32[]{:S(2)}) async-start(), calls=%async_computation.17 | async-start | bytes 3354624 | tf_op jit(solution)/shard_map/all_gather | solution.py:376
  40.8 69.3 %all-to-all-start = ((bf16[8,24,1600]{2,1,0:T(8,128)(2,1)}), bf16[8,24,1600]{2,1,0:T(8,128)(2,1)S(1)}, u32[]{:S(2)}, u32[]{:S(2)}) async-start(bf16[8,24,1600]{2,1,0:T(8,128)(2,1)} %bitcast.2), calls=%async_computation | async-start | bytes 1277952 | tf_op jit(solution)/shard_map/all_to_all | solution.py:118
  47.1 388.2 %all-gather.13.cloned.1.call-start = ((), (), s32[]{:S(2)}) async-start(), calls=%async_computation.12 | async-start | bytes 10137600 | tf_op jit(solution)/shard_map/all_gather | solution.py:376
  110.1 42.9 %all-to-all-start.2 = ((bf16[8,24,1600]{2,1,0:T(8,128)(2,1)}), bf16[8,24,1600]{2,1,0:T(8,128)(2,1)}, u32[]{:S(2)}, u32[]{:S(2)}) async-start(bf16[8,24,1600]{2,1,0:T(8,128)(2,1)} %bitcast.112), calls=%async_computation.2 | async-start | bytes 1277952 | tf_op jit(solution)/shard_map/all_to_all | solution.py:118
  117.1 772.8 %reduce-scatter.19.cloned.1.call-start = ((), (), s32[]{:S(2)}) async-start(), calls=%async_computation.19 | async-start | bytes 516096
  118.9 37.7 %collective-permute-start.21 = (bf16[96,1600]{1,0:T(8,128)(2,1)}, bf16[96,1600]{1,0:T(8,128)(2,1)}, u32[]{:S(2)}, u32[]{:S(2)}) collective-permute-start(bf16[96,1600]{1,0:T(8,128)(2,1)} %get-tuple-element.344), channel_id=1, source_target_pairs={{0,8},{8,0},{16,24},{24,16},{1,9},{9,1},{17,25},{25,17},{2,10},{10... | collective-permute-start | bytes 921608 | tf_op jit(solution)/shard_map/ppermute | solution.py:55
  120.6 39.6 %collective-permute-start.22 = (bf16[96,1600]{1,0:T(8,128)(2,1)}, bf16[96,1600]{1,0:T(8,128)(2,1)}, u32[]{:S(2)}, u32[]{:S(2)}) collective-permute-start(bf16[96,1600]{1,0:T(8,128)(2,1)} %get-tuple-element.344), channel_id=1, source_target_pairs={{0,16},{8,24},{16,0},{24,8},{1,17},{9,25},{17,1},{25,9},{2,18},{10... | collective-permute-start | bytes 921608 | tf_op jit(solution)/shard_map/ppermute | solution.py:55
  122.1 39.8 %collective-permute-start.23 = (bf16[96,1600]{1,0:T(8,128)(2,1)}, bf16[96,1600]{1,0:T(8,128)(2,1)}, u32[]{:S(2)}, u32[]{:S(2)}) collective-permute-start(bf16[96,1600]{1,0:T(8,128)(2,1)} %get-tuple-element.344), channel_id=1, source_target_pairs={{0,24},{8,16},{16,8},{24,0},{1,25},{9,17},{17,9},{25,1},{2,26},{10... | collective-permute-start | bytes 921608 | tf_op jit(solution)/shard_map/ppermute | solution.py:55
  122.4 41.4 %collective-permute-start = (bf16[96,1600]{1,0:T(8,128)(2,1)}, bf16[96,1600]{1,0:T(8,128)(2,1)}, u32[]{:S(2)}, u32[]{:S(2)}) collective-permute-start(bf16[96,1600]{1,0:T(8,128)(2,1)} %get-tuple-element.343), channel_id=1, source_target_pairs={{0,8},{8,0},{16,24},{24,16},{1,9},{9,1},{17,25},{25,17},{2,10},{10... | collective-permute-start | bytes 921608 | tf_op jit(solution)/shard_map/ppermute | solution.py:55
  124.1 44.0 %collective-permute-start.1 = (bf16[96,1600]{1,0:T(8,128)(2,1)}, bf16[96,1600]{1,0:T(8,128)(2,1)}, u32[]{:S(2)}, u32[]{:S(2)}) collective-permute-start(bf16[96,1600]{1,0:T(8,128)(2,1)} %get-tuple-element.343), channel_id=1, source_target_pairs={{0,16},{8,24},{16,0},{24,8},{1,17},{9,25},{17,1},{25,9},{2,18},{10... | collective-permute-start | bytes 921608 | tf_op jit(solution)/shard_map/ppermute | solution.py:55
  177.7 29.8 %collective-permute-start.59 = (bf16[96,1600]{1,0:T(8,128)(2,1)S(1)}, bf16[96,1600]{1,0:T(8,128)(2,1)}, u32[]{:S(2)}, u32[]{:S(2)}) collective-permute-start(bf16[96,1600]{1,0:T(8,128)(2,1)S(1)} %get-tuple-element.342), channel_id=1, source_target_pairs={{0,24},{8,16},{16,8},{24,0},{1,25},{9,17},{17,9},{25,1},{2,26},{10... | collective-permute-start | bytes 921608 | tf_op jit(solution)/shard_map/ppermute | solution.py:55
  448.3 36.5 %collective-permute-start.18 = (bf16[96,1600]{1,0:T(8,128)(2,1)S(1)}, bf16[96,1600]{1,0:T(8,128)(2,1)S(1)}, u32[]{:S(2)}, u32[]{:S(2)}) collective-permute-start(bf16[96,1600]{1,0:T(8,128)(2,1)S(1)} %get-tuple-element.255), channel_id=1, source_target_pairs={{0,8},{8,0},{16,24},{24,16},{1,9},{9,1},{17,25},{25,17},{2,10},{10... | collective-permute-start | bytes 921608 | tf_op jit(solution)/shard_map/ppermute | solution.py:55
  448.8 37.7 %collective-permute-start.19 = (bf16[96,1600]{1,0:T(8,128)(2,1)S(1)}, bf16[96,1600]{1,0:T(8,128)(2,1)S(1)}, u32[]{:S(2)}, u32[]{:S(2)}) collective-permute-start(bf16[96,1600]{1,0:T(8,128)(2,1)S(1)} %get-tuple-element.257), channel_id=1, source_target_pairs={{0,16},{8,24},{16,0},{24,8},{1,17},{9,25},{17,1},{25,9},{2,18},{10... | collective-permute-start | bytes 921608 | tf_op jit(solution)/shard_map/ppermute | solution.py:55
  450.5 36.5 %collective-permute-start.20 = (bf16[96,1600]{1,0:T(8,128)(2,1)S(1)}, bf16[96,1600]{1,0:T(8,128)(2,1)S(1)}, u32[]{:S(2)}, u32[]{:S(2)}) collective-permute-start(bf16[96,1600]{1,0:T(8,128)(2,1)S(1)} %get-tuple-element.256), channel_id=1, source_target_pairs={{0,24},{8,16},{16,8},{24,0},{1,25},{9,17},{17,9},{25,1},{2,26},{10... | collective-permute-start | bytes 921608 | tf_op jit(solution)/shard_map/ppermute | solution.py:55
  459.7 29.0 %collective-permute-start.42 = (bf16[96,1600]{1,0:T(8,128)(2,1)S(1)}, bf16[96,1600]{1,0:T(8,128)(2,1)S(1)}, u32[]{:S(2)}, u32[]{:S(2)}) collective-permute-start(bf16[96,1600]{1,0:T(8,128)(2,1)S(1)} %get-tuple-element.258), channel_id=1, source_target_pairs={{0,8},{8,0},{16,24},{24,16},{1,9},{9,1},{17,25},{25,17},{2,10},{10... | collective-permute-start | bytes 921608 | tf_op jit(solution)/shard_map/ppermute | solution.py:55
  460.2 29.9 %collective-permute-start.43 = (bf16[96,1600]{1,0:T(8,128)(2,1)S(1)}, bf16[96,1600]{1,0:T(8,128)(2,1)S(1)}, u32[]{:S(2)}, u32[]{:S(2)}) collective-permute-start(bf16[96,1600]{1,0:T(8,128)(2,1)S(1)} %get-tuple-element.260), channel_id=1, source_target_pairs={{0,16},{8,24},{16,0},{24,8},{1,17},{9,25},{17,1},{25,9},{2,18},{10... | collective-permute-start | bytes 921608 | tf_op jit(solution)/shard_map/ppermute | solution.py:55
  490.1 25.6 %collective-permute-start.60 = (bf16[96,1600]{1,0:T(8,128)(2,1)S(1)}, bf16[96,1600]{1,0:T(8,128)(2,1)S(1)}, u32[]{:S(2)}, u32[]{:S(2)}) collective-permute-start(bf16[96,1600]{1,0:T(8,128)(2,1)S(1)} %get-tuple-element.267), channel_id=1, source_target_pairs={{0,8},{8,0},{16,24},{24,16},{1,9},{9,1},{17,25},{25,17},{2,10},{10... | collective-permute-start | bytes 921608 | tf_op jit(solution)/shard_map/ppermute | solution.py:55
  504.9 24.5 %collective-permute-start.45 = (bf16[96,1600]{1,0:T(8,128)(2,1)S(1)}, bf16[96,1600]{1,0:T(8,128)(2,1)S(1)}, u32[]{:S(2)}, u32[]{:S(2)}) collective-permute-start(bf16[96,1600]{1,0:T(8,128)(2,1)S(1)} %get-tuple-element.214), channel_id=1, source_target_pairs={{0,8},{8,0},{16,24},{24,16},{1,9},{9,1},{17,25},{25,17},{2,10},{10... | collective-permute-start | bytes 921608 | tf_op jit(solution)/shard_map/ppermute | solution.py:55
  560.4 45.6 %collective-permute-start.48 = (f32[2,384]{1,0:T(2,128)S(1)}, f32[2,384]{1,0:T(2,128)S(1)}, u32[]{:S(2)}, u32[]{:S(2)}) collective-permute-start(f32[2,384]{1,0:T(2,128)S(1)} %get-tuple-element.385), channel_id=1, source_target_pairs={{0,8},{8,0},{16,24},{24,16},{1,9},{9,1},{17,25},{25,17},{2,10},{10... | collective-permute-start | bytes 9224 | tf_op jit(solution)/shard_map/ppermute | solution.py:55
  561.4 44.6 %collective-permute-start.49 = (f32[2,384]{1,0:T(2,128)S(1)}, f32[2,384]{1,0:T(2,128)S(1)}, u32[]{:S(2)}, u32[]{:S(2)}) collective-permute-start(f32[2,384]{1,0:T(2,128)S(1)} %get-tuple-element.385), channel_id=1, source_target_pairs={{0,16},{8,24},{16,0},{24,8},{1,17},{9,25},{17,1},{25,9},{2,18},{10... | collective-permute-start | bytes 9224 | tf_op jit(solution)/shard_map/ppermute | solution.py:55
  562.4 43.8 %collective-permute-start.50 = (f32[2,384]{1,0:T(2,128)S(1)}, f32[2,384]{1,0:T(2,128)S(1)}, u32[]{:S(2)}, u32[]{:S(2)}) collective-permute-start(f32[2,384]{1,0:T(2,128)S(1)} %get-tuple-element.385), channel_id=1, source_target_pairs={{0,24},{8,16},{16,8},{24,0},{1,25},{9,17},{17,9},{25,1},{2,26},{10... | collective-permute-start | bytes 9224 | tf_op jit(solution)/shard_map/ppermute | solution.py:55
  692.0 216.2 %reduce-scatter.13.cloned.1.call-start = ((), (), s32[]{:S(2)}) async-start(), calls=%async_computation.14 | async-start | bytes 3354624 | tf_op jit(solution)/shard_map/reduce_scatter | solution.py:385
  698.0 235.0 %reduce-scatter.21.cloned.1.call-start = ((), (), s32[]{:S(2)}) async-start(), calls=%async_computation.20 | async-start | bytes 1843200
  725.6 210.6 %reduce-scatter.17.cloned.1.call-start = ((), (), s32[]{:S(2)}) async-start(), calls=%async_computation.16 | async-start | bytes 5271552 | tf_op jit(solution)/shard_map/reduce_scatter | solution.py:385
  735.1 228.6 %reduce-scatter.11.cloned.1.call-start = ((), (), s32[]{:S(2)}) async-start(), calls=%async_computation.13 | async-start | bytes 9216000 | tf_op jit(solution)/shard_map/reduce_scatter | solution.py:385
  780.3 282.6 %reduce-scatter.15.cloned.1.call-start = ((), (), s32[]{:S(2)}) async-start(), calls=%async_computation.15 | async-start | bytes 10137600 | tf_op jit(solution)/shard_map/reduce_scatter | solution.py:385
  834.0 65.3 %all-to-all-start.3 = ((bf16[8,24,1600]{2,1,0:T(8,128)(2,1)}), bf16[8,24,1600]{2,1,0:T(8,128)(2,1)S(1)}, u32[]{:S(2)}, u32[]{:S(2)}) async-start(bf16[8,24,1600]{2,1,0:T(8,128)(2,1)} %bitcast.192), calls=%async_computation.3 | async-start | bytes 1277952 | tf_op jit(solution)/shard_map/all_to_all | solution.py:118
  899.3 32.4 %all-to-all-start.1 = ((bf16[8,24,1600]{2,1,0:T(8,128)(2,1)}), bf16[8,24,1600]{2,1,0:T(8,128)(2,1)S(1)}, u32[]{:S(2)}, u32[]{:S(2)}) async-start(bf16[8,24,1600]{2,1,0:T(8,128)(2,1)} %bitcast.108), calls=%async_computation.1 | async-start | bytes 1277952 | tf_op jit(solution)/shard_map/all_to_all | solution.py:118
  910.6 25.2 %collective-permute-start.87 = (bf16[100,400]{0,1:T(8,128)(2,1)S(1)}, bf16[100,400]{0,1:T(8,128)(2,1)S(1)}, u32[]{:S(2)}, u32[]{:S(2)}) collective-permute-start(bf16[100,400]{0,1:T(8,128)(2,1)S(1)} %bitcast.717), channel_id=1, source_target_pairs={{0,8},{8,0},{16,24},{24,16},{1,9},{9,1},{17,25},{25,17},{2,10},{10... | collective-permute-start | bytes 240008 | tf_op jit(solution)/shard_map/ppermute | solution.py:55
  (309 other events, 5374.9 us)
Sparse Core Ops, SparseCore 0:
  9.7 28.1 all-gather.10
  40.0 67.9 all-gather.16
  110.3 92.4 all-gather.8
  204.9 35.6 all-gather.14
  242.6 86.0 all-gather.12
  692.1 28.8 reduce-scatter.18
  723.4 37.4 reduce-scatter.12
  763.3 33.7 reduce-scatter.20
  799.4 60.9 reduce-scatter.16
  862.6 101.0 reduce-scatter.10
  966.2 96.6 reduce-scatter.14

commit v2 on v1

--- a/solution.py
+++ b/solution.py
@@ -2,6 +2,7 @@
 
 import jax
 import jax.numpy as jnp
+import numpy as np
 from jax import lax
 from jax.experimental import pallas as pl
 from jax.experimental.pallas import tpu as pltpu
@@ -303,6 +304,468 @@
         name="scan_backward",
     )(dtm, dtu, dcore, b_wide, c_wide, rates)
     return ddtu, ddt, da, db[0].reshape(steps, STATE), dc[0].reshape(steps, STATE)
+
+
+def regroup_kernel(plan, source_count, out_count, *refs):
+    sources = refs[:source_count]
+    maps = refs[source_count : len(refs) - out_count]
+    outs = refs[len(refs) - out_count :]
+    for out, block, tile, wide, terms in plan:
+        at = pl.ds(tile * LANES, wide)
+        total = None
+        for source, which, low, high in terms:
+            held = sources[source]
+            held = held[..., low:high] if len(held.shape) == 2 else held[which[1], :, low:high]
+            wanted = maps[which[0]][:, at] - low
+            places = lax.broadcasted_iota(jnp.int32, (high - low, wide), 0)
+            hot = (places == wanted).astype(F32).astype(BF)
+            term = dot(held, hot, 1, 0)
+            total = term if total is None else total + term
+        ref = outs[out]
+        if total is None:
+            total = jnp.zeros((ref.shape[-2], wide), F32)
+        if len(ref.shape) == 2:
+            ref[:, at] = total.astype(ref.dtype)
+        else:
+            ref[block, :, at] = total.astype(ref.dtype)
+
+
+def regroup(sources, outs, moves, here):
+    plan, maps = [], []
+    tables = []
+    for source, from_block, out, block, table in moves:
+        maps.append(jnp.asarray(table)[here][None] if len(table) > 1 else jnp.asarray(table))
+        tables.append((source, from_block, out, block, table))
+    for out, shape in enumerate(outs):
+        for block in range(shape.shape[0] if len(shape.shape) == 3 else 1):
+            for tile in range(-(-shape.shape[-1] // LANES)):
+                wide = min(LANES, shape.shape[-1] - tile * LANES)
+                terms = []
+                for which, (source, from_block, to, to_block, table) in enumerate(tables):
+                    used = table[:, tile * LANES : tile * LANES + wide]
+                    if (to, to_block) != (out, block) or not (used >= 0).any():
+                        continue
+                    low = int(used[used >= 0].min()) // LANES * LANES
+                    high = min(-(-(int(used.max()) + 1) // LANES) * LANES, sources[source].shape[-1])
+                    terms.append((source, (which, from_block), low, high))
+                plan.append((out, block, tile, wide, tuple(terms)))
+    vmem = pl.BlockSpec(memory_space=pltpu.VMEM)
+    return pl.pallas_call(
+        partial(regroup_kernel, plan, len(sources), len(outs)),
+        out_shape=list(outs),
+        in_specs=[vmem] * (len(sources) + len(maps)),
+        out_specs=[vmem] * len(outs),
+        compiler_params=pltpu.CompilerParams(vmem_limit_bytes=VMEM_BYTES),
+        name="regroup",
+    )(*sources, *maps)
+
+
+def pieces_table(chunks, size, piece, wide, start=0):
+    at = np.arange(chunks * wide)
+    chunk, place = at // wide, at % wide
+    count = size // piece
+    table = start + chunk * size + place + piece * np.arange(count)[:, None]
+    return np.where(place < piece, table, -1).astype(np.int32)
+
+
+def run_table(starts, count):
+    return (np.asarray(starts)[:, None] + np.arange(count)).astype(np.int32)
+
+
+def placed(table, at, width):
+    out = np.full((table.shape[0], width), -1, np.int32)
+    out[:, at : at + table.shape[1]] = table
+    return out
+
+
+def meet(peers):
+    barrier = pltpu.get_barrier_semaphore()
+    for peer in peers:
+        pl.semaphore_signal(barrier, inc=1, device_id=peer, device_id_type=pl.DeviceIdType.MESH)
+    pl.semaphore_wait(barrier, len(peers))
+
+
+def deal_kernel(count, size, *refs):
+    sources, outs = refs[:count], refs[count : 2 * count]
+    own_sem, send_sem, recv_sem = refs[2 * count :]
+    here, row = lax.axis_index("seq"), lax.axis_index("fsdp")
+    others = [lax.rem(here + k, size) for k in range(1, size)]
+    meet([(there, row) for there in others])
+    copies = []
+    for i, (source, out) in enumerate(zip(sources, outs)):
+        copies.append(pltpu.make_async_copy(source.at[here], out.at[here], own_sem.at[i]))
+        copies[-1].start()
+        for k, there in enumerate(others):
+            at = i * (size - 1) + k
+            copies.append(
+                pltpu.make_async_remote_copy(
+                    src_ref=source.at[there],
+                    dst_ref=out.at[here],
+                    send_sem=send_sem.at[at],
+                    recv_sem=recv_sem.at[at],
+                    device_id=(there, row),
+                    device_id_type=pl.DeviceIdType.MESH,
+                )
+            )
+            copies[-1].start()
+    for copy in copies:
+        copy.wait()
+
+
+def deal(arrays, collective_id):
+    size, count = lax.axis_size("seq"), len(arrays)
+    hbm = pl.BlockSpec(memory_space=pl.ANY)
+    return pl.pallas_call(
+        partial(deal_kernel, count, size),
+        out_shape=[jax.ShapeDtypeStruct(a.shape, a.dtype) for a in arrays],
+        in_specs=[hbm] * count,
+        out_specs=[hbm] * count,
+        scratch_shapes=[
+            pltpu.SemaphoreType.DMA((count,)),
+            pltpu.SemaphoreType.DMA((count * (size - 1),)),
+            pltpu.SemaphoreType.DMA((count * (size - 1),)),
+        ],
+        compiler_params=pltpu.CompilerParams(collective_id=collective_id, has_side_effects=True),
+        cost_estimate=pl.CostEstimate(
+            flops=0, bytes_accessed=sum(a.size for a in arrays), transcendentals=0
+        ),
+        name="deal",
+    )(*arrays)
+
+
+def total_kernel(sizes, in_ref, out_ref, one, two, send_sem, recv_sem, send_two, recv_two):
+    seq, fsdp = lax.axis_index("seq"), lax.axis_index("fsdp")
+    across = [lax.rem(seq + k, sizes[0]) for k in range(1, sizes[0])]
+    along = [lax.rem(fsdp + k, sizes[1]) for k in range(1, sizes[1])]
+    meet([(there, fsdp) for there in across] + [(seq, there) for there in along])
+
+    def spread(slots, me, devices, send, recv):
+        copies = []
+        for k, device in enumerate(devices):
+            copies.append(
+                pltpu.make_async_remote_copy(
+                    src_ref=slots.at[me],
+                    dst_ref=slots.at[me],
+                    send_sem=send.at[k],
+                    recv_sem=recv.at[k],
+                    device_id=device,
+                    device_id_type=pl.DeviceIdType.MESH,
+                )
+            )
+            copies[-1].start()
+        for copy in copies:
+            copy.wait()
+        total = slots[0]
+        for i in range(1, slots.shape[0]):
+            total = total + slots[i]
+        return total
+
+    one[seq] = in_ref[...]
+    two[fsdp] = spread(one, seq, [(there, fsdp) for there in across], send_sem, recv_sem)
+    out_ref[...] = spread(two, fsdp, [(seq, there) for there in along], send_two, recv_two)
+
+
+def total_of(block, collective_id):
+    sizes = (lax.axis_size("seq"), lax.axis_size("fsdp"))
+    vmem = pl.BlockSpec(memory_space=pltpu.VMEM)
+    return pl.pallas_call(
+        partial(total_kernel, sizes),
+        out_shape=jax.ShapeDtypeStruct(block.shape, block.dtype),
+        in_specs=[vmem],
+        out_specs=vmem,
+        scratch_shapes=[pltpu.VMEM((n,) + block.shape, F32) for n in sizes]
+        + [pltpu.SemaphoreType.DMA((n - 1,)) for n in sizes for _ in range(2)],
+        compiler_params=pltpu.CompilerParams(collective_id=collective_id, has_side_effects=True),
+        name="total",
+    )(block)
+
+
+def remote(source, target, send, recv, device):
+    return pltpu.make_async_remote_copy(
+        src_ref=source,
+        dst_ref=target,
+        send_sem=send,
+        recv_sem=recv,
+        device_id=device,
+        device_id_type=pl.DeviceIdType.MESH,
+    )
+
+
+def block_rows(size, tok, m, d):
+    return pl.ds(pl.multiple_of((m * size + d) * tok, tok), tok)
+
+
+def spread_rows(size, tok, micro, own, whole, own_sem, send_sem, recv_sem, first):
+    here, row = lax.axis_index("seq"), lax.axis_index("fsdp")
+    copies = []
+    for m in range(micro):
+        source, target = own.at[pl.ds(m * tok, tok)], whole.at[block_rows(size, tok, m, here)]
+        for k in range(1, size):
+            at = first + m * (size - 1) + k - 1
+            there = (lax.rem(here + k, size), row)
+            copies.append(remote(source, target, send_sem.at[at], recv_sem.at[at], there))
+        at = first // (size - 1) + m
+        copies.append(pltpu.make_async_copy(source, target, own_sem.at[at]))
+    for copy in copies:
+        copy.start()
+    return copies
+
+
+def pack_peers(size):
+    here, row = lax.axis_index("seq"), lax.axis_index("fsdp")
+    return [(lax.rem(here + k, size), row) for k in range(1, size)]
+
+
+def gather_kernel(size, tok, micro, count, *refs):
+    owns, wholes = refs[:count], refs[count : 2 * count]
+    own_sem, send_sem, recv_sem = refs[2 * count :]
+    meet(pack_peers(size))
+    copies = []
+    for i in range(count):
+        first = i * micro * (size - 1)
+        copies += spread_rows(
+            size, tok, micro, owns[i], wholes[i], own_sem, send_sem, recv_sem, first
+        )
+    for copy in copies:
+        copy.wait()
+
+
+def gather_rows(arrays, micro, collective_id):
+    size, count = lax.axis_size("seq"), len(arrays)
+    tok = arrays[0].shape[0] // micro
+    hbm = pl.BlockSpec(memory_space=pl.ANY)
+    links = count * micro * (size - 1)
+    return pl.pallas_call(
+        partial(gather_kernel, size, tok, micro, count),
+        out_shape=[jax.ShapeDtypeStruct((a.shape[0] * size, a.shape[1]), a.dtype) for a in arrays],
+        in_specs=[hbm] * count,
+        out_specs=[hbm] * count,
+        scratch_shapes=[
+            pltpu.SemaphoreType.DMA((count * micro,)),
+            pltpu.SemaphoreType.DMA((links,)),
+            pltpu.SemaphoreType.DMA((links,)),
+        ],
+        compiler_params=pltpu.CompilerParams(collective_id=collective_id, has_side_effects=True),
+        name="gather_rows",
+    )(*arrays)
+
+
+def spans_of(width, most=512):
+    return [(low, min(low + most, width)) for low in range(0, width, most)]
+
+
+def mixer_kernel(size, tok, micro, *refs):
+    contexts, ssm_outs = refs[:micro], refs[micro : 2 * micro]
+    sums_ref, x_ref, gain_att, gain_ssm, gain_ffn, w_att, w_ssm = refs[2 * micro : 2 * micro + 7]
+    att, ssm, scale_att, scale_ssm, hidden, mixer, ffn = refs[2 * micro + 7 : 2 * micro + 14]
+    sums, sent, got, ffn_own, sums_send, sums_recv, send, recv, own_sem, ffn_send, ffn_recv = refs[
+        2 * micro + 14 :
+    ]
+    here, row = lax.axis_index("seq"), lax.axis_index("fsdp")
+    peers = pack_peers(size)
+    meet(peers)
+    sums[here] = sums_ref[...]
+    copies = [
+        remote(sums.at[here], sums.at[here], sums_send.at[k], sums_recv.at[k], peer)
+        for k, peer in enumerate(peers)
+    ]
+    for copy in copies:
+        copy.start()
+    for copy in copies:
+        copy.wait()
+    total = sums[0]
+    for i in range(1, size):
+        total = total + sums[i]
+    place = lax.broadcasted_iota(jnp.int32, (8, LANES), 0)
+    for kind, scale, width in ((0, scale_att, ATT), (1, scale_ssm, INNER)):
+        column = lax.dot_general(
+            total,
+            (place == kind).astype(F32),
+            (((0,), (0,)), ((), ())),
+            precision=lax.Precision.HIGHEST,
+            preferred_element_type=F32,
+        )
+        scale[...] = lax.rsqrt(column / width + EPS)
+    pack = size * tok
+    for m in range(micro):
+        rows = pl.ds(m * pack, pack)
+        att[rows] = (contexts[m][...] * scale_att[rows, :1] * gain_att[...]).astype(BF)
+        ssm[rows] = (ssm_outs[m][...] * scale_ssm[rows, :1] * gain_ssm[...]).astype(BF)
+
+    def product(d, low, high):
+        left = [jnp.concatenate([ref[block_rows(size, tok, m, d)] for m in range(micro)]) for ref in (att, ssm)]
+        return 0.5 * (
+            dot(left[0], w_att[:, low:high], 1, 0) + dot(left[1], w_ssm[:, low:high], 1, 0)
+        )
+
+    copies = []
+    for k, peer in enumerate(peers):
+        for low, high in spans_of(D):
+            sent[k, :, low:high] = product(peer[0], low, high).astype(BF)
+        copies.append(remote(sent.at[k], got.at[k], send.at[k], recv.at[k], peer))
+        copies[-1].start()
+    for low, high in spans_of(D):
+        mixer[:, low:high] = product(here, low, high)
+    for copy in copies:
+        copy.wait()
+    for m in range(micro):
+        rows = pl.ds(m * tok, tok)
+        out = mixer[rows]
+        for k in range(size - 1):
+            out = out + got[k, rows].astype(F32)
+        mixer[rows] = out
+        whole = x_ref[rows].astype(F32) + out
+        hidden[rows] = whole
+        scale = lax.rsqrt(jnp.mean(whole * whole, axis=-1, keepdims=True) + EPS)
+        ffn_own[rows] = (whole * scale * gain_ffn[...]).astype(BF)
+    for copy in spread_rows(size, tok, micro, ffn_own, ffn, own_sem, ffn_send, ffn_recv, 0):
+        copy.wait()
+
+
+def mixer_rows(contexts, ssm_outs, sums, x_own, gains, w_att, w_ssm, collective_id):
+    size, micro = lax.axis_size("seq"), len(contexts)
+    own = x_own.shape[0]
+    rows, tok = own * size, own // micro
+    vmem, hbm = pl.BlockSpec(memory_space=pltpu.VMEM), pl.BlockSpec(memory_space=pl.ANY)
+    shape = jax.ShapeDtypeStruct
+    dma = pltpu.SemaphoreType.DMA
+    return pl.pallas_call(
+        partial(mixer_kernel, size, tok, micro),
+        out_shape=[
+            shape((rows, w_att.shape[0]), BF),
+            shape((rows, w_ssm.shape[0]), BF),
+            shape((rows, LANES), F32),
+            shape((rows, LANES), F32),
+            shape((own, D), F32),
+            shape((own, D), F32),
+            shape((rows, D), BF),
+        ],
+        in_specs=[vmem] * (2 * micro + 7),
+        out_specs=[vmem] * 6 + [hbm],
+        scratch_shapes=[
+            pltpu.VMEM((size,) + sums.shape, F32),
+            pltpu.VMEM((size - 1, own, D), BF),
+            pltpu.VMEM((size - 1, own, D), BF),
+            pltpu.VMEM((own, D), BF),
+            dma((size - 1,)),
+            dma((size - 1,)),
+            dma((size - 1,)),
+            dma((size - 1,)),
+            dma((micro,)),
+            dma((micro * (size - 1),)),
+            dma((micro * (size - 1),)),
+        ],
+        compiler_params=pltpu.CompilerParams(
+            collective_id=collective_id, has_side_effects=True, vmem_limit_bytes=VMEM_BYTES
+        ),
+        name="mixer_rows",
+    )(*contexts, *ssm_outs, sums, x_own, *gains, w_att, w_ssm)
+
+
+def ffn_kernel(size, tok, micro, *refs):
+    ffn, cot, hidden, cot_own, gain, w_gu, w_down = refs[:7]
+    act, dgu, down, d_hidden, d_gain, dmix = refs[7:13]
+    sent, got, dmix_own, send, recv, own_sem, dmix_send, dmix_recv = refs[13:]
+    here, row = lax.axis_index("seq"), lax.axis_index("fsdp")
+    wide = w_down.shape[0]
+    meet(pack_peers(size))
+
+    def copy_of(k):
+        return remote(
+            sent.at[k], got.at[k], send.at[k], recv.at[k], (lax.rem(here + k + 1, size), row)
+        )
+
+    def block(k, carry):
+        d = lax.rem(here + k + 1, size)
+        spots = [block_rows(size, tok, m, d) for m in range(micro)]
+        rows_in = jnp.concatenate([ffn[spot] for spot in spots])
+        cots = jnp.concatenate([cot[spot] for spot in spots])
+        for low, high in spans_of(wide):
+            gate = dot(rows_in, w_gu[:, low:high], 1, 0)
+            up = dot(rows_in, w_gu[:, wide + low : wide + high], 1, 0)
+            d_act = dot(cots, w_down[low:high, :], 1, 1)
+            sig = 1.0 / (1.0 + jnp.exp(-gate))
+            silu = gate * sig
+            pieces = (
+                (act, low, silu * up),
+                (dgu, low, d_act * up * (sig * (1.0 + gate - silu))),
+                (dgu, wide + low, d_act * silu),
+            )
+            for ref, at, values in pieces:
+                values = values.astype(BF)
+                for m, spot in enumerate(spots):
+                    ref[spot, at : at + high - low] = values[m * tok : (m + 1) * tok]
+        d_all = jnp.concatenate([dgu[spot] for spot in spots])
+        for low, high in spans_of(D):
+            sent[k, :, low:high] = dot(d_all, w_gu[low:high, :], 1, 1).astype(BF)
+
+        @pl.when(k < size - 1)
+        def _():
+            copy_of(k).start()
+
+        acts = jnp.concatenate([act[spot] for spot in spots])
+        for low, high in spans_of(D):
+            down[d, :, low:high] = dot(acts, w_down[:, low:high], 1, 0).astype(BF)
+        return carry
+
+    lax.fori_loop(0, size, block, 0)
+    for k in range(size - 1):
+        copy_of(k).wait()
+    gain_sum = jnp.zeros((1, D), F32)
+    for m in range(micro):
+        rows = pl.ds(m * tok, tok)
+        d_in = sent[size - 1, rows].astype(F32)
+        for k in range(size - 1):
+            d_in = d_in + got[k, rows].astype(F32)
+        whole = hidden[rows]
+        scale = lax.rsqrt(jnp.mean(whole * whole, axis=-1, keepdims=True) + EPS)
+        normal = whole * scale
+        gain_sum = gain_sum + jnp.sum(d_in * normal, axis=0, keepdims=True)
+        scaled = d_in * gain[...]
+        inward = jnp.mean(scaled * normal, axis=-1, keepdims=True)
+        out = cot_own[rows].astype(F32) + scale * (scaled - normal * inward)
+        d_hidden[rows] = out
+        dmix_own[rows] = out.astype(BF)
+    d_gain[...] = gain_sum
+    for copy in spread_rows(size, tok, micro, dmix_own, dmix, own_sem, dmix_send, dmix_recv, 0):
+        copy.wait()
+
+
+def ffn_rows(ffn, cot, hidden, cot_own, gain, w_gu, w_down, micro, collective_id):
+    size = lax.axis_size("seq")
+    own, rows = hidden.shape[0], ffn.shape[0]
+    wide = w_down.shape[0]
+    tok = own // micro
+    vmem, hbm = pl.BlockSpec(memory_space=pltpu.VMEM), pl.BlockSpec(memory_space=pl.ANY)
+    shape = jax.ShapeDtypeStruct
+    dma = pltpu.SemaphoreType.DMA
+    return pl.pallas_call(
+        partial(ffn_kernel, size, tok, micro),
+        out_shape=[
+            shape((rows, wide), BF),
+            shape((rows, 2 * wide), BF),
+            shape((size, own, D), BF),
+            shape((own, D), F32),
+            shape((1, D), F32),
+            shape((rows, D), BF),
+        ],
+        in_specs=[vmem] * 7,
+        out_specs=[vmem] * 5 + [hbm],
+        scratch_shapes=[
+            pltpu.VMEM((size, own, D), BF),
+            pltpu.VMEM((size - 1, own, D), BF),
+            pltpu.VMEM((own, D), BF),
+            dma((size - 1,)),
+            dma((size - 1,)),
+            dma((micro,)),
+            dma((micro * (size - 1),)),
+            dma((micro * (size - 1),)),
+        ],
+        compiler_params=pltpu.CompilerParams(
+            collective_id=collective_id, has_side_effects=True, vmem_limit_bytes=VMEM_BYTES
+        ),
+        name="ffn_rows",
+    )(ffn, cot, hidden, cot_own, gain, w_gu, w_down)
 
 
 def conv_act(position, inner, tap_weights, tap_bias):
@@ -400,30 +863,55 @@
 
     send_hot, land_hot = routing(route, tok)
     x_own = bring(tokens.reshape(micro * tok, D), send_hot, land_hot)
-    x_own = x_own.reshape(micro, tok, D)
     q_start = first_head * HEAD
-    mix_parts = part(w_mix_in, 1, 2 * N, ch // N)
-    small_shard = jnp.concatenate(
-        [w_x, w_dt, w_small, jnp.zeros((w_x.shape[0], 1), BF)], axis=1
-    )
-    w_in = gather(
-        jnp.concatenate(
-            [
-                span(w_qkv, 1, q_start, width),
-                span(w_qkv, 1, ATT + s * HEAD, 2 * HEAD),
-                span(w_qkv, 1, ATT + KV_WIDTH + s * HEAD, 2 * HEAD),
-                mix_parts,
-            ],
-            axis=1,
-        )
-    )
-    w_small_part = gather(part(small_shard, 0, 1, ch // N))
-    w_out_part = gather(part(w_out_ssm, 0, 1, ch // N))
-    w_att_cols = gather(span(w_out_att, 1, s * cols, cols))
-    w_gu = gather(jnp.concatenate([part(w_gate, 1, N, ffs // N), part(w_up, 1, N, ffs // N)], axis=1))
-    w_down_part = gather(part(w_down, 0, 1, ffs // N))
+    chw, ffw = ch // N, ffs // N
+    q_starts = [h * HEAD for h in first_heads[:S]]
+    kv_starts = [ATT + HEAD * i for i in range(S)]
+    at_k, at_v, at_q = 2 * ch, 2 * ch + 2 * HEAD, 2 * ch + 4 * HEAD
+    at_att = at_q + width
+    in_wide = at_att + cols
+    mix_table = pieces_table(2 * N, INNER // N, ch_piece, chw)
+    in_part = regroup(
+        [w_mix_in, jnp.pad(w_qkv, ((0, 0), (0, -w_qkv.shape[1] % LANES))), w_out_att],
+        [jax.ShapeDtypeStruct((rows_d, in_wide), BF)],
+        [
+            (0, None, 0, 0, placed(mix_table, 0, in_wide)),
+            (1, None, 0, 0, placed(run_table(kv_starts, 2 * HEAD), at_k, in_wide)),
+            (1, None, 0, 0, placed(run_table([a + KV_WIDTH for a in kv_starts], 2 * HEAD), at_v, in_wide)),
+            (2, None, 0, 0, placed(run_table([cols * i for i in range(S)], cols), at_att, in_wide)),
+            (1, None, 0, 0, placed(run_table(q_starts, width), at_q, in_wide)),
+        ],
+        s,
+    )[0]
+    small_part = part(
+        jnp.concatenate([w_x, w_dt, w_small, jnp.zeros((w_x.shape[0], 1), BF)], axis=1), 0, 1, chw
+    )
+    small_wide = small_part.shape[1]
+    gathered_in = gather(
+        jnp.concatenate([in_part, jnp.pad(small_part, ((0, rows_d - chw), (0, 0)))], axis=1)
+    )
     cot_own = bring(cotangent.reshape(micro * tok, D), send_hot, land_hot)
-    cot_own = cot_own.reshape(micro, tok, D)
+    x_rows = gather_rows([x_own], micro, 3)[0]
+    cot_own, x_rows = lax.optimization_barrier((cot_own, x_rows))
+    cot_rows = gather_rows([cot_own], micro, 6)[0]
+    gathered_in, x_rows, cot_rows = lax.optimization_barrier((gathered_in, x_rows, cot_rows))
+    out_piece, gathered_in = lax.optimization_barrier((part(w_out_ssm, 0, 1, chw), gathered_in))
+    w_out_part = gather(out_piece)
+    w_in = gathered_in[:, :at_att]
+    w_att_cols = gathered_in[:, at_att:in_wide]
+    w_small_part = (
+        gathered_in[:, in_wide:].reshape(N, rows_d, small_wide)[:, :chw].reshape(ch, small_wide)
+    )
+    ff_table = pieces_table(N, ff // N, ff_piece, ffw)
+    gu_part = regroup(
+        [w_gate, w_up],
+        [jax.ShapeDtypeStruct((rows_d, 2 * ffs), BF)],
+        [
+            (0, None, 0, 0, placed(ff_table, 0, 2 * ffs)),
+            (1, None, 0, 0, placed(ff_table, ffs, 2 * ffs)),
+        ],
+        s,
+    )[0]
 
     w_att_pad = jnp.pad(w_att_cols, ((0, width), (0, 0)))
     w_att_part = (
@@ -450,19 +938,16 @@
     def to_own(partial_rows):
         return seq_scatter(partial_rows.reshape(S, tok, partial_rows.shape[-1]))
 
-    stats = jnp.zeros((6,), F32)
-    gains = [jnp.zeros((n,), F32) for n in (D, width, ch, D)]
-    kept = []
-    results = []
-    for m in range(micro):
+    def opening(m):
+        x_pack = x_rows[m * pack : (m + 1) * pack].astype(F32)
+        normed_low = rms_scale(x_pack, gain_in).astype(BF)
+        return normed_low, dot(normed_low, w_in, 1, 0).astype(BF)
+
+    def first_half(m, normed_low, opened):
         segment, position = seq_layout(lengths[m, 0], pack)
         visible = (segment[:, None] == segment[None, :]) & (position[None, :] <= position[:, None])
-        x_mine = x_own[m].astype(F32)
-        x_pack = to_pack(x_own[m]).astype(F32)
-        normed_low = rms_scale(x_pack, gain_in).astype(BF)
-        opened = dot(normed_low, w_in, 1, 0).astype(BF)
-        q = opened[:, :width].reshape(pack, most, HEAD)
-        kv = opened[:, width : width + 4 * HEAD].reshape(pack, 4, HEAD)
+        q = opened[:, at_q:].reshape(pack, most, HEAD)
+        kv = opened[:, at_k:at_q].reshape(pack, 4, HEAD)
         pick_low = in_low[None, :, None]
         keys = jnp.where(pick_low, kv[:, 0:1], kv[:, 1:2])
         values = jnp.where(pick_low, kv[:, 2:3], kv[:, 3:4])
@@ -475,9 +960,8 @@
         context = (
             jnp.einsum("htu,uhd->thd", probs.astype(BF), values, preferred_element_type=F32)
         ).reshape(pack, width) * live
-        at = width + 4 * HEAD
-        inner = opened[:, at : at + ch].astype(F32)
-        gate_z = opened[:, at + ch :].astype(F32)
+        inner = opened[:, :ch].astype(F32)
+        gate_z = opened[:, ch : 2 * ch].astype(F32)
         inner_u, conv_back = jax.vjp(partial(conv_act, position), inner, conv_w, conv_b)
         u_low = inner_u.astype(BF)
         projected = seq_sum(dot(w_x_part, u_low, 0, 1).astype(BF)).astype(BF)
@@ -495,44 +979,29 @@
         row_sums = jnp.stack(
             [jnp.sum(context * context, axis=1), jnp.sum(ssm_out * ssm_out, axis=1)]
         )
-        row_sums = seq_sum(row_sums)
-        scale_att = lax.rsqrt(row_sums[0] / ATT + EPS)[:, None]
-        scale_ssm = lax.rsqrt(row_sums[1] / INNER + EPS)[:, None]
-        att_low = (context * scale_att * gain_att_part).astype(BF)
-        ssm_low = (ssm_out * scale_ssm * gain_ssm_part).astype(BF)
-        mixer_out = to_own(
-            0.5 * (dot(att_low, w_att_part, 1, 0) + dot(ssm_low, w_out_part, 1, 0))
-        )
-        hidden = x_mine + mixer_out
-        ffn_in, ffn_norm_back = jax.vjp(rms_scale, hidden, gain_ffn)
-        ffn_low = to_pack(ffn_in.astype(BF))
-        gate_proj = dot(ffn_low, w_gu[:, :ffs], 1, 0)
-        up_proj = dot(ffn_low, w_gu[:, ffs:], 1, 0)
-        act_val, act_back = jax.vjp(swiglu, gate_proj, up_proj)
-        act_low = act_val.astype(BF)
-        ffn_out = to_own(dot(act_low, w_down_part, 1, 0))
-        result = hidden + ffn_out
-        results.append(result.astype(BF))
-        here = lax.dynamic_slice_in_dim(row_sums, s * tok, tok, 1)
-        stats = stats + jnp.stack(
-            [
-                squares(x_mine),
-                jnp.sum(here[0]),
-                jnp.sum(here[1]),
-                squares(mixer_out),
-                squares(ffn_out),
-                squares(result),
-            ]
-        )
-        cot_mine = cot_own[m].astype(F32)
-        cot_low = to_pack(cot_own[m])
-        d_act = dot(cot_low, w_down_part, 1, 1)
-        d_gate, d_up = act_back(d_act)
-        dgu_low = jnp.concatenate([d_gate, d_up], axis=1).astype(BF)
-        d_ffn_in = to_own(dot(dgu_low, w_gu, 1, 1))
-        d_hidden_norm, d_gain_ffn = ffn_norm_back(d_ffn_in)
-        d_hidden = cot_mine + d_hidden_norm
-        dmix_low = to_pack(d_hidden.astype(BF))
+        return dict(
+            position=position,
+            normed=normed_low,
+            q=q,
+            keys=keys,
+            values=values,
+            probs=probs,
+            context=context,
+            inner_u=inner_u,
+            conv_back=conv_back,
+            u=u_low,
+            dt_in=dt_in,
+            dt_lin=dt_lin,
+            step_dt=step_dt,
+            scan=(dtm, dtu, b_wide, c_wide),
+            ssm_out=ssm_out,
+            gate_back=gate_back,
+            row_sums=row_sums,
+        )
+
+    def second_half(h):
+        context, ssm_out = h["context"], h["ssm_out"]
+        scale_att, scale_ssm, dmix_low = h["scale_att"], h["scale_ssm"], h["dmix"]
         d_att = 0.5 * dot(dmix_low, w_att_part, 1, 1) * live
         d_ssm = lax.optimization_barrier(0.5 * dot(dmix_low, w_out_part, 1, 1))
         d_gain_att = jnp.sum(d_att * context * scale_att, axis=0)
@@ -546,13 +1015,51 @@
             t_att * scale_att - context * scale_att**3 * (back_sums[0] / ATT)[:, None]
         ) * live
         d_ssm_out = t_ssm * scale_ssm - ssm_out * scale_ssm**3 * (back_sums[1] / INNER)[:, None]
-        d_core, d_u_gate, d_skip, d_gate_z = gate_back(d_ssm_out)
+        d_core, d_u_gate, d_skip, d_gate_z = h["gate_back"](d_ssm_out)
+        h.update(
+            d_core=d_core,
+            d_u_gate=d_u_gate,
+            d_skip=d_skip,
+            d_gate_z=d_gate_z,
+            d_context=d_context.astype(BF),
+            gains=(d_gain_att, d_gain_ssm),
+        )
+
+    def attention_half(h):
+        probs, keys, values, q = h["probs"], h["keys"], h["values"], h["q"]
+        dctx_low = h["d_context"].reshape(pack, most, HEAD)
+        d_values = jnp.einsum(
+            "htu,thd->uhd", probs.astype(BF), dctx_low, preferred_element_type=F32
+        )
+        d_probs = jnp.einsum("thd,uhd->htu", dctx_low, values, preferred_element_type=F32)
+        dscore_low = (
+            probs * (d_probs - jnp.sum(probs * d_probs, axis=-1, keepdims=True))
+        ).astype(BF)
+        d_q = jnp.einsum("htu,uhd->thd", dscore_low, keys, preferred_element_type=F32) * 0.125
+        d_keys = jnp.einsum("htu,thd->uhd", dscore_low, q, preferred_element_type=F32) * 0.125
+        pick_low = in_low[None, :, None]
+
+        def kv_sum(d_heads):
+            return [
+                jnp.sum(jnp.where(pick_low, d_heads, 0.0), axis=1),
+                jnp.sum(jnp.where(pick_low, 0.0, d_heads), axis=1),
+            ]
+
+        d_rest = jnp.concatenate(
+            [h["d_gate_z"]]
+            + kv_sum(d_keys)
+            + kv_sum(d_values)
+            + [d_q.reshape(pack, width), jnp.zeros((pack, cols), F32)],
+            axis=1,
+        ).astype(BF)
+        h.update(d_rest=d_rest, d_normed=dot(d_rest, gathered_in[:, ch:in_wide], 1, 1))
+
+    def third_half(h):
+        dtm, dtu, b_wide, c_wide = h["scan"]
         ddtu, ddt, d_rates, d_in_b, d_out_c = scan_backward(
-            dtm, dtu, d_core, b_wide, c_wide, rates
-        )
-        d_decay = d_rates.T
-        d_step = ddt + ddtu * inner_u
-        d_lin = d_step * jax.nn.sigmoid(dt_lin)
+            dtm, dtu, h["d_core"], b_wide, c_wide, rates
+        )
+        d_lin = (ddt + ddtu * h["inner_u"]) * jax.nn.sigmoid(h["dt_lin"])
         d_dt_bias = jnp.sum(d_lin, axis=0)
         ddt_low = d_lin.astype(BF)
         dproj = jnp.concatenate(
@@ -565,133 +1072,233 @@
             axis=0,
         )
         dproj_low = seq_sum(dproj.astype(BF)).astype(BF)
-        d_inner_u = d_u_gate + ddtu * step_dt + dot(dproj_low, w_x_part, 0, 1)
-        d_inner, d_conv_w, d_conv_b = conv_back(d_inner_u)
-        small_grad = jnp.concatenate(
-            [d_conv_w, d_conv_b[:, None], d_dt_bias[:, None], d_skip[:, None], d_decay * decay_a],
-            axis=1,
-        )
-        dctx_low = d_context.astype(BF).reshape(pack, most, HEAD)
-        d_values = jnp.einsum(
-            "htu,thd->uhd", probs.astype(BF), dctx_low, preferred_element_type=F32
-        )
-        d_probs = jnp.einsum("thd,uhd->htu", dctx_low, values, preferred_element_type=F32)
-        dscore_low = (
-            probs * (d_probs - jnp.sum(probs * d_probs, axis=-1, keepdims=True))
-        ).astype(BF)
-        d_q = jnp.einsum("htu,uhd->thd", dscore_low, keys, preferred_element_type=F32) * 0.125
-        d_keys = jnp.einsum("htu,thd->uhd", dscore_low, q, preferred_element_type=F32) * 0.125
-        low_part, high_part = pick_low, ~pick_low
-
-        def kv_sum(d_heads):
-            return [
-                jnp.sum(jnp.where(low_part, d_heads, 0.0), axis=1),
-                jnp.sum(jnp.where(high_part, d_heads, 0.0), axis=1),
-            ]
-
-        d_opened = jnp.concatenate(
-            [d_q.reshape(pack, width)] + kv_sum(d_keys) + kv_sum(d_values) + [d_inner, d_gate_z],
-            axis=1,
-        ).astype(BF)
-        d_normed = to_own(dot(d_opened, w_in, 1, 1))
-        _, norm_back = jax.vjp(rms_scale, x_mine, gain_in)
+        d_inner_u = h["d_u_gate"] + ddtu * h["step_dt"] + dot(dproj_low, w_x_part, 0, 1)
+        d_inner, d_conv_w, d_conv_b = h["conv_back"](d_inner_u)
+        d_inner_low = d_inner.astype(BF)
+        small = [d_conv_w, d_conv_b[:, None], d_dt_bias[:, None], h["d_skip"][:, None]]
+        small_grad = jnp.concatenate(small + [d_rates.T * decay_a], axis=1)
+        h.update(ddt=ddt_low, dproj=dproj_low, d_inner=d_inner_low, small=small_grad)
+
+    def last_half(h):
+        d_normed = to_own(h["d_normed"] + dot(h["d_inner"], w_in[:, :ch], 1, 1))
+        _, norm_back = jax.vjp(rms_scale, h["x_mine"], gain_in)
         d_x_norm, d_gain_in = norm_back(d_normed)
-        d_x = d_hidden + d_x_norm
-        gains = [
-            a + b for a, b in zip(gains, (d_gain_in, d_gain_att, d_gain_ssm, d_gain_ffn))
-        ]
-        kept.append(
-            dict(
-                act=act_low,
-                cot=cot_low,
-                ffn=ffn_low,
-                dgu=dgu_low,
-                att=att_low,
-                ssm=ssm_low,
-                dmix=dmix_low,
-                u=u_low,
-                dproj=dproj_low,
-                dt_in=dt_in,
-                ddt=ddt_low,
-                normed=normed_low,
-                opened=d_opened,
-                small=small_grad,
-                dx=d_x.astype(BF),
-            )
-        )
+        h.update(d_gain_in=d_gain_in, dx=(h["d_hidden"] + d_x_norm).astype(BF))
 
     def both(name, axis=0):
-        return jnp.concatenate([one[name] for one in kept], axis=axis)
-
-    g_down = scatter(dot(both("act"), both("cot"), 0, 0))
-    g_gu = scatter(dot(both("ffn"), both("dgu"), 0, 0))
-    g_att_rows = (0.5 * dot(both("att"), both("dmix"), 0, 0)).astype(BF)
+        return jnp.concatenate([one[name] for one in halves], axis=axis)
+
+    def hold(names, *extra):
+        held = [[one[name] for name in names] for one in halves]
+        held, extra = lax.optimization_barrier((held, extra))
+        for one, values in zip(halves, held):
+            one.update(zip(names, values))
+        return extra
+
+    def by_shard(whole):
+        return whole.astype(BF).reshape(N, whole.shape[0] // N, whole.shape[1])
+
+    opened = [opening(m) for m in range(micro)]
+    opened, gu_part, down_part = lax.optimization_barrier(
+        (opened, gu_part, part(w_down, 0, 1, ffw))
+    )
+    w_gu, w_down_part = gather(gu_part), gather(down_part)
+    halves = [first_half(m, *opened[m]) for m in range(micro)]
+    sums = jnp.concatenate([one["row_sums"] for one in halves], axis=1)
+    att_low, ssm_low, scale_att, scale_ssm, hidden, mixer_out, ffn_low = mixer_rows(
+        [one["context"] for one in halves],
+        [one["ssm_out"] for one in halves],
+        jnp.pad(sums, ((0, 6), (0, 0))),
+        x_own,
+        (gain_att_part[None], gain_ssm_part[None], gain_ffn[None]),
+        w_att_part,
+        w_out_part,
+        4,
+    )
+    act_low, dgu_low, down_parts, d_hidden, d_gain_ffn, dmix_low = ffn_rows(
+        ffn_low, cot_rows, hidden, cot_own, gain_ffn[None], w_gu, w_down_part, micro, 5
+    )
+    gu_whole = dot(ffn_low, dgu_low, 0, 0).astype(BF)
+    down_whole = dot(act_low, cot_rows, 0, 0).astype(BF)
+    dmix_low, gu_whole, down_whole = lax.optimization_barrier((dmix_low, gu_whole, down_whole))
+    for m, half in enumerate(halves):
+        rows = slice(m * pack, (m + 1) * pack)
+        mine = slice(m * tok, (m + 1) * tok)
+        half.update(
+            scale_att=scale_att[rows, :1],
+            scale_ssm=scale_ssm[rows, :1],
+            dmix=dmix_low[rows],
+            x_mine=x_own[mine].astype(F32),
+            d_hidden=d_hidden[mine],
+        )
+    r_gu, r_down = scatter(gu_whole), scatter(down_whole)
+    for half in halves:
+        second_half(half)
+    ssm_whole = (0.5 * dot(ssm_low, dmix_low, 0, 0)).astype(BF)
+    g_att_rows = (0.5 * dot(att_low, dmix_low, 0, 0)).astype(BF)
     g_att_blocks = seq_deal(g_att_rows.reshape(width, S, cols).transpose(1, 0, 2))
     g_att_whole = jnp.concatenate(
         [g_att_blocks[i, : head_counts[i] * HEAD] for i in range(S)], axis=0
     )
-    g_att = scatter(g_att_whole).astype(F32)
-    g_ssm = scatter(0.5 * dot(both("ssm"), both("dmix"), 0, 0))
-    g_xdt = jnp.concatenate(
+    for half in halves:
+        attention_half(half)
+    halves[0]["d_rest"], r_gu = lax.optimization_barrier((halves[0]["d_rest"], r_gu))
+    rest_whole = dot(both("normed"), both("d_rest"), 0, 0).astype(BF)
+    rest_whole = lax.dynamic_update_slice(rest_whole, g_att_whole, (0, at_att - ch))
+    r_down, ssm_whole, rest_whole = hold(["d_core"], r_down, ssm_whole, rest_whole)
+    r_ssm, r_rest = scatter(ssm_whole), scatter(rest_whole)
+    for half in halves:
+        third_half(half)
+    r_ssm, r_rest = hold(["d_inner"], r_ssm, r_rest)
+    for half in halves:
+        last_half(half)
+    small_whole = jnp.concatenate(
         [
             dot(both("u"), both("dproj", 1), 0, 1)[:, :PROJ],
             dot(both("ddt"), both("dt_in", 1), 0, 1),
-            kept[0]["small"] + kept[1]["small"],
+            halves[0]["small"] + halves[1]["small"],
             jnp.zeros((ch, 1), F32),
         ],
         axis=1,
     )
-    g_xdt = scatter(g_xdt)
-    g_in = scatter(dot(both("normed"), both("opened"), 0, 0))
-
-    def rows_back(shard):
-        blocks = seq_deal(shard.reshape(shard.shape[0], S, cols).transpose(1, 0, 2))
-        return blocks.reshape(S * shard.shape[0], cols).astype(F32)
-
-    def cols_back(shard, chunks, piece):
-        rows = shard.shape[0]
-        blocks = shard.reshape(rows, S, chunks // S, -1)[..., :piece].transpose(1, 0, 2, 3)
-        got = seq_deal(blocks)
-        return got.transpose(1, 2, 0, 3).reshape(rows, chunks * piece).astype(F32)
-
-    out_down = rows_back(g_down[:ff_piece])
-    out_ssm = rows_back(g_ssm[:ch_piece])
-    out_gate = cols_back(g_gu[:, :ffs], N, ff_piece)
-    out_up = cols_back(g_gu[:, ffs:], N, ff_piece)
-    at = width + 4 * HEAD
-    out_mix = cols_back(g_in[:, at:], 2 * N, ch_piece)
-    kv_at = jnp.zeros((rows_d, 2 * KV_WIDTH), BF)
-    kv_at = lax.dynamic_update_slice_in_dim(kv_at, g_in[:, width : width + 2 * HEAD], s * HEAD, 1)
-    kv_at = lax.dynamic_update_slice_in_dim(
-        kv_at, g_in[:, width + 2 * HEAD : at], KV_WIDTH + s * HEAD, 1
-    )
-    q_at = jnp.zeros((rows_d, ATT + width), BF)
-    q_live = jnp.where(live > 0, g_in[:, :width], 0)
-    q_at = lax.dynamic_update_slice_in_dim(q_at, q_live, q_start, 1)
-    qkv_at = jnp.concatenate([q_at[:, :ATT], kv_at], axis=1)
-    out_qkv = seq_scatter(qkv_at.reshape(rows_d, S, -1).transpose(1, 0, 2))
-    small_all = seq_gather(g_xdt[:ch_piece]).reshape(-1, g_xdt.shape[1]).astype(F32)
+    last_whole = dot(both("normed"), both("d_inner"), 0, 0).astype(BF)
+    (small_whole, last_whole) = hold(["dx"], small_whole, last_whole)
+    r_small, r_last = scatter(small_whole), scatter(last_whole)
+    input_grads = give(both("dx"), send_hot, land_hot)
+
+    per = N // S
+    gate_take = np.concatenate(
+        [np.arange(ff_piece) + ffw * i for i in range(per)]
+    )
+    half_wide = -(-per * ff_piece // LANES) * LANES
+    moves = []
+    for d in range(S):
+        for i in range(2):
+            table = gate_take[None] + d * per * ffw + i * ffs
+            moves.append((0, None, 0, d, placed(table, i * half_wide, 2 * half_wide)))
+        moves.append((1, None, 1, d, run_table([d * cols], cols)))
+        moves.append((2, None, 2, d, run_table([d * cols], cols)))
+    blocks = regroup(
+        [r_gu, r_ssm, r_down],
+        [
+            jax.ShapeDtypeStruct((S, rows_d, 2 * half_wide), BF),
+            jax.ShapeDtypeStruct((S, r_ssm.shape[0], cols), BF),
+            jax.ShapeDtypeStruct((S, r_down.shape[0], cols), BF),
+        ],
+        moves,
+        s,
+    )
+    blocks, _ = lax.optimization_barrier((list(blocks), last_whole))
+    gu_got, ssm_got, down_got, ffn_got = deal(blocks + [down_parts], 0)
+    ffn_out = jnp.sum(ffn_got.astype(F32), axis=0)
+    result = hidden + ffn_out
+    outputs = give(result.astype(BF), send_hot, land_hot)
+    out_ssm = ssm_got[:, :ch_piece].reshape(S * ch_piece, cols).astype(F32)
+    out_down = down_got[:, :ff_piece].reshape(S * ff_piece, cols).astype(F32)
+    ff_mine, mix_mine = ff // S, 2 * INNER // S
+    moves = []
+    at = np.arange(ff_mine)
+    for source in range(S):
+        chunk, inside = at // (S * ff_piece), at % (S * ff_piece)
+        table = np.where(
+            inside // ff_piece == source, chunk * ff_piece + inside % ff_piece, -1
+        )[None].astype(np.int32)
+        moves.append((0, source, 0, 0, table))
+        moves.append((0, source, 1, 0, np.where(table >= 0, table + half_wide, -1)))
+    out_gate, out_up = regroup(
+        [gu_got], [jax.ShapeDtypeStruct((rows_d, ff_mine), F32)] * 2, moves, s
+    )
+
+    qkv_wide = (ATT + 2 * KV_WIDTH) // S
+    mix_slot = -(-mix_mine // S // LANES) * LANES
+    at = np.arange(mix_mine // S)
+    moves = []
+    starts = np.array(q_starts)[:, None]
+    counts = np.array(head_counts)[:, None] * HEAD
+    for d in range(S):
+        chunk = at // ch_piece + d * (2 * N // S)
+        table = chunk * chw + at % ch_piece
+        wide = mix_slot + qkv_wide
+        inner_part = np.where(chunk < N, table, -1)[None].astype(np.int32)
+        gate_part = np.where(chunk >= N, table - ch, -1)[None].astype(np.int32)
+        moves.append((0, None, 0, d, placed(inner_part, 0, wide)))
+        moves.append((1, None, 0, d, placed(gate_part, 0, wide)))
+        column = np.arange(qkv_wide)[None] + d * qkv_wide
+        from_q = np.where(
+            (column >= starts) & (column < starts + counts), column - starts + at_q - ch, -1
+        )
+        base = np.array(kv_starts)[:, None]
+        from_k = np.where(
+            (column >= base) & (column < base + 2 * HEAD), column - base + at_k - ch, -1
+        )
+        base = base + KV_WIDTH
+        from_v = np.where(
+            (column >= base) & (column < base + 2 * HEAD), column - base + at_v - ch, -1
+        )
+        table = np.maximum(np.maximum(from_q, from_k), from_v).astype(np.int32)
+        moves.append((1, None, 0, d, placed(table, mix_slot, wide)))
+    in_blocks = regroup(
+        [r_last, r_rest], [jax.ShapeDtypeStruct((S, rows_d, wide), BF)], moves, s
+    )[0]
+    in_got, small_got = deal(
+        [in_blocks, jnp.broadcast_to(r_small, (S,) + r_small.shape)], 1
+    )
+    moves = []
+    at = np.arange(mix_mine)
+    for source in range(S):
+        chunk, inside = at // (S * ch_piece), at % (S * ch_piece)
+        table = np.where(
+            inside // ch_piece == source, chunk * ch_piece + inside % ch_piece, -1
+        )[None].astype(np.int32)
+        moves.append((0, source, 0, 0, table))
+        moves.append((0, source, 1, 0, run_table([mix_slot], qkv_wide)))
+    out_mix, out_qkv = regroup(
+        [in_got],
+        [
+            jax.ShapeDtypeStruct((rows_d, mix_mine), F32),
+            jax.ShapeDtypeStruct((rows_d, qkv_wide), F32),
+        ],
+        moves,
+        s,
+    )
+    g_att = r_rest[:, at_att - ch :].astype(F32)
+    small_all = small_got[:, :ch_piece].reshape(S * ch_piece, small_wide).astype(F32)
     out_x = span(small_all[:, :PROJ], 1, s * (PROJ // S), PROJ // S)
     out_dt = span(small_all[:, PROJ : PROJ + DT_RANK], 1, s * (DT_RANK // S), DT_RANK // S)
     out_small = small_all[:, PROJ + DT_RANK : PROJ + DT_RANK + CONV + 3 + STATE]
 
+    def added(values):
+        total = values[0]
+        for further in values[1:]:
+            total = total + further
+        return total
+
+    d_gain_att, d_gain_ssm = [added([one["gains"][i] for one in halves]) for i in range(2)]
     att_at = lax.dynamic_update_slice_in_dim(
-        jnp.zeros((ATT + width,), F32), gains[1] * live[0], q_start, 0
+        jnp.zeros((ATT + width,), F32), d_gain_att * live[0], q_start, 0
     )[:ATT]
     ssm_at = lax.dynamic_update_index_in_dim(
-        jnp.zeros((N, S, ch_piece), F32), gains[2].reshape(N, -1)[:, :ch_piece], s, 1
+        jnp.zeros((N, S, ch_piece), F32), d_gain_ssm.reshape(N, -1)[:, :ch_piece], s, 1
     ).reshape(INNER)
-    sums = lax.psum(
-        jnp.concatenate([gains[0], att_at, ssm_at, gains[3], stats]), ("seq", "fsdp")
-    )
-    ends = [0, D, D + ATT, D + ATT + INNER, D + ATT + INNER + D, D + ATT + INNER + D + 6]
+    d_gain_in = added([one["d_gain_in"] for one in halves])
+    stats = jnp.stack(
+        [
+            squares(x_own.astype(F32)),
+            jnp.sum(sums[0]),
+            jnp.sum(sums[1]),
+            squares(mixer_out),
+            squares(ffn_out),
+            squares(result),
+        ]
+    )
+    ends = np.cumsum([0, D, ATT, INNER, D, 6])
+    line = jnp.concatenate([d_gain_in, att_at, ssm_at, d_gain_ffn[0], stats])
+    sums = total_of(jnp.pad(line, (0, -line.shape[0] % 1024)).reshape(-1, LANES), 2).reshape(-1)
     g_gain_in, g_gain_att, g_gain_ssm, g_gain_ffn, stat_sum = [
         sums[a:b] for a, b in zip(ends[:-1], ends[1:])
     ]
     widths = jnp.array([D, ATT, INNER, D, D, D], F32)
     rms = jnp.sqrt(stat_sum / (widths * (micro * pack * N)))
-    outputs = give(jnp.concatenate(results, axis=0), send_hot, land_hot)
-    input_grads = give(both("dx"), send_hot, land_hot)
     return (
         outputs.reshape(tokens.shape),
         input_grads.reshape(tokens.shape),

time: 1110 us -> 1050 us (0.946)
  Pallas kernels: 94.7 us -> 435 us
  waiting for transfers between devices: 237 us -> 91.6 us
  starting transfers between devices: 145 us -> 56.2 us
  blocking collectives: 57.4 us -> 0 us
  matrix products: 199 us -> 148 us
  local copies, waits for them, and re-layouts: 249 us -> 207 us
  other arithmetic: 97.2 us -> 79.5 us
    pallas_call x0 -> x13, Pallas kernels: none -> 340 us  [the longest x1 86.7 us: ffn_rows(): pl.pallas_call(partial(ffn_kernel, size, tok, micro), out_shape=[shape((r...]
    ppermute x99 -> x30, waiting for transfers between devices: 116 us -> 16.4 us  [swap(): return lax.ppermute(array, 'seq', [(i, i ^ k) for i in range(size)])]
    ppermute x99 -> x30, starting transfers between devices: 122 us -> 35.3 us  [swap(): return lax.ppermute(array, 'seq', [(i, i ^ k) for i in range(size)])]
    reduce_scatter x4 -> x5, waiting for transfers between devices: 76 us -> 21.7 us  [scatter(): lax.psum_scatter(whole, 'fsdp', scatter_dimension=0, tiled=True)[:rows]]
    dot_general x45 -> x34, matrix products: 184 us -> 134 us  [dot(): lax.dot_general(left_op, right_op, (((left_dim,), (right_dim,)), ((), ())...]
    psum x1 -> x0, blocking collectives: 40.3 us -> none  [local(): lax.psum(jnp.concatenate([gains[0], att_at, ssm_at, gains[3], stats]), ('...]
    reshape x7 -> x4, local copies, waits for them, and re-layouts: 38.9 us -> 2.17 us  [part(): shaped = shard.reshape(shape[:axis] + (chunks, S, piece) + shape[axis + 1:])]
    unnamed x469 -> x360, local copies, waits for them, and re-layouts: 36.9 us -> 16.8 us
  transfers between devices with their start and end apart: 114 -> 44, of which waited for: 39 -> 7; matrix products, arithmetic and copies ran while one was open for 43% -> 36% of each run, Pallas kernels for 6% -> 31%
where the time goes in v2:
time: 1050 us; the launch traced here: 1030 us
  Pallas kernels  435 us (41%)
  local copies, waits for them, and re-layouts  207 us (20%)
  matrix products  148 us (14%)
  waiting for transfers between devices  91.6 us (9%)
  other arithmetic  79.5 us (8%)
  starting transfers between devices  56.2 us (5%)
  between operations  17.7 us (2%)
    dot_general x34, matrix products, dot(): lax.dot_general(left_op, right_op, (((left_dim,), (right_dim,)), ((), ())...  134 us
    pallas_call x1, Pallas kernels, ffn_rows(): pl.pallas_call(partial(ffn_kernel, size, tok, micro), out_shape=[shape((r...  86.7 us
    pallas_call x2, Pallas kernels, deal(): pl.pallas_call(partial(deal_kernel, count, size), out_shape=[jax.ShapeDty...  80.3 us
    pallas_call x1, Pallas kernels, mixer_rows(): pl.pallas_call(partial(mixer_kernel, size, tok, micro), out_shape=[shape(...  69.7 us
    pallas_call x2, Pallas kernels, scan_backward(): pl.pallas_call(partial(scan_back_kernel, groups, steps), out_shape=[rows,...  66.3 us
    pallas_call x2, Pallas kernels, gather_rows(): pl.pallas_call(partial(gather_kernel, size, tok, micro, count), out_shape...  63.3 us
    all_to_all x4, waiting for transfers between devices, exchange(): return lax.all_to_all(rows, 'fsdp', split_axis=0, concat_axis=0, tiled=True)  43.2 us
    ppermute x30, starting transfers between devices, swap(): return lax.ppermute(array, 'seq', [(i, i ^ k) for i in range(size)])  35.3 us
  transfers between devices with their start and end apart: 44, of which 7 were waited for; matrix products, arithmetic and copies ran while one was open for 36% of the time, Pallas kernels for 31%

profile of v2, /device:TPU:0, one launch (start us, length us, event | category | flops | bytes accessed | tf_op | source)
XLA Modules:
  0.0 1034.9 jit_solution(18281347247748851343)
XLA Ops:
  15.0 6.1 regroup.6
  25.8 6.3 all-to-all-start.1
  33.3 32.0 %all-to-all-done.1 = bf16[8,24,1600]{2,1,0:T(8,128)(2,1)S(1)} async-done(((bf16[8,24,1600]{2,1,0:T(8,128)(2,1)}), bf16[8,24,1600]{2,1,0:T(8,128)(2,1)S(1)}, u32[]{:S(2)}, u32[]{:S(2)}) %all-to-all-start.1) | async-done | bytes 614432 | tf_op jit(solution)/shard_map/all_to_all | solution.py:119
  74.4 31.9 %gather_rows.2 = bf16[768,1600]{1,0:T(8,128)(2,1)} custom-call(bf16[192,1600]{1,0:T(8,128)(2,1)} %get-tuple-element.437.refs_0_.refs_5_), custom_call_target="tpu_custom_call" | custom-call | tf_op jit(solution)/shard_map/gather_rows/pallas_call | solution.py:538
  107.5 31.4 %gather_rows.3.refs_1_ = bf16[768,1600]{1,0:T(8,128)(2,1)} custom-call(bf16[192,1600]{1,0:T(8,128)(2,1)} %convolution_convert_fusion.10.refs_0_.refs_3_), custom_call_target="tpu_custom_call" | custom-call | tf_op jit(solution)/shard_map/gather_rows/pallas_call | solution.py:538
  138.9 8.9 all-gather.5.cloned.1.call-done
  151.3 6.3 regroup.7
  160.9 9.7 fusion.13
  267.0 14.4 %scan_forward.2 = f32[384,896]{1,0:T(8,128)} custom-call(f32[384,896]{1,0:T(8,128)} %get-tuple-element.368.dtm_ref, f32[384,896]{1,0:T(8,128)} %get-tuple-element.367.dtu_ref, f32[384,16,128]{2,1,0:T(8,128)} %broadcast_in_dim.433.b_ref, f32[384,16,128]{2,1,0:T(8,128)} %broadcast_in_dim.434.c_ref, f32[16,896]{1,0:T(8,128)} %fusion.187.a_ref), custom_call_target="tpu_custom_call" | custom-call | flops 88080384 | bytes 40000000 | tf_op jit(solution)/shard_map/scan_forward/pallas_call | solution.py:268
  289.1 14.3 %scan_forward.3 = f32[384,896]{1,0:T(8,128)} custom-call(f32[384,896]{1,0:T(8,128)} %get-tuple-element.366.dtm_ref, f32[384,896]{1,0:T(8,128)} %get-tuple-element.365.dtu_ref, f32[384,16,128]{2,1,0:T(8,128)} %broadcast_in_dim.440.b_ref, f32[384,16,128]{2,1,0:T(8,128)} %broadcast_in_dim.441.c_ref, f32[16,896]{1,0:T(8,128)} %fusion.187.a_ref), custom_call_target="tpu_custom_call" | custom-call | flops 88080384 | bytes 40000000 | tf_op jit(solution)/shard_map/scan_forward/pallas_call | solution.py:268
  313.0 13.2 %collective-permute-done.7 = bf16[448,400]{1,0:T(8,128)(2,1)S(1)} collective-permute-done((bf16[448,400]{1,0:T(8,128)(2,1)S(1)}, bf16[448,400]{1,0:T(8,128)(2,1)S(1)}, u32[]{:S(2)}, u32[]{:S(2)}) %collective-permute-start.7) | collective-permute-done | bytes 358432 | tf_op jit(solution)/shard_map/ppermute | solution.py:56
  335.4 69.7 %mixer_rows.1 = (bf16[768,448]{1,0:T(8,128)(2,1)}, bf16[768,896]{1,0:T(8,128)(2,1)}, f32[768,128]{1,0:T(8,128)}, f32[768,128]{1,0:T(8,128)}, f32[192,1600]{1,0:T...) custom-call(f32[384,448]{1,0:T(8,128)} %get-tuple-element.413.refs_0_, f32[384,448]{1,0:T(8,128)} %get-tuple-element.412.refs_1_, ...), custom_call_target="tpu_custom_call" | custom-call | tf_op jit(solution)/shard_map/mixer_rows/pallas_call | solution.py:632
  405.1 86.7 %ffn_rows.1 = (bf16[768,1408]{1,0:T(8,128)(2,1)}, bf16[768,2816]{1,0:T(8,128)(2,1)}, bf16[4,192,1600]{2,1,0:T(8,128)(2,1)}, f32[192,1600]{1,0:T(8,128)}, f32[1,1600]{1,0:T(1,128)}, /*index=5*/bf16[768,1600]{1,0:T(8,128)(2,1)}) custom-call(bf16[768,1600]{1,0:T(8,128)(2,1)} %get-tuple-element.97.refs_0_, bf16[768,1600]{1,0:T(8,128)(2,1)} %gather_rows.3.refs_1_, ...), custom_call_target="tpu_custom_call" | custom-call | tf_op jit(solution)/shard_map/ffn_rows/pallas_call | solution.py:742
  491.8 8.6 convolution_convert_fusion.2
  500.5 13.1 %convolution_convert_fusion = bf16[1600,2816]{1,0:T(8,128)(2,1)} fusion(bf16[768,1600]{1,0:T(8,128)(2,1)} %get-tuple-element.97.refs_0_, bf16[768,2816]{1,0:T(8,128)(2,1)} %get-tuple-element.102), kind=kOutput, calls=%fused_computation.2 | convolution fusion | flops 6925107200 | bytes 15794176 | tf_op jit(solution)/shard_map/dot_general | solution.py:31
  546.1 6.9 multiply_reduce_fusion.4
  625.1 9.5 convolution_convert_fusion.1
  634.6 17.4 %dynamic_update_slice.125 = bf16[1600,2000]{1,0:T(8,128)(2,1)} dynamic-update-slice(bf16[1600,2000]{1,0:T(8,128)(2,1)} %convolution_convert_fusion.1, bf16[1600,400]{1,0:T(8,128)(2,1)} %pad_maximum_fusion.1, s32[]{:T(128)} %constant.323.clone.1, s32[]{:T(128)} %constant.347.clone.1) | dynamic-update-slice | bytes 2560004 | tf_op jit(solution)/shard_map/dynamic_update_slice | solution.py:1147
  652.0 11.2 %reduce-scatter.13.cloned.1.call-done.refs_2_ = bf16[176,1600]{1,0:T(8,128)(2,1)} async-done(((bf16[1408,1600]{1,0:T(8,128)(2,1)}), bf16[176,1600]{1,0:T(8,128)(2,1)}) %reduce-scatter.13.cloned.1.call-update) | async-done | bytes 563216 | tf_op jit(solution)/shard_map/reduce_scatter | solution.py:848
  667.2 33.1 %scan_backward.3 = (f32[384,896]{1,0:T(8,128)}, f32[384,896]{1,0:T(8,128)}, f32[16,896]{1,0:T(8,128)}, f32[8,6144]{1,0:T(8,128)}, f32[8,6144]{1,0:T(8,128)}) custom-call(f32[384,896]{1,0:T(8,128)} %get-tuple-element.366.dtm_ref, f32[384,896]{1,0:T(8,128)} %get-tuple-element.365.dtu_ref, f32[384,896]{1,0:T(8,128)} %get-tuple-element.120.dcore_ref, ...), custom_call_target="tpu_custom_call" | custom-call | flops 220200960 | bytes 100000000 | tf_op jit(solution)/shard_map/scan_backward/pallas_call | solution.py:288
  705.7 33.2 %scan_backward.2 = (f32[384,896]{1,0:T(8,128)}, f32[384,896]{1,0:T(8,128)}, f32[16,896]{1,0:T(8,128)}, f32[8,6144]{1,0:T(8,128)}, f32[8,6144]{1,0:T(8,128)}) custom-call(f32[384,896]{1,0:T(8,128)} %get-tuple-element.368.dtm_ref, f32[384,896]{1,0:T(8,128)} %get-tuple-element.367.dtu_ref, f32[384,896]{1,0:T(8,128)} %get-tuple-element.115.dcore_ref, ...), custom_call_target="tpu_custom_call" | custom-call | flops 220200960 | bytes 100000000 | tf_op jit(solution)/shard_map/scan_backward/pallas_call | solution.py:288
  766.9 9.1 multiply_reduce_fusion.8
  783.7 9.2 multiply_reduce_fusion.13
  805.9 8.0 fusion.21
  824.7 8.0 fusion.24
  842.1 6.0 convolution_convert_fusion.3
  871.5 58.0 %deal.2 = (bf16[4,200,768]{2,1,0:T(8,128)(2,1)}, bf16[4,112,400]{2,1,0:T(8,128)(2,1)}, bf16[4,176,400]{2,1,0:T(8,128)(2,1)}, bf16[4,192,1600]{2,1,0:T(8,128)(2,1)}) custom-call(bf16[4,200,768]{2,1,0:T(8,128)(2,1)} %get-tuple-element.138.refs_0_, bf16[4,112,400]{2,1,0:T(8,128)(2,1)} %get-tuple-element.139.refs_1_, ...), custom_call_target="tpu_custom_call" | custom-call | bytes 2304000 | tf_op jit(solution)/shard_map/deal/pallas_call | solution.py:418
  940.2 12.8 %total.1 = f32[64,128]{1,0:T(8,128)} custom-call(f32[64,128]{1,0:T(8,128)} %pad_bitcast_fusion.3.in_ref), custom_call_target="tpu_custom_call" | custom-call | tf_op jit(solution)/shard_map/total/pallas_call | solution.py:471
  954.3 5.8 all-to-all-start.2
  967.9 11.2 %all-to-all-done.2 = bf16[8,24,1600]{2,1,0:T(8,128)(2,1)S(1)} async-done(((bf16[8,24,1600]{2,1,0:T(8,128)(2,1)}), bf16[8,24,1600]{2,1,0:T(8,128)(2,1)S(1)}, u32[]{:S(2)}, u32[]{:S(2)}) %all-to-all-start.2) | async-done | bytes 614432 | tf_op jit(solution)/shard_map/all_to_all | solution.py:119
  984.9 10.5 %reduce-scatter.19.cloned.1.call-done = bf16[112,256]{1,0:T(8,128)(2,1)} async-done(((bf16[896,256]{1,0:T(8,128)(2,1)}), bf16[112,256]{1,0:T(8,128)(2,1)}) %reduce-scatter.19.cloned.1.call-update) | async-done | bytes 57360 | tf_op jit(solution)/shard_map/reduce_scatter | solution.py:848
  996.9 22.4 %deal.3 = (bf16[4,200,1072]{2,1,0:T(8,128)(2,1)}, bf16[4,112,256]{2,1,0:T(8,128)(2,1)}) custom-call(bf16[4,200,1072]{2,1,0:T(8,128)(2,1)} %regroup.9.refs_0_, bf16[4,112,256]{2,1,0:T(8,128)(2,1)} %broadcast_in_dim.486.refs_1_), custom_call_target="tpu_custom_call" | custom-call | bytes 972288 | tf_op jit(solution)/shard_map/deal/pallas_call | solution.py:418
  (787 shorter events, 392.4 us)
Async XLA Ops:
  7.2 140.6 %all-gather.5.cloned.1.call-start = ((), (), s32[]{:S(2)}) async-start(), calls=%async_computation.10 | async-start | bytes 11520000 | tf_op jit(solution)/shard_map/all_gather | solution.py:839
  25.8 39.5 %all-to-all-start.1 = ((bf16[8,24,1600]{2,1,0:T(8,128)(2,1)}), bf16[8,24,1600]{2,1,0:T(8,128)(2,1)S(1)}, u32[]{:S(2)}, u32[]{:S(2)}) async-start(bf16[8,24,1600]{2,1,0:T(8,128)(2,1)} %bitcast.8), calls=%async_computation.1 | async-start | bytes 1277952 | tf_op jit(solution)/shard_map/all_to_all | solution.py:119
  66.1 40.2 %all-to-all-start = ((bf16[8,24,1600]{2,1,0:T(8,128)(2,1)}), bf16[8,24,1600]{2,1,0:T(8,128)(2,1)S(1)}, u32[]{:S(2)}, u32[]{:S(2)}) async-start(bf16[8,24,1600]{2,1,0:T(8,128)(2,1)} %bitcast.5), calls=%async_computation | async-start | bytes 1277952 | tf_op jit(solution)/shard_map/all_to_all | solution.py:119
  70.1 265.3 %all-gather.7.cloned.1.call-start = ((), (), s32[]{:S(2)}) async-start(), calls=%async_computation.11 | async-start | bytes 3354624 | tf_op jit(solution)/shard_map/all_gather | solution.py:839
  147.9 257.3 %all-gather.11.cloned.1.call-start = ((), (), s32[]{:S(2)}) async-start(), calls=%async_computation.13 | async-start | bytes 5271552 | tf_op jit(solution)/shard_map/all_gather | solution.py:839
  174.4 230.7 %all-gather.9.cloned.1.call-start = ((), (), s32[]{:S(2)}) async-start(), calls=%async_computation.12 | async-start | bytes 10137600 | tf_op jit(solution)/shard_map/all_gather | solution.py:839
  175.0 450.1 %reduce-scatter.11.cloned.1.call-start = ((), (), s32[]{:S(2)}) async-start(), calls=%async_computation.14 | async-start | bytes 10137600 | tf_op jit(solution)/shard_map/reduce_scatter | solution.py:848
  198.1 40.0 %collective-permute-start = (bf16[144,384]{1,0:T(8,128)(2,1)}, bf16[144,384]{1,0:T(8,128)(2,1)}, u32[]{:S(2)}, u32[]{:S(2)}) collective-permute-start(bf16[144,384]{1,0:T(8,128)(2,1)} %get-tuple-element.428), channel_id=1, source_target_pairs={{0,8},{8,0},{16,24},{24,16},{1,9},{9,1},{17,25},{25,17},{2,10},{10... | collective-permute-start | bytes 331784 | tf_op jit(solution)/shard_map/ppermute | solution.py:56
  199.5 43.6 %collective-permute-start.1 = (bf16[144,384]{1,0:T(8,128)(2,1)}, bf16[144,384]{1,0:T(8,128)(2,1)}, u32[]{:S(2)}, u32[]{:S(2)}) collective-permute-start(bf16[144,384]{1,0:T(8,128)(2,1)} %get-tuple-element.428), channel_id=1, source_target_pairs={{0,16},{8,24},{16,0},{24,8},{1,17},{9,25},{17,1},{25,9},{2,18},{10... | collective-permute-start | bytes 331784 | tf_op jit(solution)/shard_map/ppermute | solution.py:56
  201.1 43.7 %collective-permute-start.2 = (bf16[144,384]{1,0:T(8,128)(2,1)}, bf16[144,384]{1,0:T(8,128)(2,1)}, u32[]{:S(2)}, u32[]{:S(2)}) collective-permute-start(bf16[144,384]{1,0:T(8,128)(2,1)} %get-tuple-element.428), channel_id=1, source_target_pairs={{0,24},{8,16},{16,8},{24,0},{1,25},{9,17},{17,9},{25,1},{2,26},{10... | collective-permute-start | bytes 331784 | tf_op jit(solution)/shard_map/ppermute | solution.py:56
  203.5 36.6 %collective-permute-start.3 = (bf16[144,384]{1,0:T(8,128)(2,1)}, bf16[144,384]{1,0:T(8,128)(2,1)}, u32[]{:S(2)}, u32[]{:S(2)}) collective-permute-start(bf16[144,384]{1,0:T(8,128)(2,1)} %get-tuple-element.425), channel_id=1, source_target_pairs={{0,8},{8,0},{16,24},{24,16},{1,9},{9,1},{17,25},{25,17},{2,10},{10... | collective-permute-start | bytes 331784 | tf_op jit(solution)/shard_map/ppermute | solution.py:56
  205.0 42.4 %collective-permute-start.4 = (bf16[144,384]{1,0:T(8,128)(2,1)}, bf16[144,384]{1,0:T(8,128)(2,1)}, u32[]{:S(2)}, u32[]{:S(2)}) collective-permute-start(bf16[144,384]{1,0:T(8,128)(2,1)} %get-tuple-element.425), channel_id=1, source_target_pairs={{0,16},{8,24},{16,0},{24,8},{1,17},{9,25},{17,1},{25,9},{2,18},{10... | collective-permute-start | bytes 331784 | tf_op jit(solution)/shard_map/ppermute | solution.py:56
  240.2 63.2 %collective-permute-start.6 = (bf16[448,400]{1,0:T(8,128)(2,1)}, bf16[448,400]{1,0:T(8,128)(2,1)}, u32[]{:S(2)}, u32[]{:S(2)}) collective-permute-start(bf16[448,400]{1,0:T(8,128)(2,1)} %dynamic-slice_bitcast_fusion.3), channel_id=1, source_target_pairs={{0,8},{8,0},{16,24},{24,16},{1,9},{9,1},{17,25},{25,17},{2,10},{10... | collective-permute-start | bytes 1075208 | tf_op jit(solution)/shard_map/ppermute | solution.py:56
  305.7 20.5 %collective-permute-start.7 = (bf16[448,400]{1,0:T(8,128)(2,1)S(1)}, bf16[448,400]{1,0:T(8,128)(2,1)S(1)}, u32[]{:S(2)}, u32[]{:S(2)}) collective-permute-start(bf16[448,400]{1,0:T(8,128)(2,1)S(1)} %get-tuple-element.352), channel_id=1, source_target_pairs={{0,16},{8,24},{16,0},{24,8},{1,17},{9,25},{17,1},{25,9},{2,18},{10... | collective-permute-start | bytes 1075208 | tf_op jit(solution)/shard_map/ppermute | solution.py:56
  513.6 149.6 %reduce-scatter.13.cloned.1.call-start = ((), (), s32[]{:S(2)}) async-start(), calls=%async_computation.15 | async-start | bytes 5271552 | tf_op jit(solution)/shard_map/reduce_scatter | solution.py:848
  525.6 20.1 %collective-permute-start.12 = (f32[2,384]{1,0:T(2,128)S(1)}, f32[2,384]{1,0:T(2,128)S(1)}, u32[]{:S(2)}, u32[]{:S(2)}) collective-permute-start(f32[2,384]{1,0:T(2,128)S(1)} %get-tuple-element.396), channel_id=1, source_target_pairs={{0,8},{8,0},{16,24},{24,16},{1,9},{9,1},{17,25},{25,17},{2,10},{10... | collective-permute-start | bytes 9224 | tf_op jit(solution)/shard_map/ppermute | solution.py:56
  526.8 18.9 %collective-permute-start.13 = (f32[2,384]{1,0:T(2,128)S(1)}, f32[2,384]{1,0:T(2,128)S(1)}, u32[]{:S(2)}, u32[]{:S(2)}) collective-permute-start(f32[2,384]{1,0:T(2,128)S(1)} %get-tuple-element.396), channel_id=1, source_target_pairs={{0,16},{8,24},{16,0},{24,8},{1,17},{9,25},{17,1},{25,9},{2,18},{10... | collective-permute-start | bytes 9224 | tf_op jit(solution)/shard_map/ppermute | solution.py:56
  527.7 18.1 %collective-permute-start.14 = (f32[2,384]{1,0:T(2,128)S(1)}, f32[2,384]{1,0:T(2,128)S(1)}, u32[]{:S(2)}, u32[]{:S(2)}) collective-permute-start(f32[2,384]{1,0:T(2,128)S(1)} %get-tuple-element.396), channel_id=1, source_target_pairs={{0,24},{8,16},{16,8},{24,0},{1,25},{9,17},{17,9},{25,1},{2,26},{10... | collective-permute-start | bytes 9224 | tf_op jit(solution)/shard_map/ppermute | solution.py:56
  539.5 76.3 %collective-permute-start.15 = (bf16[448,400]{1,0:T(8,128)(2,1)}, bf16[448,400]{1,0:T(8,128)(2,1)}, u32[]{:S(2)}, u32[]{:S(2)}) collective-permute-start(bf16[448,400]{1,0:T(8,128)(2,1)} %bitcast.336), channel_id=1, source_target_pairs={{0,8},{8,0},{16,24},{24,16},{1,9},{9,1},{17,25},{25,17},{2,10},{10... | collective-permute-start | bytes 1075208 | tf_op jit(solution)/shard_map/ppermute | solution.py:56
  567.0 50.6 %collective-permute-start.16 = (bf16[448,400]{1,0:T(8,128)(2,1)}, bf16[448,400]{1,0:T(8,128)(2,1)}, u32[]{:S(2)}, u32[]{:S(2)}) collective-permute-start(bf16[448,400]{1,0:T(8,128)(2,1)} %bitcast.337), channel_id=1, source_target_pairs={{0,16},{8,24},{16,0},{24,8},{1,17},{9,25},{17,1},{25,9},{2,18},{10... | collective-permute-start | bytes 1075208 | tf_op jit(solution)/shard_map/ppermute | solution.py:56
  570.0 232.2 %reduce-scatter.15.cloned.1.call-start = ((), (), s32[]{:S(2)}) async-start(), calls=%async_computation.16 | async-start | bytes 3354624 | tf_op jit(solution)/shard_map/reduce_scatter | solution.py:848
  570.2 49.3 %collective-permute-start.17 = (bf16[448,400]{1,0:T(8,128)(2,1)}, bf16[448,400]{1,0:T(8,128)(2,1)}, u32[]{:S(2)}, u32[]{:S(2)}) collective-permute-start(bf16[448,400]{1,0:T(8,128)(2,1)} %bitcast.338), channel_id=1, source_target_pairs={{0,24},{8,16},{16,8},{24,0},{1,25},{9,17},{17,9},{25,1},{2,26},{10... | collective-permute-start | bytes 1075208 | tf_op jit(solution)/shard_map/ppermute | solution.py:56
  663.3 138.9 %reduce-scatter.17.cloned.1.call-start = ((), (), s32[]{:S(2)}) async-start(), calls=%async_computation.17 | async-start | bytes 7372800 | tf_op jit(solution)/shard_map/reduce_scatter | solution.py:848
  664.0 316.4 %reduce-scatter.21.cloned.1.call-start = ((), (), s32[]{:S(2)}) async-start(), calls=%async_computation.19 | async-start | bytes 3225600
  753.6 22.5 %collective-permute-start.18 = (bf16[144,384]{1,0:T(8,128)(2,1)}, bf16[144,384]{1,0:T(8,128)(2,1)}, u32[]{:S(2)}, u32[]{:S(2)}) collective-permute-start(bf16[144,384]{1,0:T(8,128)(2,1)} %get-tuple-element.419), channel_id=1, source_target_pairs={{0,8},{8,0},{16,24},{24,16},{1,9},{9,1},{17,25},{25,17},{2,10},{10... | collective-permute-start | bytes 331784 | tf_op jit(solution)/shard_map/ppermute | solution.py:56
  755.1 22.6 %collective-permute-start.19 = (bf16[144,384]{1,0:T(8,128)(2,1)}, bf16[144,384]{1,0:T(8,128)(2,1)}, u32[]{:S(2)}, u32[]{:S(2)}) collective-permute-start(bf16[144,384]{1,0:T(8,128)(2,1)} %get-tuple-element.419), channel_id=1, source_target_pairs={{0,16},{8,24},{16,0},{24,8},{1,17},{9,25},{17,1},{25,9},{2,18},{10... | collective-permute-start | bytes 331784 | tf_op jit(solution)/shard_map/ppermute | solution.py:56
  817.6 23.9 %collective-permute-start.24 = (bf16[96,1600]{1,0:T(8,128)(2,1)}, bf16[96,1600]{1,0:T(8,128)(2,1)S(1)}, u32[]{:S(2)}, u32[]{:S(2)}) collective-permute-start(bf16[96,1600]{1,0:T(8,128)(2,1)} %get-tuple-element.340), channel_id=1, source_target_pairs={{0,8},{8,0},{16,24},{24,16},{1,9},{9,1},{17,25},{25,17},{2,10},{10... | collective-permute-start | bytes 921608 | tf_op jit(solution)/shard_map/ppermute | solution.py:56
  819.1 29.1 %collective-permute-start.25 = (bf16[96,1600]{1,0:T(8,128)(2,1)}, bf16[96,1600]{1,0:T(8,128)(2,1)}, u32[]{:S(2)}, u32[]{:S(2)}) collective-permute-start(bf16[96,1600]{1,0:T(8,128)(2,1)} %get-tuple-element.342), channel_id=1, source_target_pairs={{0,16},{8,24},{16,0},{24,8},{1,17},{9,25},{17,1},{25,9},{2,18},{10... | collective-permute-start | bytes 921608 | tf_op jit(solution)/shard_map/ppermute | solution.py:56
  820.5 27.7 %collective-permute-start.26 = (bf16[96,1600]{1,0:T(8,128)(2,1)}, bf16[96,1600]{1,0:T(8,128)(2,1)}, u32[]{:S(2)}, u32[]{:S(2)}) collective-permute-start(bf16[96,1600]{1,0:T(8,128)(2,1)} %get-tuple-element.341), channel_id=1, source_target_pairs={{0,24},{8,16},{16,8},{24,0},{1,25},{9,17},{17,9},{25,1},{2,26},{10... | collective-permute-start | bytes 921608 | tf_op jit(solution)/shard_map/ppermute | solution.py:56
  867.3 86.9 %all-to-all-start.3 = ((bf16[8,24,1600]{2,1,0:T(8,128)(2,1)}), bf16[8,24,1600]{2,1,0:T(8,128)(2,1)S(1)}, u32[]{:S(2)}, u32[]{:S(2)}) async-start(bf16[8,24,1600]{2,1,0:T(8,128)(2,1)} %bitcast.129), calls=%async_computation.7 | async-start | bytes 1277952 | tf_op jit(solution)/shard_map/all_to_all | solution.py:119
  954.3 24.9 %all-to-all-start.2 = ((bf16[8,24,1600]{2,1,0:T(8,128)(2,1)}), bf16[8,24,1600]{2,1,0:T(8,128)(2,1)S(1)}, u32[]{:S(2)}, u32[]{:S(2)}) async-start(bf16[8,24,1600]{2,1,0:T(8,128)(2,1)} %bitcast.320), calls=%async_computation.6 | async-start | bytes 1277952 | tf_op jit(solution)/shard_map/all_to_all | solution.py:119
  960.1 35.2 %reduce-scatter.19.cloned.1.call-start = ((), (), s32[]{:S(2)}) async-start(), calls=%async_computation.18 | async-start | bytes 516096 | tf_op jit(solution)/shard_map/reduce_scatter | solution.py:848
  (192 other events, 1366.6 us)
Sparse Core Ops, SparseCore 0:
  23.7 124.1 all-gather.4
  149.5 35.8 all-gather.6
  187.0 50.2 all-gather.10
  239.4 86.0 all-gather.8
  513.7 93.8 reduce-scatter.10
  609.9 53.2 reduce-scatter.12
  665.6 37.4 reduce-scatter.14
  705.4 71.9 reduce-scatter.16
  854.3 48.8 reduce-scatter.20
  963.5 31.8 reduce-scatter.18

commit v3 on v2

--- a/solution.py
+++ b/solution.py
@@ -129,6 +129,60 @@
     return dot(send_hot, exchange(sent), 0, 0).astype(BF)
 
 
+def meet(peers):
+    barrier = pltpu.get_barrier_semaphore()
+    for peer in peers:
+        pl.semaphore_signal(barrier, inc=1, device_id=peer, device_id_type=pl.DeviceIdType.MESH)
+    pl.semaphore_wait(barrier, len(peers))
+
+
+def remote(source, target, send, recv, device):
+    return pltpu.make_async_remote_copy(
+        src_ref=source,
+        dst_ref=target,
+        send_sem=send,
+        recv_sem=recv,
+        device_id=device,
+        device_id_type=pl.DeviceIdType.MESH,
+    )
+
+
+def pack_peers(size):
+    here, row = lax.axis_index("seq"), lax.axis_index("fsdp")
+    return [(lax.rem(here + k, size), row) for k in range(1, size)]
+
+
+def start_deal(source, out, size, own_sem, send_sem, recv_sem, first=0, start=True):
+    here, row = lax.axis_index("seq"), lax.axis_index("fsdp")
+    copies = [pltpu.make_async_copy(source.at[here], out.at[here], own_sem)]
+    for k in range(1, size):
+        there = lax.rem(here + k, size)
+        copies.append(
+            remote(
+                source.at[there],
+                out.at[here],
+                send_sem.at[first + k - 1],
+                recv_sem.at[first + k - 1],
+                (there, row),
+            )
+        )
+    if start:
+        for copy in copies:
+            copy.start()
+    return copies
+
+
+def deal_sems(size, count=1):
+    links = pltpu.SemaphoreType.DMA((count * (size - 1),))
+    return [pltpu.SemaphoreType.DMA((count,)), links, links]
+
+
+VMEM_BYTES = 60 * 2**20
+VMEM = pl.BlockSpec(memory_space=pltpu.VMEM)
+HBM = pl.BlockSpec(memory_space=pl.ANY)
+SHAPE = jax.ShapeDtypeStruct
+
+
 def lane_groups(channels, most=4):
     tiles, out, first = channels // LANES, [], 0
     while first < tiles:
@@ -138,7 +192,39 @@
     return out
 
 
-def scan_kernel(groups, steps, dtm_ref, dtu_ref, b_ref, c_ref, a_ref, core_ref):
+def sigmoid(v):
+    return 1.0 / (1.0 + jnp.exp(-v))
+
+
+def softplus(v):
+    return jnp.maximum(v, 0.0) + jnp.log1p(jnp.exp(-jnp.abs(v)))
+
+
+def steps_of(lin_ref, u_ref, position_ref, dtm, dtu):
+    step = softplus(lin_ref[...])
+    dtu[...] = step * u_ref[...]
+    dtm[...] = jnp.where(position_ref[...] > 0, step, 1e30)
+
+
+def both_of(ref, t):
+    row = ref[t].astype(F32)
+    return row[:STATE], row[STATE:]
+
+
+def scan_kernel(size, groups, *refs):
+    u_ref, lin_ref, bc_ref, a_ref, position_ref, gate_ref, skip_ref, held = refs[:8]
+    core, out, sums, got, dtm, dtu, own_sem, held_send, held_recv = refs[8:]
+    steps = u_ref.shape[0]
+
+    def copies(start):
+        return start_deal(held, got, size, own_sem.at[0], held_send, held_recv, start=start)
+
+    @pl.when(pl.program_id(0) == 0)
+    def _():
+        meet(pack_peers(size))
+        copies(True)
+
+    steps_of(lin_ref, u_ref, position_ref, dtm, dtu)
     place = lax.broadcasted_iota(jnp.int32, (8, LANES), 0)
     for first, count in groups:
         spans = [pl.ds((first + i) * LANES, LANES) for i in range(count)]
@@ -146,44 +232,97 @@
 
         def block(k, held):
             held = list(held)
-            base = pl.multiple_of(k * 8, 8)
-            rows = pl.ds(base, 8)
-            dts = [dtm_ref[rows, span] for span in spans]
-            dus = [dtu_ref[rows, span] for span in spans]
+            rows = pl.ds(pl.multiple_of(k * 8, 8), 8)
+            dts = [dtm[rows, span] for span in spans]
+            dus = [dtu[rows, span] for span in spans]
             ys = [jnp.zeros((8, LANES), F32)] * count
             for j in range(8):
-                b_now, c_now = b_ref[base + j], c_ref[base + j]
+                b_now, c_now = both_of(bc_ref, k * 8 + j)
                 for i in range(count):
                     decay = jnp.exp(dts[i][j : j + 1] * rates[i])
                     held[i] = decay * held[i] + dus[i][j : j + 1] * b_now
                     y = jnp.sum(held[i] * c_now, axis=0, keepdims=True)
                     ys[i] = jnp.where(place == j, y, ys[i])
             for i, span in enumerate(spans):
-                core_ref[rows, span] = ys[i]
+                core[rows, span] = ys[i]
             return tuple(held)
 
         zero = jnp.zeros((STATE, LANES), F32)
         lax.fori_loop(0, steps // 8, block, (zero,) * count)
-
-
-def scan_back_kernel(
-    groups,
-    steps,
-    dtm_ref,
-    dtu_ref,
-    dcore_ref,
-    b_ref,
-    c_ref,
-    a_ref,
-    ddtu_ref,
-    ddt_ref,
-    da_ref,
-    db_ref,
-    dc_ref,
-    hs,
-    acc_b,
-    acc_c,
-):
+    gate = gate_ref[...].astype(F32)
+    result = (core[...] + skip_ref[...] * u_ref[...]) * (gate * sigmoid(gate))
+    out[...] = result
+    sums[...] = row_sums(result * result)
+
+    @pl.when(pl.program_id(0) == pl.num_programs(0) - 1)
+    def _():
+        for copy in copies(False):
+            copy.wait()
+
+
+def row_sums(values):
+    return lax.dot_general(
+        jnp.ones((8, values.shape[1]), F32),
+        values,
+        (((1,), (1,)), ((), ())),
+        precision=lax.Precision.HIGHEST,
+        preferred_element_type=F32,
+    )
+
+
+def scan_forward(u, lin, bc, rates, position, opened, skip, held, micro, collective_id):
+    size = lax.axis_size("seq")
+    rows, channels = u.shape
+    steps = rows // micro
+    block = pl.BlockSpec((steps, channels), lambda m: (m, 0))
+    lane = pl.BlockSpec((8, steps), lambda m: (0, m))
+    return pl.pallas_call(
+        partial(scan_kernel, size, lane_groups(channels)),
+        grid=(micro,),
+        out_shape=[SHAPE((rows, channels), F32)] * 2
+        + [SHAPE((8, rows), F32), SHAPE(held.shape, held.dtype)],
+        in_specs=[
+            block,
+            block,
+            pl.BlockSpec((steps, 2 * STATE, LANES), lambda m: (m, 0, 0)),
+            pl.BlockSpec(rates.shape, lambda m: (0, 0)),
+            pl.BlockSpec((steps, 1), lambda m: (m, 0)),
+            pl.BlockSpec((steps, channels), lambda m: (m, 1)),
+            pl.BlockSpec((1, channels), lambda m: (0, 0)),
+            HBM,
+        ],
+        out_specs=[block, block, lane, HBM],
+        scratch_shapes=[pltpu.VMEM((steps, channels), F32)] * 2 + deal_sems(size),
+        compiler_params=pltpu.CompilerParams(
+            collective_id=collective_id, has_side_effects=True, vmem_limit_bytes=VMEM_BYTES
+        ),
+        name="scan_forward",
+    )(u, lin, bc, rates, position, opened, skip, held)
+
+
+def scan_back_kernel(size, count, groups, *refs):
+    dcore_ref, u_ref, lin_ref, bc_ref, a_ref, position_ref, skip_ref = refs[:7]
+    helds, refs = refs[7 : 7 + count], refs[7 + count :]
+    du_ref, dlin_ref, bias_ref, da_ref, db_ref, dc_ref = refs[:6]
+    gots, refs = refs[6 : 6 + count], refs[6 + count :]
+    dtm, dtu, ddtu, ddt, hs, acc_b, acc_c, own_sem, held_send, held_recv = refs
+    steps = u_ref.shape[0]
+
+    def copies():
+        out = []
+        for i, (held, got) in enumerate(zip(helds, gots)):
+            out += start_deal(
+                held, got, size, own_sem.at[i], held_send, held_recv, i * (size - 1), start=False
+            )
+        return out
+
+    @pl.when(pl.program_id(0) == 0)
+    def _():
+        meet(pack_peers(size))
+        for copy in copies():
+            copy.start()
+
+    steps_of(lin_ref, u_ref, position_ref, dtm, dtu)
     place = lax.broadcasted_iota(jnp.int32, (8, LANES), 0)
     zero = jnp.zeros((STATE, LANES), F32)
     for at, (first, count) in enumerate(groups):
@@ -197,10 +336,10 @@
             held = list(held)
             base = pl.multiple_of(k * 8, 8)
             rows = pl.ds(base, 8)
-            dts = [dtm_ref[rows, span] for span in spans]
-            dus = [dtu_ref[rows, span] for span in spans]
+            dts = [dtm[rows, span] for span in spans]
+            dus = [dtu[rows, span] for span in spans]
             for j in range(8):
-                b_now = b_ref[base + j]
+                b_now, _ = both_of(bc_ref, base + j)
                 for i in range(count):
                     decay = jnp.exp(dts[i][j : j + 1] * rates[i])
                     held[i] = decay * held[i] + dus[i][j : j + 1] * b_now
@@ -211,16 +350,17 @@
 
         def back(k, carry):
             carry = list(carry)
-            base = pl.multiple_of(steps - 8 - k * 8, 8)
+            block_at = steps // 8 - 1 - k
+            base = pl.multiple_of(block_at * 8, 8)
             rows = pl.ds(base, 8)
-            dts = [dtm_ref[rows, span] for span in spans]
-            dus = [dtu_ref[rows, span] for span in spans]
+            dts = [dtm[rows, span] for span in spans]
+            dus = [dtu[rows, span] for span in spans]
             dys = [dcore_ref[rows, span] for span in spans]
             out_u = [jnp.zeros((8, LANES), F32)] * count
             out_t = [jnp.zeros((8, LANES), F32)] * count
             for j in reversed(range(8)):
                 t = base + j
-                b_now, c_now = b_ref[t], c_ref[t]
+                b_now, c_now = both_of(bc_ref, t)
                 sum_b = sum_c = zero
                 for i in range(count):
                     later, rate_sum = carry[i]
@@ -242,68 +382,90 @@
                     acc_b[t] = acc_b[t] + sum_b
                     acc_c[t] = acc_c[t] + sum_c
             for i, span in enumerate(spans):
-                ddtu_ref[rows, span] = out_u[i]
-                ddt_ref[rows, span] = out_t[i]
+                ddtu[rows, span] = out_u[i]
+                ddt[rows, span] = out_t[i]
             return tuple(carry)
 
         ends = lax.fori_loop(0, steps // 8, back, ((zero, zero),) * count)
         for i, span in enumerate(spans):
             da_ref[:, span] = ends[i][1]
-    ones = jnp.ones((8, LANES), F32)
     for acc, out in ((acc_b, db_ref), (acc_c, dc_ref)):
-        out[...] = lax.dot_general(
-            ones,
-            acc[...].reshape(steps * STATE, LANES),
-            (((1,), (1,)), ((), ())),
-            precision=lax.Precision.HIGHEST,
-            preferred_element_type=F32,
-        )
-
-
-VMEM_BYTES = 60 * 2**20
-
-
-def scan_forward(dtm, dtu, b_wide, c_wide, rates):
-    steps, channels = dtm.shape
-    return pl.pallas_call(
-        partial(scan_kernel, lane_groups(channels), steps),
-        out_shape=jax.ShapeDtypeStruct((steps, channels), F32),
-        in_specs=[pl.BlockSpec(memory_space=pltpu.VMEM)] * 5,
-        out_specs=pl.BlockSpec(memory_space=pltpu.VMEM),
-        compiler_params=pltpu.CompilerParams(vmem_limit_bytes=VMEM_BYTES),
-        cost_estimate=pl.CostEstimate(
-            flops=16 * steps * channels * STATE,
-            bytes_accessed=40_000_000,
-            transcendentals=steps * channels * STATE,
-        ),
-        name="scan_forward",
-    )(dtm, dtu, b_wide, c_wide, rates)
-
-
-def scan_backward(dtm, dtu, dcore, b_wide, c_wide, rates):
-    steps, channels = dtm.shape
+        out[...] = row_sums(acc[...].reshape(steps * STATE, LANES))
+    lin = lin_ref[...]
+    to_step = ddtu[...]
+    du_ref[...] = dcore_ref[...] * skip_ref[...] + to_step * softplus(lin)
+    d_lin = (ddt[...] + to_step * u_ref[...]) * sigmoid(lin)
+    dlin_ref[...] = d_lin.astype(BF)
+    bias_ref[...] = jnp.sum(d_lin, axis=0, keepdims=True)
+
+    @pl.when(pl.program_id(0) == pl.num_programs(0) - 1)
+    def _():
+        for copy in copies():
+            copy.wait()
+
+
+def scan_backward(dcore, u, lin, bc, rates, position, skip, helds, micro, collective_id):
+    size = lax.axis_size("seq")
+    rows, channels = u.shape
+    steps = rows // micro
     groups = lane_groups(channels)
-    rows = jax.ShapeDtypeStruct((steps, channels), F32)
-    flat = jax.ShapeDtypeStruct((8, steps * STATE), F32)
-    ddtu, ddt, da, db, dc = pl.pallas_call(
-        partial(scan_back_kernel, groups, steps),
-        out_shape=[rows, rows, jax.ShapeDtypeStruct((STATE, channels), F32), flat, flat],
-        in_specs=[pl.BlockSpec(memory_space=pltpu.VMEM)] * 6,
-        out_specs=[pl.BlockSpec(memory_space=pltpu.VMEM)] * 5,
-        scratch_shapes=[
+    block = pl.BlockSpec((steps, channels), lambda m: (m, 0))
+    rate = pl.BlockSpec(rates.shape, lambda m: (0, 0))
+    line = pl.BlockSpec((1, channels), lambda m: (0, 0))
+    flat = pl.BlockSpec((None, 8, steps * STATE), lambda m: (m, 0, 0))
+    wide = pltpu.VMEM((steps, channels), F32)
+    du, dlin, bias, da, db, dc, *gots = pl.pallas_call(
+        partial(scan_back_kernel, size, len(helds), groups),
+        grid=(micro,),
+        out_shape=[
+            SHAPE((rows, channels), F32),
+            SHAPE((rows, channels), BF),
+            SHAPE((micro, 1, channels), F32),
+            SHAPE((micro, STATE, channels), F32),
+            SHAPE((micro, 8, steps * STATE), F32),
+            SHAPE((micro, 8, steps * STATE), F32),
+        ]
+        + [SHAPE(held.shape, held.dtype) for held in helds],
+        in_specs=[
+            block,
+            block,
+            block,
+            pl.BlockSpec((steps, 2 * STATE, LANES), lambda m: (m, 0, 0)),
+            rate,
+            pl.BlockSpec((steps, 1), lambda m: (m, 0)),
+            line,
+        ]
+        + [HBM] * len(helds),
+        out_specs=[
+            block,
+            block,
+            pl.BlockSpec((None, 1, channels), lambda m: (m, 0, 0)),
+            pl.BlockSpec((None, STATE, channels), lambda m: (m, 0, 0)),
+            flat,
+            flat,
+        ]
+        + [HBM] * len(helds),
+        scratch_shapes=[wide] * 4
+        + [
             pltpu.VMEM((steps + 1, STATE, groups[0][1] * LANES), F32),
             pltpu.VMEM((steps, STATE, LANES), F32),
             pltpu.VMEM((steps, STATE, LANES), F32),
-        ],
-        compiler_params=pltpu.CompilerParams(vmem_limit_bytes=VMEM_BYTES),
-        cost_estimate=pl.CostEstimate(
-            flops=40 * steps * channels * STATE,
-            bytes_accessed=100_000_000,
-            transcendentals=2 * steps * channels * STATE,
+        ]
+        + deal_sems(size, len(helds)),
+        compiler_params=pltpu.CompilerParams(
+            collective_id=collective_id, has_side_effects=True, vmem_limit_bytes=VMEM_BYTES
         ),
         name="scan_backward",
-    )(dtm, dtu, dcore, b_wide, c_wide, rates)
-    return ddtu, ddt, da, db[0].reshape(steps, STATE), dc[0].reshape(steps, STATE)
+    )(dcore, u, lin, bc, rates, position, skip, *helds)
+    return (
+        du,
+        dlin,
+        jnp.sum(bias[:, 0], axis=0),
+        jnp.sum(da, axis=0),
+        db[:, 0].reshape(rows, STATE),
+        dc[:, 0].reshape(rows, STATE),
+        gots,
+    )
 
 
 def regroup_kernel(plan, source_count, out_count, *refs):
@@ -378,36 +540,15 @@
     return out
 
 
-def meet(peers):
-    barrier = pltpu.get_barrier_semaphore()
-    for peer in peers:
-        pl.semaphore_signal(barrier, inc=1, device_id=peer, device_id_type=pl.DeviceIdType.MESH)
-    pl.semaphore_wait(barrier, len(peers))
-
-
 def deal_kernel(count, size, *refs):
     sources, outs = refs[:count], refs[count : 2 * count]
     own_sem, send_sem, recv_sem = refs[2 * count :]
-    here, row = lax.axis_index("seq"), lax.axis_index("fsdp")
-    others = [lax.rem(here + k, size) for k in range(1, size)]
-    meet([(there, row) for there in others])
+    meet(pack_peers(size))
     copies = []
     for i, (source, out) in enumerate(zip(sources, outs)):
-        copies.append(pltpu.make_async_copy(source.at[here], out.at[here], own_sem.at[i]))
-        copies[-1].start()
-        for k, there in enumerate(others):
-            at = i * (size - 1) + k
-            copies.append(
-                pltpu.make_async_remote_copy(
-                    src_ref=source.at[there],
-                    dst_ref=out.at[here],
-                    send_sem=send_sem.at[at],
-                    recv_sem=recv_sem.at[at],
-                    device_id=(there, row),
-                    device_id_type=pl.DeviceIdType.MESH,
-                )
-            )
-            copies[-1].start()
+        copies += start_deal(
+            source, out, size, own_sem.at[i], send_sem, recv_sem, i * (size - 1)
+        )
     for copy in copies:
         copy.wait()
 
@@ -420,75 +561,63 @@
         out_shape=[jax.ShapeDtypeStruct(a.shape, a.dtype) for a in arrays],
         in_specs=[hbm] * count,
         out_specs=[hbm] * count,
-        scratch_shapes=[
-            pltpu.SemaphoreType.DMA((count,)),
-            pltpu.SemaphoreType.DMA((count * (size - 1),)),
-            pltpu.SemaphoreType.DMA((count * (size - 1),)),
-        ],
+        scratch_shapes=deal_sems(size, count),
         compiler_params=pltpu.CompilerParams(collective_id=collective_id, has_side_effects=True),
         cost_estimate=pl.CostEstimate(
-            flops=0, bytes_accessed=sum(a.size for a in arrays), transcendentals=0
+            flops=0, bytes_accessed=1024, transcendentals=0
         ),
         name="deal",
     )(*arrays)
 
 
-def total_kernel(sizes, in_ref, out_ref, one, two, send_sem, recv_sem, send_two, recv_two):
+def spread(slots, me, devices, send, recv):
+    copies = []
+    for k, device in enumerate(devices):
+        copies.append(remote(slots.at[me], slots.at[me], send.at[k], recv.at[k], device))
+        copies[-1].start()
+    for copy in copies:
+        copy.wait()
+    total = slots[0]
+    for i in range(1, slots.shape[0]):
+        total = total + slots[i]
+    return total
+
+
+def last_kernel(sizes, count, *refs):
+    sources, in_ref = refs[:count], refs[count]
+    outs, out_ref = refs[count + 1 : 2 * count + 1], refs[2 * count + 1]
+    one, two, send_one, recv_one, send_two, recv_two, own_sem, send_sem, recv_sem = refs[
+        2 * count + 2 :
+    ]
     seq, fsdp = lax.axis_index("seq"), lax.axis_index("fsdp")
-    across = [lax.rem(seq + k, sizes[0]) for k in range(1, sizes[0])]
-    along = [lax.rem(fsdp + k, sizes[1]) for k in range(1, sizes[1])]
-    meet([(there, fsdp) for there in across] + [(seq, there) for there in along])
-
-    def spread(slots, me, devices, send, recv):
-        copies = []
-        for k, device in enumerate(devices):
-            copies.append(
-                pltpu.make_async_remote_copy(
-                    src_ref=slots.at[me],
-                    dst_ref=slots.at[me],
-                    send_sem=send.at[k],
-                    recv_sem=recv.at[k],
-                    device_id=device,
-                    device_id_type=pl.DeviceIdType.MESH,
-                )
-            )
-            copies[-1].start()
-        for copy in copies:
-            copy.wait()
-        total = slots[0]
-        for i in range(1, slots.shape[0]):
-            total = total + slots[i]
-        return total
-
+    across = [(lax.rem(seq + k, sizes[0]), fsdp) for k in range(1, sizes[0])]
+    along = [(seq, lax.rem(fsdp + k, sizes[1])) for k in range(1, sizes[1])]
+    meet(across + along)
     one[seq] = in_ref[...]
-    two[fsdp] = spread(one, seq, [(there, fsdp) for there in across], send_sem, recv_sem)
-    out_ref[...] = spread(two, fsdp, [(seq, there) for there in along], send_two, recv_two)
-
-
-def total_of(block, collective_id):
-    sizes = (lax.axis_size("seq"), lax.axis_size("fsdp"))
-    vmem = pl.BlockSpec(memory_space=pltpu.VMEM)
+    two[fsdp] = spread(one, seq, across, send_one, recv_one)
+    copies = []
+    for i, (source, out) in enumerate(zip(sources, outs)):
+        copies += start_deal(
+            source, out, sizes[0], own_sem.at[i], send_sem, recv_sem, i * (sizes[0] - 1)
+        )
+    out_ref[...] = spread(two, fsdp, along, send_two, recv_two)
+    for copy in copies:
+        copy.wait()
+
+
+def last_exchange(arrays, block, collective_id):
+    sizes, count = (lax.axis_size("seq"), lax.axis_size("fsdp")), len(arrays)
     return pl.pallas_call(
-        partial(total_kernel, sizes),
-        out_shape=jax.ShapeDtypeStruct(block.shape, block.dtype),
-        in_specs=[vmem],
-        out_specs=vmem,
+        partial(last_kernel, sizes, count),
+        out_shape=[SHAPE(a.shape, a.dtype) for a in arrays] + [SHAPE(block.shape, block.dtype)],
+        in_specs=[HBM] * count + [VMEM],
+        out_specs=[HBM] * count + [VMEM],
         scratch_shapes=[pltpu.VMEM((n,) + block.shape, F32) for n in sizes]
-        + [pltpu.SemaphoreType.DMA((n - 1,)) for n in sizes for _ in range(2)],
+        + [pltpu.SemaphoreType.DMA((n - 1,)) for n in sizes for _ in range(2)]
+        + deal_sems(sizes[0], count),
         compiler_params=pltpu.CompilerParams(collective_id=collective_id, has_side_effects=True),
-        name="total",
-    )(block)
-
-
-def remote(source, target, send, recv, device):
-    return pltpu.make_async_remote_copy(
-        src_ref=source,
-        dst_ref=target,
-        send_sem=send,
-        recv_sem=recv,
-        device_id=device,
-        device_id_type=pl.DeviceIdType.MESH,
-    )
+        name="last_exchange",
+    )(*arrays, block)
 
 
 def block_rows(size, tok, m, d):
@@ -509,11 +638,6 @@
     for copy in copies:
         copy.start()
     return copies
-
-
-def pack_peers(size):
-    here, row = lax.axis_index("seq"), lax.axis_index("fsdp")
-    return [(lax.rem(here + k, size), row) for k in range(1, size)]
 
 
 def gather_kernel(size, tok, micro, count, *refs):
@@ -554,13 +678,20 @@
     return [(low, min(low + most, width)) for low in range(0, width, most)]
 
 
+def joined(blocks, out):
+    wide = blocks.shape[2]
+    for i in range(blocks.shape[0]):
+        out[:, i * wide : (i + 1) * wide] = blocks[i]
+    return out
+
+
 def mixer_kernel(size, tok, micro, *refs):
-    contexts, ssm_outs = refs[:micro], refs[micro : 2 * micro]
-    sums_ref, x_ref, gain_att, gain_ssm, gain_ffn, w_att, w_ssm = refs[2 * micro : 2 * micro + 7]
-    att, ssm, scale_att, scale_ssm, hidden, mixer, ffn = refs[2 * micro + 7 : 2 * micro + 14]
+    context, ssm_out, sums_ref, x_ref, gain_att, gain_ssm, gain_ffn, w_att, w_ssm = refs[:9]
+    att, ssm, scale_att, scale_ssm, hidden, mixer, ffn = refs[9:16]
     sums, sent, got, ffn_own, sums_send, sums_recv, send, recv, own_sem, ffn_send, ffn_recv = refs[
-        2 * micro + 14 :
+        16:-1
     ]
+    w_att = joined(w_att, refs[-1])
     here, row = lax.axis_index("seq"), lax.axis_index("fsdp")
     peers = pack_peers(size)
     meet(peers)
@@ -586,11 +717,8 @@
             preferred_element_type=F32,
         )
         scale[...] = lax.rsqrt(column / width + EPS)
-    pack = size * tok
-    for m in range(micro):
-        rows = pl.ds(m * pack, pack)
-        att[rows] = (contexts[m][...] * scale_att[rows, :1] * gain_att[...]).astype(BF)
-        ssm[rows] = (ssm_outs[m][...] * scale_ssm[rows, :1] * gain_ssm[...]).astype(BF)
+    att[...] = (context[...] * scale_att[:, :1] * gain_att[...]).astype(BF)
+    ssm[...] = (ssm_out[...] * scale_ssm[:, :1] * gain_ssm[...]).astype(BF)
 
     def product(d, low, high):
         left = [jnp.concatenate([ref[block_rows(size, tok, m, d)] for m in range(micro)]) for ref in (att, ssm)]
@@ -622,8 +750,8 @@
         copy.wait()
 
 
-def mixer_rows(contexts, ssm_outs, sums, x_own, gains, w_att, w_ssm, collective_id):
-    size, micro = lax.axis_size("seq"), len(contexts)
+def mixer_rows(context, ssm_out, sums, x_own, gains, w_att, w_ssm, micro, collective_id):
+    size = lax.axis_size("seq")
     own = x_own.shape[0]
     rows, tok = own * size, own // micro
     vmem, hbm = pl.BlockSpec(memory_space=pltpu.VMEM), pl.BlockSpec(memory_space=pl.ANY)
@@ -632,7 +760,7 @@
     return pl.pallas_call(
         partial(mixer_kernel, size, tok, micro),
         out_shape=[
-            shape((rows, w_att.shape[0]), BF),
+            shape((rows, w_att.shape[1]), BF),
             shape((rows, w_ssm.shape[0]), BF),
             shape((rows, LANES), F32),
             shape((rows, LANES), F32),
@@ -640,7 +768,7 @@
             shape((own, D), F32),
             shape((rows, D), BF),
         ],
-        in_specs=[vmem] * (2 * micro + 7),
+        in_specs=[vmem] * 9,
         out_specs=[vmem] * 6 + [hbm],
         scratch_shapes=[
             pltpu.VMEM((size,) + sums.shape, F32),
@@ -654,12 +782,13 @@
             dma((micro,)),
             dma((micro * (size - 1),)),
             dma((micro * (size - 1),)),
+            pltpu.VMEM((w_att.shape[1], D), BF),
         ],
         compiler_params=pltpu.CompilerParams(
             collective_id=collective_id, has_side_effects=True, vmem_limit_bytes=VMEM_BYTES
         ),
         name="mixer_rows",
-    )(*contexts, *ssm_outs, sums, x_own, *gains, w_att, w_ssm)
+    )(context, ssm_out, sums, x_own, *gains, w_att, w_ssm)
 
 
 def ffn_kernel(size, tok, micro, *refs):
@@ -768,27 +897,358 @@
     )(ffn, cot, hidden, cot_own, gain, w_gu, w_down)
 
 
-def conv_act(position, inner, tap_weights, tap_bias):
-    row_count = inner.shape[0]
-    ext_rows = jnp.pad(inner, ((CONV - 1, 0), (0, 0)))
-    conv_sum = tap_bias[None, :] + jnp.zeros(inner.shape, F32)
-    for tap_idx in range(CONV):
-        shifted = ext_rows[CONV - 1 - tap_idx : CONV - 1 - tap_idx + row_count]
-        conv_sum = (
-            conv_sum
-            + tap_weights[:, tap_idx][None, :]
-            * shifted
-            * (position >= tap_idx).astype(F32)[:, None]
+def attention_kernel(most, at_k, opened_ref, position_ref, context, probs, sums):
+    s, size = lax.axis_index("seq"), lax.axis_size("seq")
+    first = (HEADS * s + size - 1) // size
+    last = (HEADS * (s + 1) + size - 1) // size
+    pack = position_ref.shape[0]
+    at = 4 * HEAD
+    in_ref = opened_ref.at[:, at_k : at_k + (4 + most) * HEAD]
+    rows = lax.broadcasted_iota(jnp.int32, (pack, pack), 0)
+    columns = lax.broadcasted_iota(jnp.int32, (pack, pack), 1)
+    visible = (columns <= rows) & (columns >= rows - position_ref[...])
+    for h in range(most):
+        low = (first + h) // (HEADS // KV_HEADS) <= s
+        q = in_ref[:, at + h * HEAD : at + (h + 1) * HEAD]
+        key = jnp.where(low, in_ref[:, :HEAD], in_ref[:, HEAD : 2 * HEAD])
+        value = jnp.where(low, in_ref[:, 2 * HEAD : 3 * HEAD], in_ref[:, 3 * HEAD : 4 * HEAD])
+        masked = jnp.where(visible, dot(q, key, 1, 1) * 0.125, -1e30)
+        terms = jnp.exp(masked - jnp.max(masked, axis=1, keepdims=True))
+        prob = terms / jnp.sum(terms, axis=1, keepdims=True)
+        probs[h] = prob
+        out = dot(prob.astype(BF), value, 1, 0)
+        context[:, h * HEAD : (h + 1) * HEAD] = jnp.where(first + h < last, out, 0.0)
+    held = context[...]
+    sums[...] = row_sums(held * held)
+
+
+def attention(opened, at_k, position, most, micro):
+    rows, wide = opened.shape
+    pack = rows // micro
+    return pl.pallas_call(
+        partial(attention_kernel, most, at_k),
+        grid=(micro,),
+        out_shape=[
+            SHAPE((rows, most * HEAD), F32),
+            SHAPE((micro, most, pack, pack), F32),
+            SHAPE((8, rows), F32),
+        ],
+        in_specs=[
+            pl.BlockSpec((pack, wide), lambda m: (m, 0)),
+            pl.BlockSpec((pack, 1), lambda m: (m, 0)),
+        ],
+        out_specs=[
+            pl.BlockSpec((pack, most * HEAD), lambda m: (m, 0)),
+            pl.BlockSpec((None, most, pack, pack), lambda m: (m, 0, 0, 0)),
+            pl.BlockSpec((8, pack), lambda m: (0, m)),
+        ],
+        compiler_params=pltpu.CompilerParams(vmem_limit_bytes=VMEM_BYTES),
+        name="attention",
+    )(opened, position)
+
+
+def sum_slots(slots, send, recv):
+    here, row = lax.axis_index("seq"), lax.axis_index("fsdp")
+    copies = [
+        remote(slots.at[here], slots.at[here], send.at[k], recv.at[k], peer)
+        for k, peer in enumerate(pack_peers(slots.shape[0]))
+    ]
+    for copy in copies:
+        copy.start()
+    for copy in copies:
+        copy.wait()
+    total = slots[0].astype(F32)
+    for i in range(1, slots.shape[0]):
+        total = total + slots[i].astype(F32)
+    return total
+
+
+def taps_of(inner, position, taps, bias):
+    shifted = [inner]
+    for k in range(1, CONV):
+        shifted.append(jnp.where(position >= k, pltpu.roll(inner, k, axis=0), 0.0))
+    conv = bias
+    for k in range(CONV):
+        conv = conv + taps[k : k + 1] * shifted[k]
+    return conv, shifted
+
+
+def ssm_open_kernel(
+    size, micro, opened_ref, position_ref, taps, bias, w_x, w_dt, dt_bias, u_ref, lin_ref, proj_ref, bc_ref, slots, send, recv
+):
+    meet(pack_peers(size))
+    steps = opened_ref.shape[0] // micro
+    for m in range(micro):
+        rows = pl.ds(m * steps, steps)
+        for low, high in spans_of(w_x.shape[1], LANES):
+            inner = opened_ref[rows, low:high].astype(F32)
+            conv, _ = taps_of(inner, position_ref[rows], taps[:, low:high], bias[:, low:high])
+            u_ref[rows, low:high] = conv * sigmoid(conv)
+    slots[lax.axis_index("seq")] = dot(w_x[...], u_ref[...].astype(BF), 1, 1).astype(BF)
+    proj = sum_slots(slots, send, recv).astype(BF)
+    proj_ref[...] = proj
+    bc_ref[...] = proj[: 2 * STATE]
+    lin_ref[...] = dot(proj[2 * STATE :], w_dt[...], 0, 0) + dt_bias[...]
+
+
+def ssm_open(opened, position, taps, bias, w_x, w_dt, dt_bias, micro, collective_id):
+    size = lax.axis_size("seq")
+    rows = opened.shape[0]
+    wide, channels = w_x.shape
+    dma = pltpu.SemaphoreType.DMA((size - 1,))
+    return pl.pallas_call(
+        partial(ssm_open_kernel, size, micro),
+        out_shape=[
+            SHAPE((rows, channels), F32),
+            SHAPE((rows, channels), F32),
+            SHAPE((wide, rows), BF),
+            SHAPE((2 * STATE, rows), BF),
+        ],
+        in_specs=[VMEM] * 7,
+        out_specs=[VMEM] * 4,
+        scratch_shapes=[pltpu.VMEM((size, wide, rows), BF), dma, dma],
+        compiler_params=pltpu.CompilerParams(
+            collective_id=collective_id, has_side_effects=True, vmem_limit_bytes=VMEM_BYTES
+        ),
+        name="ssm_open",
+    )(opened, position, taps, bias, w_x, w_dt, dt_bias)
+
+
+def ssm_close_kernel(
+    size, micro, count, *refs
+):
+    dlin_ref, db_ref, dc_ref, du_ref, opened_ref, position_ref, taps, bias, w_x, w_dt = refs[:10]
+    helds, (dproj_ref, dinner_ref, sums_ref) = refs[10 : 10 + count], refs[10 + count : 13 + count]
+    gots = refs[13 + count : 13 + 2 * count]
+    slots, total, send, recv, own_sem, held_send, held_recv = refs[13 + 2 * count :]
+    meet(pack_peers(size))
+    here = lax.axis_index("seq")
+    place = lax.broadcasted_iota(jnp.int32, (STATE, STATE), 0)
+    eye = (place == lax.broadcasted_iota(jnp.int32, (STATE, STATE), 1)).astype(F32)
+    for i, ref in enumerate((db_ref, dc_ref)):
+        turned = lax.dot_general(
+            eye,
+            ref[...],
+            (((1,), (1,)), ((), ())),
+            precision=lax.Precision.HIGHEST,
+            preferred_element_type=F32,
         )
-    return jax.nn.silu(conv_sum)
-
-
-def gate_mix(core, inner_u, skip_d, gate_z):
-    return (core + skip_d[None, :] * inner_u) * jax.nn.silu(gate_z)
-
-
-def swiglu(gate_proj, up_proj):
-    return jax.nn.silu(gate_proj) * up_proj
+        slots[here, i * STATE : (i + 1) * STATE] = turned.astype(BF)
+    slots[here, 2 * STATE :] = dot(w_dt[...], dlin_ref[...], 1, 1).astype(BF)
+    dproj = sum_slots(slots, send, recv).astype(BF)
+    copies = []
+    for i, (held, got) in enumerate(zip(helds, gots)):
+        copies += start_deal(
+            held, got, size, own_sem.at[i], held_send, held_recv, i * (size - 1)
+        )
+    dproj_ref[...] = dproj
+    steps = opened_ref.shape[0] // micro
+    total[...] = du_ref[...] + dot(dproj, w_x[...], 0, 0)
+    for low, high in spans_of(w_x.shape[1], LANES):
+        lines = [jnp.zeros((1, high - low), F32) for _ in range(CONV + 1)]
+        for m in range(micro):
+            rows = pl.ds(m * steps, steps)
+            inner = opened_ref[rows, low:high].astype(F32)
+            position = position_ref[rows]
+            tap = taps[:, low:high]
+            conv, shifted = taps_of(inner, position, tap, bias[:, low:high])
+            sig = sigmoid(conv)
+            d_conv = total[rows, low:high] * (sig * (1.0 + conv * (1.0 - sig)))
+            d_inner = tap[0:1] * d_conv
+            for k in range(CONV):
+                lines[k] = lines[k] + jnp.sum(d_conv * shifted[k], axis=0, keepdims=True)
+                if k:
+                    masked = jnp.where(position >= k, d_conv, 0.0)
+                    d_inner = d_inner + tap[k : k + 1] * pltpu.roll(masked, steps - k, axis=0)
+            lines[CONV] = lines[CONV] + jnp.sum(d_conv, axis=0, keepdims=True)
+            dinner_ref[rows, low:high] = d_inner.astype(BF)
+        sums_ref[:, low:high] = jnp.concatenate(
+            lines + [jnp.zeros((8 - CONV - 1, high - low), F32)], axis=0
+        )
+    for copy in copies:
+        copy.wait()
+
+
+def ssm_close(dlin, db, dc, du, opened, position, taps, bias, w_x, w_dt, helds, micro, collective_id):
+    size = lax.axis_size("seq")
+    rows = opened.shape[0]
+    wide, channels = w_x.shape
+    dma = pltpu.SemaphoreType.DMA((size - 1,))
+    return pl.pallas_call(
+        partial(ssm_close_kernel, size, micro, len(helds)),
+        out_shape=[
+            SHAPE((wide, rows), BF),
+            SHAPE((rows, channels), BF),
+            SHAPE((8, channels), F32),
+        ]
+        + [SHAPE(held.shape, held.dtype) for held in helds],
+        in_specs=[VMEM] * 10 + [HBM] * len(helds),
+        out_specs=[VMEM] * 3 + [HBM] * len(helds),
+        scratch_shapes=[
+            pltpu.VMEM((size, wide, rows), BF),
+            pltpu.VMEM((rows, channels), F32),
+            dma,
+            dma,
+        ]
+        + deal_sems(size, max(1, len(helds))),
+        compiler_params=pltpu.CompilerParams(
+            collective_id=collective_id, has_side_effects=True, vmem_limit_bytes=VMEM_BYTES
+        ),
+        name="ssm_close",
+    )(dlin, db, dc, du, opened, position, taps, bias, w_x, w_dt, *helds)
+
+
+def branch_back_kernel(size, *refs):
+    dmix, w_att, w_ssm, context, ssm_out, core, u, gate_ref = refs[:8]
+    scale_att, scale_ssm, gain_att, gain_ssm, live, skip = refs[8:14]
+    d_context, d_core, d_gate, d_gain_att, d_gain_ssm, d_skip = refs[14:20]
+    t_att, t_ssm, slots, send, recv = refs[20:-1]
+    w_att = joined(w_att, refs[-1])
+    meet(pack_peers(size))
+    place = lax.broadcasted_iota(jnp.int32, (8, LANES), 0)
+    kinds = (
+        (w_att, context, scale_att, gain_att, d_gain_att, t_att),
+        (w_ssm, ssm_out, scale_ssm, gain_ssm, d_gain_ssm, t_ssm),
+    )
+    sums = []
+    for w, value, scale, gain, d_gain, t in kinds:
+        total = None
+        for low, high in spans_of(w.shape[0], 2 * LANES):
+            grad = 0.5 * dot(dmix[...], w[low:high, :], 1, 1)
+            held = value[:, low:high]
+            d_gain[:, low:high] = jnp.sum(grad * held * scale[:, :1], axis=0, keepdims=True)
+            scaled = grad * gain[:, low:high]
+            t[:, low:high] = scaled
+            term = row_sums(scaled * held)
+            total = term if total is None else total + term
+        sums.append(total)
+    rows8 = lax.broadcasted_iota(jnp.int32, sums[0].shape, 0)
+    slots[lax.axis_index("seq")] = jnp.where(rows8 == 0, sums[0], sums[1])
+    total = sum_slots(slots, send, recv)
+    columns = [
+        lax.dot_general(
+            total,
+            (place == kind).astype(F32),
+            (((0,), (0,)), ((), ())),
+            precision=lax.Precision.HIGHEST,
+            preferred_element_type=F32,
+        )
+        for kind in range(2)
+    ]
+    scale = scale_att[:, :1]
+    inward = scale * scale * scale * (columns[0][:, :1] / ATT)
+    d_context[...] = ((t_att[...] * scale - context[...] * inward) * live[...]).astype(BF)
+    scale = scale_ssm[:, :1]
+    inward = scale * scale * scale * (columns[1][:, :1] / INNER)
+    for low, high in spans_of(w_ssm.shape[0], 2 * LANES):
+        at = slice(low, high)
+        d_out = t_ssm[:, at] * scale - ssm_out[:, at] * inward
+        gate = gate_ref[:, at].astype(F32)
+        sig = sigmoid(gate)
+        silu = gate * sig
+        held = d_out * silu
+        d_core[:, at] = held
+        d_skip[:, at] = jnp.sum(held * u[:, at], axis=0, keepdims=True)
+        mixed = core[:, at] + skip[:, at] * u[:, at]
+        d_gate[:, at] = (d_out * mixed * (sig * (1.0 + gate - silu))).astype(BF)
+
+
+def branch_back(
+    dmix, w_att, w_ssm, context, ssm_out, core, u, gate_z, scales, gains, live, skip, collective_id
+):
+    size = lax.axis_size("seq")
+    rows, wide, channels = dmix.shape[0], w_att.shape[1], w_ssm.shape[0]
+    dma = pltpu.SemaphoreType.DMA((size - 1,))
+    return pl.pallas_call(
+        partial(branch_back_kernel, size),
+        out_shape=[
+            SHAPE((rows, wide), BF),
+            SHAPE((rows, channels), F32),
+            SHAPE((rows, channels), BF),
+            SHAPE((1, wide), F32),
+            SHAPE((1, channels), F32),
+            SHAPE((1, channels), F32),
+        ],
+        in_specs=[VMEM] * 14,
+        out_specs=[VMEM] * 6,
+        scratch_shapes=[
+            pltpu.VMEM((rows, wide), F32),
+            pltpu.VMEM((rows, channels), F32),
+            pltpu.VMEM((size, 8, rows), F32),
+            dma,
+            dma,
+        ]
+        + [pltpu.VMEM((wide, D), BF)],
+        compiler_params=pltpu.CompilerParams(
+            collective_id=collective_id, has_side_effects=True, vmem_limit_bytes=VMEM_BYTES
+        ),
+        name="branch_back",
+    )(dmix, w_att, w_ssm, context, ssm_out, core, u, gate_z, *scales, *gains, live, skip)
+
+
+def close_kernel(size, tok, micro, rest, d_inner, w, x_ref, gain, d_hidden, dx, d_gain, sent, got, send, recv):
+    here, row = lax.axis_index("seq"), lax.axis_index("fsdp")
+    meet(pack_peers(size))
+
+    def copy_of(k):
+        return remote(
+            sent.at[k], got.at[k], send.at[k], recv.at[k], (lax.rem(here + k + 1, size), row)
+        )
+
+    def block(k, carry):
+        d = lax.rem(here + k + 1, size)
+        spots = [block_rows(size, tok, m, d) for m in range(micro)]
+        rows = jnp.concatenate([d_inner[spot] for spot in spots])
+        held = jnp.concatenate([rest[spot] for spot in spots])
+        for low, high in spans_of(D):
+            part = held[:, low:high].astype(F32) + dot(rows, w[low:high, :], 1, 1)
+            sent[k, :, low:high] = part.astype(BF)
+
+        @pl.when(k < size - 1)
+        def _():
+            copy_of(k).start()
+
+        return carry
+
+    lax.fori_loop(0, size, block, 0)
+    for k in range(size - 1):
+        copy_of(k).wait()
+    gain_sum = jnp.zeros((1, D), F32)
+    for m in range(micro):
+        rows = pl.ds(m * tok, tok)
+        d_in = sent[size - 1, rows].astype(F32)
+        for k in range(size - 1):
+            d_in = d_in + got[k, rows].astype(F32)
+        whole = x_ref[rows].astype(F32)
+        scale = lax.rsqrt(jnp.mean(whole * whole, axis=-1, keepdims=True) + EPS)
+        normal = whole * scale
+        gain_sum = gain_sum + jnp.sum(d_in * normal, axis=0, keepdims=True)
+        scaled = d_in * gain[...]
+        inward = jnp.mean(scaled * normal, axis=-1, keepdims=True)
+        dx[rows] = (d_hidden[rows] + scale * (scaled - normal * inward)).astype(BF)
+    d_gain[...] = gain_sum
+
+
+def close_rows(rest, d_inner, w, x_own, gain, d_hidden, micro, collective_id):
+    size = lax.axis_size("seq")
+    own = x_own.shape[0]
+    dma = pltpu.SemaphoreType.DMA((size - 1,))
+    return pl.pallas_call(
+        partial(close_kernel, size, own // micro, micro),
+        out_shape=[SHAPE((own, D), BF), SHAPE((1, D), F32)],
+        in_specs=[VMEM] * 6,
+        out_specs=[VMEM] * 2,
+        scratch_shapes=[
+            pltpu.VMEM((size, own, D), BF),
+            pltpu.VMEM((size - 1, own, D), BF),
+            dma,
+            dma,
+        ],
+        compiler_params=pltpu.CompilerParams(
+            collective_id=collective_id, has_side_effects=True, vmem_limit_bytes=VMEM_BYTES
+        ),
+        name="close_rows",
+    )(rest, d_inner, w, x_own, gain, d_hidden)
 
 
 def squares(row_vals):
@@ -845,7 +1305,8 @@
         if fill:
             whole = jnp.pad(whole.reshape(N, rows, wide), ((0, 0), (0, fill), (0, 0)))
             whole = whole.reshape(N * (rows + fill), wide)
-        return lax.psum_scatter(whole, "fsdp", scatter_dimension=0, tiled=True)[:rows]
+        whole = lax.psum_scatter(whole, "fsdp", scatter_dimension=0, tiled=True)
+        return lax.optimization_barrier(whole)[:rows]
 
     def part(shard, axis, chunks, wide):
         shape = shard.shape
@@ -914,285 +1375,212 @@
     )[0]
 
     w_att_pad = jnp.pad(w_att_cols, ((0, width), (0, 0)))
-    w_att_part = (
-        seq_deal(jnp.stack([w_att_pad[h * HEAD : h * HEAD + width] for h in first_heads[:S]]))
-        .transpose(1, 0, 2)
-        .reshape(width, D)
-    )
-
-    w_x_part = jnp.pad(w_small_part[:, :PROJ], ((0, 0), (0, PROJ_PAD - PROJ)))
-    w_dt_part = w_small_part[:, PROJ : PROJ + DT_RANK]
+    w_att_blocks = jnp.stack([w_att_pad[h * HEAD : h * HEAD + width] for h in first_heads[:S]])
+
+    w_x_turned = w_small_part[:, :PROJ].T
+    w_x_turned = jnp.pad(
+        jnp.concatenate([w_x_turned[DT_RANK:], w_x_turned[:DT_RANK]], axis=0),
+        ((0, PROJ_PAD - PROJ), (0, 0)),
+    )
+    w_dt_turned = jnp.pad(
+        w_small_part[:, PROJ : PROJ + DT_RANK].T, ((0, PROJ_PAD - PROJ), (0, 0))
+    )
     small_par = w_small_part[:, PROJ + DT_RANK : PROJ + DT_RANK + CONV + 3 + STATE].astype(F32)
-    conv_w = small_par[:, :CONV]
-    conv_b = small_par[:, CONV]
-    dt_bias = small_par[:, CONV + 1]
-    skip_d = small_par[:, CONV + 2]
-    decay_a = -jnp.exp(small_par[:, CONV + 3 :])
-    rates = decay_a.T
-    gain_att_part = span(jnp.pad(gain_att, (0, width)), 0, q_start, width)
-    gain_ssm_part = part(gain_ssm, 0, N, ch // N)
-
-    def to_pack(block):
-        return seq_gather(block).reshape(pack, block.shape[-1])
-
-    def to_own(partial_rows):
-        return seq_scatter(partial_rows.reshape(S, tok, partial_rows.shape[-1]))
-
-    def opening(m):
-        x_pack = x_rows[m * pack : (m + 1) * pack].astype(F32)
-        normed_low = rms_scale(x_pack, gain_in).astype(BF)
-        return normed_low, dot(normed_low, w_in, 1, 0).astype(BF)
-
-    def first_half(m, normed_low, opened):
-        segment, position = seq_layout(lengths[m, 0], pack)
-        visible = (segment[:, None] == segment[None, :]) & (position[None, :] <= position[:, None])
-        q = opened[:, at_q:].reshape(pack, most, HEAD)
-        kv = opened[:, at_k:at_q].reshape(pack, 4, HEAD)
-        pick_low = in_low[None, :, None]
-        keys = jnp.where(pick_low, kv[:, 0:1], kv[:, 1:2])
-        values = jnp.where(pick_low, kv[:, 2:3], kv[:, 3:4])
-        scores = jnp.einsum("thd,uhd->htu", q, keys, preferred_element_type=F32) * 0.125
-        masked = jnp.where(visible, scores, -1e30)
-        row_top = jnp.max(masked, axis=-1, keepdims=True)
-        exp_terms = jnp.exp(masked - row_top)
-        row_total = jnp.sum(exp_terms, axis=-1, keepdims=True)
-        probs = exp_terms / row_total
-        context = (
-            jnp.einsum("htu,uhd->thd", probs.astype(BF), values, preferred_element_type=F32)
-        ).reshape(pack, width) * live
-        inner = opened[:, :ch].astype(F32)
-        gate_z = opened[:, ch : 2 * ch].astype(F32)
-        inner_u, conv_back = jax.vjp(partial(conv_act, position), inner, conv_w, conv_b)
-        u_low = inner_u.astype(BF)
-        projected = seq_sum(dot(w_x_part, u_low, 0, 1).astype(BF)).astype(BF)
-        dt_in = projected[:DT_RANK]
-        in_b = projected[DT_RANK : DT_RANK + STATE].astype(F32)
-        out_c = projected[DT_RANK + STATE : PROJ].astype(F32)
-        dt_lin = dot(dt_in, w_dt_part, 0, 1) + dt_bias[None, :]
-        step_dt = jax.nn.softplus(dt_lin)
-        dtm = jnp.where((position > 0)[:, None], step_dt, 1e30)
-        dtu = step_dt * inner_u
-        b_wide = jnp.broadcast_to(in_b.T[:, :, None], (pack, STATE, LANES))
-        c_wide = jnp.broadcast_to(out_c.T[:, :, None], (pack, STATE, LANES))
-        core = scan_forward(dtm, dtu, b_wide, c_wide, rates)
-        ssm_out, gate_back = jax.vjp(gate_mix, core, inner_u, skip_d, gate_z)
-        row_sums = jnp.stack(
-            [jnp.sum(context * context, axis=1), jnp.sum(ssm_out * ssm_out, axis=1)]
-        )
-        return dict(
-            position=position,
-            normed=normed_low,
-            q=q,
-            keys=keys,
-            values=values,
-            probs=probs,
-            context=context,
-            inner_u=inner_u,
-            conv_back=conv_back,
-            u=u_low,
-            dt_in=dt_in,
-            dt_lin=dt_lin,
-            step_dt=step_dt,
-            scan=(dtm, dtu, b_wide, c_wide),
-            ssm_out=ssm_out,
-            gate_back=gate_back,
-            row_sums=row_sums,
-        )
-
-    def second_half(h):
-        context, ssm_out = h["context"], h["ssm_out"]
-        scale_att, scale_ssm, dmix_low = h["scale_att"], h["scale_ssm"], h["dmix"]
-        d_att = 0.5 * dot(dmix_low, w_att_part, 1, 1) * live
-        d_ssm = lax.optimization_barrier(0.5 * dot(dmix_low, w_out_part, 1, 1))
-        d_gain_att = jnp.sum(d_att * context * scale_att, axis=0)
-        d_gain_ssm = jnp.sum(d_ssm * ssm_out * scale_ssm, axis=0)
-        t_att = d_att * gain_att_part
-        t_ssm = d_ssm * gain_ssm_part
-        back_sums = seq_sum(
-            jnp.stack([jnp.sum(t_att * context, axis=1), jnp.sum(t_ssm * ssm_out, axis=1)])
-        )
-        d_context = (
-            t_att * scale_att - context * scale_att**3 * (back_sums[0] / ATT)[:, None]
-        ) * live
-        d_ssm_out = t_ssm * scale_ssm - ssm_out * scale_ssm**3 * (back_sums[1] / INNER)[:, None]
-        d_core, d_u_gate, d_skip, d_gate_z = h["gate_back"](d_ssm_out)
-        h.update(
-            d_core=d_core,
-            d_u_gate=d_u_gate,
-            d_skip=d_skip,
-            d_gate_z=d_gate_z,
-            d_context=d_context.astype(BF),
-            gains=(d_gain_att, d_gain_ssm),
-        )
-
-    def attention_half(h):
-        probs, keys, values, q = h["probs"], h["keys"], h["values"], h["q"]
-        dctx_low = h["d_context"].reshape(pack, most, HEAD)
-        d_values = jnp.einsum(
-            "htu,thd->uhd", probs.astype(BF), dctx_low, preferred_element_type=F32
-        )
-        d_probs = jnp.einsum("thd,uhd->htu", dctx_low, values, preferred_element_type=F32)
-        dscore_low = (
-            probs * (d_probs - jnp.sum(probs * d_probs, axis=-1, keepdims=True))
-        ).astype(BF)
-        d_q = jnp.einsum("htu,uhd->thd", dscore_low, keys, preferred_element_type=F32) * 0.125
-        d_keys = jnp.einsum("htu,thd->uhd", dscore_low, q, preferred_element_type=F32) * 0.125
-        pick_low = in_low[None, :, None]
-
-        def kv_sum(d_heads):
-            return [
-                jnp.sum(jnp.where(pick_low, d_heads, 0.0), axis=1),
-                jnp.sum(jnp.where(pick_low, 0.0, d_heads), axis=1),
-            ]
-
-        d_rest = jnp.concatenate(
-            [h["d_gate_z"]]
-            + kv_sum(d_keys)
-            + kv_sum(d_values)
-            + [d_q.reshape(pack, width), jnp.zeros((pack, cols), F32)],
-            axis=1,
-        ).astype(BF)
-        h.update(d_rest=d_rest, d_normed=dot(d_rest, gathered_in[:, ch:in_wide], 1, 1))
-
-    def third_half(h):
-        dtm, dtu, b_wide, c_wide = h["scan"]
-        ddtu, ddt, d_rates, d_in_b, d_out_c = scan_backward(
-            dtm, dtu, h["d_core"], b_wide, c_wide, rates
-        )
-        d_lin = (ddt + ddtu * h["inner_u"]) * jax.nn.sigmoid(h["dt_lin"])
-        d_dt_bias = jnp.sum(d_lin, axis=0)
-        ddt_low = d_lin.astype(BF)
-        dproj = jnp.concatenate(
-            [
-                dot(w_dt_part, ddt_low, 0, 1),
-                d_in_b.T,
-                d_out_c.T,
-                jnp.zeros((PROJ_PAD - PROJ, pack), F32),
-            ],
-            axis=0,
-        )
-        dproj_low = seq_sum(dproj.astype(BF)).astype(BF)
-        d_inner_u = h["d_u_gate"] + ddtu * h["step_dt"] + dot(dproj_low, w_x_part, 0, 1)
-        d_inner, d_conv_w, d_conv_b = h["conv_back"](d_inner_u)
-        d_inner_low = d_inner.astype(BF)
-        small = [d_conv_w, d_conv_b[:, None], d_dt_bias[:, None], h["d_skip"][:, None]]
-        small_grad = jnp.concatenate(small + [d_rates.T * decay_a], axis=1)
-        h.update(ddt=ddt_low, dproj=dproj_low, d_inner=d_inner_low, small=small_grad)
-
-    def last_half(h):
-        d_normed = to_own(h["d_normed"] + dot(h["d_inner"], w_in[:, :ch], 1, 1))
-        _, norm_back = jax.vjp(rms_scale, h["x_mine"], gain_in)
-        d_x_norm, d_gain_in = norm_back(d_normed)
-        h.update(d_gain_in=d_gain_in, dx=(h["d_hidden"] + d_x_norm).astype(BF))
-
-    def both(name, axis=0):
-        return jnp.concatenate([one[name] for one in halves], axis=axis)
-
-    def hold(names, *extra):
-        held = [[one[name] for name in names] for one in halves]
-        held, extra = lax.optimization_barrier((held, extra))
-        for one, values in zip(halves, held):
-            one.update(zip(names, values))
-        return extra
-
-    def by_shard(whole):
-        return whole.astype(BF).reshape(N, whole.shape[0] // N, whole.shape[1])
-
-    opened = [opening(m) for m in range(micro)]
+    small_lines = small_par.T
+    taps = jnp.pad(small_lines[:CONV], ((0, 8 - CONV), (0, 0)))
+    conv_b, dt_bias, skip = [small_lines[CONV + i][None] for i in range(3)]
+    rates = -jnp.exp(small_lines[CONV + 3 :])
+    gain_att_part = span(jnp.pad(gain_att, (0, width)), 0, q_start, width)[None]
+    gain_ssm_part = part(gain_ssm, 0, N, ch // N)[None]
+
+    position = jax.vmap(lambda one: seq_layout(one, pack)[1])(lengths[:, 0])
+    position = position.reshape(micro * pack, 1)
+
+    normed_low = rms_scale(x_rows.astype(F32), gain_in).astype(BF)
+    opened = dot(normed_low, w_in, 1, 0).astype(BF)
     opened, gu_part, down_part = lax.optimization_barrier(
         (opened, gu_part, part(w_down, 0, 1, ffw))
     )
     w_gu, w_down_part = gather(gu_part), gather(down_part)
-    halves = [first_half(m, *opened[m]) for m in range(micro)]
-    sums = jnp.concatenate([one["row_sums"] for one in halves], axis=1)
+    gate_z = opened[:, ch : 2 * ch]
+    u, lin, projected, bc = ssm_open(
+        opened, position, taps, conv_b, w_x_turned, w_dt_turned, dt_bias, micro, 7
+    )
+    q = opened[:, at_q:].reshape(micro, pack, most, HEAD)
+    kv = opened[:, at_k:at_q].reshape(micro, pack, 4, HEAD)
+    pick_low = in_low[None, None, :, None]
+    keys = jnp.where(pick_low, kv[:, :, 0:1], kv[:, :, 1:2])
+    values = jnp.where(pick_low, kv[:, :, 2:3], kv[:, :, 3:4])
+    context, probs, att_sums = attention(opened, at_k, position, most, micro)
+    bc = jnp.broadcast_to(bc.T[:, :, None], (micro * pack, 2 * STATE, LANES))
+    core, ssm_out, ssm_sums, w_att_part = scan_forward(
+        u, lin, bc, rates, position, opened, skip, w_att_blocks, micro, 11
+    )
+    sums = jnp.stack([att_sums[0], ssm_sums[0]])
     att_low, ssm_low, scale_att, scale_ssm, hidden, mixer_out, ffn_low = mixer_rows(
-        [one["context"] for one in halves],
-        [one["ssm_out"] for one in halves],
+        context,
+        ssm_out,
         jnp.pad(sums, ((0, 6), (0, 0))),
         x_own,
-        (gain_att_part[None], gain_ssm_part[None], gain_ffn[None]),
+        (gain_att_part, gain_ssm_part, gain_ffn[None]),
         w_att_part,
         w_out_part,
+        micro,
         4,
     )
     act_low, dgu_low, down_parts, d_hidden, d_gain_ffn, dmix_low = ffn_rows(
         ffn_low, cot_rows, hidden, cot_own, gain_ffn[None], w_gu, w_down_part, micro, 5
     )
+
     gu_whole = dot(ffn_low, dgu_low, 0, 0).astype(BF)
+    act_low, gu_whole = lax.optimization_barrier((act_low, gu_whole))
+    r_gu = scatter(gu_whole)
     down_whole = dot(act_low, cot_rows, 0, 0).astype(BF)
-    dmix_low, gu_whole, down_whole = lax.optimization_barrier((dmix_low, gu_whole, down_whole))
-    for m, half in enumerate(halves):
-        rows = slice(m * pack, (m + 1) * pack)
-        mine = slice(m * tok, (m + 1) * tok)
-        half.update(
-            scale_att=scale_att[rows, :1],
-            scale_ssm=scale_ssm[rows, :1],
-            dmix=dmix_low[rows],
-            x_mine=x_own[mine].astype(F32),
-            d_hidden=d_hidden[mine],
-        )
-    r_gu, r_down = scatter(gu_whole), scatter(down_whole)
-    for half in halves:
-        second_half(half)
+    dmix_low, down_whole = lax.optimization_barrier((dmix_low, down_whole))
+    r_down = scatter(down_whole)
+    d_context, d_core, d_gate_z, d_gain_att, d_gain_ssm, d_skip = branch_back(
+        dmix_low,
+        w_att_part,
+        w_out_part,
+        context,
+        ssm_out,
+        core,
+        u,
+        gate_z,
+        (scale_att, scale_ssm),
+        (gain_att_part, gain_ssm_part),
+        live,
+        skip,
+        8,
+    )
     ssm_whole = (0.5 * dot(ssm_low, dmix_low, 0, 0)).astype(BF)
     g_att_rows = (0.5 * dot(att_low, dmix_low, 0, 0)).astype(BF)
-    g_att_blocks = seq_deal(g_att_rows.reshape(width, S, cols).transpose(1, 0, 2))
-    g_att_whole = jnp.concatenate(
-        [g_att_blocks[i, : head_counts[i] * HEAD] for i in range(S)], axis=0
-    )
-    for half in halves:
-        attention_half(half)
-    halves[0]["d_rest"], r_gu = lax.optimization_barrier((halves[0]["d_rest"], r_gu))
-    rest_whole = dot(both("normed"), both("d_rest"), 0, 0).astype(BF)
-    rest_whole = lax.dynamic_update_slice(rest_whole, g_att_whole, (0, at_att - ch))
-    r_down, ssm_whole, rest_whole = hold(["d_core"], r_down, ssm_whole, rest_whole)
-    r_ssm, r_rest = scatter(ssm_whole), scatter(rest_whole)
-    for half in halves:
-        third_half(half)
-    r_ssm, r_rest = hold(["d_inner"], r_ssm, r_rest)
-    for half in halves:
-        last_half(half)
-    small_whole = jnp.concatenate(
-        [
-            dot(both("u"), both("dproj", 1), 0, 1)[:, :PROJ],
-            dot(both("ddt"), both("dt_in", 1), 0, 1),
-            halves[0]["small"] + halves[1]["small"],
-            jnp.zeros((ch, 1), F32),
+    att_blocks = g_att_rows.reshape(width, S, cols).transpose(1, 0, 2)
+    dctx_low = d_context.reshape(micro, pack, most, HEAD)
+    d_values = jnp.einsum(
+        "mhtu,mthd->muhd", probs.astype(BF), dctx_low, preferred_element_type=F32
+    )
+    d_probs = jnp.einsum("mthd,muhd->mhtu", dctx_low, values, preferred_element_type=F32)
+    dscore_low = (
+        probs * (d_probs - jnp.sum(probs * d_probs, axis=-1, keepdims=True))
+    ).astype(BF)
+    d_q = jnp.einsum("mhtu,muhd->mthd", dscore_low, keys, preferred_element_type=F32) * 0.125
+    d_keys = jnp.einsum("mhtu,mthd->muhd", dscore_low, q, preferred_element_type=F32) * 0.125
+
+    def kv_sum(d_heads):
+        return [
+            jnp.sum(jnp.where(pick_low, d_heads, 0.0), axis=2),
+            jnp.sum(jnp.where(pick_low, 0.0, d_heads), axis=2),
+        ]
+
+    d_rest = jnp.concatenate(
+        [d_gate_z]
+        + [
+            one.astype(BF).reshape(micro * pack, -1)
+            for one in kv_sum(d_keys) + kv_sum(d_values) + [d_q]
         ],
         axis=1,
     )
-    last_whole = dot(both("normed"), both("d_inner"), 0, 0).astype(BF)
-    (small_whole, last_whole) = hold(["dx"], small_whole, last_whole)
-    r_small, r_last = scatter(small_whole), scatter(last_whole)
-    input_grads = give(both("dx"), send_hot, land_hot)
-
+    rest_rows = dot(d_rest, gathered_in[:, ch:at_att], 1, 1).astype(BF)
+    rest_whole = dot(normed_low, d_rest, 0, 0).astype(BF)
+    d_core, r_gu, ssm_whole, rest_whole, rest_rows = lax.optimization_barrier(
+        (d_core, r_gu, ssm_whole, rest_whole, rest_rows)
+    )
+    r_ssm, r_rest = scatter(ssm_whole), scatter(rest_whole)
     per = N // S
-    gate_take = np.concatenate(
-        [np.arange(ff_piece) + ffw * i for i in range(per)]
-    )
+    gate_take = np.concatenate([np.arange(ff_piece) + ffw * i for i in range(per)])
     half_wide = -(-per * ff_piece // LANES) * LANES
     moves = []
     for d in range(S):
         for i in range(2):
             table = gate_take[None] + d * per * ffw + i * ffs
             moves.append((0, None, 0, d, placed(table, i * half_wide, 2 * half_wide)))
-        moves.append((1, None, 1, d, run_table([d * cols], cols)))
-        moves.append((2, None, 2, d, run_table([d * cols], cols)))
-    blocks = regroup(
-        [r_gu, r_ssm, r_down],
-        [
-            jax.ShapeDtypeStruct((S, rows_d, 2 * half_wide), BF),
-            jax.ShapeDtypeStruct((S, r_ssm.shape[0], cols), BF),
-            jax.ShapeDtypeStruct((S, r_down.shape[0], cols), BF),
-        ],
-        moves,
-        s,
-    )
-    blocks, _ = lax.optimization_barrier((list(blocks), last_whole))
-    gu_got, ssm_got, down_got, ffn_got = deal(blocks + [down_parts], 0)
+    (gu_blocks,) = regroup([r_gu], [SHAPE((S, rows_d, 2 * half_wide), BF)], moves, s)
+    d_u, d_lin, d_dt_bias, d_rates, d_in_b, d_out_c, (ffn_got, gu_got, g_att_blocks) = (
+        scan_backward(
+            d_core, u, lin, bc, rates, position, skip, [down_parts, gu_blocks, att_blocks], micro, 0
+        )
+    )
     ffn_out = jnp.sum(ffn_got.astype(F32), axis=0)
     result = hidden + ffn_out
     outputs = give(result.astype(BF), send_hot, land_hot)
+    g_att_whole = jnp.concatenate(
+        [g_att_blocks[i, : head_counts[i] * HEAD] for i in range(S)], axis=0
+    )
+    moves = []
+    for d in range(S):
+        moves.append((0, None, 0, d, run_table([d * cols], cols)))
+        moves.append((1, None, 1, d, run_table([d * cols], cols)))
+    row_blocks = regroup(
+        [r_ssm, r_down],
+        [SHAPE((S, r_ssm.shape[0], cols), BF), SHAPE((S, r_down.shape[0], cols), BF)],
+        moves,
+        s,
+    )
+    dproj_low, d_inner, conv_sums = ssm_close(
+        d_lin,
+        d_in_b,
+        d_out_c,
+        d_u,
+        opened,
+        position,
+        taps,
+        conv_b,
+        w_x_turned,
+        w_dt_turned,
+        [],
+        micro,
+        9,
+    )
+    g_x = dot(u.astype(BF), dproj_low, 0, 1)
+    small_whole = jnp.concatenate(
+        [
+            g_x[:, 2 * STATE : PROJ],
+            g_x[:, : 2 * STATE],
+            dot(d_lin, projected[2 * STATE : PROJ], 0, 1),
+            conv_sums[: CONV + 1].T,
+            d_dt_bias[:, None],
+            d_skip[0][:, None],
+            (d_rates * rates).T,
+            jnp.zeros((ch, 1), F32),
+        ],
+        axis=1,
+    ).astype(BF)
+    small_whole = jnp.pad(
+        small_whole.reshape(N, chw, small_wide), ((0, 0), (0, rows_d - chw), (0, 0))
+    ).reshape(N * rows_d, small_wide)
+    last_whole = jnp.concatenate(
+        [dot(normed_low, d_inner, 0, 0).astype(BF), g_att_whole, small_whole], axis=1
+    )
+    d_inner, last_whole, r_rest = lax.optimization_barrier((d_inner, last_whole, r_rest))
+    r_last = scatter(last_whole)
+    dx, d_gain_in = close_rows(
+        rest_rows, d_inner, gathered_in[:, :ch], x_own, gain_in[None], d_hidden, micro, 10
+    )
+
+    att_at = lax.dynamic_update_slice_in_dim(
+        jnp.zeros((ATT + width,), F32), d_gain_att[0] * live[0], q_start, 0
+    )[:ATT]
+    ssm_at = lax.dynamic_update_index_in_dim(
+        jnp.zeros((N, S, ch_piece), F32), d_gain_ssm[0].reshape(N, -1)[:, :ch_piece], s, 1
+    ).reshape(INNER)
+    stats = jnp.stack(
+        [
+            squares(x_own.astype(F32)),
+            jnp.sum(sums[0]),
+            jnp.sum(sums[1]),
+            squares(mixer_out),
+            squares(ffn_out),
+            squares(result),
+        ]
+    )
+    ends = np.cumsum([0, D, ATT, INNER, D, 6])
+    line = jnp.concatenate([d_gain_in[0], att_at, ssm_at, d_gain_ffn[0], stats])
+    line = jnp.pad(line, (0, -line.shape[0] % 1024)).reshape(-1, LANES)
+    row_blocks, dx = lax.optimization_barrier((list(row_blocks), dx))
+    ssm_got, down_got = deal(row_blocks, 1)
+    input_grads = give(dx, send_hot, land_hot)
+    ssm_got, r_last = lax.optimization_barrier((ssm_got, r_last))
     out_ssm = ssm_got[:, :ch_piece].reshape(S * ch_piece, cols).astype(F32)
     out_down = down_got[:, :ff_piece].reshape(S * ff_piece, cols).astype(F32)
     ff_mine, mix_mine = ff // S, 2 * INNER // S
@@ -1240,8 +1628,9 @@
     in_blocks = regroup(
         [r_last, r_rest], [jax.ShapeDtypeStruct((S, rows_d, wide), BF)], moves, s
     )[0]
-    in_got, small_got = deal(
-        [in_blocks, jnp.broadcast_to(r_small, (S,) + r_small.shape)], 1
+    r_small = r_last[:chw, ch + cols :]
+    in_got, small_got, sums_all = last_exchange(
+        [in_blocks, jnp.broadcast_to(r_small, (S,) + r_small.shape)], line, 2
     )
     moves = []
     at = np.arange(mix_mine)
@@ -1261,39 +1650,13 @@
         moves,
         s,
     )
-    g_att = r_rest[:, at_att - ch :].astype(F32)
+    g_att = r_last[:, ch : ch + cols].astype(F32)
     small_all = small_got[:, :ch_piece].reshape(S * ch_piece, small_wide).astype(F32)
     out_x = span(small_all[:, :PROJ], 1, s * (PROJ // S), PROJ // S)
     out_dt = span(small_all[:, PROJ : PROJ + DT_RANK], 1, s * (DT_RANK // S), DT_RANK // S)
     out_small = small_all[:, PROJ + DT_RANK : PROJ + DT_RANK + CONV + 3 + STATE]
 
-    def added(values):
-        total = values[0]
-        for further in values[1:]:
-            total = total + further
-        return total
-
-    d_gain_att, d_gain_ssm = [added([one["gains"][i] for one in halves]) for i in range(2)]
-    att_at = lax.dynamic_update_slice_in_dim(
-        jnp.zeros((ATT + width,), F32), d_gain_att * live[0], q_start, 0
-    )[:ATT]
-    ssm_at = lax.dynamic_update_index_in_dim(
-        jnp.zeros((N, S, ch_piece), F32), d_gain_ssm.reshape(N, -1)[:, :ch_piece], s, 1
-    ).reshape(INNER)
-    d_gain_in = added([one["d_gain_in"] for one in halves])
-    stats = jnp.stack(
-        [
-            squares(x_own.astype(F32)),
-            jnp.sum(sums[0]),
-            jnp.sum(sums[1]),
-            squares(mixer_out),
-            squares(ffn_out),
-            squares(result),
-        ]
-    )
-    ends = np.cumsum([0, D, ATT, INNER, D, 6])
-    line = jnp.concatenate([d_gain_in, att_at, ssm_at, d_gain_ffn[0], stats])
-    sums = total_of(jnp.pad(line, (0, -line.shape[0] % 1024)).reshape(-1, LANES), 2).reshape(-1)
+    sums = sums_all.reshape(-1)
     g_gain_in, g_gain_att, g_gain_ssm, g_gain_ffn, stat_sum = [
         sums[a:b] for a, b in zip(ends[:-1], ends[1:])
     ]

time: 1050 us -> 856 us (0.82)
  local copies, waits for them, and re-layouts: 207 us -> 107 us
  Pallas kernels: 435 us -> 533 us
  other arithmetic: 79.5 us -> 24.5 us
  matrix products: 148 us -> 97.3 us
  waiting for transfers between devices: 91.6 us -> 48 us
  starting transfers between devices: 56.2 us -> 21.9 us
    pallas_call x5 -> x8, Pallas kernels: 108 us -> 264 us  [the longest x1 71.9 us: scan_backward(): pl.pallas_call(partial(scan_back_kernel, size, len(helds), groups), grid=...]
    pallas_call x2 -> x1, Pallas kernels: 80.3 us -> 17.4 us  [deal(): pl.pallas_call(partial(deal_kernel, count, size), out_shape=[jax.ShapeDty...]
    dot_general x34 -> x18, matrix products: 134 us -> 81.7 us  [dot(): lax.dot_general(left_op, right_op, (((left_dim,), (right_dim,)), ((), ())...]
    dynamic_update_slice x26 -> x0, local copies, waits for them, and re-layouts: 41 us -> none  [the longest x1 17.4 us: local(): lax.dynamic_update_slice(rest_whole, g_att_whole, (0, at_att - ch))]
    ppermute x30 -> x0, starting transfers between devices: 35.3 us -> none  [swap(): return lax.ppermute(array, 'seq', [(i, i ^ k) for i in range(size)])]
    another operation x42 -> x6, local copies, waits for them, and re-layouts: 32.8 us -> 3.27 us  [the longest x1 0.92 us: scan_backward(): db[:, 0].reshape(rows, STATE)]
    reduce_sum x13 -> x3, other arithmetic: 27.8 us -> 1.39 us  [the longest x1 1.36 us: local(): jnp.sum(sums[0])]
    ppermute x30 -> x0, waiting for transfers between devices: 16.4 us -> none  [swap(): return lax.ppermute(array, 'seq', [(i, i ^ k) for i in range(size)])]
  transfers between devices with their start and end apart: 44 -> 13, of which waited for: 7 -> 3; matrix products, arithmetic and copies ran while one was open for 36% -> 22% of each run, Pallas kernels for 31% -> 47%
where the time goes in v3:
time: 856 us; the launch traced here: 848 us
  Pallas kernels  533 us (62%)
  local copies, waits for them, and re-layouts  107 us (12%)
  matrix products  97.3 us (11%)
  waiting for transfers between devices  48 us (6%)
  other arithmetic  24.5 us (3%)
  starting transfers between devices  21.9 us (3%)
  between operations  15.9 us (2%)
    pallas_call x1, Pallas kernels, ffn_rows(): pl.pallas_call(partial(ffn_kernel, size, tok, micro), out_shape=[shape((r...  88 us
    dot_general x18, matrix products, dot(): lax.dot_general(left_op, right_op, (((left_dim,), (right_dim,)), ((), ())...  81.7 us
    pallas_call x1, Pallas kernels, scan_backward(): pl.pallas_call(partial(scan_back_kernel, size, len(helds), groups), grid=...  71.9 us
    pallas_call x1, Pallas kernels, mixer_rows(): pl.pallas_call(partial(mixer_kernel, size, tok, micro), out_shape=[shape(...  70.9 us
    pallas_call x2, Pallas kernels, gather_rows(): pl.pallas_call(partial(gather_kernel, size, tok, micro, count), out_shape...  63.3 us
    pallas_call x1, Pallas kernels, close_rows(): pl.pallas_call(partial(close_kernel, size, own // micro, micro), out_shap...  35.8 us
    pallas_call x1, Pallas kernels, last_exchange(): pl.pallas_call(partial(last_kernel, sizes, count), out_shape=[SHAPE(a.sha...  33.2 us
    pallas_call x1, Pallas kernels, scan_forward(): pl.pallas_call(partial(scan_kernel, size, lane_groups(channels)), grid=(m...  32.7 us
  transfers between devices with their start and end apart: 13, of which 3 were waited for; matrix products, arithmetic and copies ran while one was open for 22% of the time, Pallas kernels for 47%

profile of v3, /device:TPU:0, one launch (start us, length us, event | category | flops | bytes accessed | tf_op | source)
XLA Modules:
  0.0 848.2 jit_solution(3884790962083765974)
XLA Ops:
  16.1 6.1 regroup.7
  26.9 6.3 all-to-all-start.1
  34.4 32.0 %all-to-all-done.1 = bf16[8,24,1600]{2,1,0:T(8,128)(2,1)S(1)} async-done(((bf16[8,24,1600]{2,1,0:T(8,128)(2,1)}), bf16[8,24,1600]{2,1,0:T(8,128)(2,1)S(1)}, u32[]{:S(2)}, u32[]{:S(2)}) %all-to-all-start.1) | async-done | bytes 614432 | tf_op jit(solution)/shard_map/all_to_all | solution.py:119
  76.2 31.9 %gather_rows.2 = bf16[768,1600]{1,0:T(8,128)(2,1)} custom-call(bf16[192,1600]{1,0:T(8,128)(2,1)} %get-tuple-element.287.refs_0_.refs_3_.x_ref), custom_call_target="tpu_custom_call" | custom-call | tf_op jit(solution)/shard_map/gather_rows/pallas_call | solution.py:662
  109.3 31.4 %gather_rows.3.refs_1_ = bf16[768,1600]{1,0:T(8,128)(2,1)} custom-call(bf16[192,1600]{1,0:T(8,128)(2,1)} %convolution_convert_fusion.10.refs_0_.refs_3_), custom_call_target="tpu_custom_call" | custom-call | tf_op jit(solution)/shard_map/gather_rows/pallas_call | solution.py:662
  140.7 8.2 all-gather.5.cloned.1.call-done
  152.3 6.2 regroup.8
  161.2 11.1 %fusion.7.opened_ref.refs_5_.refs_4_ = bf16[768,2496]{1,0:T(8,128)(2,1)} fusion(bf16[1600,3152]{1,0:T(8,128)(2,1)} %all-gather.5.cloned.1.call-done, bf16[768,1600]{1,0:T(8,128)(2,1)S(1)} %copy-done.6, f32[1600]{0:T(1024)S(1)} %copy-done.26, f32[768]{0:T(1024)S(1)} %add_rsqrt_fusion), kind=kOutput, calls=%fused_computation.16 | convolution fusion | flops 6141001728 | bytes 14492928 | tf_op jit(solution)/shard_map/dot_general | solution.py:31
  183.6 18.2 %attention.1 = (f32[768,448]{1,0:T(8,128)}, f32[2,7,384,384]{3,2,1,0:T(8,128)}, f32[8,768]{1,0:T(8,128)}) custom-call(bf16[768,2496]{1,0:T(8,128)(2,1)} %fusion.7.opened_ref.refs_5_.refs_4_, s32[768,1]{1,0:T(8,128)} %bitcast.156), custom_call_target="tpu_custom_call" | custom-call | tf_op jit(solution)/shard_map/attention/pallas_call | solution.py:928
  203.7 21.5 %ssm_open.1 = (f32[768,896]{1,0:T(8,128)}, f32[768,896]{1,0:T(8,128)}, bf16[144,768]{1,0:T(8,128)(2,1)}, bf16[32,768]{1,0:T(8,128)(2,1)}) custom-call(bf16[768,2496]{1,0:T(8,128)(2,1)} %fusion.7.opened_ref.refs_5_.refs_4_, s32[768,1]{1,0:T(8,128)} %bitcast.157, f32[8,896]{1,0:T(8,128)} %slice_select_fusion.taps.refs_6_, ...), custom_call_target="tpu_custom_call" | custom-call | tf_op jit(solution)/shard_map/ssm_open/pallas_call | solution.py:999
  230.5 6.8 broadcast_in_dim.135.refs_2_.refs_3_
  237.3 32.7 %scan_forward.1 = (f32[768,896]{1,0:T(8,128)}, f32[768,896]{1,0:T(8,128)}, f32[8,768]{1,0:T(8,128)}, bf16[4,448,400]{2,1,0:T(8,128)(2,1)}) custom-call(f32[768,896]{1,0:T(8,128)} %get-tuple-element.107.refs_0_.refs_6_.refs_1_, f32[768,896]{1,0:T(8,128)} %get-tuple-element.108.refs_1_.refs_2_, bf16[768,32,128]{2,1,0:T(8,128)(2,1)} %broadcast_in_dim.135.refs_2_.refs_3_, ...), custom_call_target="tpu_custom_call" | custom-call | tf_op jit(solution)/shard_map/scan_forward/pallas_call | solution.py:279
  273.3 70.9 %mixer_rows.1 = (bf16[768,448]{1,0:T(8,128)(2,1)}, bf16[768,896]{1,0:T(8,128)(2,1)}, f32[768,128]{1,0:T(8,128)}, f32[768,128]{1,0:T(8,128)}, f32[192,1600]{1,0:T...) custom-call(f32[768,448]{1,0:T(8,128)} %get-tuple-element.106.refs_0_.refs_3_, ...), custom_call_target="tpu_custom_call" | custom-call | tf_op jit(solution)/shard_map/mixer_rows/pallas_call | solution.py:760
  344.3 88.0 %ffn_rows.1 = (bf16[768,1408]{1,0:T(8,128)(2,1)}, bf16[768,2816]{1,0:T(8,128)(2,1)}, bf16[4,192,1600]{2,1,0:T(8,128)(2,1)}, f32[192,1600]{1,0:T(8,128)}, f32[1,1600]{1,0:T(1,128)}, /*index=5*/bf16[768,1600]{1,0:T(8,128)(2,1)}) custom-call(bf16[768,1600]{1,0:T(8,128)(2,1)} %get-tuple-element.116.refs_0_, bf16[768,1600]{1,0:T(8,128)(2,1)} %gather_rows.3.refs_1_, ...), custom_call_target="tpu_custom_call" | custom-call | tf_op jit(solution)/shard_map/ffn_rows/pallas_call | solution.py:871
  432.3 12.5 %convolution_convert_fusion = bf16[1600,2816]{1,0:T(8,128)(2,1)} fusion(bf16[768,1600]{1,0:T(8,128)(2,1)S(1)} %copy-done.8, bf16[768,2816]{1,0:T(8,128)(2,1)} %get-tuple-element.122), kind=kOutput, calls=%fused_computation | convolution fusion | flops 6925107200 | bytes 15794176 | tf_op jit(solution)/shard_map/dot_general | solution.py:31
  454.2 8.7 %convolution_convert_fusion.2 = bf16[1408,1600]{1,0:T(8,128)(2,1)} fusion(bf16[768,1408]{1,0:T(8,128)(2,1)} %get-tuple-element.123, bf16[768,1600]{1,0:T(8,128)(2,1)} %gather_rows.3.refs_1_), kind=kOutput, calls=%fused_computation.6 | convolution fusion | flops 3462553600 | bytes 9125888 | tf_op jit(solution)/shard_map/dot_general | solution.py:31
  462.9 27.3 %branch_back.1 = (bf16[768,448]{1,0:T(8,128)(2,1)}, f32[768,896]{1,0:T(8,128)}, bf16[768,896]{1,0:T(8,128)(2,1)}, f32[1,448]{1,0:T(1,128)}, f32[1,896]{1,0:T(1,128)}, /*index=5*/f32[1,896]{1,0:T(1,128)}) custom-call(bf16[768,1600]{1,0:T(8,128)(2,1)} %get-tuple-element.124.refs_0_, bf16[4,448,400]{2,1,0:T(8,128)(2,1)} %get-tuple-element.113.refs_7_.refs_1_, ...), custom_call_target="tpu_custom_call" | custom-call | tf_op jit(solution)/shard_map/branch_back/pallas_call | solution.py:1162
  493.8 5.1 multiply_reduce_fusion
  512.2 4.6 select_reduce_fusion
  517.5 5.6 concatenate.43
  523.1 5.6 multiply_convert_fusion.1
  528.8 9.6 %convolution_convert_fusion.1 = bf16[1600,1600]{1,0:T(8,128)(2,1)} fusion(bf16[768,1600]{1,0:T(8,128)(2,1)} %concatenate.43, bf16[768,1600]{1,0:T(8,128)(2,1)} %gather_rows.2, f32[1600]{0:T(1024)S(1)} %copy-done.26, f32[768]{0:T(1024)S(1)} %add_rsqrt_fusion), kind=kOutput, calls=%fused_computation.5 | convolution fusion | flops 3939635200 | bytes 10044672 | tf_op jit(solution)/shard_map/dot_general | solution.py:31
  538.4 9.3 %fusion.12.rest = bf16[768,1600]{1,0:T(8,128)(2,1)} fusion(bf16[768,1600]{1,0:T(8,128)(2,1)} %concatenate.43, bf16[1600,3152]{1,0:T(8,128)(2,1)} %all-gather.5.cloned.1.call-done), kind=kOutput, calls=%fused_computation.20 | convolution fusion | flops 3933388800 | bytes 10338304 | tf_op jit(solution)/shard_map/dot_general | solution.py:31
  561.9 71.9 %scan_backward.1 = (f32[768,896]{1,0:T(8,128)}, bf16[768,896]{1,0:T(8,128)(2,1)}, f32[2,1,896]{2,1,0:T(1,128)}, f32[2,16,896]{2,1,0:T(8,128)}, f32[2,8,6144]{2,1...) custom-call(f32[768,896]{1,0:T(8,128)} %get-tuple-element.134.refs_0, ...), custom_call_target="tpu_custom_call" | custom-call | tf_op jit(solution)/shard_map/scan_backward/pallas_call | solution.py:417
  637.9 23.4 %ssm_close.1 = (bf16[144,768]{1,0:T(8,128)(2,1)}, bf16[768,896]{1,0:T(8,128)(2,1)}, f32[8,896]{1,0:T(8,128)}) custom-call(bf16[768,896]{1,0:T(8,128)(2,1)} %get-tuple-element.144.refs_0_, f32[768,16]{1,0:T(8,128)} %reshape_squeeze.9.refs_1_, f32[768,16]{1,0:T(8,128)} %reshape_squeeze.10.refs_2_, f32[768,896]{1,0:T(8,128)} %get-tuple-element.147.refs_3_, ...), custom_call_target="tpu_custom_call" | custom-call | tf_op jit(solution)/shard_map/ssm_close/pallas_call | solution.py:1077
  673.1 4.5 convolution_convert_fusion.3
  677.6 8.2 concatenate.53
  701.4 5.7 reduce-scatter.12.cloned.1.call-done.refs_0_
  710.0 35.8 %close_rows.1 = (bf16[192,1600]{1,0:T(8,128)(2,1)}, f32[1,1600]{1,0:T(1,128)}) custom-call(bf16[768,1600]{1,0:T(8,128)(2,1)} %fusion.12.rest, bf16[768,896]{1,0:T(8,128)(2,1)} %get-tuple-element.157.d_inner, bf16[1600,896]{1,0:T(8,128)(2,1)} %slice.217.w, bf16[192,1600]{1,0:T(8,128)(2,1)} %get-tuple-element.287.refs_0_.refs_3_.x_ref, ...), custom_call_target="tpu_custom_call" | custom-call | tf_op jit(solution)/shard_map/close_rows/pallas_call | solution.py:1236
  748.1 7.5 all-to-all-start.3
  761.7 17.4 %deal.1 = (bf16[4,112,400]{2,1,0:T(8,128)(2,1)}, bf16[4,176,400]{2,1,0:T(8,128)(2,1)}) custom-call(bf16[4,112,400]{2,1,0:T(8,128)(2,1)} %get-tuple-element.161.refs_0_, bf16[4,176,400]{2,1,0:T(8,128)(2,1)} %get-tuple-element.162.refs_1_), custom_call_target="tpu_custom_call" | custom-call | bytes 1024 | tf_op jit(solution)/shard_map/deal/pallas_call | solution.py:559
  795.0 33.2 %last_exchange.1 = (bf16[4,200,1072]{2,1,0:T(8,128)(2,1)}, bf16[4,112,256]{2,1,0:T(8,128)(2,1)}, f32[64,128]{1,0:T(8,128)}) custom-call(bf16[4,200,1072]{2,1,0:T(8,128)(2,1)} %regroup.11.refs_0_, bf16[4,112,256]{2,1,0:T(8,128)(2,1)} %broadcast_in_dim.152.refs_1_, f32[64,128]{1,0:T(8,128)} %pad_bitcast_fusion.3.refs_2_), custom_call_target="tpu_custom_call" | custom-call | tf_op jit(solution)/shard_map/last_exchange/pallas_call | solution.py:610
  (305 shorter events, 165.0 us)
Async XLA Ops:
  7.2 18.5 %copy-start = (bf16[2,96,1600]{2,1,0:T(8,128)(2,1)S(1)}, bf16[2,96,1600]{2,1,0:T(8,128)(2,1)}, u32[]{:S(2)}) copy-start(bf16[2,96,1600]{2,1,0:T(8,128)(2,1)} %param.72) | copy-start | bytes 1843204
  7.2 141.7 %all-gather.5.cloned.1.call-start = ((), (), s32[]{:S(2)}) async-start(), calls=%async_computation.9 | async-start | bytes 11520000 | tf_op jit(solution)/shard_map/all_gather | solution.py:1299
  24.6 8.6 %copy-start.14 = (bf16[2,96,1600]{2,1,0:T(8,128)(2,1)S(1)}, bf16[2,96,1600]{2,1,0:T(8,128)(2,1)}, u32[]{:S(2)}) copy-start(bf16[2,96,1600]{2,1,0:T(8,128)(2,1)} %param.73) | copy-start | bytes 1843204
  25.7 41.5 %copy-start.19 = (s32[192]{0:T(256)}, s32[192]{0:T(256)S(1)}, u32[]{:S(2)}) copy-start(s32[192]{0:T(256)S(1)} %multiply_add_fusion) | copy-start | bytes 2308
  25.7 46.4 %copy-start.11 = (bf16[400,1600]{1,0:T(8,128)(2,1)S(1)}, bf16[400,1600]{1,0:T(8,128)(2,1)}, u32[]{:S(2)}) copy-start(bf16[400,1600]{1,0:T(8,128)(2,1)} %param.85) | copy-start | bytes 3840004
  26.9 39.5 %all-to-all-start.1 = ((bf16[8,24,1600]{2,1,0:T(8,128)(2,1)}), bf16[8,24,1600]{2,1,0:T(8,128)(2,1)S(1)}, u32[]{:S(2)}, u32[]{:S(2)}) async-start(bf16[8,24,1600]{2,1,0:T(8,128)(2,1)} %bitcast.7), calls=%async_computation.1 | async-start | bytes 1277952 | tf_op jit(solution)/shard_map/all_to_all | solution.py:119
  67.2 40.9 %all-to-all-start = ((bf16[8,24,1600]{2,1,0:T(8,128)(2,1)}), bf16[8,24,1600]{2,1,0:T(8,128)(2,1)S(1)}, u32[]{:S(2)}, u32[]{:S(2)}) async-start(bf16[8,24,1600]{2,1,0:T(8,128)(2,1)} %bitcast.4), calls=%async_computation | async-start | bytes 1277952 | tf_op jit(solution)/shard_map/all_to_all | solution.py:119
  71.2 202.1 %all-gather.7.cloned.1.call-start = ((), (), s32[]{:S(2)}) async-start(), calls=%async_computation.10 | async-start | bytes 3354624 | tf_op jit(solution)/shard_map/all_gather | solution.py:1299
  72.1 36.0 %copy-start.22 = (s32[192]{0:T(256)}, s32[192]{0:T(256)S(1)}, u32[]{:S(2)}) copy-start(s32[192]{0:T(256)S(1)} %eq.91) | copy-start | bytes 2308
  108.1 41.1 %copy-start.9 = (bf16[688,1600]{1,0:T(8,128)(2,1)S(1)}, bf16[688,1600]{1,0:T(8,128)(2,1)}, u32[]{:S(2)}) copy-start(bf16[688,1600]{1,0:T(8,128)(2,1)} %param.89) | copy-start | bytes 6604804
  149.0 195.3 %all-gather.11.cloned.1.call-start = ((), (), s32[]{:S(2)}) async-start(), calls=%async_computation.12 | async-start | bytes 5271552 | tf_op jit(solution)/shard_map/all_gather | solution.py:1299
  152.3 8.2 copy-start.6
  161.2 11.8 %copy-start.32 = (s32[2,1,3]{2,1,0:T(1,128)S(1)}, s32[2,1,3]{2,1,0:T(1,128)}, u32[]{:S(2)}) copy-start(s32[2,1,3]{2,1,0:T(1,128)} %param.75) | copy-start | bytes 76
  161.2 13.3 %copy-start.39 = (s32[5]{0:T(128)S(1)}, s32[5]{0:T(128)}, u32[]{:S(2)}) copy-start(s32[5]{0:T(128)} %constant.197.clone) | copy-start | bytes 64
  161.2 14.6 %copy-start.21 = (f32[3200]{0:T(1024)S(1)}, f32[3200]{0:T(1024)}, u32[]{:S(2)}) copy-start(f32[3200]{0:T(1024)} %param.83) | copy-start | bytes 38404
  161.2 15.4 %copy-start.24 = (f32[1600]{0:T(1024)S(1)}, f32[1600]{0:T(1024)}, u32[]{:S(2)}) copy-start(f32[1600]{0:T(1024)} %param.86) | copy-start | bytes 19204
  161.2 16.0 %copy-start.25 = (f32[1600]{0:T(1024)S(1)}, f32[1600]{0:T(1024)}, u32[]{:S(2)}) copy-start(f32[1600]{0:T(1024)} %param.82) | copy-start | bytes 19204
  172.3 171.9 %all-gather.9.cloned.1.call-start = ((), (), s32[]{:S(2)}) async-start(), calls=%async_computation.11 | async-start | bytes 10137600 | tf_op jit(solution)/shard_map/all_gather | solution.py:1299
  172.9 374.8 %reduce-scatter.10.cloned.1.call-start = ((), (), s32[]{:S(2)}) async-start(), calls=%async_computation.13 | async-start | bytes 10137600 | tf_op jit(solution)/shard_map/reduce_scatter | solution.py:1308
  183.6 19.5 %copy-start.36 = (pred[8]{0:T(512)(128)(4,1)S(1)}, pred[8]{0:T(512)(128)(4,1)}, u32[]{:S(2)}) copy-start(pred[8]{0:T(512)(128)(4,1)} %constant.186.clone.1) | copy-start | bytes 28
  344.3 88.1 %copy-start.8 = (bf16[768,1600]{1,0:T(8,128)(2,1)S(1)}, bf16[768,1600]{1,0:T(8,128)(2,1)}, u32[]{:S(2)}) copy-start(bf16[768,1600]{1,0:T(8,128)(2,1)} %get-tuple-element.116.refs_0_) | copy-start | bytes 7372804
  444.9 240.9 %reduce-scatter.16.cloned.1.call-start = ((), (), s32[]{:S(2)}) async-start(), calls=%async_computation.16 | async-start | bytes 5990400
  547.7 153.6 %reduce-scatter.14.cloned.1.call-start = ((), (), s32[]{:S(2)}) async-start(), calls=%async_computation.15 | async-start | bytes 5271552 | tf_op jit(solution)/shard_map/reduce_scatter | solution.py:1308
  548.5 158.6 %reduce-scatter.12.cloned.1.call-start = ((), (), s32[]{:S(2)}) async-start(), calls=%async_computation.14 | async-start | bytes 3354624 | tf_op jit(solution)/shard_map/reduce_scatter | solution.py:1308
  549.2 239.5 %reduce-scatter.18.cloned.1.call-start = ((), (), s32[]{:S(2)}) async-start(), calls=%async_computation.17 | async-start | bytes 5990400
  637.9 23.4 %copy-start.2 = (f32[768,896]{1,0:T(8,128)S(1)}, f32[768,896]{1,0:T(8,128)}, u32[]{:S(2)}) copy-start(f32[768,896]{1,0:T(8,128)} %get-tuple-element.107.refs_0_.refs_6_.refs_1_) | copy-start | bytes 8257540
  689.4 58.7 %all-to-all-start.2 = ((bf16[8,24,1600]{2,1,0:T(8,128)(2,1)}), bf16[8,24,1600]{2,1,0:T(8,128)(2,1)S(1)}, u32[]{:S(2)}, u32[]{:S(2)}) async-start(bf16[8,24,1600]{2,1,0:T(8,128)(2,1)} %bitcast.171), calls=%async_computation.3 | async-start | bytes 1277952 | tf_op jit(solution)/shard_map/all_to_all | solution.py:119
  745.8 9.8 %copy-start.35 = (f32[1,448]{1,0:T(1,128)S(1)}, f32[1,448]{1,0:T(1,128)}, u32[]{:S(2)}) copy-start(f32[1,448]{1,0:T(1,128)} %get-tuple-element.168) | copy-start | bytes 5380
  748.1 12.3 %copy-start.20 = (s32[192]{0:T(256)S(1)}, s32[192]{0:T(256)}, u32[]{:S(2)}) copy-start(s32[192]{0:T(256)} %copy-done.19) | copy-start | bytes 2308
  748.1 38.4 %all-to-all-start.3 = ((bf16[8,24,1600]{2,1,0:T(8,128)(2,1)}), bf16[8,24,1600]{2,1,0:T(8,128)(2,1)}, u32[]{:S(2)}, u32[]{:S(2)}) async-start(bf16[8,24,1600]{2,1,0:T(8,128)(2,1)} %bitcast.169), calls=%async_computation.6 | async-start | bytes 1277952 | tf_op jit(solution)/shard_map/all_to_all | solution.py:119
  828.2 8.3 copy-start.15
  833.1 8.3 copy-start.1
  (25 other events, 85.3 us)
Sparse Core Ops, SparseCore 0:
  24.8 124.0 all-gather.4
  151.2 35.8 all-gather.6
  189.3 50.3 all-gather.10
  241.7 85.9 all-gather.8
  445.0 93.2 reduce-scatter.9
  547.9 58.8 reduce-scatter.15
  609.2 53.8 reduce-scatter.13
  665.5 41.5 reduce-scatter.11
  709.5 76.2 reduce-scatter.17

commit v4 on v3

--- a/solution.py
+++ b/solution.py
@@ -152,6 +152,104 @@
     return [(lax.rem(here + k, size), row) for k in range(1, size)]
 
 
+def block_rows(size, tok, m, d):
+    return pl.ds(pl.multiple_of((m * size + d) * tok, tok), tok)
+
+
+def flip(place, k):
+    return (place // 2 + k // 2) % 2 * 2 + (place % 2 + k % 2) % 2
+
+
+def crossing():
+    here, row = lax.axis_index("seq"), lax.axis_index("fsdp")
+    return here, (flip(here, 1), row), (flip(here, 2), row)
+
+
+class Relay:
+    def __init__(self, tok, own, whole, own_sem, send, recv):
+        here, one, two = crossing()
+        self.whole, self.tok, self.one, self.two = whole, tok, one, two
+        spots = [self.spot(m, here) for m in range(2)]
+        first, second = own.at[pl.ds(0, tok)], own.at[pl.ds(tok, tok)]
+        self.near = [
+            remote(first, spots[0], send.at[0], recv.at[0], one),
+            remote(second, spots[1], send.at[1], recv.at[1], two),
+            remote(second, spots[1], send.at[2], recv.at[2], one),
+            remote(first, spots[0], send.at[3], recv.at[3], two),
+        ]
+        self.far = [
+            remote(self.spot(0, one[0]), self.spot(0, one[0]), send.at[4], recv.at[4], two),
+            remote(self.spot(1, two[0]), self.spot(1, two[0]), send.at[5], recv.at[5], one),
+        ]
+        self.kept = [
+            pltpu.make_async_copy(source, spot, own_sem.at[m])
+            for m, (source, spot) in enumerate(zip((first, second), spots))
+        ]
+
+    def spot(self, m, d):
+        return self.whole.at[block_rows(4, self.tok, m, d)]
+
+    def start(self):
+        for copy in self.near + self.kept:
+            copy.start()
+
+    def pass_on(self):
+        for near, far in zip(self.near, self.far):
+            near.wait_recv()
+            far.start()
+
+    def finish(self):
+        for copy in self.near[:2]:
+            copy.wait_send()
+        for copy in self.near[2:] + self.far + self.kept:
+            copy.wait()
+
+
+class Gathering:
+    def __init__(self, tok, sent, got, send, recv):
+        here, one, two = crossing()
+        self.here, self.tok, self.sent, self.got = here, tok, sent, got
+        ways = [(0, 0, one), (0, 1, two), (1, 1, two), (2, 0, one), (1, 0, two), (2, 1, one)]
+        self.copies = [
+            remote(sent.at[k, pl.ds(m * tok, tok)], got.at[i], send.at[i], recv.at[i], way)
+            for i, (k, m, way) in enumerate(ways)
+        ]
+
+    def device(self, k):
+        return flip(self.here, 3 - k)
+
+    def send(self, k):
+        for i, block in enumerate((0, 0, 1, 2)):
+
+            @pl.when(k == block)
+            def _(i=i):
+                self.copies[i].start()
+
+    def add(self, k):
+        @pl.when(k == 3)
+        def _():
+            for i, (block, m) in enumerate(((1, 0), (2, 1))):
+                self.copies[i].wait_recv()
+                rows = pl.ds(m * self.tok, self.tok)
+                total = self.sent[block, rows].astype(F32) + self.got[i].astype(F32)
+                self.sent[block, rows] = total.astype(BF)
+                self.copies[4 + i].start()
+
+    def finish(self):
+        for copy in self.copies[:2]:
+            copy.wait_send()
+        for copy in self.copies[2:]:
+            copy.wait()
+
+    def total(self, m, own):
+        pair = (3, 4) if m == 0 else (2, 5)
+        return own + self.got[pair[0]].astype(F32) + self.got[pair[1]].astype(F32)
+
+
+def crossing_sems():
+    return [pltpu.SemaphoreType.DMA((6,))] * 2
+
+
 def start_deal(source, out, size, own_sem, send_sem, recv_sem, first=0, start=True):
     here, row = lax.axis_index("seq"), lax.axis_index("fsdp")
     copies = [pltpu.make_async_copy(source.at[here], out.at[here], own_sem)]
@@ -170,6 +268,41 @@
         for copy in copies:
             copy.start()
     return copies
+
+
+def start_half(source, out, size, first, own_sem, send_sem, recv_sem):
+    here, row = lax.axis_index("seq"), lax.axis_index("fsdp")
+    half = size // 2
+    own = pltpu.make_async_copy(source.at[lax.rem(here, half)], out.at[here], own_sem)
+    mine = (here >= first) & (here < first + half)
+
+    def copy_to(j):
+        return remote(
+            source.at[j], out.at[here], send_sem.at[j], recv_sem.at[here], (first + j, row)
+        )
+
+    pl.when(mine)(own.start)
+    for j in range(half):
+        pl.when(here != first + j)(lambda j=j: copy_to(j).start())
+
+    def wait():
+        pl.when(mine)(own.wait)
+        for j in range(half):
+            pl.when(here != first + j)(lambda j=j: copy_to(j).wait_send())
+
+        @pl.when(mine)
+        def _():
+            for k in range(1, size):
+                there = lax.rem(here + k, size)
+                remote(
+                    source.at[0], out.at[there], send_sem.at[0], recv_sem.at[there], (there, row)
+                ).wait_recv()
+
+    return wait
+
+
+def half_sems(size):
+    return [pltpu.SemaphoreType.DMA((n,)) for n in (1, size // 2, size)]
 
 
 def deal_sems(size, count=1):
@@ -469,6 +602,7 @@
 
 
 def regroup_kernel(plan, source_count, out_count, *refs):
+    here = lax.axis_index("seq")
     sources = refs[:source_count]
     maps = refs[source_count : len(refs) - out_count]
     outs = refs[len(refs) - out_count :]
@@ -478,7 +612,11 @@
         for source, which, low, high in terms:
             held = sources[source]
             held = held[..., low:high] if len(held.shape) == 2 else held[which[1], :, low:high]
-            wanted = maps[which[0]][:, at] - low
+            table = maps[which[0]]
+            wanted = table[0:1, at]
+            for i in range(1, table.shape[0]):
+                wanted = jnp.where(here == i, table[i : i + 1, at], wanted)
+            wanted = wanted - low
             places = lax.broadcasted_iota(jnp.int32, (high - low, wide), 0)
             hot = (places == wanted).astype(F32).astype(BF)
             term = dot(held, hot, 1, 0)
@@ -492,11 +630,11 @@
             ref[block, :, at] = total.astype(ref.dtype)
 
 
-def regroup(sources, outs, moves, here):
+def regroup(sources, outs, moves):
     plan, maps = [], []
     tables = []
     for source, from_block, out, block, table in moves:
-        maps.append(jnp.asarray(table)[here][None] if len(table) > 1 else jnp.asarray(table))
+        maps.append(jnp.asarray(table))
         tables.append((source, from_block, out, block, table))
     for out, shape in enumerate(outs):
         for block in range(shape.shape[0] if len(shape.shape) == 3 else 1):
@@ -540,10 +678,12 @@
     return out
 
 
-def deal_kernel(count, size, *refs):
-    sources, outs = refs[:count], refs[count : 2 * count]
-    own_sem, send_sem, recv_sem = refs[2 * count :]
+def deal_kernel(count, size, first, *refs):
+    sources, half_source = refs[:count], refs[count]
+    outs, half_out = refs[count + 1 : 2 * count + 1], refs[2 * count + 1]
+    own_sem, send_sem, recv_sem, half_own, half_send, half_recv = refs[2 * count + 2 :]
     meet(pack_peers(size))
+    wait = start_half(half_source, half_out, size, first, half_own.at[0], half_send, half_recv)
     copies = []
     for i, (source, out) in enumerate(zip(sources, outs)):
         copies += start_deal(
@@ -551,23 +691,22 @@
         )
     for copy in copies:
         copy.wait()
-
-
-def deal(arrays, collective_id):
+    wait()
+
+
+def deal(arrays, halves, first, collective_id):
     size, count = lax.axis_size("seq"), len(arrays)
-    hbm = pl.BlockSpec(memory_space=pl.ANY)
     return pl.pallas_call(
-        partial(deal_kernel, count, size),
-        out_shape=[jax.ShapeDtypeStruct(a.shape, a.dtype) for a in arrays],
-        in_specs=[hbm] * count,
-        out_specs=[hbm] * count,
-        scratch_shapes=deal_sems(size, count),
+        partial(deal_kernel, count, size, first),
+        out_shape=[SHAPE(a.shape, a.dtype) for a in arrays]
+        + [SHAPE((size,) + halves.shape[1:], halves.dtype)],
+        in_specs=[HBM] * (count + 1),
+        out_specs=[HBM] * (count + 1),
+        scratch_shapes=deal_sems(size, count) + half_sems(size),
         compiler_params=pltpu.CompilerParams(collective_id=collective_id, has_side_effects=True),
-        cost_estimate=pl.CostEstimate(
-            flops=0, bytes_accessed=1024, transcendentals=0
-        ),
+        cost_estimate=pl.CostEstimate(flops=0, bytes_accessed=1024, transcendentals=0),
         name="deal",
-    )(*arrays)
+    )(*arrays, halves)
 
 
 def spread(slots, me, devices, send, recv):
@@ -584,17 +723,18 @@
 
 
 def last_kernel(sizes, count, *refs):
-    sources, in_ref = refs[:count], refs[count]
-    outs, out_ref = refs[count + 1 : 2 * count + 1], refs[2 * count + 1]
-    one, two, send_one, recv_one, send_two, recv_two, own_sem, send_sem, recv_sem = refs[
-        2 * count + 2 :
-    ]
+    sources, half_source, in_ref = refs[:count], refs[count], refs[count + 1]
+    outs, half_out, out_ref = refs[count + 2 : 2 * count + 2], *refs[2 * count + 2 : 2 * count + 4]
+    refs = refs[2 * count + 4 :]
+    one, two, send_one, recv_one, send_two, recv_two, own_sem, send_sem, recv_sem = refs[:9]
+    half_own, half_send, half_recv = refs[9:]
     seq, fsdp = lax.axis_index("seq"), lax.axis_index("fsdp")
     across = [(lax.rem(seq + k, sizes[0]), fsdp) for k in range(1, sizes[0])]
     along = [(seq, lax.rem(fsdp + k, sizes[1])) for k in range(1, sizes[1])]
     meet(across + along)
     one[seq] = in_ref[...]
     two[fsdp] = spread(one, seq, across, send_one, recv_one)
+    wait = start_half(half_source, half_out, sizes[0], 0, half_own.at[0], half_send, half_recv)
     copies = []
     for i, (source, out) in enumerate(zip(sources, outs)):
         copies += start_deal(
@@ -603,75 +743,46 @@
     out_ref[...] = spread(two, fsdp, along, send_two, recv_two)
     for copy in copies:
         copy.wait()
-
-
-def last_exchange(arrays, block, collective_id):
+    wait()
+
+
+def last_exchange(arrays, halves, block, collective_id):
     sizes, count = (lax.axis_size("seq"), lax.axis_size("fsdp")), len(arrays)
     return pl.pallas_call(
         partial(last_kernel, sizes, count),
-        out_shape=[SHAPE(a.shape, a.dtype) for a in arrays] + [SHAPE(block.shape, block.dtype)],
-        in_specs=[HBM] * count + [VMEM],
-        out_specs=[HBM] * count + [VMEM],
+        out_shape=[SHAPE(a.shape, a.dtype) for a in arrays]
+        + [SHAPE((sizes[0],) + halves.shape[1:], halves.dtype), SHAPE(block.shape, block.dtype)],
+        in_specs=[HBM] * (count + 1) + [VMEM],
+        out_specs=[HBM] * (count + 1) + [VMEM],
         scratch_shapes=[pltpu.VMEM((n,) + block.shape, F32) for n in sizes]
         + [pltpu.SemaphoreType.DMA((n - 1,)) for n in sizes for _ in range(2)]
-        + deal_sems(sizes[0], count),
+        + deal_sems(sizes[0], count)
+        + half_sems(sizes[0]),
         compiler_params=pltpu.CompilerParams(collective_id=collective_id, has_side_effects=True),
+        cost_estimate=pl.CostEstimate(flops=0, bytes_accessed=1024, transcendentals=0),
         name="last_exchange",
-    )(*arrays, block)
-
-
-def block_rows(size, tok, m, d):
-    return pl.ds(pl.multiple_of((m * size + d) * tok, tok), tok)
-
-
-def spread_rows(size, tok, micro, own, whole, own_sem, send_sem, recv_sem, first):
-    here, row = lax.axis_index("seq"), lax.axis_index("fsdp")
-    copies = []
-    for m in range(micro):
-        source, target = own.at[pl.ds(m * tok, tok)], whole.at[block_rows(size, tok, m, here)]
-        for k in range(1, size):
-            at = first + m * (size - 1) + k - 1
-            there = (lax.rem(here + k, size), row)
-            copies.append(remote(source, target, send_sem.at[at], recv_sem.at[at], there))
-        at = first // (size - 1) + m
-        copies.append(pltpu.make_async_copy(source, target, own_sem.at[at]))
-    for copy in copies:
-        copy.start()
-    return copies
-
-
-def gather_kernel(size, tok, micro, count, *refs):
-    owns, wholes = refs[:count], refs[count : 2 * count]
-    own_sem, send_sem, recv_sem = refs[2 * count :]
+    )(*arrays, halves, block)
+
+
+def gather_kernel(size, tok, own, whole, own_sem, send, recv):
     meet(pack_peers(size))
-    copies = []
-    for i in range(count):
-        first = i * micro * (size - 1)
-        copies += spread_rows(
-            size, tok, micro, owns[i], wholes[i], own_sem, send_sem, recv_sem, first
-        )
-    for copy in copies:
-        copy.wait()
-
-
-def gather_rows(arrays, micro, collective_id):
-    size, count = lax.axis_size("seq"), len(arrays)
-    tok = arrays[0].shape[0] // micro
-    hbm = pl.BlockSpec(memory_space=pl.ANY)
-    links = count * micro * (size - 1)
+    relay = Relay(tok, own, whole, own_sem, send, recv)
+    relay.start()
+    relay.pass_on()
+    relay.finish()
+
+
+def gather_rows(own, micro, collective_id):
+    size, rows = lax.axis_size("seq"), own.shape[0]
     return pl.pallas_call(
-        partial(gather_kernel, size, tok, micro, count),
-        out_shape=[jax.ShapeDtypeStruct((a.shape[0] * size, a.shape[1]), a.dtype) for a in arrays],
-        in_specs=[hbm] * count,
-        out_specs=[hbm] * count,
-        scratch_shapes=[
-            pltpu.SemaphoreType.DMA((count * micro,)),
-            pltpu.SemaphoreType.DMA((links,)),
-            pltpu.SemaphoreType.DMA((links,)),
-        ],
+        partial(gather_kernel, size, rows // micro),
+        out_shape=SHAPE((rows * size, own.shape[1]), own.dtype),
+        in_specs=[HBM],
+        out_specs=HBM,
+        scratch_shapes=[pltpu.SemaphoreType.DMA((micro,))] + crossing_sems(),
         compiler_params=pltpu.CompilerParams(collective_id=collective_id, has_side_effects=True),
         name="gather_rows",
-    )(*arrays)
+    )(own)
 
 
 def spans_of(width, most=512):
@@ -726,28 +837,27 @@
             dot(left[0], w_att[:, low:high], 1, 0) + dot(left[1], w_ssm[:, low:high], 1, 0)
         )
 
-    copies = []
-    for k, peer in enumerate(peers):
+    gathering = Gathering(tok, sent, got, send, recv)
+    for k in range(3):
         for low, high in spans_of(D):
-            sent[k, :, low:high] = product(peer[0], low, high).astype(BF)
-        copies.append(remote(sent.at[k], got.at[k], send.at[k], recv.at[k], peer))
-        copies[-1].start()
+            sent[k, :, low:high] = product(gathering.device(k), low, high).astype(BF)
+        gathering.send(k)
+    gathering.add(3)
     for low, high in spans_of(D):
         mixer[:, low:high] = product(here, low, high)
-    for copy in copies:
-        copy.wait()
+    gathering.finish()
     for m in range(micro):
         rows = pl.ds(m * tok, tok)
-        out = mixer[rows]
-        for k in range(size - 1):
-            out = out + got[k, rows].astype(F32)
+        out = gathering.total(m, mixer[rows])
         mixer[rows] = out
         whole = x_ref[rows].astype(F32) + out
         hidden[rows] = whole
         scale = lax.rsqrt(jnp.mean(whole * whole, axis=-1, keepdims=True) + EPS)
         ffn_own[rows] = (whole * scale * gain_ffn[...]).astype(BF)
-    for copy in spread_rows(size, tok, micro, ffn_own, ffn, own_sem, ffn_send, ffn_recv, 0):
-        copy.wait()
+    relay = Relay(tok, ffn_own, ffn, own_sem, ffn_send, ffn_recv)
+    relay.start()
+    relay.pass_on()
+    relay.finish()
 
 
 def mixer_rows(context, ssm_out, sums, x_own, gains, w_att, w_ssm, micro, collective_id):
@@ -773,15 +883,13 @@
         scratch_shapes=[
             pltpu.VMEM((size,) + sums.shape, F32),
             pltpu.VMEM((size - 1, own, D), BF),
-            pltpu.VMEM((size - 1, own, D), BF),
+            pltpu.VMEM((6, tok, D), BF),
             pltpu.VMEM((own, D), BF),
             dma((size - 1,)),
             dma((size - 1,)),
-            dma((size - 1,)),
-            dma((size - 1,)),
+            *crossing_sems(),
             dma((micro,)),
-            dma((micro * (size - 1),)),
-            dma((micro * (size - 1),)),
+            *crossing_sems(),
             pltpu.VMEM((w_att.shape[1], D), BF),
         ],
         compiler_params=pltpu.CompilerParams(
@@ -799,14 +907,12 @@
     wide = w_down.shape[0]
     meet(pack_peers(size))
 
-    def copy_of(k):
-        return remote(
-            sent.at[k], got.at[k], send.at[k], recv.at[k], (lax.rem(here + k + 1, size), row)
-        )
+    gathering = Gathering(tok, sent, got, send, recv)
 
     def block(k, carry):
-        d = lax.rem(here + k + 1, size)
+        d = gathering.device(k)
         spots = [block_rows(size, tok, m, d) for m in range(micro)]
+        gathering.add(k)
         rows_in = jnp.concatenate([ffn[spot] for spot in spots])
         cots = jnp.concatenate([cot[spot] for spot in spots])
         for low, high in spans_of(wide):
@@ -827,25 +933,18 @@
         d_all = jnp.concatenate([dgu[spot] for spot in spots])
         for low, high in spans_of(D):
             sent[k, :, low:high] = dot(d_all, w_gu[low:high, :], 1, 1).astype(BF)
-
-        @pl.when(k < size - 1)
-        def _():
-            copy_of(k).start()
-
+        gathering.send(k)
         acts = jnp.concatenate([act[spot] for spot in spots])
         for low, high in spans_of(D):
             down[d, :, low:high] = dot(acts, w_down[:, low:high], 1, 0).astype(BF)
         return carry
 
     lax.fori_loop(0, size, block, 0)
-    for k in range(size - 1):
-        copy_of(k).wait()
+    gathering.finish()
     gain_sum = jnp.zeros((1, D), F32)
     for m in range(micro):
         rows = pl.ds(m * tok, tok)
-        d_in = sent[size - 1, rows].astype(F32)
-        for k in range(size - 1):
-            d_in = d_in + got[k, rows].astype(F32)
+        d_in = gathering.total(m, sent[size - 1, rows].astype(F32))
         whole = hidden[rows]
         scale = lax.rsqrt(jnp.mean(whole * whole, axis=-1, keepdims=True) + EPS)
         normal = whole * scale
@@ -856,8 +955,10 @@
         d_hidden[rows] = out
         dmix_own[rows] = out.astype(BF)
     d_gain[...] = gain_sum
-    for copy in spread_rows(size, tok, micro, dmix_own, dmix, own_sem, dmix_send, dmix_recv, 0):
-        copy.wait()
+    relay = Relay(tok, dmix_own, dmix, own_sem, dmix_send, dmix_recv)
+    relay.start()
+    relay.pass_on()
+    relay.finish()
 
 
 def ffn_rows(ffn, cot, hidden, cot_own, gain, w_gu, w_down, micro, collective_id):
@@ -882,13 +983,11 @@
         out_specs=[vmem] * 5 + [hbm],
         scratch_shapes=[
             pltpu.VMEM((size, own, D), BF),
-            pltpu.VMEM((size - 1, own, D), BF),
+            pltpu.VMEM((6, tok, D), BF),
             pltpu.VMEM((own, D), BF),
-            dma((size - 1,)),
-            dma((size - 1,)),
+            *crossing_sems(),
             dma((micro,)),
-            dma((micro * (size - 1),)),
-            dma((micro * (size - 1),)),
+            *crossing_sems(),
         ],
         compiler_params=pltpu.CompilerParams(
             collective_id=collective_id, has_side_effects=True, vmem_limit_bytes=VMEM_BYTES
@@ -1190,35 +1289,26 @@
     here, row = lax.axis_index("seq"), lax.axis_index("fsdp")
     meet(pack_peers(size))
 
-    def copy_of(k):
-        return remote(
-            sent.at[k], got.at[k], send.at[k], recv.at[k], (lax.rem(here + k + 1, size), row)
-        )
+    gathering = Gathering(tok, sent, got, send, recv)
 
     def block(k, carry):
-        d = lax.rem(here + k + 1, size)
+        d = gathering.device(k)
         spots = [block_rows(size, tok, m, d) for m in range(micro)]
+        gathering.add(k)
         rows = jnp.concatenate([d_inner[spot] for spot in spots])
         held = jnp.concatenate([rest[spot] for spot in spots])
         for low, high in spans_of(D):
             part = held[:, low:high].astype(F32) + dot(rows, w[low:high, :], 1, 1)
             sent[k, :, low:high] = part.astype(BF)
-
-        @pl.when(k < size - 1)
-        def _():
-            copy_of(k).start()
-
+        gathering.send(k)
         return carry
 
     lax.fori_loop(0, size, block, 0)
-    for k in range(size - 1):
-        copy_of(k).wait()
+    gathering.finish()
     gain_sum = jnp.zeros((1, D), F32)
     for m in range(micro):
         rows = pl.ds(m * tok, tok)
-        d_in = sent[size - 1, rows].astype(F32)
-        for k in range(size - 1):
-            d_in = d_in + got[k, rows].astype(F32)
+        d_in = gathering.total(m, sent[size - 1, rows].astype(F32))
         whole = x_ref[rows].astype(F32)
         scale = lax.rsqrt(jnp.mean(whole * whole, axis=-1, keepdims=True) + EPS)
         normal = whole * scale
@@ -1240,9 +1330,8 @@
         out_specs=[VMEM] * 2,
         scratch_shapes=[
             pltpu.VMEM((size, own, D), BF),
-            pltpu.VMEM((size - 1, own, D), BF),
-            dma,
-            dma,
+            pltpu.VMEM((6, own // micro, D), BF),
+            *crossing_sems(),
         ],
         compiler_params=pltpu.CompilerParams(
             collective_id=collective_id, has_side_effects=True, vmem_limit_bytes=VMEM_BYTES
@@ -1333,7 +1422,7 @@
     in_wide = at_att + cols
     mix_table = pieces_table(2 * N, INNER // N, ch_piece, chw)
     in_part = regroup(
-        [w_mix_in, jnp.pad(w_qkv, ((0, 0), (0, -w_qkv.shape[1] % LANES))), w_out_att],
+        [w_mix_in, w_qkv, w_out_att],
         [jax.ShapeDtypeStruct((rows_d, in_wide), BF)],
         [
             (0, None, 0, 0, placed(mix_table, 0, in_wide)),
@@ -1342,7 +1431,6 @@
             (2, None, 0, 0, placed(run_table([cols * i for i in range(S)], cols), at_att, in_wide)),
             (1, None, 0, 0, placed(run_table(q_starts, width), at_q, in_wide)),
         ],
-        s,
     )[0]
     small_part = part(
         jnp.concatenate([w_x, w_dt, w_small, jnp.zeros((w_x.shape[0], 1), BF)], axis=1), 0, 1, chw
@@ -1352,9 +1440,9 @@
         jnp.concatenate([in_part, jnp.pad(small_part, ((0, rows_d - chw), (0, 0)))], axis=1)
     )
     cot_own = bring(cotangent.reshape(micro * tok, D), send_hot, land_hot)
-    x_rows = gather_rows([x_own], micro, 3)[0]
+    x_rows = gather_rows(x_own, micro, 3)
     cot_own, x_rows = lax.optimization_barrier((cot_own, x_rows))
-    cot_rows = gather_rows([cot_own], micro, 6)[0]
+    cot_rows = gather_rows(cot_own, micro, 6)
     gathered_in, x_rows, cot_rows = lax.optimization_barrier((gathered_in, x_rows, cot_rows))
     out_piece, gathered_in = lax.optimization_barrier((part(w_out_ssm, 0, 1, chw), gathered_in))
     w_out_part = gather(out_piece)
@@ -1371,7 +1459,6 @@
             (0, None, 0, 0, placed(ff_table, 0, 2 * ffs)),
             (1, None, 0, 0, placed(ff_table, ffs, 2 * ffs)),
         ],
-        s,
     )[0]
 
     w_att_pad = jnp.pad(w_att_cols, ((0, width), (0, 0)))
@@ -1495,7 +1582,7 @@
         for i in range(2):
             table = gate_take[None] + d * per * ffw + i * ffs
             moves.append((0, None, 0, d, placed(table, i * half_wide, 2 * half_wide)))
-    (gu_blocks,) = regroup([r_gu], [SHAPE((S, rows_d, 2 * half_wide), BF)], moves, s)
+    (gu_blocks,) = regroup([r_gu], [SHAPE((S, rows_d, 2 * half_wide), BF)], moves)
     d_u, d_lin, d_dt_bias, d_rates, d_in_b, d_out_c, (ffn_got, gu_got, g_att_blocks) = (
         scan_backward(
             d_core, u, lin, bc, rates, position, skip, [down_parts, gu_blocks, att_blocks], micro, 0
@@ -1506,16 +1593,6 @@
     outputs = give(result.astype(BF), send_hot, land_hot)
     g_att_whole = jnp.concatenate(
         [g_att_blocks[i, : head_counts[i] * HEAD] for i in range(S)], axis=0
-    )
-    moves = []
-    for d in range(S):
-        moves.append((0, None, 0, d, run_table([d * cols], cols)))
-        moves.append((1, None, 1, d, run_table([d * cols], cols)))
-    row_blocks = regroup(
-        [r_ssm, r_down],
-        [SHAPE((S, r_ssm.shape[0], cols), BF), SHAPE((S, r_down.shape[0], cols), BF)],
-        moves,
-        s,
     )
     dproj_low, d_inner, conv_sums = ssm_close(
         d_lin,
@@ -1577,13 +1654,50 @@
     ends = np.cumsum([0, D, ATT, INNER, D, 6])
     line = jnp.concatenate([d_gain_in[0], att_at, ssm_at, d_gain_ffn[0], stats])
     line = jnp.pad(line, (0, -line.shape[0] % 1024)).reshape(-1, LANES)
-    row_blocks, dx = lax.optimization_barrier((list(row_blocks), dx))
-    ssm_got, down_got = deal(row_blocks, 1)
+    moves = []
+    for d in range(S):
+        moves.append((0, None, 0, d, run_table([d * cols], cols)))
+        moves.append((1, None, 1, d, run_table([d * cols], cols)))
+    qkv_wide = (ATT + 2 * KV_WIDTH) // S
+    starts = np.array(q_starts)[:, None]
+    counts = np.array(head_counts)[:, None] * HEAD
+    base = np.array(kv_starts)[:, None]
+    for d in range(S):
+        column = np.arange(qkv_wide)[None] + d * qkv_wide
+        table = np.full((S, qkv_wide), -1)
+        for low, count, source in (
+            (starts, counts, at_q),
+            (base, 2 * HEAD, at_k),
+            (base + KV_WIDTH, 2 * HEAD, at_v),
+        ):
+            inside = (column >= low) & (column < low + count)
+            table = np.where(inside, column - low + source - ch, table)
+        moves.append((2, None, 2, d, table.astype(np.int32)))
+    mix_mine = 2 * INNER // S
+    at = np.arange(mix_mine // S)
+    mix_tables = [
+        ((at // ch_piece + j * (2 * N // S)) * chw + at % ch_piece)[None].astype(np.int32)
+        for j in range(S // 2)
+    ]
+    for j in range(S // 2):
+        moves.append((2, None, 3, j, mix_tables[j]))
+    (*row_blocks, gate_blocks) = regroup(
+        [r_ssm, r_down, r_rest],
+        [
+            SHAPE((S, r_ssm.shape[0], cols), BF),
+            SHAPE((S, r_down.shape[0], cols), BF),
+            SHAPE((S, rows_d, qkv_wide), BF),
+            SHAPE((S // 2, rows_d, mix_mine // S), BF),
+        ],
+        moves,
+    )
+    row_blocks, gate_blocks, dx = lax.optimization_barrier((row_blocks, gate_blocks, dx))
+    ssm_got, down_got, qkv_got, gate_got = deal(row_blocks, gate_blocks, S // 2, 1)
     input_grads = give(dx, send_hot, land_hot)
     ssm_got, r_last = lax.optimization_barrier((ssm_got, r_last))
     out_ssm = ssm_got[:, :ch_piece].reshape(S * ch_piece, cols).astype(F32)
     out_down = down_got[:, :ff_piece].reshape(S * ff_piece, cols).astype(F32)
-    ff_mine, mix_mine = ff // S, 2 * INNER // S
+    ff_mine = ff // S
     moves = []
     at = np.arange(ff_mine)
     for source in range(S):
@@ -1594,44 +1708,19 @@
         moves.append((0, source, 0, 0, table))
         moves.append((0, source, 1, 0, np.where(table >= 0, table + half_wide, -1)))
     out_gate, out_up = regroup(
-        [gu_got], [jax.ShapeDtypeStruct((rows_d, ff_mine), F32)] * 2, moves, s
-    )
-
-    qkv_wide = (ATT + 2 * KV_WIDTH) // S
-    mix_slot = -(-mix_mine // S // LANES) * LANES
-    at = np.arange(mix_mine // S)
-    moves = []
-    starts = np.array(q_starts)[:, None]
-    counts = np.array(head_counts)[:, None] * HEAD
-    for d in range(S):
-        chunk = at // ch_piece + d * (2 * N // S)
-        table = chunk * chw + at % ch_piece
-        wide = mix_slot + qkv_wide
-        inner_part = np.where(chunk < N, table, -1)[None].astype(np.int32)
-        gate_part = np.where(chunk >= N, table - ch, -1)[None].astype(np.int32)
-        moves.append((0, None, 0, d, placed(inner_part, 0, wide)))
-        moves.append((1, None, 0, d, placed(gate_part, 0, wide)))
-        column = np.arange(qkv_wide)[None] + d * qkv_wide
-        from_q = np.where(
-            (column >= starts) & (column < starts + counts), column - starts + at_q - ch, -1
-        )
-        base = np.array(kv_starts)[:, None]
-        from_k = np.where(
-            (column >= base) & (column < base + 2 * HEAD), column - base + at_k - ch, -1
-        )
-        base = base + KV_WIDTH
-        from_v = np.where(
-            (column >= base) & (column < base + 2 * HEAD), column - base + at_v - ch, -1
-        )
-        table = np.maximum(np.maximum(from_q, from_k), from_v).astype(np.int32)
-        moves.append((1, None, 0, d, placed(table, mix_slot, wide)))
-    in_blocks = regroup(
-        [r_last, r_rest], [jax.ShapeDtypeStruct((S, rows_d, wide), BF)], moves, s
-    )[0]
+        [gu_got], [jax.ShapeDtypeStruct((rows_d, ff_mine), F32)] * 2, moves
+    )
+
+    (inner_blocks,) = regroup(
+        [r_last],
+        [SHAPE((S // 2, rows_d, mix_mine // S), BF)],
+        [(0, None, 0, j, mix_tables[j]) for j in range(S // 2)],
+    )
     r_small = r_last[:chw, ch + cols :]
-    in_got, small_got, sums_all = last_exchange(
-        [in_blocks, jnp.broadcast_to(r_small, (S,) + r_small.shape)], line, 2
-    )
+    small_got, inner_got, sums_all = last_exchange(
+        [jnp.broadcast_to(r_small, (S,) + r_small.shape)], inner_blocks, line, 2
+    )
+    out_qkv = jnp.sum(qkv_got.astype(F32), axis=0)
     moves = []
     at = np.arange(mix_mine)
     for source in range(S):
@@ -1640,15 +1729,8 @@
             inside // ch_piece == source, chunk * ch_piece + inside % ch_piece, -1
         )[None].astype(np.int32)
         moves.append((0, source, 0, 0, table))
-        moves.append((0, source, 1, 0, run_table([mix_slot], qkv_wide)))
-    out_mix, out_qkv = regroup(
-        [in_got],
-        [
-            jax.ShapeDtypeStruct((rows_d, mix_mine), F32),
-            jax.ShapeDtypeStruct((rows_d, qkv_wide), F32),
-        ],
-        moves,
-        s,
+    (out_mix,) = regroup(
+        [jnp.where(s < S // 2, inner_got, gate_got)], [SHAPE((rows_d, mix_mine), F32)], moves
     )
     g_att = r_last[:, ch : ch + cols].astype(F32)
     small_all = small_got[:, :ch_piece].reshape(S * ch_piece, small_wide).astype(F32)

time: 856 us -> 824 us (0.963)
  Pallas kernels: 533 us -> 492 us
  waiting for transfers between devices: 48 us -> 65.3 us
  local copies, waits for them, and re-layouts: 107 us -> 96.2 us
    pallas_call x1, Pallas kernels: 70.9 us -> 56.9 us  [mixer_rows(): pl.pallas_call(partial(mixer_kernel, size, tok, micro), out_shape=[shape(...]
    pallas_call x1, Pallas kernels: 88 us -> 76.1 us  [ffn_rows(): pl.pallas_call(partial(ffn_kernel, size, tok, micro), out_shape=[shape((r...]
    pallas_call x1, Pallas kernels: 33.2 us -> 22.9 us  [last_exchange(): pl.pallas_call(partial(last_kernel, sizes, count), out_shape=[SHAPE(a.sha...]
    all_gather x4, waiting for transfers between devices: 8.27 us -> 17.1 us  [gather(): return lax.all_gather(shard, 'fsdp', axis=0, tiled=True)]
  transfers between devices with their start and end apart: 13 -> 13, of which waited for: 3 -> 4; matrix products, arithmetic and copies ran while one was open for 22% -> 23% of each run, Pallas kernels for 47% -> 47%
where the time goes in v4:
time: 824 us; the launch traced here: 816 us
  Pallas kernels  492 us (60%)
  matrix products  97.4 us (12%)
  local copies, waits for them, and re-layouts  96.2 us (12%)
  waiting for transfers between devices  65.3 us (8%)
  other arithmetic  27.2 us (3%)
  starting transfers between devices  22.2 us (3%)
  between operations  15.9 us (2%)
    dot_general x18, matrix products, dot(): lax.dot_general(left_op, right_op, (((left_dim,), (right_dim,)), ((), ())...  81.8 us
    pallas_call x1, Pallas kernels, ffn_rows(): pl.pallas_call(partial(ffn_kernel, size, tok, micro), out_shape=[shape((r...  76.1 us
    pallas_call x1, Pallas kernels, scan_backward(): pl.pallas_call(partial(scan_back_kernel, size, len(helds), groups), grid=...  72.3 us
    pallas_call x1, Pallas kernels, mixer_rows(): pl.pallas_call(partial(mixer_kernel, size, tok, micro), out_shape=[shape(...  56.9 us
    pallas_call x2, Pallas kernels, gather_rows(): pl.pallas_call(partial(gather_kernel, size, rows // micro), out_shape=SHA...  49.2 us
    all_to_all x4, waiting for transfers between devices, exchange(): return lax.all_to_all(rows, 'fsdp', split_axis=0, concat_axis=0, tiled=True)  37.4 us
    pallas_call x1, Pallas kernels, deal(): pl.pallas_call(partial(deal_kernel, count, size, first), out_shape=[SHAPE...  35.1 us
    pallas_call x1, Pallas kernels, scan_forward(): pl.pallas_call(partial(scan_kernel, size, lane_groups(channels)), grid=(m...  32.7 us
  transfers between devices with their start and end apart: 13, of which 4 were waited for; matrix products, arithmetic and copies ran while one was open for 23% of the time, Pallas kernels for 47%

profile of v4, /device:TPU:0, one launch (start us, length us, event | category | flops | bytes accessed | tf_op | source)
XLA Modules:
  0.0 816.3 jit_solution(446357235109953349)
XLA Ops:
  9.7 6.1 regroup.7
  20.5 6.3 all-to-all-start.1
  28.0 32.0 %all-to-all-done.1 = bf16[8,24,1600]{2,1,0:T(8,128)(2,1)S(1)} async-done(((bf16[8,24,1600]{2,1,0:T(8,128)(2,1)}), bf16[8,24,1600]{2,1,0:T(8,128)(2,1)S(1)}, u32[]{:S(2)}, u32[]{:S(2)}) %all-to-all-start.1) | async-done | bytes 614432 | tf_op jit(solution)/shard_map/all_to_all | solution.py:119
  69.8 25.0 %gather_rows.2 = bf16[768,1600]{1,0:T(8,128)(2,1)} custom-call(bf16[192,1600]{1,0:T(8,128)(2,1)} %get-tuple-element.295.own.refs_3_.x_ref), custom_call_target="tpu_custom_call" | custom-call | tf_op jit(solution)/shard_map/gather_rows/pallas_call | solution.py:777
  94.8 5.4 all-to-all-done
  101.3 24.2 %gather_rows.3.refs_1_ = bf16[768,1600]{1,0:T(8,128)(2,1)} custom-call(bf16[192,1600]{1,0:T(8,128)(2,1)} %convolution_convert_fusion.10.own.refs_3_), custom_call_target="tpu_custom_call" | custom-call | tf_op jit(solution)/shard_map/gather_rows/pallas_call | solution.py:777
  125.5 17.0 %all-gather.5.cloned.1.call-done = bf16[1600,3152]{1,0:T(8,128)(2,1)} async-done(((bf16[200,3152]{1,0:T(8,128)(2,1)}), bf16[1600,3152]{1,0:T(8,128)(2,1)}) %all-gather.5.cloned.1.call-update) | async-done | bytes 10086416 | tf_op jit(solution)/shard_map/all_gather | solution.py:1388
  144.5 6.3 regroup.8
  153.4 11.0 %fusion.7.opened_ref.refs_5_.refs_4_ = bf16[768,2496]{1,0:T(8,128)(2,1)} fusion(bf16[1600,3152]{1,0:T(8,128)(2,1)} %all-gather.5.cloned.1.call-done, bf16[768,1600]{1,0:T(8,128)(2,1)S(1)} %copy-done.6, f32[1600]{0:T(1024)S(1)} %copy-done.28, f32[768]{0:T(1024)S(1)} %add_rsqrt_fusion), kind=kOutput, calls=%fused_computation.16 | convolution fusion | flops 6141001728 | bytes 14492928 | tf_op jit(solution)/shard_map/dot_general | solution.py:31
  175.6 18.2 %attention.1 = (f32[768,448]{1,0:T(8,128)}, f32[2,7,384,384]{3,2,1,0:T(8,128)}, f32[8,768]{1,0:T(8,128)}) custom-call(bf16[768,2496]{1,0:T(8,128)(2,1)} %fusion.7.opened_ref.refs_5_.refs_4_, s32[768,1]{1,0:T(8,128)} %bitcast.156), custom_call_target="tpu_custom_call" | custom-call | tf_op jit(solution)/shard_map/attention/pallas_call | solution.py:1027
  195.8 21.6 %ssm_open.1 = (f32[768,896]{1,0:T(8,128)}, f32[768,896]{1,0:T(8,128)}, bf16[144,768]{1,0:T(8,128)(2,1)}, bf16[32,768]{1,0:T(8,128)(2,1)}) custom-call(bf16[768,2496]{1,0:T(8,128)(2,1)} %fusion.7.opened_ref.refs_5_.refs_4_, s32[768,1]{1,0:T(8,128)} %bitcast.157, f32[8,896]{1,0:T(8,128)} %slice_select_fusion.taps.refs_6_, ...), custom_call_target="tpu_custom_call" | custom-call | tf_op jit(solution)/shard_map/ssm_open/pallas_call | solution.py:1098
  222.6 6.8 broadcast_in_dim.135.refs_2_.refs_3_
  229.4 32.7 %scan_forward.1 = (f32[768,896]{1,0:T(8,128)}, f32[768,896]{1,0:T(8,128)}, f32[8,768]{1,0:T(8,128)}, bf16[4,448,400]{2,1,0:T(8,128)(2,1)}) custom-call(f32[768,896]{1,0:T(8,128)} %get-tuple-element.111.refs_0_.refs_6_.refs_1_, f32[768,896]{1,0:T(8,128)} %get-tuple-element.112.refs_1_.refs_2_, bf16[768,32,128]{2,1,0:T(8,128)(2,1)} %broadcast_in_dim.135.refs_2_.refs_3_, ...), custom_call_target="tpu_custom_call" | custom-call | tf_op jit(solution)/shard_map/scan_forward/pallas_call | solution.py:412
  265.4 56.9 %mixer_rows.1 = (bf16[768,448]{1,0:T(8,128)(2,1)}, bf16[768,896]{1,0:T(8,128)(2,1)}, f32[768,128]{1,0:T(8,128)}, f32[768,128]{1,0:T(8,128)}, f32[192,1600]{1,0:T...) custom-call(f32[768,448]{1,0:T(8,128)} %get-tuple-element.110.refs_0_.refs_3_, ...), custom_call_target="tpu_custom_call" | custom-call | tf_op jit(solution)/shard_map/mixer_rows/pallas_call | solution.py:870
  322.4 76.1 %ffn_rows.1 = (bf16[768,1408]{1,0:T(8,128)(2,1)}, bf16[768,2816]{1,0:T(8,128)(2,1)}, bf16[4,192,1600]{2,1,0:T(8,128)(2,1)}, f32[192,1600]{1,0:T(8,128)}, f32[1,1600]{1,0:T(1,128)}, /*index=5*/bf16[768,1600]{1,0:T(8,128)(2,1)}) custom-call(bf16[768,1600]{1,0:T(8,128)(2,1)} %get-tuple-element.120.refs_0_, bf16[768,1600]{1,0:T(8,128)(2,1)} %gather_rows.3.refs_1_, ...), custom_call_target="tpu_custom_call" | custom-call | tf_op jit(solution)/shard_map/ffn_rows/pallas_call | solution.py:972
  398.5 12.5 %convolution_convert_fusion = bf16[1600,2816]{1,0:T(8,128)(2,1)} fusion(bf16[768,1600]{1,0:T(8,128)(2,1)S(1)} %copy-done.8, bf16[768,2816]{1,0:T(8,128)(2,1)} %get-tuple-element.126), kind=kOutput, calls=%fused_computation | convolution fusion | flops 6925107200 | bytes 15794176 | tf_op jit(solution)/shard_map/dot_general | solution.py:31
  420.3 8.8 %convolution_convert_fusion.2 = bf16[1408,1600]{1,0:T(8,128)(2,1)} fusion(bf16[768,1408]{1,0:T(8,128)(2,1)} %get-tuple-element.127, bf16[768,1600]{1,0:T(8,128)(2,1)} %gather_rows.3.refs_1_), kind=kOutput, calls=%fused_computation.6 | convolution fusion | flops 3462553600 | bytes 9125888 | tf_op jit(solution)/shard_map/dot_general | solution.py:31
  429.0 27.3 %branch_back.1 = (bf16[768,448]{1,0:T(8,128)(2,1)}, f32[768,896]{1,0:T(8,128)}, bf16[768,896]{1,0:T(8,128)(2,1)}, f32[1,448]{1,0:T(1,128)}, f32[1,896]{1,0:T(1,128)}, /*index=5*/f32[1,896]{1,0:T(1,128)}) custom-call(bf16[768,1600]{1,0:T(8,128)(2,1)} %get-tuple-element.128.refs_0_, bf16[4,448,400]{2,1,0:T(8,128)(2,1)} %get-tuple-element.117.refs_7_.refs_1_, ...), custom_call_target="tpu_custom_call" | custom-call | tf_op jit(solution)/shard_map/branch_back/pallas_call | solution.py:1261
  459.9 5.1 multiply_reduce_fusion
  478.3 4.6 select_reduce_fusion
  483.6 5.6 concatenate.43
  489.2 5.7 multiply_convert_fusion.1
  494.8 9.7 %convolution_convert_fusion.1 = bf16[1600,1600]{1,0:T(8,128)(2,1)} fusion(bf16[768,1600]{1,0:T(8,128)(2,1)} %concatenate.43, bf16[768,1600]{1,0:T(8,128)(2,1)} %gather_rows.2, f32[1600]{0:T(1024)S(1)} %copy-done.28, f32[768]{0:T(1024)S(1)} %add_rsqrt_fusion), kind=kOutput, calls=%fused_computation.5 | convolution fusion | flops 3939635200 | bytes 10044672 | tf_op jit(solution)/shard_map/dot_general | solution.py:31
  504.5 9.3 %fusion.12.rest = bf16[768,1600]{1,0:T(8,128)(2,1)} fusion(bf16[768,1600]{1,0:T(8,128)(2,1)} %concatenate.43, bf16[1600,3152]{1,0:T(8,128)(2,1)} %all-gather.5.cloned.1.call-done), kind=kOutput, calls=%fused_computation.20 | convolution fusion | flops 3933388800 | bytes 10338304 | tf_op jit(solution)/shard_map/dot_general | solution.py:31
  528.0 72.3 %scan_backward.1 = (f32[768,896]{1,0:T(8,128)}, bf16[768,896]{1,0:T(8,128)(2,1)}, f32[2,1,896]{2,1,0:T(1,128)}, f32[2,16,896]{2,1,0:T(8,128)}, f32[2,8,6144]{2,1...) custom-call(f32[768,896]{1,0:T(8,128)} %get-tuple-element.138.refs_0, ...), custom_call_target="tpu_custom_call" | custom-call | tf_op jit(solution)/shard_map/scan_backward/pallas_call | solution.py:550
  604.5 23.0 %ssm_close.1 = (bf16[144,768]{1,0:T(8,128)(2,1)}, bf16[768,896]{1,0:T(8,128)(2,1)}, f32[8,896]{1,0:T(8,128)}) custom-call(bf16[768,896]{1,0:T(8,128)(2,1)} %get-tuple-element.145.refs_0_, f32[768,16]{1,0:T(8,128)} %reshape_squeeze.9.refs_1_, f32[768,16]{1,0:T(8,128)} %reshape_squeeze.10.refs_2_, f32[768,896]{1,0:T(8,128)} %get-tuple-element.148.refs_3_, ...), custom_call_target="tpu_custom_call" | custom-call | tf_op jit(solution)/shard_map/ssm_close/pallas_call | solution.py:1176
  643.7 8.2 %concatenate.53 = bf16[1600,1552]{1,0:T(8,128)(2,1)} concatenate(bf16[1600,896]{1,0:T(8,128)(2,1)} %convolution_convert_fusion.3, bf16[1600,400]{1,0:T(8,128)(2,1)S(1)} %pad_maximum_fusion.1, bf16[1600,256]{1,0:T(8,128)(2,1)S(1)} %bitcast.167), dimensions={1} | concatenate | bytes 9932800 | tf_op jit(solution)/shard_map/concatenate | solution.py:1629
  664.5 8.9 %reduce-scatter.12.cloned.1.call-done.refs_0_ = bf16[112,1600]{1,0:T(8,128)(2,1)} async-done(((bf16[896,1600]{1,0:T(8,128)(2,1)}), bf16[112,1600]{1,0:T(8,128)(2,1)}) %reduce-scatter.12.cloned.1.call-update) | async-done | bytes 358416 | tf_op jit(solution)/shard_map/reduce_scatter | solution.py:1397
  673.4 28.2 %close_rows.1 = (bf16[192,1600]{1,0:T(8,128)(2,1)}, f32[1,1600]{1,0:T(1,128)}) custom-call(bf16[768,1600]{1,0:T(8,128)(2,1)} %fusion.12.rest, bf16[768,896]{1,0:T(8,128)(2,1)} %get-tuple-element.164.d_inner, bf16[1600,896]{1,0:T(8,128)(2,1)} %slice.217.w, bf16[192,1600]{1,0:T(8,128)(2,1)} %get-tuple-element.295.own.refs_3_.x_ref, ...), custom_call_target="tpu_custom_call" | custom-call | tf_op jit(solution)/shard_map/close_rows/pallas_call | solution.py:1326
  708.1 7.8 all-to-all-start.3
  722.3 35.1 %deal.1 = (bf16[4,112,400]{2,1,0:T(8,128)(2,1)}, bf16[4,176,400]{2,1,0:T(8,128)(2,1)}, bf16[4,200,560]{2,1,0:T(8,128)(2,1)}, bf16[4,200,400]{2,1,0:T(8,128)(2,1)}) custom-call(bf16[4,112,400]{2,1,0:T(8,128)(2,1)} %get-tuple-element.168.refs_0_, bf16[4,176,400]{2,1,0:T(8,128)(2,1)} %get-tuple-element.169.refs_1_, ...), custom_call_target="tpu_custom_call" | custom-call | bytes 1024 | tf_op jit(solution)/shard_map/deal/pallas_call | solution.py:699
  772.1 22.9 %last_exchange.1 = (bf16[4,112,256]{2,1,0:T(8,128)(2,1)}, bf16[4,200,400]{2,1,0:T(8,128)(2,1)}, f32[64,128]{1,0:T(8,128)}) custom-call(bf16[4,112,256]{2,1,0:T(8,128)(2,1)} %broadcast_in_dim.152.refs_0_, bf16[2,200,400]{2,1,0:T(8,128)(2,1)} %regroup.11.refs_1_, f32[64,128]{1,0:T(8,128)} %pad_bitcast_fusion.3.refs_2_), custom_call_target="tpu_custom_call" | custom-call | bytes 1024 | tf_op jit(solution)/shard_map/last_exchange/pallas_call | solution.py:751
  (303 shorter events, 160.2 us)
Async XLA Ops:
  7.2 12.1 %copy-start = (bf16[2,96,1600]{2,1,0:T(8,128)(2,1)S(1)}, bf16[2,96,1600]{2,1,0:T(8,128)(2,1)}, u32[]{:S(2)}) copy-start(bf16[2,96,1600]{2,1,0:T(8,128)(2,1)} %param.62) | copy-start | bytes 1843204
  7.2 135.3 %all-gather.5.cloned.1.call-start = ((), (), s32[]{:S(2)}) async-start(), calls=%async_computation.9 | async-start | bytes 11520000 | tf_op jit(solution)/shard_map/all_gather | solution.py:1388
  18.2 8.6 %copy-start.17 = (bf16[2,96,1600]{2,1,0:T(8,128)(2,1)S(1)}, bf16[2,96,1600]{2,1,0:T(8,128)(2,1)}, u32[]{:S(2)}) copy-start(bf16[2,96,1600]{2,1,0:T(8,128)(2,1)} %param.63) | copy-start | bytes 1843204
  19.3 41.5 %copy-start.21 = (s32[192]{0:T(256)}, s32[192]{0:T(256)S(1)}, u32[]{:S(2)}) copy-start(s32[192]{0:T(256)S(1)} %multiply_add_fusion) | copy-start | bytes 2308
  19.3 46.4 %copy-start.11 = (bf16[400,1600]{1,0:T(8,128)(2,1)S(1)}, bf16[400,1600]{1,0:T(8,128)(2,1)}, u32[]{:S(2)}) copy-start(bf16[400,1600]{1,0:T(8,128)(2,1)} %param.75) | copy-start | bytes 3840004
  20.5 39.5 %all-to-all-start.1 = ((bf16[8,24,1600]{2,1,0:T(8,128)(2,1)}), bf16[8,24,1600]{2,1,0:T(8,128)(2,1)S(1)}, u32[]{:S(2)}, u32[]{:S(2)}) async-start(bf16[8,24,1600]{2,1,0:T(8,128)(2,1)} %bitcast.7), calls=%async_computation.1 | async-start | bytes 1277952 | tf_op jit(solution)/shard_map/all_to_all | solution.py:119
  60.8 39.3 %all-to-all-start = ((bf16[8,24,1600]{2,1,0:T(8,128)(2,1)}), bf16[8,24,1600]{2,1,0:T(8,128)(2,1)S(1)}, u32[]{:S(2)}, u32[]{:S(2)}) async-start(bf16[8,24,1600]{2,1,0:T(8,128)(2,1)} %bitcast.4), calls=%async_computation | async-start | bytes 1277952 | tf_op jit(solution)/shard_map/all_to_all | solution.py:119
  64.8 200.6 %all-gather.7.cloned.1.call-start = ((), (), s32[]{:S(2)}) async-start(), calls=%async_computation.10 | async-start | bytes 3354624 | tf_op jit(solution)/shard_map/all_gather | solution.py:1388
  65.7 34.5 %copy-start.24 = (s32[192]{0:T(256)}, s32[192]{0:T(256)S(1)}, u32[]{:S(2)}) copy-start(s32[192]{0:T(256)S(1)} %eq.91) | copy-start | bytes 2308
  94.8 48.0 %copy-start.9 = (bf16[688,1600]{1,0:T(8,128)(2,1)S(1)}, bf16[688,1600]{1,0:T(8,128)(2,1)}, u32[]{:S(2)}) copy-start(bf16[688,1600]{1,0:T(8,128)(2,1)} %param.79) | copy-start | bytes 6604804
  142.6 179.8 %all-gather.11.cloned.1.call-start = ((), (), s32[]{:S(2)}) async-start(), calls=%async_computation.12 | async-start | bytes 5271552 | tf_op jit(solution)/shard_map/all_gather | solution.py:1388
  153.4 11.7 %copy-start.34 = (s32[2,1,3]{2,1,0:T(1,128)S(1)}, s32[2,1,3]{2,1,0:T(1,128)}, u32[]{:S(2)}) copy-start(s32[2,1,3]{2,1,0:T(1,128)} %param.65) | copy-start | bytes 76
  153.4 13.2 %copy-start.41 = (s32[5]{0:T(128)S(1)}, s32[5]{0:T(128)}, u32[]{:S(2)}) copy-start(s32[5]{0:T(128)} %constant.194.clone) | copy-start | bytes 64
  153.4 14.5 %copy-start.23 = (f32[3200]{0:T(1024)S(1)}, f32[3200]{0:T(1024)}, u32[]{:S(2)}) copy-start(f32[3200]{0:T(1024)} %param.73) | copy-start | bytes 38404
  153.4 15.3 %copy-start.26 = (f32[1600]{0:T(1024)S(1)}, f32[1600]{0:T(1024)}, u32[]{:S(2)}) copy-start(f32[1600]{0:T(1024)} %param.76) | copy-start | bytes 19204
  153.4 15.9 %copy-start.27 = (f32[1600]{0:T(1024)S(1)}, f32[1600]{0:T(1024)}, u32[]{:S(2)}) copy-start(f32[1600]{0:T(1024)} %param.72) | copy-start | bytes 19204
  164.5 157.9 %all-gather.9.cloned.1.call-start = ((), (), s32[]{:S(2)}) async-start(), calls=%async_computation.11 | async-start | bytes 10137600 | tf_op jit(solution)/shard_map/all_gather | solution.py:1388
  165.1 348.8 %reduce-scatter.10.cloned.1.call-start = ((), (), s32[]{:S(2)}) async-start(), calls=%async_computation.13 | async-start | bytes 10137600 | tf_op jit(solution)/shard_map/reduce_scatter | solution.py:1397
  175.6 19.5 %copy-start.38 = (pred[8]{0:T(512)(128)(4,1)S(1)}, pred[8]{0:T(512)(128)(4,1)}, u32[]{:S(2)}) copy-start(pred[8]{0:T(512)(128)(4,1)} %constant.183.clone.1) | copy-start | bytes 28
  322.4 76.1 %copy-start.8 = (bf16[768,1600]{1,0:T(8,128)(2,1)S(1)}, bf16[768,1600]{1,0:T(8,128)(2,1)}, u32[]{:S(2)}) copy-start(bf16[768,1600]{1,0:T(8,128)(2,1)} %get-tuple-element.120.refs_0_) | copy-start | bytes 7372804
  411.0 240.9 %reduce-scatter.16.cloned.1.call-start = ((), (), s32[]{:S(2)}) async-start(), calls=%async_computation.16 | async-start | bytes 5990400
  513.9 150.7 %reduce-scatter.14.cloned.1.call-start = ((), (), s32[]{:S(2)}) async-start(), calls=%async_computation.15 | async-start | bytes 5271552 | tf_op jit(solution)/shard_map/reduce_scatter | solution.py:1397
  514.6 158.8 %reduce-scatter.12.cloned.1.call-start = ((), (), s32[]{:S(2)}) async-start(), calls=%async_computation.14 | async-start | bytes 3354624 | tf_op jit(solution)/shard_map/reduce_scatter | solution.py:1397
  515.4 252.8 %reduce-scatter.18.cloned.1.call-start = ((), (), s32[]{:S(2)}) async-start(), calls=%async_computation.17 | async-start | bytes 5990400
  604.5 23.0 %copy-start.2 = (f32[768,896]{1,0:T(8,128)S(1)}, f32[768,896]{1,0:T(8,128)}, u32[]{:S(2)}) copy-start(f32[768,896]{1,0:T(8,128)} %get-tuple-element.111.refs_0_.refs_6_.refs_1_) | copy-start | bytes 8257540
  655.6 52.6 %all-to-all-start.2 = ((bf16[8,24,1600]{2,1,0:T(8,128)(2,1)}), bf16[8,24,1600]{2,1,0:T(8,128)(2,1)S(1)}, u32[]{:S(2)}, u32[]{:S(2)}) async-start(bf16[8,24,1600]{2,1,0:T(8,128)(2,1)} %bitcast.171), calls=%async_computation.3 | async-start | bytes 1277952 | tf_op jit(solution)/shard_map/all_to_all | solution.py:119
  701.6 14.3 %copy-start.37 = (f32[1,448]{1,0:T(1,128)S(1)}, f32[1,448]{1,0:T(1,128)}, u32[]{:S(2)}) copy-start(f32[1,448]{1,0:T(1,128)} %get-tuple-element.176) | copy-start | bytes 5380
  701.6 14.4 %copy-start.35 = (f32[1,896]{1,0:T(1,128)S(1)}, f32[1,896]{1,0:T(1,128)}, u32[]{:S(2)}) copy-start(f32[1,896]{1,0:T(1,128)} %get-tuple-element.177) | copy-start | bytes 10756
  701.6 14.9 %copy-start.31 = (f32[1,1600]{1,0:T(1,128)S(1)}, f32[1,1600]{1,0:T(1,128)}, u32[]{:S(2)}) copy-start(f32[1,1600]{1,0:T(1,128)} %get-tuple-element.178) | copy-start | bytes 19204
  708.1 12.9 %copy-start.22 = (s32[192]{0:T(256)S(1)}, s32[192]{0:T(256)}, u32[]{:S(2)}) copy-start(s32[192]{0:T(256)} %copy-done.21) | copy-start | bytes 2308
  708.1 57.7 %all-to-all-start.3 = ((bf16[8,24,1600]{2,1,0:T(8,128)(2,1)}), bf16[8,24,1600]{2,1,0:T(8,128)(2,1)}, u32[]{:S(2)}, u32[]{:S(2)}) async-start(bf16[8,24,1600]{2,1,0:T(8,128)(2,1)} %bitcast.169), calls=%async_computation.6 | async-start | bytes 1277952 | tf_op jit(solution)/shard_map/all_to_all | solution.py:119
  797.1 8.3 %copy-start.15 = (bf16[4,200,400]{2,1,0:T(8,128)(2,1)S(1)}, bf16[4,200,400]{2,1,0:T(8,128)(2,1)}, u32[]{:S(2)}) copy-start(bf16[4,200,400]{2,1,0:T(8,128)(2,1)} %get-tuple-element.182) | copy-start | bytes 1920004
  (27 other events, 103.6 us)
Sparse Core Ops, SparseCore 0:
  18.4 124.1 all-gather.4
  144.7 35.8 all-gather.6
  182.8 50.2 all-gather.10
  235.3 86.0 all-gather.8
  411.1 93.4 reduce-scatter.9
  514.0 58.9 reduce-scatter.15
  575.3 53.9 reduce-scatter.13
  631.7 41.6 reduce-scatter.11
  675.7 75.6 reduce-scatter.17

commit v5 on v4

--- a/solution.py
+++ b/solution.py
@@ -901,8 +901,8 @@
 
 def ffn_kernel(size, tok, micro, *refs):
     ffn, cot, hidden, cot_own, gain, w_gu, w_down = refs[:7]
-    act, dgu, down, d_hidden, d_gain, dmix = refs[7:13]
-    sent, got, dmix_own, send, recv, own_sem, dmix_send, dmix_recv = refs[13:]
+    act, dgu, down, d_hidden, d_gain, dmix, grad = refs[7:14]
+    sent, got, dmix_own, send, recv, own_sem, dmix_send, dmix_recv, turned = refs[14:]
     here, row = lax.axis_index("seq"), lax.axis_index("fsdp")
     wide = w_down.shape[0]
     meet(pack_peers(size))
@@ -957,7 +957,19 @@
     d_gain[...] = gain_sum
     relay = Relay(tok, dmix_own, dmix, own_sem, dmix_send, dmix_recv)
     relay.start()
+    for low, high in spans_of(D, 2 * LANES):
+        turned[low:high, :] = ffn[:, low:high].T
+
+    def columns(j, carry):
+        span = pl.ds(pl.multiple_of(j * 2 * LANES, 2 * LANES), 2 * LANES)
+        for low, high in spans_of(D):
+            grad[low:high, span] = dot(turned[low:high, :], dgu[:, span], 1, 0).astype(BF)
+        return carry
+
+    pieces = 2 * wide // (2 * LANES)
+    lax.fori_loop(0, pieces // 4, columns, 0)
     relay.pass_on()
+    lax.fori_loop(pieces // 4, pieces, columns, 0)
     relay.finish()
 
 
@@ -978,9 +990,10 @@
             shape((own, D), F32),
             shape((1, D), F32),
             shape((rows, D), BF),
+            shape((D, 2 * wide), BF),
         ],
         in_specs=[vmem] * 7,
-        out_specs=[vmem] * 5 + [hbm],
+        out_specs=[vmem] * 5 + [hbm, vmem],
         scratch_shapes=[
             pltpu.VMEM((size, own, D), BF),
             pltpu.VMEM((6, tok, D), BF),
@@ -988,6 +1001,7 @@
             *crossing_sems(),
             dma((micro,)),
             *crossing_sems(),
+            pltpu.VMEM((D, rows), BF),
         ],
         compiler_params=pltpu.CompilerParams(
             collective_id=collective_id, has_side_effects=True, vmem_limit_bytes=VMEM_BYTES
@@ -1198,11 +1212,16 @@
 
 
 def branch_back_kernel(size, *refs):
-    dmix, w_att, w_ssm, context, ssm_out, core, u, gate_ref = refs[:8]
+    dmix, w_att, w_ssm, context, ssm_out, core, u, opened = refs[:8]
     scale_att, scale_ssm, gain_att, gain_ssm, live, skip = refs[8:14]
     d_context, d_core, d_gate, d_gain_att, d_gain_ssm, d_skip = refs[14:20]
-    t_att, t_ssm, slots, send, recv = refs[20:-1]
-    w_att = joined(w_att, refs[-1])
+    t_att, t_ssm, slots, send, recv, w_whole, gate_ref, gate_sem = refs[20:]
+    channels = gate_ref.shape[1]
+    fetch = pltpu.make_async_copy(
+        opened.at[:, pl.ds(channels, channels)], gate_ref, gate_sem.at[0]
+    )
+    fetch.start()
+    w_att = joined(w_att, w_whole)
     meet(pack_peers(size))
     place = lax.broadcasted_iota(jnp.int32, (8, LANES), 0)
     kinds = (
@@ -1224,6 +1243,7 @@
     rows8 = lax.broadcasted_iota(jnp.int32, sums[0].shape, 0)
     slots[lax.axis_index("seq")] = jnp.where(rows8 == 0, sums[0], sums[1])
     total = sum_slots(slots, send, recv)
+    fetch.wait()
     columns = [
         lax.dot_general(
             total,
@@ -1253,7 +1273,7 @@
 
 
 def branch_back(
-    dmix, w_att, w_ssm, context, ssm_out, core, u, gate_z, scales, gains, live, skip, collective_id
+    dmix, w_att, w_ssm, context, ssm_out, core, u, opened, scales, gains, live, skip, collective_id
 ):
     size = lax.axis_size("seq")
     rows, wide, channels = dmix.shape[0], w_att.shape[1], w_ssm.shape[0]
@@ -1268,7 +1288,7 @@
             SHAPE((1, channels), F32),
             SHAPE((1, channels), F32),
         ],
-        in_specs=[VMEM] * 14,
+        in_specs=[VMEM] * 7 + [HBM] + [VMEM] * 6,
         out_specs=[VMEM] * 6,
         scratch_shapes=[
             pltpu.VMEM((rows, wide), F32),
@@ -1277,18 +1297,27 @@
             dma,
             dma,
         ]
-        + [pltpu.VMEM((wide, D), BF)],
+        + [
+            pltpu.VMEM((wide, D), BF),
+            pltpu.VMEM((rows, channels), BF),
+            pltpu.SemaphoreType.DMA((1,)),
+        ],
         compiler_params=pltpu.CompilerParams(
             collective_id=collective_id, has_side_effects=True, vmem_limit_bytes=VMEM_BYTES
         ),
         name="branch_back",
-    )(dmix, w_att, w_ssm, context, ssm_out, core, u, gate_z, *scales, *gains, live, skip)
-
-
-def close_kernel(size, tok, micro, rest, d_inner, w, x_ref, gain, d_hidden, dx, d_gain, sent, got, send, recv):
+    )(dmix, w_att, w_ssm, context, ssm_out, core, u, opened, *scales, *gains, live, skip)
+
+
+def close_kernel(
+    size, tok, micro, rest, d_inner, whole_w, x_ref, gain, d_hidden, dx, d_gain, sent, got, send, recv, w, w_sem
+):
+    fetch = pltpu.make_async_copy(whole_w.at[:, pl.ds(0, w.shape[1])], w, w_sem.at[0])
+    fetch.start()
     here, row = lax.axis_index("seq"), lax.axis_index("fsdp")
     meet(pack_peers(size))
 
+    fetch.wait()
     gathering = Gathering(tok, sent, got, send, recv)
 
     def block(k, carry):
@@ -1326,12 +1355,14 @@
     return pl.pallas_call(
         partial(close_kernel, size, own // micro, micro),
         out_shape=[SHAPE((own, D), BF), SHAPE((1, D), F32)],
-        in_specs=[VMEM] * 6,
+        in_specs=[VMEM] * 2 + [HBM] + [VMEM] * 3,
         out_specs=[VMEM] * 2,
         scratch_shapes=[
             pltpu.VMEM((size, own, D), BF),
             pltpu.VMEM((6, own // micro, D), BF),
             *crossing_sems(),
+            pltpu.VMEM((w.shape[0], d_inner.shape[1]), BF),
+            pltpu.SemaphoreType.DMA((1,)),
         ],
         compiler_params=pltpu.CompilerParams(
             collective_id=collective_id, has_side_effects=True, vmem_limit_bytes=VMEM_BYTES
@@ -1489,7 +1520,6 @@
         (opened, gu_part, part(w_down, 0, 1, ffw))
     )
     w_gu, w_down_part = gather(gu_part), gather(down_part)
-    gate_z = opened[:, ch : 2 * ch]
     u, lin, projected, bc = ssm_open(
         opened, position, taps, conv_b, w_x_turned, w_dt_turned, dt_bias, micro, 7
     )
@@ -1515,12 +1545,10 @@
         micro,
         4,
     )
-    act_low, dgu_low, down_parts, d_hidden, d_gain_ffn, dmix_low = ffn_rows(
+    act_low, _, down_parts, d_hidden, d_gain_ffn, dmix_low, gu_whole = ffn_rows(
         ffn_low, cot_rows, hidden, cot_own, gain_ffn[None], w_gu, w_down_part, micro, 5
     )
 
-    gu_whole = dot(ffn_low, dgu_low, 0, 0).astype(BF)
-    act_low, gu_whole = lax.optimization_barrier((act_low, gu_whole))
     r_gu = scatter(gu_whole)
     down_whole = dot(act_low, cot_rows, 0, 0).astype(BF)
     dmix_low, down_whole = lax.optimization_barrier((dmix_low, down_whole))
@@ -1533,7 +1561,7 @@
         ssm_out,
         core,
         u,
-        gate_z,
+        opened,
         (scale_att, scale_ssm),
         (gain_att_part, gain_ssm_part),
         live,
@@ -1568,8 +1596,9 @@
         ],
         axis=1,
     )
+    rest_whole = dot(normed_low, d_rest, 0, 0).astype(BF)
+    d_rest, rest_whole = lax.optimization_barrier((d_rest, rest_whole))
     rest_rows = dot(d_rest, gathered_in[:, ch:at_att], 1, 1).astype(BF)
-    rest_whole = dot(normed_low, d_rest, 0, 0).astype(BF)
     d_core, r_gu, ssm_whole, rest_whole, rest_rows = lax.optimization_barrier(
         (d_core, r_gu, ssm_whole, rest_whole, rest_rows)
     )
@@ -1629,10 +1658,26 @@
     last_whole = jnp.concatenate(
         [dot(normed_low, d_inner, 0, 0).astype(BF), g_att_whole, small_whole], axis=1
     )
-    d_inner, last_whole, r_rest = lax.optimization_barrier((d_inner, last_whole, r_rest))
+    ff_mine = ff // S
+    moves = []
+    at = np.arange(ff_mine)
+    for source in range(S):
+        chunk, inside = at // (S * ff_piece), at % (S * ff_piece)
+        table = np.where(
+            inside // ff_piece == source, chunk * ff_piece + inside % ff_piece, -1
+        )[None].astype(np.int32)
+        moves.append((0, source, 0, 0, table))
+        moves.append((0, source, 1, 0, np.where(table >= 0, table + half_wide, -1)))
+    out_gate, out_up = regroup(
+        [gu_got], [jax.ShapeDtypeStruct((rows_d, ff_mine), F32)] * 2, moves
+    )
+
+    d_inner, last_whole, r_rest, out_gate, out_up = lax.optimization_barrier(
+        (d_inner, last_whole, r_rest, out_gate, out_up)
+    )
     r_last = scatter(last_whole)
     dx, d_gain_in = close_rows(
-        rest_rows, d_inner, gathered_in[:, :ch], x_own, gain_in[None], d_hidden, micro, 10
+        rest_rows, d_inner, gathered_in, x_own, gain_in[None], d_hidden, micro, 10
     )
 
     att_at = lax.dynamic_update_slice_in_dim(
@@ -1652,8 +1697,10 @@
         ]
     )
     ends = np.cumsum([0, D, ATT, INNER, D, 6])
-    line = jnp.concatenate([d_gain_in[0], att_at, ssm_at, d_gain_ffn[0], stats])
-    line = jnp.pad(line, (0, -line.shape[0] % 1024)).reshape(-1, LANES)
+    line = jnp.concatenate([jnp.zeros((D,), F32), att_at, ssm_at, d_gain_ffn[0], stats])
+    line = jnp.pad(line, (0, -line.shape[0] % 1024))
+    line, d_gain_in = lax.optimization_barrier((line, d_gain_in))
+    line = lax.dynamic_update_slice(line, d_gain_in[0], (0,)).reshape(-1, LANES)
     moves = []
     for d in range(S):
         moves.append((0, None, 0, d, run_table([d * cols], cols)))
@@ -1681,6 +1728,7 @@
     ]
     for j in range(S // 2):
         moves.append((2, None, 3, j, mix_tables[j]))
+    dx, r_ssm, r_down, r_rest = lax.optimization_barrier((dx, r_ssm, r_down, r_rest))
     (*row_blocks, gate_blocks) = regroup(
         [r_ssm, r_down, r_rest],
         [
@@ -1697,20 +1745,6 @@
     ssm_got, r_last = lax.optimization_barrier((ssm_got, r_last))
     out_ssm = ssm_got[:, :ch_piece].reshape(S * ch_piece, cols).astype(F32)
     out_down = down_got[:, :ff_piece].reshape(S * ff_piece, cols).astype(F32)
-    ff_mine = ff // S
-    moves = []
-    at = np.arange(ff_mine)
-    for source in range(S):
-        chunk, inside = at // (S * ff_piece), at % (S * ff_piece)
-        table = np.where(
-            inside // ff_piece == source, chunk * ff_piece + inside % ff_piece, -1
-        )[None].astype(np.int32)
-        moves.append((0, source, 0, 0, table))
-        moves.append((0, source, 1, 0, np.where(table >= 0, table + half_wide, -1)))
-    out_gate, out_up = regroup(
-        [gu_got], [jax.ShapeDtypeStruct((rows_d, ff_mine), F32)] * 2, moves
-    )
-
     (inner_blocks,) = regroup(
         [r_last],
         [SHAPE((S // 2, rows_d, mix_mine // S), BF)],

time: 824 us -> 801 us (0.972)
  matrix products: 97.4 us -> 82.4 us
    dot_general x18 -> x17, matrix products: 81.8 us -> 67.6 us  [dot(): lax.dot_general(left_op, right_op, (((left_dim,), (right_dim,)), ((), ())...]
  transfers between devices with their start and end apart: 13 -> 13, of which waited for: 4 -> 4; matrix products, arithmetic and copies ran while one was open for 23% -> 23% of each run, Pallas kernels for 47% -> 48%
where the time goes in v5:
time: 801 us; the launch traced here: 794 us
  Pallas kernels  496 us (62%)
  local copies, waits for them, and re-layouts  91.4 us (11%)
  matrix products  82.4 us (10%)
  waiting for transfers between devices  57.4 us (7%)
  other arithmetic  30.9 us (4%)
  starting transfers between devices  19.5 us (2%)
  between operations  15.9 us (2%)
    pallas_call x1, Pallas kernels, ffn_rows(): pl.pallas_call(partial(ffn_kernel, size, tok, micro), out_shape=[shape((r...  78.7 us
    pallas_call x1, Pallas kernels, scan_backward(): pl.pallas_call(partial(scan_back_kernel, size, len(helds), groups), grid=...  72.3 us
    dot_general x17, matrix products, dot(): lax.dot_general(left_op, right_op, (((left_dim,), (right_dim,)), ((), ())...  67.6 us
    pallas_call x1, Pallas kernels, mixer_rows(): pl.pallas_call(partial(mixer_kernel, size, tok, micro), out_shape=[shape(...  57 us
    pallas_call x2, Pallas kernels, gather_rows(): pl.pallas_call(partial(gather_kernel, size, rows // micro), out_shape=SHA...  49.2 us
    all_to_all x4, waiting for transfers between devices, exchange(): return lax.all_to_all(rows, 'fsdp', split_axis=0, concat_axis=0, tiled=True)  37.4 us
    pallas_call x1, Pallas kernels, deal(): pl.pallas_call(partial(deal_kernel, count, size, first), out_shape=[SHAPE...  35.1 us
    pallas_call x1, Pallas kernels, scan_forward(): pl.pallas_call(partial(scan_kernel, size, lane_groups(channels)), grid=(m...  32.6 us
  transfers between devices with their start and end apart: 13, of which 4 were waited for; matrix products, arithmetic and copies ran while one was open for 23% of the time, Pallas kernels for 48%

profile of v5, /device:TPU:0, one launch (start us, length us, event | category | flops | bytes accessed | tf_op | source)
XLA Modules:
  0.0 793.6 jit_solution(13361651213672924131)
XLA Ops:
  9.7 6.1 regroup.7
  20.5 6.3 all-to-all-start.1
  28.0 32.0 %all-to-all-done.1 = bf16[8,24,1600]{2,1,0:T(8,128)(2,1)S(1)} async-done(((bf16[8,24,1600]{2,1,0:T(8,128)(2,1)}), bf16[8,24,1600]{2,1,0:T(8,128)(2,1)S(1)}, u32[]{:S(2)}, u32[]{:S(2)}) %all-to-all-start.1) | async-done | bytes 614432 | tf_op jit(solution)/shard_map/all_to_all | solution.py:119
  69.8 25.0 %gather_rows.2 = bf16[768,1600]{1,0:T(8,128)(2,1)} custom-call(bf16[192,1600]{1,0:T(8,128)(2,1)} %get-tuple-element.311.own.refs_3_.x_ref), custom_call_target="tpu_custom_call" | custom-call | tf_op jit(solution)/shard_map/gather_rows/pallas_call | solution.py:777
  94.8 5.4 all-to-all-done
  101.3 24.2 %gather_rows.3.refs_1_ = bf16[768,1600]{1,0:T(8,128)(2,1)} custom-call(bf16[192,1600]{1,0:T(8,128)(2,1)} %convolution_convert_fusion.9.own.refs_3_), custom_call_target="tpu_custom_call" | custom-call | tf_op jit(solution)/shard_map/gather_rows/pallas_call | solution.py:777
  125.5 17.0 %all-gather.5.cloned.1.call-done.whole_w = bf16[1600,3152]{1,0:T(8,128)(2,1)} async-done(((bf16[200,3152]{1,0:T(8,128)(2,1)}), bf16[1600,3152]{1,0:T(8,128)(2,1)}) %all-gather.5.cloned.1.call-update) | async-done | bytes 10086416 | tf_op jit(solution)/shard_map/all_gather | solution.py:1419
  144.5 6.3 regroup.8
  153.5 11.1 %fusion.7.opened_ref.refs_5_.refs_7_.refs_4_ = bf16[768,2496]{1,0:T(8,128)(2,1)} fusion(bf16[1600,3152]{1,0:T(8,128)(2,1)} %all-gather.5.cloned.1.call-done.whole_w, bf16[768,1600]{1,0:T(8,128)(2,1)S(1)} %copy-done.5, f32[1600]{0:T(1024)S(1)} %copy-done.32, f32[768]{0:T(1024)S(1)} %add_rsqrt_fusion), kind=kOutput, calls=%fused_computation.15 | convolution fusion | flops 6141001728 | bytes 14492928 | tf_op jit(solution)/shard_map/dot_general | solution.py:31
  175.5 18.1 %attention.1 = (f32[768,448]{1,0:T(8,128)}, f32[2,7,384,384]{3,2,1,0:T(8,128)}, f32[8,768]{1,0:T(8,128)}) custom-call(bf16[768,2496]{1,0:T(8,128)(2,1)} %fusion.7.opened_ref.refs_5_.refs_7_.refs_4_, s32[768,1]{1,0:T(8,128)} %bitcast.153), custom_call_target="tpu_custom_call" | custom-call | tf_op jit(solution)/shard_map/attention/pallas_call | solution.py:1041
  195.7 21.5 %ssm_open.1 = (f32[768,896]{1,0:T(8,128)}, f32[768,896]{1,0:T(8,128)}, bf16[144,768]{1,0:T(8,128)(2,1)}, bf16[32,768]{1,0:T(8,128)(2,1)}) custom-call(bf16[768,2496]{1,0:T(8,128)(2,1)} %fusion.7.opened_ref.refs_5_.refs_7_.refs_4_, s32[768,1]{1,0:T(8,128)} %bitcast.154, f32[8,896]{1,0:T(8,128)} %slice_select_fusion.taps.refs_6_, ...), custom_call_target="tpu_custom_call" | custom-call | tf_op jit(solution)/shard_map/ssm_open/pallas_call | solution.py:1112
  222.5 6.7 broadcast_in_dim.138.refs_2_.refs_3_
  229.2 32.6 %scan_forward.1 = (f32[768,896]{1,0:T(8,128)}, f32[768,896]{1,0:T(8,128)}, f32[8,768]{1,0:T(8,128)}, bf16[4,448,400]{2,1,0:T(8,128)(2,1)}) custom-call(f32[768,896]{1,0:T(8,128)} %get-tuple-element.119.refs_0_.refs_6_.refs_1_, f32[768,896]{1,0:T(8,128)} %get-tuple-element.120.refs_1_.refs_2_, bf16[768,32,128]{2,1,0:T(8,128)(2,1)} %broadcast_in_dim.138.refs_2_.refs_3_, ...), custom_call_target="tpu_custom_call" | custom-call | tf_op jit(solution)/shard_map/scan_forward/pallas_call | solution.py:412
  265.2 57.0 %mixer_rows.1 = (bf16[768,448]{1,0:T(8,128)(2,1)}, bf16[768,896]{1,0:T(8,128)(2,1)}, f32[768,128]{1,0:T(8,128)}, f32[768,128]{1,0:T(8,128)}, f32[192,1600]{1,0:T...) custom-call(f32[768,448]{1,0:T(8,128)} %get-tuple-element.118.refs_0_.refs_3_, ...), custom_call_target="tpu_custom_call" | custom-call | tf_op jit(solution)/shard_map/mixer_rows/pallas_call | solution.py:870
  322.2 78.7 %ffn_rows.1 = (bf16[768,1408]{1,0:T(8,128)(2,1)}, bf16[768,2816]{1,0:T(8,128)(2,1)}, bf16[4,192,1600]{2,1,0:T(8,128)(2,1)}, f32[192,1600]{1,0:T(8,128)}, f32[1,1...) custom-call(bf16[768,1600]{1,0:T(8,128)(2,1)} %get-tuple-element.128.refs_0_, ...), custom_call_target="tpu_custom_call" | custom-call | tf_op jit(solution)/shard_map/ffn_rows/pallas_call | solution.py:984
  408.0 8.7 %convolution_convert_fusion.1 = bf16[1408,1600]{1,0:T(8,128)(2,1)} fusion(bf16[768,1408]{1,0:T(8,128)(2,1)} %get-tuple-element.133, bf16[768,1600]{1,0:T(8,128)(2,1)} %gather_rows.3.refs_1_), kind=kOutput, calls=%fused_computation.5 | convolution fusion | flops 3462553600 | bytes 9125888 | tf_op jit(solution)/shard_map/dot_general | solution.py:31
  416.7 27.1 %branch_back.1 = (bf16[768,448]{1,0:T(8,128)(2,1)}, f32[768,896]{1,0:T(8,128)}, bf16[768,896]{1,0:T(8,128)(2,1)}, f32[1,448]{1,0:T(1,128)}, f32[1,896]{1,0:T(1,128)}, /*index=5*/f32[1,896]{1,0:T(1,128)}) custom-call(bf16[768,1600]{1,0:T(8,128)(2,1)} %get-tuple-element.134.refs_0_, bf16[4,448,400]{2,1,0:T(8,128)(2,1)} %get-tuple-element.125.refs_7_.refs_1_, ...), custom_call_target="tpu_custom_call" | custom-call | tf_op jit(solution)/shard_map/branch_back/pallas_call | solution.py:1281
  447.3 5.1 multiply_reduce_fusion
  463.4 4.5 select_reduce_fusion
  470.6 5.2 concatenate.43
  475.8 9.1 %convolution_convert_fusion = bf16[1600,1600]{1,0:T(8,128)(2,1)} fusion(bf16[768,1600]{1,0:T(8,128)(2,1)} %concatenate.43, bf16[768,1600]{1,0:T(8,128)(2,1)S(1)} %copy-done.6, f32[1600]{0:T(1024)S(1)} %copy-done.32, f32[768]{0:T(1024)S(1)} %add_rsqrt_fusion), kind=kOutput, calls=%fused_computation.4 | convolution fusion | flops 3939635200 | bytes 10044672 | tf_op jit(solution)/shard_map/dot_general | solution.py:31
  484.9 6.6 multiply_convert_fusion.1
  491.5 8.9 %fusion.12.rest = bf16[768,1600]{1,0:T(8,128)(2,1)} fusion(bf16[768,1600]{1,0:T(8,128)(2,1)S(1)} %copy-done.10, bf16[1600,3152]{1,0:T(8,128)(2,1)} %all-gather.5.cloned.1.call-done.whole_w), kind=kOutput, calls=%fused_computation.19 | convolution fusion | flops 3933388800 | bytes 10240000 | tf_op jit(solution)/shard_map/dot_general | solution.py:31
  515.1 72.3 %scan_backward.1 = (f32[768,896]{1,0:T(8,128)}, bf16[768,896]{1,0:T(8,128)(2,1)}, f32[2,1,896]{2,1,0:T(1,128)}, f32[2,16,896]{2,1,0:T(8,128)}, f32[2,8,6144]{2,1...) custom-call(f32[768,896]{1,0:T(8,128)} %get-tuple-element.146.refs_0, ...), custom_call_target="tpu_custom_call" | custom-call | tf_op jit(solution)/shard_map/scan_backward/pallas_call | solution.py:550
  591.5 22.9 %ssm_close.1 = (bf16[144,768]{1,0:T(8,128)(2,1)}, bf16[768,896]{1,0:T(8,128)(2,1)}, f32[8,896]{1,0:T(8,128)}) custom-call(bf16[768,896]{1,0:T(8,128)(2,1)} %get-tuple-element.152.refs_0_, f32[768,16]{1,0:T(8,128)} %reshape_squeeze.9.refs_1_, f32[768,16]{1,0:T(8,128)} %reshape_squeeze.10.refs_2_, f32[768,896]{1,0:T(8,128)} %get-tuple-element.155.refs_3_, ...), custom_call_target="tpu_custom_call" | custom-call | tf_op jit(solution)/shard_map/ssm_close/pallas_call | solution.py:1190
  628.3 4.4 convolution_convert_fusion.2
  632.7 8.2 %concatenate.53 = bf16[1600,1552]{1,0:T(8,128)(2,1)} concatenate(bf16[1600,896]{1,0:T(8,128)(2,1)} %convolution_convert_fusion.2, bf16[1600,400]{1,0:T(8,128)(2,1)S(1)} %pad_maximum_fusion.1, bf16[1600,256]{1,0:T(8,128)(2,1)S(1)} %bitcast.164), dimensions={1} | concatenate | bytes 9932800 | tf_op jit(solution)/shard_map/concatenate | solution.py:1658
  655.6 30.0 %close_rows.1 = (bf16[192,1600]{1,0:T(8,128)(2,1)}, f32[1,1600]{1,0:T(1,128)}) custom-call(bf16[768,1600]{1,0:T(8,128)(2,1)} %fusion.12.rest, bf16[768,896]{1,0:T(8,128)(2,1)} %get-tuple-element.168.d_inner, bf16[1600,3152]{1,0:T(8,128)(2,1)} %all-gather.5.cloned.1.call-done.whole_w, bf16[192,1600]{1,0:T(8,128)(2,1)} %get-tuple-element.311.own.refs_3_.x_ref, ...), custom_call_target="tpu_custom_call" | custom-call | tf_op jit(solution)/shard_map/close_rows/pallas_call | solution.py:1355
  685.6 4.1 regroup.11
  692.1 5.1 all-to-all-start.3
  704.0 35.1 %deal.1 = (bf16[4,112,400]{2,1,0:T(8,128)(2,1)}, bf16[4,176,400]{2,1,0:T(8,128)(2,1)}, bf16[4,200,560]{2,1,0:T(8,128)(2,1)}, bf16[4,200,400]{2,1,0:T(8,128)(2,1)}) custom-call(bf16[4,112,400]{2,1,0:T(8,128)(2,1)} %get-tuple-element.183.refs_0_, bf16[4,176,400]{2,1,0:T(8,128)(2,1)} %get-tuple-element.184.refs_1_, ...), custom_call_target="tpu_custom_call" | custom-call | bytes 1024 | tf_op jit(solution)/shard_map/deal/pallas_call | solution.py:699
  749.2 23.0 %last_exchange.1 = (bf16[4,112,256]{2,1,0:T(8,128)(2,1)}, bf16[4,200,400]{2,1,0:T(8,128)(2,1)}, f32[64,128]{1,0:T(8,128)}) custom-call(bf16[4,112,256]{2,1,0:T(8,128)(2,1)} %broadcast_in_dim.155.refs_0_, bf16[2,200,400]{2,1,0:T(8,128)(2,1)} %regroup.12.refs_1_, f32[64,128]{1,0:T(8,128)} %bitcast.194), custom_call_target="tpu_custom_call" | custom-call | bytes 1024 | tf_op jit(solution)/shard_map/last_exchange/pallas_call | solution.py:751
  (320 shorter events, 149.4 us)
Async XLA Ops:
  7.2 12.1 %copy-start = (bf16[2,96,1600]{2,1,0:T(8,128)(2,1)S(1)}, bf16[2,96,1600]{2,1,0:T(8,128)(2,1)}, u32[]{:S(2)}) copy-start(bf16[2,96,1600]{2,1,0:T(8,128)(2,1)} %param.62) | copy-start | bytes 1843204
  7.2 135.3 %all-gather.5.cloned.1.call-start = ((), (), s32[]{:S(2)}) async-start(), calls=%async_computation.9 | async-start | bytes 11520000 | tf_op jit(solution)/shard_map/all_gather | solution.py:1419
  19.3 41.5 %copy-start.25 = (s32[192]{0:T(256)}, s32[192]{0:T(256)S(1)}, u32[]{:S(2)}) copy-start(s32[192]{0:T(256)S(1)} %multiply_add_fusion) | copy-start | bytes 2308
  19.3 46.4 %copy-start.13 = (bf16[400,1600]{1,0:T(8,128)(2,1)S(1)}, bf16[400,1600]{1,0:T(8,128)(2,1)}, u32[]{:S(2)}) copy-start(bf16[400,1600]{1,0:T(8,128)(2,1)} %param.75) | copy-start | bytes 3840004
  20.5 39.5 %all-to-all-start.1 = ((bf16[8,24,1600]{2,1,0:T(8,128)(2,1)}), bf16[8,24,1600]{2,1,0:T(8,128)(2,1)S(1)}, u32[]{:S(2)}, u32[]{:S(2)}) async-start(bf16[8,24,1600]{2,1,0:T(8,128)(2,1)} %bitcast.7), calls=%async_computation.1 | async-start | bytes 1277952 | tf_op jit(solution)/shard_map/all_to_all | solution.py:119
  60.8 39.3 %all-to-all-start = ((bf16[8,24,1600]{2,1,0:T(8,128)(2,1)}), bf16[8,24,1600]{2,1,0:T(8,128)(2,1)S(1)}, u32[]{:S(2)}, u32[]{:S(2)}) async-start(bf16[8,24,1600]{2,1,0:T(8,128)(2,1)} %bitcast.4), calls=%async_computation | async-start | bytes 1277952 | tf_op jit(solution)/shard_map/all_to_all | solution.py:119
  64.8 200.4 %all-gather.7.cloned.1.call-start = ((), (), s32[]{:S(2)}) async-start(), calls=%async_computation.10 | async-start | bytes 3354624 | tf_op jit(solution)/shard_map/all_gather | solution.py:1419
  65.7 34.5 %copy-start.28 = (s32[192]{0:T(256)}, s32[192]{0:T(256)S(1)}, u32[]{:S(2)}) copy-start(s32[192]{0:T(256)S(1)} %eq.91) | copy-start | bytes 2308
  94.8 48.0 %copy-start.11 = (bf16[688,1600]{1,0:T(8,128)(2,1)S(1)}, bf16[688,1600]{1,0:T(8,128)(2,1)}, u32[]{:S(2)}) copy-start(bf16[688,1600]{1,0:T(8,128)(2,1)} %param.79) | copy-start | bytes 6604804
  142.6 179.6 %all-gather.11.cloned.1.call-start = ((), (), s32[]{:S(2)}) async-start(), calls=%async_computation.12 | async-start | bytes 5271552 | tf_op jit(solution)/shard_map/all_gather | solution.py:1419
  153.4 322.4 %copy-start.40 = (f32[768]{0:T(1024)}, f32[768]{0:T(1024)S(1)}, u32[]{:S(2)}) copy-start(f32[768]{0:T(1024)S(1)} %add_rsqrt_fusion) | copy-start | bytes 9220
  153.4 11.8 %copy-start.39 = (s32[2,1,3]{2,1,0:T(1,128)S(1)}, s32[2,1,3]{2,1,0:T(1,128)}, u32[]{:S(2)}) copy-start(s32[2,1,3]{2,1,0:T(1,128)} %param.65) | copy-start | bytes 76
  153.4 13.3 %copy-start.49 = (s32[5]{0:T(128)S(1)}, s32[5]{0:T(128)}, u32[]{:S(2)}) copy-start(s32[5]{0:T(128)} %constant.195.clone) | copy-start | bytes 64
  153.4 14.4 %copy-start.27 = (f32[3200]{0:T(1024)S(1)}, f32[3200]{0:T(1024)}, u32[]{:S(2)}) copy-start(f32[3200]{0:T(1024)} %param.73) | copy-start | bytes 38404
  153.4 15.2 %copy-start.30 = (f32[1600]{0:T(1024)S(1)}, f32[1600]{0:T(1024)}, u32[]{:S(2)}) copy-start(f32[1600]{0:T(1024)} %param.76) | copy-start | bytes 19204
  153.5 15.8 %copy-start.31 = (f32[1600]{0:T(1024)S(1)}, f32[1600]{0:T(1024)}, u32[]{:S(2)}) copy-start(f32[1600]{0:T(1024)} %param.72) | copy-start | bytes 19204
  164.5 157.7 %all-gather.9.cloned.1.call-start = ((), (), s32[]{:S(2)}) async-start(), calls=%async_computation.11 | async-start | bytes 10137600 | tf_op jit(solution)/shard_map/all_gather | solution.py:1419
  165.1 335.3 %reduce-scatter.10.cloned.1.call-start = ((), (), s32[]{:S(2)}) async-start(), calls=%async_computation.13 | async-start | bytes 10137600 | tf_op jit(solution)/shard_map/reduce_scatter | solution.py:1428
  175.5 19.5 %copy-start.45 = (pred[8]{0:T(512)(128)(4,1)S(1)}, pred[8]{0:T(512)(128)(4,1)}, u32[]{:S(2)}) copy-start(pred[8]{0:T(512)(128)(4,1)} %constant.184.clone.1) | copy-start | bytes 28
  194.4 27.5 %copy-start.20 = (f32[23,896]{1,0:T(8,128)}, f32[23,896]{1,0:T(8,128)S(1)}, u32[]{:S(2)}) copy-start(f32[23,896]{1,0:T(8,128)S(1)} %convert_bitcast_fusion.4) | copy-start | bytes 247300
  401.0 243.5 %reduce-scatter.16.cloned.1.call-start = ((), (), s32[]{:S(2)}) async-start(), calls=%async_computation.16 | async-start | bytes 5990400
  500.4 154.3 %reduce-scatter.14.cloned.1.call-start = ((), (), s32[]{:S(2)}) async-start(), calls=%async_computation.15 | async-start | bytes 5271552 | tf_op jit(solution)/shard_map/reduce_scatter | solution.py:1428
  501.2 154.4 %reduce-scatter.12.cloned.1.call-start = ((), (), s32[]{:S(2)}) async-start(), calls=%async_computation.14 | async-start | bytes 3354624 | tf_op jit(solution)/shard_map/reduce_scatter | solution.py:1428
  502.0 243.4 %reduce-scatter.18.cloned.1.call-start = ((), (), s32[]{:S(2)}) async-start(), calls=%async_computation.17 | async-start | bytes 5990400
  591.5 22.9 %copy-start.2 = (f32[768,896]{1,0:T(8,128)S(1)}, f32[768,896]{1,0:T(8,128)}, u32[]{:S(2)}) copy-start(f32[768,896]{1,0:T(8,128)} %get-tuple-element.119.refs_0_.refs_6_.refs_1_) | copy-start | bytes 8257540
  648.1 43.9 %all-to-all-start.2 = ((bf16[8,24,1600]{2,1,0:T(8,128)(2,1)}), bf16[8,24,1600]{2,1,0:T(8,128)(2,1)S(1)}, u32[]{:S(2)}, u32[]{:S(2)}) async-start(bf16[8,24,1600]{2,1,0:T(8,128)(2,1)} %bitcast.168), calls=%async_computation.3 | async-start | bytes 1277952 | tf_op jit(solution)/shard_map/all_to_all | solution.py:119
  685.6 11.6 %copy-start.44 = (f32[1,448]{1,0:T(1,128)S(1)}, f32[1,448]{1,0:T(1,128)}, u32[]{:S(2)}) copy-start(f32[1,448]{1,0:T(1,128)} %get-tuple-element.190) | copy-start | bytes 5380
  685.6 11.7 %copy-start.42 = (f32[1,896]{1,0:T(1,128)S(1)}, f32[1,896]{1,0:T(1,128)}, u32[]{:S(2)}) copy-start(f32[1,896]{1,0:T(1,128)} %get-tuple-element.191) | copy-start | bytes 10756
  685.6 12.2 %copy-start.36 = (f32[1,1600]{1,0:T(1,128)S(1)}, f32[1,1600]{1,0:T(1,128)}, u32[]{:S(2)}) copy-start(f32[1,1600]{1,0:T(1,128)} %get-tuple-element.192) | copy-start | bytes 19204
  689.8 13.0 %copy-start.26 = (s32[192]{0:T(256)S(1)}, s32[192]{0:T(256)}, u32[]{:S(2)}) copy-start(s32[192]{0:T(256)} %copy-done.25) | copy-start | bytes 2308
  692.1 11.9 %copy-start.37 = (f32[1,1600]{1,0:T(1,128)S(1)}, f32[1,1600]{1,0:T(1,128)}, u32[]{:S(2)}) copy-start(f32[1,1600]{1,0:T(1,128)} %get-tuple-element.196) | copy-start | bytes 19204
  692.1 50.9 %all-to-all-start.3 = ((bf16[8,24,1600]{2,1,0:T(8,128)(2,1)}), bf16[8,24,1600]{2,1,0:T(8,128)(2,1)}, u32[]{:S(2)}, u32[]{:S(2)}) async-start(bf16[8,24,1600]{2,1,0:T(8,128)(2,1)} %bitcast.166), calls=%async_computation.6 | async-start | bytes 1277952 | tf_op jit(solution)/shard_map/all_to_all | solution.py:119
  (37 other events, 152.9 us)
Sparse Core Ops, SparseCore 0:
  18.4 124.0 all-gather.4
  144.8 35.8 all-gather.6
  182.9 50.2 all-gather.10
  235.3 86.0 all-gather.8
  401.1 93.3 reduce-scatter.9
  500.6 58.8 reduce-scatter.15
  561.8 53.8 reduce-scatter.13
  618.1 37.4 reduce-scatter.11
  658.0 70.2 reduce-scatter.17

commit v6 on v5

--- a/solution.py
+++ b/solution.py
@@ -901,8 +901,8 @@
 
 def ffn_kernel(size, tok, micro, *refs):
     ffn, cot, hidden, cot_own, gain, w_gu, w_down = refs[:7]
-    act, dgu, down, d_hidden, d_gain, dmix, grad = refs[7:14]
-    sent, got, dmix_own, send, recv, own_sem, dmix_send, dmix_recv, turned = refs[14:]
+    act, dgu, down, d_hidden, d_gain, dmix, grad, grad_down = refs[7:15]
+    sent, got, dmix_own, send, recv, own_sem, dmix_send, dmix_recv, turned, turned_act = refs[15:]
     here, row = lax.axis_index("seq"), lax.axis_index("fsdp")
     wide = w_down.shape[0]
     meet(pack_peers(size))
@@ -970,6 +970,12 @@
     lax.fori_loop(0, pieces // 4, columns, 0)
     relay.pass_on()
     lax.fori_loop(pieces // 4, pieces, columns, 0)
+    for low, high in spans_of(wide, 2 * LANES):
+        turned_act[low:high, :] = act[:, low:high].T
+    for first, last in spans_of(D):
+        for low, high in spans_of(wide):
+            part = dot(turned_act[low:high, :], cot[:, first:last], 1, 0)
+            grad_down[low:high, first:last] = part.astype(BF)
     relay.finish()
 
 
@@ -991,9 +997,10 @@
             shape((1, D), F32),
             shape((rows, D), BF),
             shape((D, 2 * wide), BF),
+            shape((wide, D), BF),
         ],
         in_specs=[vmem] * 7,
-        out_specs=[vmem] * 5 + [hbm, vmem],
+        out_specs=[vmem] * 5 + [hbm, vmem, vmem],
         scratch_shapes=[
             pltpu.VMEM((size, own, D), BF),
             pltpu.VMEM((6, tok, D), BF),
@@ -1002,6 +1009,7 @@
             dma((micro,)),
             *crossing_sems(),
             pltpu.VMEM((D, rows), BF),
+            pltpu.VMEM((wide, rows), BF),
         ],
         compiler_params=pltpu.CompilerParams(
             collective_id=collective_id, has_side_effects=True, vmem_limit_bytes=VMEM_BYTES
@@ -1545,13 +1553,11 @@
         micro,
         4,
     )
-    act_low, _, down_parts, d_hidden, d_gain_ffn, dmix_low, gu_whole = ffn_rows(
+    _, _, down_parts, d_hidden, d_gain_ffn, dmix_low, gu_whole, down_whole = ffn_rows(
         ffn_low, cot_rows, hidden, cot_own, gain_ffn[None], w_gu, w_down_part, micro, 5
     )
 
     r_gu = scatter(gu_whole)
-    down_whole = dot(act_low, cot_rows, 0, 0).astype(BF)
-    dmix_low, down_whole = lax.optimization_barrier((dmix_low, down_whole))
     r_down = scatter(down_whole)
     d_context, d_core, d_gate_z, d_gain_att, d_gain_ssm, d_skip = branch_back(
         dmix_low,

time: 801 us -> 797 us (level)
  matrix products: 82.4 us -> 74.1 us
    dot_general x17 -> x16, matrix products: 67.6 us -> 59.3 us  [dot(): lax.dot_general(left_op, right_op, (((left_dim,), (right_dim,)), ((), ())...]
  transfers between devices with their start and end apart: 13 -> 13, of which waited for: 4 -> 5; matrix products, arithmetic and copies ran while one was open for 23% -> 22% of each run, Pallas kernels for 48% -> 48%
where the time goes in v6:
time: 797 us; the launch traced here: 790 us
  Pallas kernels  495 us (62%)
  local copies, waits for them, and re-layouts  91.7 us (12%)
  matrix products  74.1 us (9%)
  waiting for transfers between devices  62.7 us (8%)
  other arithmetic  30.9 us (4%)
  starting transfers between devices  20 us (3%)
  between operations  15.9 us (2%)
    pallas_call x1, Pallas kernels, ffn_rows(): pl.pallas_call(partial(ffn_kernel, size, tok, micro), out_shape=[shape((r...  79.8 us
    pallas_call x1, Pallas kernels, scan_backward(): pl.pallas_call(partial(scan_back_kernel, size, len(helds), groups), grid=...  72.9 us
    dot_general x16, matrix products, dot(): lax.dot_general(left_op, right_op, (((left_dim,), (right_dim,)), ((), ())...  59.3 us
    pallas_call x1, Pallas kernels, mixer_rows(): pl.pallas_call(partial(mixer_kernel, size, tok, micro), out_shape=[shape(...  57.2 us
    pallas_call x2, Pallas kernels, gather_rows(): pl.pallas_call(partial(gather_kernel, size, rows // micro), out_shape=SHA...  49.2 us
    all_to_all x4, waiting for transfers between devices, exchange(): return lax.all_to_all(rows, 'fsdp', split_axis=0, concat_axis=0, tiled=True)  37.4 us
    pallas_call x1, Pallas kernels, deal(): pl.pallas_call(partial(deal_kernel, count, size, first), out_shape=[SHAPE...  35.1 us
    pallas_call x1, Pallas kernels, scan_forward(): pl.pallas_call(partial(scan_kernel, size, lane_groups(channels)), grid=(m...  32.4 us
  transfers between devices with their start and end apart: 13, of which 5 were waited for; matrix products, arithmetic and copies ran while one was open for 22% of the time, Pallas kernels for 48%

profile of v6, /device:TPU:0, one launch (start us, length us, event | category | flops | bytes accessed | tf_op | source)
XLA Modules:
  0.0 789.9 jit_solution(6184156420900808442)
XLA Ops:
  9.7 6.1 regroup.7
  20.5 6.3 all-to-all-start.1
  28.0 32.0 %all-to-all-done.1 = bf16[8,24,1600]{2,1,0:T(8,128)(2,1)S(1)} async-done(((bf16[8,24,1600]{2,1,0:T(8,128)(2,1)}), bf16[8,24,1600]{2,1,0:T(8,128)(2,1)S(1)}, u32[]{:S(2)}, u32[]{:S(2)}) %all-to-all-start.1) | async-done | bytes 614432 | tf_op jit(solution)/shard_map/all_to_all | solution.py:119
  69.8 25.0 %gather_rows.2 = bf16[768,1600]{1,0:T(8,128)(2,1)} custom-call(bf16[192,1600]{1,0:T(8,128)(2,1)} %get-tuple-element.307.own.refs_3_.x_ref), custom_call_target="tpu_custom_call" | custom-call | tf_op jit(solution)/shard_map/gather_rows/pallas_call | solution.py:777
  94.8 5.4 all-to-all-done
  101.3 24.2 %gather_rows.3.refs_1_ = bf16[768,1600]{1,0:T(8,128)(2,1)} custom-call(bf16[192,1600]{1,0:T(8,128)(2,1)} %convolution_convert_fusion.8.own.refs_3_), custom_call_target="tpu_custom_call" | custom-call | tf_op jit(solution)/shard_map/gather_rows/pallas_call | solution.py:777
  125.5 17.0 %all-gather.5.cloned.1.call-done.whole_w = bf16[1600,3152]{1,0:T(8,128)(2,1)} async-done(((bf16[200,3152]{1,0:T(8,128)(2,1)}), bf16[1600,3152]{1,0:T(8,128)(2,1)}) %all-gather.5.cloned.1.call-update) | async-done | bytes 10086416 | tf_op jit(solution)/shard_map/all_gather | solution.py:1427
  144.8 6.3 regroup.8
  153.8 11.1 %fusion.7.opened_ref.refs_5_.refs_7_.refs_4_ = bf16[768,2496]{1,0:T(8,128)(2,1)} fusion(bf16[1600,3152]{1,0:T(8,128)(2,1)} %all-gather.5.cloned.1.call-done.whole_w, bf16[768,1600]{1,0:T(8,128)(2,1)S(1)} %copy-done.5, f32[1600]{0:T(1024)S(1)} %copy-done.32, f32[768]{0:T(1024)S(1)} %add_rsqrt_fusion), kind=kOutput, calls=%fused_computation.14 | convolution fusion | flops 6141001728 | bytes 14492928 | tf_op jit(solution)/shard_map/dot_general | solution.py:31
  175.9 18.0 %attention.1 = (f32[768,448]{1,0:T(8,128)}, f32[2,7,384,384]{3,2,1,0:T(8,128)}, f32[8,768]{1,0:T(8,128)}) custom-call(bf16[768,2496]{1,0:T(8,128)(2,1)} %fusion.7.opened_ref.refs_5_.refs_7_.refs_4_, s32[768,1]{1,0:T(8,128)} %bitcast.151), custom_call_target="tpu_custom_call" | custom-call | tf_op jit(solution)/shard_map/attention/pallas_call | solution.py:1049
  195.9 21.6 %ssm_open.1 = (f32[768,896]{1,0:T(8,128)}, f32[768,896]{1,0:T(8,128)}, bf16[144,768]{1,0:T(8,128)(2,1)}, bf16[32,768]{1,0:T(8,128)(2,1)}) custom-call(bf16[768,2496]{1,0:T(8,128)(2,1)} %fusion.7.opened_ref.refs_5_.refs_7_.refs_4_, s32[768,1]{1,0:T(8,128)} %bitcast.152, f32[8,896]{1,0:T(8,128)} %slice_select_fusion.taps.refs_6_, ...), custom_call_target="tpu_custom_call" | custom-call | tf_op jit(solution)/shard_map/ssm_open/pallas_call | solution.py:1120
  222.8 6.7 broadcast_in_dim.138.refs_2_.refs_3_
  229.5 32.4 %scan_forward.1 = (f32[768,896]{1,0:T(8,128)}, f32[768,896]{1,0:T(8,128)}, f32[8,768]{1,0:T(8,128)}, bf16[4,448,400]{2,1,0:T(8,128)(2,1)}) custom-call(f32[768,896]{1,0:T(8,128)} %get-tuple-element.117.refs_0_.refs_6_.refs_1_, f32[768,896]{1,0:T(8,128)} %get-tuple-element.118.refs_1_.refs_2_, bf16[768,32,128]{2,1,0:T(8,128)(2,1)} %broadcast_in_dim.138.refs_2_.refs_3_, ...), custom_call_target="tpu_custom_call" | custom-call | tf_op jit(solution)/shard_map/scan_forward/pallas_call | solution.py:412
  265.3 57.2 %mixer_rows.1 = (bf16[768,448]{1,0:T(8,128)(2,1)}, bf16[768,896]{1,0:T(8,128)(2,1)}, f32[768,128]{1,0:T(8,128)}, f32[768,128]{1,0:T(8,128)}, f32[192,1600]{1,0:T...) custom-call(f32[768,448]{1,0:T(8,128)} %get-tuple-element.116.refs_0_.refs_3_, ...), custom_call_target="tpu_custom_call" | custom-call | tf_op jit(solution)/shard_map/mixer_rows/pallas_call | solution.py:870
  322.5 79.8 %ffn_rows.1 = (bf16[768,1408]{1,0:T(8,128)(2,1)}, bf16[768,2816]{1,0:T(8,128)(2,1)}, bf16[4,192,1600]{2,1,0:T(8,128)(2,1)}, f32[192,1600]{1,0:T(8,128)}, f32[1,1...) custom-call(bf16[768,1600]{1,0:T(8,128)(2,1)} %get-tuple-element.126.refs_0_, ...), custom_call_target="tpu_custom_call" | custom-call | tf_op jit(solution)/shard_map/ffn_rows/pallas_call | solution.py:990
  409.4 26.6 %branch_back.1 = (bf16[768,448]{1,0:T(8,128)(2,1)}, f32[768,896]{1,0:T(8,128)}, bf16[768,896]{1,0:T(8,128)(2,1)}, f32[1,448]{1,0:T(1,128)}, f32[1,896]{1,0:T(1,128)}, /*index=5*/f32[1,896]{1,0:T(1,128)}) custom-call(bf16[768,1600]{1,0:T(8,128)(2,1)} %get-tuple-element.130.refs_0_, bf16[4,448,400]{2,1,0:T(8,128)(2,1)} %get-tuple-element.123.refs_7_.refs_1_, ...), custom_call_target="tpu_custom_call" | custom-call | tf_op jit(solution)/shard_map/branch_back/pallas_call | solution.py:1289
  439.8 5.1 multiply_reduce_fusion
  455.9 4.5 select_reduce_fusion
  463.1 5.2 concatenate.43
  468.3 8.9 %convolution_convert_fusion = bf16[1600,1600]{1,0:T(8,128)(2,1)} fusion(bf16[768,1600]{1,0:T(8,128)(2,1)} %concatenate.43, bf16[768,1600]{1,0:T(8,128)(2,1)S(1)} %copy-done.6, f32[1600]{0:T(1024)S(1)} %copy-done.32, f32[768]{0:T(1024)S(1)} %add_rsqrt_fusion), kind=kOutput, calls=%fused_computation.4 | convolution fusion | flops 3939635200 | bytes 10044672 | tf_op jit(solution)/shard_map/dot_general | solution.py:31
  477.2 6.7 multiply_convert_fusion.1
  483.9 9.3 %fusion.12.rest = bf16[768,1600]{1,0:T(8,128)(2,1)} fusion(bf16[768,1600]{1,0:T(8,128)(2,1)S(1)} %copy-done.10, bf16[1600,3152]{1,0:T(8,128)(2,1)} %all-gather.5.cloned.1.call-done.whole_w), kind=kOutput, calls=%fused_computation.18 | convolution fusion | flops 3933388800 | bytes 10240000 | tf_op jit(solution)/shard_map/dot_general | solution.py:31
  510.6 72.9 %scan_backward.1 = (f32[768,896]{1,0:T(8,128)}, bf16[768,896]{1,0:T(8,128)(2,1)}, f32[2,1,896]{2,1,0:T(1,128)}, f32[2,16,896]{2,1,0:T(8,128)}, f32[2,8,6144]{2,1...) custom-call(f32[768,896]{1,0:T(8,128)} %get-tuple-element.142.refs_0, ...), custom_call_target="tpu_custom_call" | custom-call | tf_op jit(solution)/shard_map/scan_backward/pallas_call | solution.py:550
  587.7 22.6 %ssm_close.1 = (bf16[144,768]{1,0:T(8,128)(2,1)}, bf16[768,896]{1,0:T(8,128)(2,1)}, f32[8,896]{1,0:T(8,128)}) custom-call(bf16[768,896]{1,0:T(8,128)(2,1)} %get-tuple-element.148.refs_0_, f32[768,16]{1,0:T(8,128)} %reshape_squeeze.9.refs_1_, f32[768,16]{1,0:T(8,128)} %reshape_squeeze.10.refs_2_, f32[768,896]{1,0:T(8,128)} %get-tuple-element.151.refs_3_, ...), custom_call_target="tpu_custom_call" | custom-call | tf_op jit(solution)/shard_map/ssm_close/pallas_call | solution.py:1198
  624.2 4.4 convolution_convert_fusion.1
  628.7 8.2 %concatenate.53 = bf16[1600,1552]{1,0:T(8,128)(2,1)} concatenate(bf16[1600,896]{1,0:T(8,128)(2,1)} %convolution_convert_fusion.1, bf16[1600,400]{1,0:T(8,128)(2,1)S(1)} %pad_maximum_fusion.1, bf16[1600,256]{1,0:T(8,128)(2,1)S(1)} %bitcast.162), dimensions={1} | concatenate | bytes 9932800 | tf_op jit(solution)/shard_map/concatenate | solution.py:1664
  644.1 4.1 all-to-all-start.2
  654.5 28.1 %close_rows.1 = (bf16[192,1600]{1,0:T(8,128)(2,1)}, f32[1,1600]{1,0:T(1,128)}) custom-call(bf16[768,1600]{1,0:T(8,128)(2,1)} %fusion.12.rest, bf16[768,896]{1,0:T(8,128)(2,1)} %get-tuple-element.164.d_inner, bf16[1600,3152]{1,0:T(8,128)(2,1)} %all-gather.5.cloned.1.call-done.whole_w, bf16[192,1600]{1,0:T(8,128)(2,1)} %get-tuple-element.307.own.refs_3_.x_ref, ...), custom_call_target="tpu_custom_call" | custom-call | tf_op jit(solution)/shard_map/close_rows/pallas_call | solution.py:1363
  682.6 4.2 regroup.11
  689.2 4.8 all-to-all-start.3
  700.8 35.1 %deal.1 = (bf16[4,112,400]{2,1,0:T(8,128)(2,1)}, bf16[4,176,400]{2,1,0:T(8,128)(2,1)}, bf16[4,200,560]{2,1,0:T(8,128)(2,1)}, bf16[4,200,400]{2,1,0:T(8,128)(2,1)}) custom-call(bf16[4,112,400]{2,1,0:T(8,128)(2,1)} %get-tuple-element.179.refs_0_, bf16[4,176,400]{2,1,0:T(8,128)(2,1)} %get-tuple-element.180.refs_1_, ...), custom_call_target="tpu_custom_call" | custom-call | bytes 1024 | tf_op jit(solution)/shard_map/deal/pallas_call | solution.py:699
  746.1 22.5 %last_exchange.1 = (bf16[4,112,256]{2,1,0:T(8,128)(2,1)}, bf16[4,200,400]{2,1,0:T(8,128)(2,1)}, f32[64,128]{1,0:T(8,128)}) custom-call(bf16[4,112,256]{2,1,0:T(8,128)(2,1)} %broadcast_in_dim.155.refs_0_, bf16[2,200,400]{2,1,0:T(8,128)(2,1)} %regroup.12.refs_1_, f32[64,128]{1,0:T(8,128)} %bitcast.192), custom_call_target="tpu_custom_call" | custom-call | bytes 1024 | tf_op jit(solution)/shard_map/last_exchange/pallas_call | solution.py:751
  (319 shorter events, 151.8 us)
Async XLA Ops:
  7.2 12.1 %copy-start = (bf16[2,96,1600]{2,1,0:T(8,128)(2,1)S(1)}, bf16[2,96,1600]{2,1,0:T(8,128)(2,1)}, u32[]{:S(2)}) copy-start(bf16[2,96,1600]{2,1,0:T(8,128)(2,1)} %param.62) | copy-start | bytes 1843204
  7.2 135.3 %all-gather.5.cloned.1.call-start = ((), (), s32[]{:S(2)}) async-start(), calls=%async_computation.9 | async-start | bytes 11520000 | tf_op jit(solution)/shard_map/all_gather | solution.py:1427
  19.3 41.5 %copy-start.25 = (s32[192]{0:T(256)}, s32[192]{0:T(256)S(1)}, u32[]{:S(2)}) copy-start(s32[192]{0:T(256)S(1)} %multiply_add_fusion) | copy-start | bytes 2308
  19.3 46.4 %copy-start.13 = (bf16[400,1600]{1,0:T(8,128)(2,1)S(1)}, bf16[400,1600]{1,0:T(8,128)(2,1)}, u32[]{:S(2)}) copy-start(bf16[400,1600]{1,0:T(8,128)(2,1)} %param.75) | copy-start | bytes 3840004
  20.5 39.5 %all-to-all-start.1 = ((bf16[8,24,1600]{2,1,0:T(8,128)(2,1)}), bf16[8,24,1600]{2,1,0:T(8,128)(2,1)S(1)}, u32[]{:S(2)}, u32[]{:S(2)}) async-start(bf16[8,24,1600]{2,1,0:T(8,128)(2,1)} %bitcast.7), calls=%async_computation.1 | async-start | bytes 1277952 | tf_op jit(solution)/shard_map/all_to_all | solution.py:119
  60.8 39.3 %all-to-all-start = ((bf16[8,24,1600]{2,1,0:T(8,128)(2,1)}), bf16[8,24,1600]{2,1,0:T(8,128)(2,1)S(1)}, u32[]{:S(2)}, u32[]{:S(2)}) async-start(bf16[8,24,1600]{2,1,0:T(8,128)(2,1)} %bitcast.4), calls=%async_computation | async-start | bytes 1277952 | tf_op jit(solution)/shard_map/all_to_all | solution.py:119
  64.8 200.5 %all-gather.7.cloned.1.call-start = ((), (), s32[]{:S(2)}) async-start(), calls=%async_computation.10 | async-start | bytes 3354624 | tf_op jit(solution)/shard_map/all_gather | solution.py:1427
  65.7 34.5 %copy-start.28 = (s32[192]{0:T(256)}, s32[192]{0:T(256)S(1)}, u32[]{:S(2)}) copy-start(s32[192]{0:T(256)S(1)} %eq.91) | copy-start | bytes 2308
  94.8 48.4 %copy-start.11 = (bf16[688,1600]{1,0:T(8,128)(2,1)S(1)}, bf16[688,1600]{1,0:T(8,128)(2,1)}, u32[]{:S(2)}) copy-start(bf16[688,1600]{1,0:T(8,128)(2,1)} %param.79) | copy-start | bytes 6604804
  142.6 180.0 %all-gather.11.cloned.1.call-start = ((), (), s32[]{:S(2)}) async-start(), calls=%async_computation.12 | async-start | bytes 5271552 | tf_op jit(solution)/shard_map/all_gather | solution.py:1427
  153.8 314.5 %copy-start.40 = (f32[768]{0:T(1024)}, f32[768]{0:T(1024)S(1)}, u32[]{:S(2)}) copy-start(f32[768]{0:T(1024)S(1)} %add_rsqrt_fusion) | copy-start | bytes 9220
  153.8 11.8 %copy-start.39 = (s32[2,1,3]{2,1,0:T(1,128)S(1)}, s32[2,1,3]{2,1,0:T(1,128)}, u32[]{:S(2)}) copy-start(s32[2,1,3]{2,1,0:T(1,128)} %param.65) | copy-start | bytes 76
  153.8 13.3 %copy-start.49 = (s32[5]{0:T(128)S(1)}, s32[5]{0:T(128)}, u32[]{:S(2)}) copy-start(s32[5]{0:T(128)} %constant.195.clone) | copy-start | bytes 64
  153.8 14.4 %copy-start.27 = (f32[3200]{0:T(1024)S(1)}, f32[3200]{0:T(1024)}, u32[]{:S(2)}) copy-start(f32[3200]{0:T(1024)} %param.73) | copy-start | bytes 38404
  153.8 15.2 %copy-start.30 = (f32[1600]{0:T(1024)S(1)}, f32[1600]{0:T(1024)}, u32[]{:S(2)}) copy-start(f32[1600]{0:T(1024)} %param.76) | copy-start | bytes 19204
  153.8 15.8 %copy-start.31 = (f32[1600]{0:T(1024)S(1)}, f32[1600]{0:T(1024)}, u32[]{:S(2)}) copy-start(f32[1600]{0:T(1024)} %param.72) | copy-start | bytes 19204
  164.9 157.6 %all-gather.9.cloned.1.call-start = ((), (), s32[]{:S(2)}) async-start(), calls=%async_computation.11 | async-start | bytes 10137600 | tf_op jit(solution)/shard_map/all_gather | solution.py:1427
  165.5 330.6 %reduce-scatter.10.cloned.1.call-start = ((), (), s32[]{:S(2)}) async-start(), calls=%async_computation.13 | async-start | bytes 10137600 | tf_op jit(solution)/shard_map/reduce_scatter | solution.py:1436
  175.9 19.3 %copy-start.45 = (pred[8]{0:T(512)(128)(4,1)S(1)}, pred[8]{0:T(512)(128)(4,1)}, u32[]{:S(2)}) copy-start(pred[8]{0:T(512)(128)(4,1)} %constant.184.clone.1) | copy-start | bytes 28
  194.6 27.6 %copy-start.20 = (f32[23,896]{1,0:T(8,128)}, f32[23,896]{1,0:T(8,128)S(1)}, u32[]{:S(2)}) copy-start(f32[23,896]{1,0:T(8,128)S(1)} %convert_bitcast_fusion.4) | copy-start | bytes 247300
  402.4 238.0 %reduce-scatter.16.cloned.1.call-start = ((), (), s32[]{:S(2)}) async-start(), calls=%async_computation.16 | async-start | bytes 5990400
  496.1 155.0 %reduce-scatter.14.cloned.1.call-start = ((), (), s32[]{:S(2)}) async-start(), calls=%async_computation.15 | async-start | bytes 5271552 | tf_op jit(solution)/shard_map/reduce_scatter | solution.py:1436
  496.9 157.6 %reduce-scatter.12.cloned.1.call-start = ((), (), s32[]{:S(2)}) async-start(), calls=%async_computation.14 | async-start | bytes 3354624 | tf_op jit(solution)/shard_map/reduce_scatter | solution.py:1436
  497.6 244.5 %reduce-scatter.18.cloned.1.call-start = ((), (), s32[]{:S(2)}) async-start(), calls=%async_computation.17 | async-start | bytes 5990400
  587.7 22.6 %copy-start.2 = (f32[768,896]{1,0:T(8,128)S(1)}, f32[768,896]{1,0:T(8,128)}, u32[]{:S(2)}) copy-start(f32[768,896]{1,0:T(8,128)} %get-tuple-element.117.refs_0_.refs_6_.refs_1_) | copy-start | bytes 8257540
  644.1 45.1 %all-to-all-start.2 = ((bf16[8,24,1600]{2,1,0:T(8,128)(2,1)}), bf16[8,24,1600]{2,1,0:T(8,128)(2,1)S(1)}, u32[]{:S(2)}, u32[]{:S(2)}) async-start(bf16[8,24,1600]{2,1,0:T(8,128)(2,1)} %bitcast.166), calls=%async_computation.3 | async-start | bytes 1277952 | tf_op jit(solution)/shard_map/all_to_all | solution.py:119
  682.6 11.3 %copy-start.44 = (f32[1,448]{1,0:T(1,128)S(1)}, f32[1,448]{1,0:T(1,128)}, u32[]{:S(2)}) copy-start(f32[1,448]{1,0:T(1,128)} %get-tuple-element.186) | copy-start | bytes 5380
  682.6 11.4 %copy-start.42 = (f32[1,896]{1,0:T(1,128)S(1)}, f32[1,896]{1,0:T(1,128)}, u32[]{:S(2)}) copy-start(f32[1,896]{1,0:T(1,128)} %get-tuple-element.187) | copy-start | bytes 10756
  682.6 11.9 %copy-start.36 = (f32[1,1600]{1,0:T(1,128)S(1)}, f32[1,1600]{1,0:T(1,128)}, u32[]{:S(2)}) copy-start(f32[1,1600]{1,0:T(1,128)} %get-tuple-element.188) | copy-start | bytes 19204
  686.8 12.7 %copy-start.26 = (s32[192]{0:T(256)S(1)}, s32[192]{0:T(256)}, u32[]{:S(2)}) copy-start(s32[192]{0:T(256)} %copy-done.25) | copy-start | bytes 2308
  689.2 11.6 %copy-start.37 = (f32[1,1600]{1,0:T(1,128)S(1)}, f32[1,1600]{1,0:T(1,128)}, u32[]{:S(2)}) copy-start(f32[1,1600]{1,0:T(1,128)} %get-tuple-element.192) | copy-start | bytes 19204
  689.2 50.7 %all-to-all-start.3 = ((bf16[8,24,1600]{2,1,0:T(8,128)(2,1)}), bf16[8,24,1600]{2,1,0:T(8,128)(2,1)}, u32[]{:S(2)}, u32[]{:S(2)}) async-start(bf16[8,24,1600]{2,1,0:T(8,128)(2,1)} %bitcast.164), calls=%async_computation.6 | async-start | bytes 1277952 | tf_op jit(solution)/shard_map/all_to_all | solution.py:119
  (37 other events, 153.4 us)
Sparse Core Ops, SparseCore 0:
  18.4 124.1 all-gather.4
  144.7 35.8 all-gather.6
  182.8 50.3 all-gather.10
  235.3 86.0 all-gather.8
  402.5 93.5 reduce-scatter.9
  498.4 59.5 reduce-scatter.15
  560.4 53.8 reduce-scatter.13
  616.7 37.7 reduce-scatter.11
  656.8 72.6 reduce-scatter.17
